TPU v7x, 32 devices: a whole 2x2x4 slice. The times are simulated.
32 devices in a mesh: section: 2 (over x), seq: 8 (over z, core), tp: 2 (over y).
Axes of the slice: x: 2, y: 2, z: 4, core: 2. Of those that a mesh axis runs over, the one named last changes fastest.
Arguments:
- image: bfloat16 [2, 1024, 3072], P('section', 'seq'), may hold values from -6 to 6
- text_kv: bfloat16 [2, 512, 2, 2048], P('section', 'seq', None, 'tp'), may hold values from -6 to 6
- modulation: float32 [2, 3, 3072], P('section'), may hold values from -3 to 3
- w_qkv: bfloat16 [3072, 3, 2048], P('seq', None, 'tp'), may hold values from -0.109375 to 0.109375
- w_out: bfloat16 [2048, 3072], P('tp'), may hold values from -6 to 6
- q_gain: float32 [128], replicated, may hold values from 0.1 to 1.9
- k_gain: float32 [128], replicated, may hold values from 0.1 to 1.9
- region_mask: int32 [8, 8], P('seq'), may hold values from 0 to 1, as said below
Outputs:
- block_out: bfloat16 [2, 1024, 3072], P('section', 'seq', 'tp')
Inputs may be any that keep to these rules, and one draw needn't show every extreme that they name: `region_mask`: each query tile reads its own drawn share of condition tiles, from none or one eighth up to all of them.
All inputs are finite; a program needn't handle non-finite values.
Results may differ from a plain program's by a relative error of at most 0.011.
Values may be sent and summed in bfloat16 or wider, within the bound.
No kernel may reach another device: no remote copies, remote signals or barrier semaphores. Data moves between devices by JAX's collectives and lax.ppermute only.
A program may use at most 128 MiB of HBM per device.

v0:
```python
import jax
import jax.numpy as jnp
from jax import lax
from jax.sharding import PartitionSpec as P

HEAD_DIM = 128
GRID_W = 64
TILE = 128


def passed_along(x, axis, by):
    size = lax.axis_size(axis)
    pairs = [(i, i + by) for i in range(size) if 0 <= i + by < size]
    return lax.ppermute(x, axis, pairs)


def rms_rows(x, gain):
    return x * lax.rsqrt(jnp.mean(x * x, axis=-1, keepdims=True) + 1e-06) * gain


def axis_freqs(width):
    return 10000.0 ** (-jnp.arange(0, width, 2).astype(jnp.float32) / width)


def rope_tables(rows_index, time_index):
    first = HEAD_DIM // 8
    rest = (HEAD_DIM - first) // 2
    row_pos = (rows_index // GRID_W).astype(jnp.float32)
    col_pos = (rows_index % GRID_W).astype(jnp.float32)
    time_pos = jnp.zeros_like(row_pos) + time_index
    angles = jnp.concatenate(
        [
            time_pos[:, None] * axis_freqs(first)[None],
            row_pos[:, None] * axis_freqs(rest)[None],
            col_pos[:, None] * axis_freqs(rest)[None],
        ],
        axis=-1,
    )
    return (jnp.cos(angles), jnp.sin(angles))


def apply_rope(x, cosine, sine):
    rows, heads_here = (x.shape[0], x.shape[1])
    pairs = x.reshape(rows, heads_here, HEAD_DIM // 2, 2)
    first = pairs[..., 0]
    second = pairs[..., 1]
    cosine = cosine[:, None, :]
    sine = sine[:, None, :]
    rotated = jnp.stack([first * cosine - second * sine, first * sine + second * cosine], axis=-1)
    return rotated.reshape(rows, heads_here, HEAD_DIM)


def attend_piece(carry, keys_vals, query, keep):
    num, den = carry
    rows = keys_vals.shape[0]
    heads_local = query.shape[1]
    piece_k = keys_vals[:, 0].reshape(rows, heads_local, HEAD_DIM)
    piece_v = keys_vals[:, 1].reshape(rows, heads_local, HEAD_DIM)
    scores = jnp.einsum("qhd,khd->hqk", query, piece_k, preferred_element_type=jnp.float32) * (
        1.0 / HEAD_DIM**0.5
    )
    weights = jnp.exp(scores)
    if keep is not None:
        weights = jnp.where(keep[None], weights, 0.0)
    den = den + jnp.sum(weights, axis=-1)
    num = num + jnp.einsum(
        "hqk,khd->hqd", weights.astype(jnp.bfloat16), piece_v, preferred_element_type=jnp.float32
    )
    return (num, den)


def body(image, text_kv, modulation, w_qkv, w_out, q_gain, k_gain, region_mask):
    img_rows = image.shape[1]
    width_local = w_qkv.shape[2]
    heads_local = width_local // HEAD_DIM
    tokens = image[0].astype(jnp.float32)
    mods = modulation[0]
    mean = jnp.mean(tokens, axis=-1, keepdims=True)
    var = jnp.mean((tokens - mean) ** 2, axis=-1, keepdims=True)
    normed = ((tokens - mean) * lax.rsqrt(var + 1e-06) * (1.0 + mods[1]) + mods[0]).astype(
        jnp.bfloat16
    )
    qkv = jnp.einsum(
        "td,dcf->tcf",
        normed,
        lax.all_gather(w_qkv, "seq", axis=0, tiled=True),
        preferred_element_type=jnp.float32,
    )
    section_index = lax.axis_index("section")
    time_index = (section_index == 0).astype(jnp.float32)
    rows_index = lax.axis_index("seq") * img_rows + jnp.arange(img_rows, dtype=jnp.int32)
    cosine, sine = rope_tables(rows_index, time_index)
    query = apply_rope(
        rms_rows(qkv[:, 0].reshape(img_rows, heads_local, HEAD_DIM), q_gain), cosine, sine
    ).astype(jnp.bfloat16)
    keys = apply_rope(
        rms_rows(qkv[:, 1].reshape(img_rows, heads_local, HEAD_DIM), k_gain), cosine, sine
    ).astype(jnp.bfloat16)
    values = qkv[:, 2].astype(jnp.bfloat16)
    image_kv = jnp.stack([keys.reshape(img_rows, width_local), values], axis=1)
    own_kv = jnp.concatenate([image_kv, text_kv[0]], axis=0)
    enabled = (section_index == 1).astype(jnp.int32)
    local_mask = region_mask * enabled
    init = (
        jnp.zeros((heads_local, img_rows, HEAD_DIM), jnp.float32),
        jnp.zeros((heads_local, img_rows), jnp.float32),
    )
    carry = attend_piece(init, lax.all_gather(own_kv, "seq", axis=0, tiled=True), query, None)
    cond_local = passed_along(image_kv, "section", 1)
    keep = jnp.repeat(jnp.repeat(local_mask, TILE, axis=0), TILE, axis=1) > 0
    carry = attend_piece(carry, lax.all_gather(cond_local, "seq", axis=0, tiled=True), query, keep)
    num, den = carry
    attn = (num / den[..., None]).astype(jnp.bfloat16)
    attn = jnp.transpose(attn, (1, 0, 2)).reshape(img_rows, width_local)
    term = jnp.dot(attn, w_out, preferred_element_type=jnp.float32)
    branch = lax.psum_scatter(
        term.astype(jnp.bfloat16), "tp", scatter_dimension=1, tiled=True
    ).astype(jnp.float32)
    cols = branch.shape[1]
    offset = lax.axis_index("tp") * cols
    residual = lax.dynamic_slice_in_dim(tokens, offset, cols, 1)
    gate = lax.dynamic_slice_in_dim(mods[2], offset, cols, 0)
    out = residual + gate[None, :] * branch
    return out.astype(jnp.bfloat16)[None]


def solution(mesh):
    return jax.shard_map(
        body,
        mesh=mesh,
        in_specs=(
            P("section", "seq", None),
            P("section", "seq", None, "tp"),
            P("section", None, None),
            P("seq", None, "tp"),
            P("tp", None),
            P(),
            P(),
            P("seq", None),
        ),
        out_specs=P("section", "seq", "tp"),
        check_vma=False,
    )
```

profile of v0, /device:TPU:0, one launch (start us, length us, event | category | flops | bytes accessed | tf_op | source)
XLA Modules:
  0.0 370.5 jit_solution(16559790621854325065)
XLA Ops:
  8.1 0.8 mul.265
  9.0 1.3 convert_reduce_fusion
  11.0 169.0 %all-gather.4.cloned.1.call-done = bf16[3072,3,1024]{2,0,1:T(8,128)(2,1)} async-done(((bf16[384,3,1024]{2,0,1:T(8,128)(2,1)}), bf16[3072,3,1024]{2,0,1:T(8,128)(2,1)}) %all-gather.4.cloned.1.call-update) | async-done | bytes 18874384 | tf_op jit(solution)/shard_map/all_gather | solution.py:86
  180.0 7.8 %fusion.29 = f32[128,3,1024]{2,0,1:T(8,128)S(1)} fusion(bf16[3072,3,1024]{2,0,1:T(8,128)(2,1)} %all-gather.4.cloned.1.call-done, bf16[1,128,3072]{2,1,0:T(8,128)(2,1)S(1)} %copy-done, f32[3072]{0:T(1024)S(1)} %bitcast.85, f32[3072]{0:T(1024)S(1)} %bitcast.86, f32[128]{0:T(128)S(1)} %add_rsqrt_fusion.2, f32[128]{0:T(128)S(1)} %broadcast_multiply_fusion.2), kind=kOutput, calls=%fused_computation.28 | convolution fusion | flops 2418278400 | bytes 21259264 | tf_op jit(solution)/shard_map/td,dcf->tcf/dot_general | solution.py:83
  189.8 1.4 subtract_convert_fusion.1
  192.0 3.4 collective-permute-start
  195.4 11.6 %collective-permute-done = bf16[128,2,1024]{2,0,1:T(8,128)(2,1)S(1)} collective-permute-done((bf16[128,2,1024]{2,0,1:T(8,128)(2,1)S(1)}, bf16[128,2,1024]{2,0,1:T(8,128)(2,1)S(1)}, u32[]{:S(2)}, u32[]{:S(2)}) %collective-permute-start) | collective-permute-done | bytes 524320 | tf_op jit(solution)/shard_map/ppermute | solution.py:14
  207.0 0.8 copy-done.2
  207.9 1.0 pad_maximum_fusion
  210.4 43.9 %all-gather.8.cloned.1.call-done = bf16[1024,2,1024]{2,0,1:T(8,128)(2,1)} async-done(((bf16[128,2,1024]{2,0,1:T(8,128)(2,1)}), bf16[1024,2,1024]{2,0,1:T(8,128)(2,1)}) %all-gather.8.cloned.1.call-update) | async-done | bytes 4194320 | tf_op jit(solution)/shard_map/all_gather | solution.py:111
  254.4 2.9 slice_bitcast_fusion.1
  257.3 2.0 copy.57
  259.3 2.5 copy.53
  261.8 5.1 %fusion.2 = (f32[8,128]{1,0:T(8,128)S(1)}, f32[8,128,1024]{2,1,0:T(8,128)}) fusion(pred[1024]{0:T(1024)(128)(4,1)S(1)} %broadcast_bitcast_fusion, bf16[128,8,128]{2,0,1:T(8,128)(2,1)S(1)} %copy.46, bf16[1024,8,128]{2,1,0:T(8,128)(2,1)} %bitcast.76), kind=kOutput, calls=%fused_computation.5 | convolution fusion | flops 271580160 | bytes 6558720 | tf_op jit(solution)/shard_map/qhd,khd->hqk/dot_general | solution.py:59
  266.9 52.6 %all-gather.6.cloned.1.call-done = bf16[1536,2,1024]{2,0,1:T(8,128)(2,1)} async-done(((bf16[192,2,1024]{2,0,1:T(8,128)(2,1)}), bf16[1536,2,1024]{2,0,1:T(8,128)(2,1)}) %all-gather.6.cloned.1.call-update) | async-done | bytes 6291472 | tf_op jit(solution)/shard_map/all_gather | solution.py:108
  319.5 6.0 %slice_bitcast_fusion = (bf16[192,8,8,128]{3,1,2,0:T(8,128)(2,1)S(1)}, bf16[1536,1,1024]{2,0,1:T(8,128)(2,1)}) fusion(bf16[1536,2,1024]{2,0,1:T(8,128)(2,1)} %all-gather.6.cloned.1.call-done), kind=kLoop, calls=%fused_computation.8 | loop fusion | bytes 12582912
  325.5 0.8 copy.56
  326.3 4.4 %fusion = (f32[8,128]{1,0:T(8,128)S(1)}, f32[8,128,1536]{2,1,0:T(8,128)}) fusion(bf16[128,8,128]{2,0,1:T(8,128)(2,1)S(1)} %copy.46, bf16[1536,8,128]{2,1,0:T(8,128)(2,1)S(1)} %bitcast.74), kind=kOutput, calls=%fused_computation.1 | convolution fusion | flops 405797888 | bytes 9703424 | tf_op jit(solution)/shard_map/qhd,khd->hqk/dot_general | solution.py:59
  330.7 4.8 %copy.52 = bf16[1536,1,1024]{0,2,1:T(8,128)(2,1)} copy(bf16[1536,1,1024]{2,0,1:T(8,128)(2,1)} %get-tuple-element.6) | data formatting | bytes 6291456 | tf_op jit(solution)/shard_map/reshape;squeeze | solution.py:58
  335.5 5.1 %fusion.4 = f32[8,128,128]{1,2,0:T(8,128)S(1)} fusion(bf16[1536,8,128]{0,2,1:T(8,128)(2,1)} %bitcast.73, f32[8,128,1536]{2,1,0:T(8,128)} %get-tuple-element.27), kind=kOutput, calls=%fused_computation.7 | convolution fusion | flops 405798912 | bytes 9961472 | tf_op jit(solution)/shard_map/hqk,khd->hqd/dot_general | solution.py:66
  340.6 3.3 fusion.25
  344.0 1.9 convolution_convert_fusion
  346.1 16.1 %reduce-scatter.2.cloned.1.call-done = bf16[128,1536]{1,0:T(8,128)(2,1)} async-done(((bf16[128,3072]{1,0:T(8,128)(2,1)}), bf16[128,1536]{1,0:T(8,128)(2,1)}) %reduce-scatter.2.cloned.1.call-update) | async-done | bytes 393232 | tf_op jit(solution)/shard_map/reduce_scatter | solution.py:116
  362.2 1.8 fusion.36
  (60 shorter events, 6.7 us)
Async XLA Ops:
  6.5 3.8 %copy-start = (bf16[1,128,3072]{2,1,0:T(8,128)(2,1)S(1)}, bf16[1,128,3072]{2,1,0:T(8,128)(2,1)}, u32[]{:S(2)}) copy-start(bf16[1,128,3072]{2,1,0:T(8,128)(2,1)} %param.8) | copy-start | bytes 2359300
  6.5 4.4 %copy-start.4 = (f32[1,3,3072]{2,0,1:T(1,128)S(1)}, f32[1,3,3072]{2,0,1:T(1,128)}, u32[]{:S(2)}) copy-start(f32[1,3,3072]{2,0,1:T(1,128)} %param.10) | copy-start | bytes 110596
  6.5 173.5 %all-gather.4.cloned.1.call-start = ((), (), s32[]{:S(2)}) async-start(), calls=%async_computation.1 | async-start | bytes 21233664 | tf_op jit(solution)/shard_map/all_gather | solution.py:86
  7.3 247.1 %all-gather.8.cloned.1.call-start = ((), (), s32[]{:S(2)}) async-start(), calls=%async_computation.3 | async-start | bytes 4718592 | tf_op jit(solution)/shard_map/all_gather | solution.py:111
  189.3 18.5 %copy-start.3 = (bf16[1,64,2,1024]{3,2,1,0:T(2,128)(2,1)S(1)}, bf16[1,64,2,1024]{3,2,1,0:T(2,128)(2,1)}, u32[]{:S(2)}) copy-start(bf16[1,64,2,1024]{3,2,1,0:T(2,128)(2,1)} %param.9) | copy-start | bytes 786436
  191.2 18.0 %copy-start.5 = (s32[1,8]{1,0:T(1,128)S(1)}, s32[1,8]{1,0:T(1,128)}, u32[]{:S(2)}) copy-start(s32[1,8]{1,0:T(1,128)} %param.15) | copy-start | bytes 100
  192.0 15.0 %collective-permute-start = (bf16[128,2,1024]{2,0,1:T(8,128)(2,1)S(1)}, bf16[128,2,1024]{2,0,1:T(8,128)(2,1)S(1)}, u32[]{:S(2)}, u32[]{:S(2)}) collective-permute-start(bf16[128,2,1024]{2,0,1:T(8,128)(2,1)S(1)} %pad_maximum_fusion.1), channel_id=1, source_target_pairs={{0,16},{1,17},{2,18},{3,19},{4,20},{5,21},{6,22},{7,23},{8,24},{9,... | collective-permute-start | bytes 1572872 | tf_op jit(solution)/shard_map/ppermute | solution.py:14
  207.0 0.8 copy-start.2
  207.8 111.7 %all-gather.6.cloned.1.call-start = ((), (), s32[]{:S(2)}) async-start(), calls=%async_computation.2 | async-start | bytes 7077888 | tf_op jit(solution)/shard_map/all_gather | solution.py:108
  208.9 153.2 %reduce-scatter.2.cloned.1.call-start = ((), (), s32[]{:S(2)}) async-start(), calls=%async_computation.4 | async-start | bytes 1179648 | tf_op jit(solution)/shard_map/reduce_scatter | solution.py:116
  330.7 13.2 %slice-start = ((s8[6291456]{0:T(1024)(128)(4,1)}), s8[2097152]{0:T(1024)(128)(4,1)S(1)}, s32[]{:S(2)}) async-start(s8[6291456]{0:T(1024)(128)(4,1)} %bitcast.71), calls=%async_computation.5 | async-start | bytes 4194304
  335.5 5.1 %copy-start.1 = (bf16[1024,1,1024]{0,2,1:T(8,128)(2,1)S(1)}, bf16[1024,1,1024]{0,2,1:T(8,128)(2,1)}, u32[]{:S(2)}) copy-start(bf16[1024,1,1024]{0,2,1:T(8,128)(2,1)} %copy.53) | copy-start | bytes 6291460
  335.5 8.4 %slice-start.1 = ((s8[6291456]{0:T(1024)(128)(4,1)}), s8[4194304]{0:T(1024)(128)(4,1)S(1)}, s32[]{:S(2)}) async-start(s8[6291456]{0:T(1024)(128)(4,1)} %bitcast.71), calls=%async_computation.6 | async-start | bytes 8388608
Sparse Core Ops, SparseCore 0:
  9.0 170.9 all-gather.3
  207.9 46.3 all-gather.7
  256.0 63.4 all-gather.5
  346.0 16.0 reduce-scatter.1
where the time goes:
time: 371 us
  waiting for transfers between devices  294 us (79%)
  matrix products  27.6 us (7%)
  local copies, waits for them, and re-layouts  23.1 us (6%)
  between operations  13.5 us (4%)
  other arithmetic  8.76 us (2%)
  starting transfers between devices  3.71 us (1%)
    all_gather x1, waiting for transfers between devices, body(): lax.all_gather(w_qkv, 'seq', axis=0, tiled=True)  169 us
    all_gather x1, waiting for transfers between devices, body(): lax.all_gather(own_kv, 'seq', axis=0, tiled=True)  52.6 us
    all_gather x1, waiting for transfers between devices, body(): lax.all_gather(cond_local, 'seq', axis=0, tiled=True)  43.9 us
    reduce_scatter x1, waiting for transfers between devices, body(): lax.psum_scatter(term.astype(jnp.bfloat16), 'tp', scatter_dimension=1, ti...  16.1 us
    unnamed x23, local copies, waits for them, and re-layouts  12.8 us
    ppermute x1, waiting for transfers between devices, passed_along(): return lax.ppermute(x, axis, pairs)  11.6 us
    dot_general x2, matrix products, attend_piece(): jnp.einsum('qhd,khd->hqk', query, piece_k, preferred_element_type=jnp.flo...  9.48 us
    dot_general x2, matrix products, attend_piece(): jnp.einsum('hqk,khd->hqd', weights.astype(jnp.bfloat16), piece_v, preferr...  8.4 us
  transfers between devices with their start and end apart: 5, of which 5 were waited for; matrix products, arithmetic and copies ran while one was open for 5% of the time, Pallas kernels for 0%

commit v1 on v0

--- a/solution.py
+++ b/solution.py
@@ -1,21 +1,16 @@
+import functools
+
 import jax
 import jax.numpy as jnp
 from jax import lax
+from jax.experimental import pallas as pl
+from jax.experimental.pallas import tpu as pltpu
 from jax.sharding import PartitionSpec as P
 
 HEAD_DIM = 128
 GRID_W = 64
 TILE = 128
-
-
-def passed_along(x, axis, by):
-    size = lax.axis_size(axis)
-    pairs = [(i, i + by) for i in range(size) if 0 <= i + by < size]
-    return lax.ppermute(x, axis, pairs)
-
-
-def rms_rows(x, gain):
-    return x * lax.rsqrt(jnp.mean(x * x, axis=-1, keepdims=True) + 1e-06) * gain
+VMEM_LIMIT = 48 * 1024 * 1024
 
 
 def axis_freqs(width):
@@ -39,6 +34,214 @@
     return (jnp.cos(angles), jnp.sin(angles))
 
 
+def layer_norm(tokens, mods):
+    mean = jnp.mean(tokens, axis=-1, keepdims=True)
+    var = jnp.mean((tokens - mean) ** 2, axis=-1, keepdims=True)
+    return ((tokens - mean) * lax.rsqrt(var + 1e-06) * (1.0 + mods[1]) + mods[0]).astype(
+        jnp.bfloat16
+    )
+
+
+def project_kernel(x_ref, w_ref, cos_ref, sin_ref, gain_ref, q_ref, kv_ref):
+    qkv = jnp.dot(x_ref[...], w_ref[...], preferred_element_type=jnp.float32)
+    cosine = cos_ref[...]
+    sine = sin_ref[...]
+    even = lax.broadcasted_iota(jnp.int32, cosine.shape, 1) % 2 == 0
+
+    def rotated(x, gain):
+        x = x * lax.rsqrt(jnp.mean(x * x, axis=-1, keepdims=True) + 1e-06) * gain
+        other = jnp.where(even, pltpu.roll(x, HEAD_DIM - 1, 1), pltpu.roll(x, 1, 1))
+        return (x * cosine + other * sine).astype(jnp.bfloat16)
+
+    q_ref[...] = rotated(qkv[:, :HEAD_DIM], gain_ref[0:1, :])
+    kv_ref[0] = rotated(qkv[:, HEAD_DIM : 2 * HEAD_DIM], gain_ref[1:2, :])
+    kv_ref[1] = qkv[:, 2 * HEAD_DIM :].astype(jnp.bfloat16)
+
+
+def project_head(x, w, cosine, sine, gains):
+    rows, depth = x.shape
+    block = 256
+    return pl.pallas_call(
+        project_kernel,
+        grid=(rows // block,),
+        in_specs=[
+            pl.BlockSpec((block, depth), lambda i: (i, 0)),
+            pl.BlockSpec(w.shape, lambda i: (0, 0)),
+            pl.BlockSpec((block, HEAD_DIM), lambda i: (i, 0)),
+            pl.BlockSpec((block, HEAD_DIM), lambda i: (i, 0)),
+            pl.BlockSpec((2, HEAD_DIM), lambda i: (0, 0)),
+        ],
+        out_specs=[
+            pl.BlockSpec((block, HEAD_DIM), lambda i: (i, 0)),
+            pl.BlockSpec((2, block, HEAD_DIM), lambda i: (0, i, 0)),
+        ],
+        out_shape=[
+            jax.ShapeDtypeStruct((rows, HEAD_DIM), jnp.bfloat16),
+            jax.ShapeDtypeStruct((2, rows, HEAD_DIM), jnp.bfloat16),
+        ],
+        compiler_params=pltpu.CompilerParams(vmem_limit_bytes=VMEM_LIMIT),
+        cost_estimate=pl.CostEstimate(
+            flops=2 * rows * depth * 3 * HEAD_DIM,
+            bytes_accessed=2 * (rows * depth + w.size),
+            transcendentals=0,
+        ),
+        name="project_head",
+    )(x, w, cosine, sine, gains)
+
+
+def weights_of(query, keys):
+    scores = lax.dot_general(
+        query, keys, (((1,), (1,)), ((), ())), preferred_element_type=jnp.float32
+    )
+    return jnp.exp(scores * (1.0 / HEAD_DIM**0.5))
+
+
+def own_kernel(q_ref, kv_ref, text_ref, num_ref, den_ref):
+    query = q_ref[...]
+    num = jnp.zeros(num_ref.shape, jnp.float32)
+    den = jnp.zeros((num_ref.shape[0], 1), jnp.float32)
+    for ref in (kv_ref, text_ref):
+        weights = weights_of(query, ref[0])
+        den = den + jnp.sum(weights, axis=-1, keepdims=True)
+        num = num + jnp.dot(
+            weights.astype(jnp.bfloat16), ref[1], preferred_element_type=jnp.float32
+        )
+    num_ref[...] = num
+    den_ref[...] = jnp.broadcast_to(den, den_ref.shape)
+
+
+def cond_kernel(mask_ref, q_ref, cond_ref, num_in, den_in, out_ref, num_ref, den_ref):
+    step = pl.program_id(0)
+    query = q_ref[...]
+    rows = query.shape[0]
+    tiles = mask_ref.shape[1]
+    per_block = rows // TILE
+    num_ref[...] = num_in[...]
+    den_ref[...] = den_in[...]
+    row_tile = lax.broadcasted_iota(jnp.int32, (rows, TILE), 0) // TILE
+
+    for j in range(tiles):
+        on = [mask_ref[step * per_block + r, j] for r in range(per_block)]
+        some = functools.reduce(jnp.maximum, on)
+
+        @pl.when(some > 0)
+        def _(j=j, on=on):
+            keep = jnp.zeros((rows, TILE), jnp.float32)
+            for r in range(per_block):
+                keep = jnp.where(row_tile == r, (on[r] > 0).astype(jnp.float32), keep)
+            at = pl.ds(j * TILE, TILE)
+            weights = weights_of(query, cond_ref[0, at, :]) * keep
+            den_ref[...] += jnp.sum(weights, axis=-1, keepdims=True)
+            num_ref[...] += jnp.dot(
+                weights.astype(jnp.bfloat16), cond_ref[1, at, :], preferred_element_type=jnp.float32
+            )
+
+    out_ref[...] = (num_ref[...] / den_ref[...]).astype(jnp.bfloat16)
+
+
+def attend_own(query, kv, text):
+    rows = query.shape[0]
+    block = 256
+    row_spec = pl.BlockSpec((block, HEAD_DIM), lambda i: (i, 0))
+    keys = kv.shape[1] + text.shape[1]
+    return pl.pallas_call(
+        own_kernel,
+        grid=(rows // block,),
+        in_specs=[
+            row_spec,
+            pl.BlockSpec(kv.shape, lambda i: (0, 0, 0)),
+            pl.BlockSpec(text.shape, lambda i: (0, 0, 0)),
+        ],
+        out_specs=[row_spec, row_spec],
+        out_shape=[jax.ShapeDtypeStruct((rows, HEAD_DIM), jnp.float32)] * 2,
+        compiler_params=pltpu.CompilerParams(vmem_limit_bytes=VMEM_LIMIT),
+        cost_estimate=pl.CostEstimate(
+            flops=4 * rows * keys * HEAD_DIM,
+            bytes_accessed=2 * (kv.size + text.size) + 10 * query.size,
+            transcendentals=rows * keys,
+        ),
+        name="attend_own",
+    )(query, kv, text)
+
+
+def attend_cond(mask, query, cond, num, den):
+    rows = query.shape[0]
+    block = 256
+    row_spec = pl.BlockSpec((block, HEAD_DIM), lambda i: (i, 0))
+    keys = cond.shape[1]
+    return pl.pallas_call(
+        cond_kernel,
+        grid=(rows // block,),
+        in_specs=[
+            pl.BlockSpec(memory_space=pltpu.SMEM),
+            row_spec,
+            pl.BlockSpec(cond.shape, lambda i: (0, 0, 0)),
+            row_spec,
+            row_spec,
+        ],
+        out_specs=row_spec,
+        out_shape=jax.ShapeDtypeStruct((rows, HEAD_DIM), jnp.bfloat16),
+        scratch_shapes=[
+            pltpu.VMEM((block, HEAD_DIM), jnp.float32),
+            pltpu.VMEM((block, HEAD_DIM), jnp.float32),
+        ],
+        compiler_params=pltpu.CompilerParams(vmem_limit_bytes=VMEM_LIMIT),
+        cost_estimate=pl.CostEstimate(
+            flops=4 * rows * keys * HEAD_DIM,
+            bytes_accessed=2 * cond.size + 10 * query.size,
+            transcendentals=rows * keys,
+        ),
+        name="attend_cond",
+    )(mask, query, cond, num, den)
+
+
+def head_body(image, text_kv, modulation, w_qkv, w_out, q_gain, k_gain, region_mask):
+    seq = lax.axis_size("seq")
+    img_rows = image.shape[1]
+    depth = w_qkv.shape[0]
+    rows = img_rows * seq
+    section_index = lax.axis_index("section")
+    tokens = image[0].astype(jnp.float32)
+    mods = modulation[0]
+
+    text = lax.all_to_all(
+        text_kv[0].reshape(-1, 2, seq, HEAD_DIM).transpose(2, 1, 0, 3), "seq", 0, 0
+    )
+    text = text.transpose(1, 0, 2, 3).reshape(2, -1, HEAD_DIM)
+    mask = lax.all_gather(region_mask, "seq", axis=0, tiled=True) * (section_index == 1).astype(
+        jnp.int32
+    )
+    w_mine = lax.all_to_all(
+        w_qkv.reshape(depth, 3, seq, HEAD_DIM).transpose(2, 0, 1, 3), "seq", 0, 0
+    ).reshape(depth * seq, 3 * HEAD_DIM)
+    x = lax.all_gather(layer_norm(tokens, mods), "seq", axis=0, tiled=True)
+
+    time_index = (section_index == 0).astype(jnp.float32)
+    cosine, sine = rope_tables(jnp.arange(rows, dtype=jnp.int32), time_index)
+    cosine = jnp.repeat(cosine, 2, axis=-1)
+    sine = jnp.stack([-sine, sine], axis=-1).reshape(rows, HEAD_DIM)
+    query, kv = project_head(x, w_mine, cosine, sine, jnp.stack([q_gain, k_gain]))
+    cond = lax.ppermute(kv, "section", [(0, 1)])
+    num, den = attend_own(query, kv, text)
+    attn = attend_cond(mask, query, cond, num, den)
+
+    attn = lax.all_to_all(attn.reshape(seq, img_rows, HEAD_DIM), "seq", 0, 0)
+    attn = attn.transpose(1, 0, 2).reshape(img_rows, seq * HEAD_DIM)
+    term = jnp.dot(attn, w_out, preferred_element_type=jnp.float32)
+    branch = lax.psum_scatter(
+        term.astype(jnp.bfloat16), "tp", scatter_dimension=1, tiled=True
+    ).astype(jnp.float32)
+    cols = branch.shape[1]
+    offset = lax.axis_index("tp") * cols
+    residual = lax.dynamic_slice_in_dim(image[0], offset, cols, 1).astype(jnp.float32)
+    gate = lax.dynamic_slice_in_dim(mods[2], offset, cols, 0)
+    return (residual + gate[None, :] * branch).astype(jnp.bfloat16)[None]
+
+
+def rms_rows(x, gain):
+    return x * lax.rsqrt(jnp.mean(x * x, axis=-1, keepdims=True) + 1e-06) * gain
+
+
 def apply_rope(x, cosine, sine):
     rows, heads_here = (x.shape[0], x.shape[1])
     pairs = x.reshape(rows, heads_here, HEAD_DIM // 2, 2)
@@ -69,17 +272,13 @@
     return (num, den)
 
 
-def body(image, text_kv, modulation, w_qkv, w_out, q_gain, k_gain, region_mask):
+def token_body(image, text_kv, modulation, w_qkv, w_out, q_gain, k_gain, region_mask):
     img_rows = image.shape[1]
     width_local = w_qkv.shape[2]
     heads_local = width_local // HEAD_DIM
     tokens = image[0].astype(jnp.float32)
     mods = modulation[0]
-    mean = jnp.mean(tokens, axis=-1, keepdims=True)
-    var = jnp.mean((tokens - mean) ** 2, axis=-1, keepdims=True)
-    normed = ((tokens - mean) * lax.rsqrt(var + 1e-06) * (1.0 + mods[1]) + mods[0]).astype(
-        jnp.bfloat16
-    )
+    normed = layer_norm(tokens, mods)
     qkv = jnp.einsum(
         "td,dcf->tcf",
         normed,
@@ -106,7 +305,7 @@
         jnp.zeros((heads_local, img_rows), jnp.float32),
     )
     carry = attend_piece(init, lax.all_gather(own_kv, "seq", axis=0, tiled=True), query, None)
-    cond_local = passed_along(image_kv, "section", 1)
+    cond_local = lax.ppermute(image_kv, "section", [(0, 1)])
     keep = jnp.repeat(jnp.repeat(local_mask, TILE, axis=0), TILE, axis=1) > 0
     carry = attend_piece(carry, lax.all_gather(cond_local, "seq", axis=0, tiled=True), query, keep)
     num, den = carry
@@ -122,6 +321,12 @@
     gate = lax.dynamic_slice_in_dim(mods[2], offset, cols, 0)
     out = residual + gate[None, :] * branch
     return out.astype(jnp.bfloat16)[None]
+
+
+def body(*arrays):
+    w_qkv = arrays[3]
+    one_head_each = w_qkv.shape[2] // HEAD_DIM == lax.axis_size("seq")
+    return (head_body if one_head_each else token_body)(*arrays)
 
 
 def solution(mesh):

time: 371 us -> 217 us (0.58)
  waiting for transfers between devices: 294 us -> 117 us
  blocking collectives: 0 us -> 24.1 us
  matrix products: 27.6 us -> 4.77 us
  Pallas kernels: 0 us -> 12.2 us
  starting transfers between devices: 3.71 us -> 13.8 us
    all_gather x3 -> x1, waiting for transfers between devices: 266 us -> 0.02 us  [head_body(): x = lax.all_gather(layer_norm(tokens, mods), 'seq', axis=0, tiled=True)]
    all_to_all x0 -> x2, waiting for transfers between devices: none -> 94.3 us  [the longest x1 94.3 us: head_body(): lax.all_to_all(w_qkv.reshape(depth, 3, seq, HEAD_DIM).transpose(2, 0, 1,...]
    dot_general x6 -> x1, matrix products: 27.6 us -> 4.77 us  [head_body(): term = jnp.dot(attn, w_out, preferred_element_type=jnp.float32)]
    pallas_call x0 -> x3, Pallas kernels: none -> 12.2 us  [the longest x1 7.25 us: project_head(): pl.pallas_call(project_kernel, grid=(rows // block,), in_specs=[pl.BlockS...]
    all_to_all x0 -> x1, blocking collectives: none -> 12.1 us  [head_body(): attn = lax.all_to_all(attn.reshape(seq, img_rows, HEAD_DIM), 'seq', 0, 0)]
    all_gather x0 -> x1, blocking collectives: none -> 12 us  [head_body(): lax.all_gather(region_mask, 'seq', axis=0, tiled=True)]
    ppermute x1, waiting for transfers between devices: 11.6 us -> 0.01 us  [head_body(): cond = lax.ppermute(kv, 'section', [(0, 1)])]
    all_to_all x0 -> x2, starting transfers between devices: none -> 10.4 us  [the longest x1 6.33 us: head_body(): lax.all_to_all(w_qkv.reshape(depth, 3, seq, HEAD_DIM).transpose(2, 0, 1,...]
  transfers between devices with their start and end apart: 5 -> 5, of which waited for: 5 -> 2; matrix products, arithmetic and copies ran while one was open for 5% -> 10% of each run, Pallas kernels for 0% -> 5%
where the time goes in v1:
time: 217 us
  waiting for transfers between devices  117 us (54%)
  blocking collectives  24.1 us (11%)
  local copies, waits for them, and re-layouts  20.9 us (10%)
  starting transfers between devices  13.8 us (6%)
  between operations  13.6 us (6%)
  Pallas kernels  12.2 us (6%)
  other arithmetic  10.2 us (5%)
  matrix products  4.77 us (2%)
    all_to_all x1, waiting for transfers between devices, head_body(): lax.all_to_all(w_qkv.reshape(depth, 3, seq, HEAD_DIM).transpose(2, 0, 1,...  94.3 us
    reduce_scatter x1, waiting for transfers between devices, head_body(): lax.psum_scatter(term.astype(jnp.bfloat16), 'tp', scatter_dimension=1, ti...  22.7 us
    all_to_all x1, blocking collectives, head_body(): attn = lax.all_to_all(attn.reshape(seq, img_rows, HEAD_DIM), 'seq', 0, 0)  12.1 us
    all_gather x1, blocking collectives, head_body(): lax.all_gather(region_mask, 'seq', axis=0, tiled=True)  12 us
    pallas_call x1, Pallas kernels, project_head(): pl.pallas_call(project_kernel, grid=(rows // block,), in_specs=[pl.BlockS...  7.25 us
    unnamed x16, local copies, waits for them, and re-layouts  6.97 us
    all_to_all x1, starting transfers between devices, head_body(): lax.all_to_all(w_qkv.reshape(depth, 3, seq, HEAD_DIM).transpose(2, 0, 1,...  6.33 us
    dot_general x1, matrix products, head_body(): term = jnp.dot(attn, w_out, preferred_element_type=jnp.float32)  4.77 us
  transfers between devices with their start and end apart: 5, of which 2 were waited for; matrix products, arithmetic and copies ran while one was open for 10% of the time, Pallas kernels for 5%

profile of v1, /device:TPU:0, one launch (start us, length us, event | category | flops | bytes accessed | tf_op | source)
XLA Modules:
  0.0 216.7 jit_solution(8452185842544306624)
XLA Ops:
  7.4 1.3 convert_reduce_fusion
  8.7 1.5 fusion.3
  10.2 1.3 fusion.6
  11.5 3.0 %copy.28 = bf16[384,3,1024]{0,2,1:T(8,128)(2,1)S(1)} copy(bf16[384,3,1024]{2,0,1:T(8,128)(2,1)} %param.11) | data formatting | bytes 4718592 | tf_op args[3]
  14.5 1.8 copy.29
  16.3 6.3 %all-to-all-start = ((bf16[8,384,3,128]{1,3,2,0:T(8,128)(2,1)}), bf16[8,384,3,128]{1,3,2,0:T(8,128)(2,1)S(1)}, u32[]{:S(2)}, u32[]{:S(2)}) async-start(bf16[8,384,3,128]{1,3,2,0:T(8,128)(2,1)} %copy.29), calls=%async_computation | async-start | bytes 4718592 | tf_op jit(solution)/shard_map/all_to_all | solution.py:214
  25.0 1.8 fusion.20
  27.2 1.2 reshape.225
  28.5 1.2 copy.34.sin_ref
  29.7 1.8 reshape.235
  31.5 1.7 copy.36
  33.3 94.3 %all-to-all-done = bf16[8,384,3,128]{1,3,2,0:T(8,128)(2,1)S(1)} async-done(((bf16[8,384,3,128]{1,3,2,0:T(8,128)(2,1)}), bf16[8,384,3,128]{1,3,2,0:T(8,128)(2,1)S(1)}, u32[]{:S(2)}, u32[]{:S(2)}) %all-to-all-start) | async-done | bytes 2359328 | tf_op jit(solution)/shard_map/all_to_all | solution.py:214
  127.6 4.0 %all-to-all-start.1 = ((bf16[8,2,64,128]{3,2,1,0:T(8,128)(2,1)}), bf16[8,2,64,128]{3,2,1,0:T(8,128)(2,1)}, u32[]{:S(2)}, u32[]{:S(2)}) async-start(bf16[8,2,64,128]{3,2,1,0:T(8,128)(2,1)} %copy.36), calls=%async_computation.1 | async-start | bytes 524288 | tf_op jit(solution)/shard_map/all_to_all | solution.py:207
  131.7 3.8 %copy.39 = bf16[8,384,3,128]{3,2,1,0:T(4,128)(2,1)} copy(bf16[8,384,3,128]{1,3,2,0:T(8,128)(2,1)S(1)} %all-to-all-done) | data formatting | bytes 4718592 | tf_op jit(solution)/shard_map/reshape | solution.py:216
  135.5 2.3 %copy.45 = bf16[384,8,3,128]{3,1,2,0:T(8,128)(2,1)S(1)} copy(bf16[384,8,3,128]{3,2,1,0:T(4,128)(2,1)} %bitcast.58) | data formatting | bytes 4718592
  137.8 7.3 %project_head.1 = (bf16[1024,128]{1,0:T(8,128)(2,1)S(1)}, bf16[2,1024,128]{2,1,0:T(8,128)(2,1)}) custom-call(bf16[1024,3072]{1,0:T(8,128)(2,1)} %all-gather.3.cloned.1.call-done.x_ref, bf16[3072,384]{1,0:T(8,128)(2,1)S(1)} %bitcast.55, f32[1024,128]{1,0:T(8,128)S(1)} %copy.33.cos_ref, f32[1024,128]{1,0:T(8,128)S(1)} %copy.34.sin_ref, ...), custom_call_target="tpu_custom_call" | custom-call | flops 2415919104 | bytes 8650752 | tf_op jit(solution)/shard_map/project_head/pallas_call | solution.py:64
  145.8 3.4 %collective-permute-start = (bf16[2,1024,128]{2,1,0:T(8,128)(2,1)}, bf16[2,1024,128]{2,1,0:T(8,128)(2,1)S(1)}, u32[]{:S(2)}, u32[]{:S(2)}) collective-permute-start(bf16[2,1024,128]{2,1,0:T(8,128)(2,1)} %get-tuple-element.10.kv_ref), channel_id=1, source_target_pairs={{0,16},{1,17},{2,18},{3,19},{4,20},{5,21},{6,22},{7,23},{8,24},{9,... | collective-permute-start | bytes 1572872 | tf_op jit(solution)/shard_map/ppermute | solution.py:224
  149.2 12.0 %all-gather = s32[8,1,8]{2,1,0:T(1,128)S(1)} all-gather(s32[1,1,8]{2,1,0:T(1,128)S(1)} %bitcast.65), channel_id=1, replica_groups=mesh['section'=2,'seq'=8,'tp'=2] {'seq'}, dimensions={0}, use_global_device_ids=true | all-gather | bytes 288 | tf_op jit(solution)/shard_map/all_gather | solution.py:211
  163.1 3.7 %attend_own.1 = (f32[1024,128]{1,0:T(8,128)S(1)}, f32[1024,128]{1,0:T(8,128)S(1)}) custom-call(bf16[1024,128]{1,0:T(8,128)(2,1)S(1)} %copy-done.1, bf16[2,1024,128]{2,1,0:T(8,128)(2,1)} %get-tuple-element.10.kv_ref, bf16[2,512,128]{2,1,0:T(8,128)(2,1)S(1)} %bitcast.57), custom_call_target="tpu_custom_call" | custom-call | flops 805306368 | bytes 2097152 | tf_op jit(solution)/shard_map/attend_own/pallas_call | solution.py:147
  166.9 1.2 attend_cond.1
  168.3 12.1 %all_to_all.15 = bf16[8,128,128]{1,2,0:T(8,128)(2,1)S(1)} all-to-all(bf16[8,128,128]{1,2,0:T(8,128)(2,1)S(1)} %copy.38), channel_id=1, replica_groups=mesh['section'=2,'seq'=8,'tp'=2] {'seq'}, dimensions={0} | all-to-all | bytes 524288 | tf_op jit(solution)/shard_map/all_to_all | solution.py:228
  180.4 4.8 %convolution_convert_fusion = bf16[128,3072]{1,0:T(8,128)(2,1)} fusion(bf16[128,1024]{0,1:T(8,128)(2,1)S(1)} %bitcast.60, bf16[1024,3072]{1,0:T(8,128)(2,1)} %param.12), kind=kOutput, calls=%fused_computation | convolution fusion | flops 805699584 | bytes 7340032 | tf_op jit(solution)/shard_map/dot_general | solution.py:230
  185.3 22.7 %reduce-scatter.2.cloned.1.call-done = bf16[128,1536]{1,0:T(8,128)(2,1)} async-done(((bf16[128,3072]{1,0:T(8,128)(2,1)}), bf16[128,1536]{1,0:T(8,128)(2,1)}) %reduce-scatter.2.cloned.1.call-update) | async-done | bytes 393232 | tf_op jit(solution)/shard_map/reduce_scatter | solution.py:231
  208.0 1.9 fusion.8
  (40 shorter events, 6.6 us)
Async XLA Ops:
  6.5 3.7 %copy-start.2 = (bf16[1,128,3072]{2,1,0:T(8,128)(2,1)S(1)}, bf16[1,128,3072]{2,1,0:T(8,128)(2,1)}, u32[]{:S(2)}) copy-start(bf16[1,128,3072]{2,1,0:T(8,128)(2,1)} %param.8) | copy-start | bytes 2359300
  6.5 131.3 %all-gather.3.cloned.1.call-start = ((), (), s32[]{:S(2)}) async-start(), calls=%async_computation.4 | async-start | bytes 7077888 | tf_op jit(solution)/shard_map/all_gather | solution.py:217
  16.3 111.3 %all-to-all-start = ((bf16[8,384,3,128]{1,3,2,0:T(8,128)(2,1)}), bf16[8,384,3,128]{1,3,2,0:T(8,128)(2,1)S(1)}, u32[]{:S(2)}, u32[]{:S(2)}) async-start(bf16[8,384,3,128]{1,3,2,0:T(8,128)(2,1)} %copy.29), calls=%async_computation | async-start | bytes 4718592 | tf_op jit(solution)/shard_map/all_to_all | solution.py:214
  27.2 6.1 %copy-start.5 = (f32[128]{0:T(128)S(1)}, f32[128]{0:T(128)}, u32[]{:S(2)}) copy-start(f32[128]{0:T(128)} %param.14) | copy-start | bytes 1540
  27.2 6.1 %copy-start.6 = (f32[128]{0:T(128)S(1)}, f32[128]{0:T(128)}, u32[]{:S(2)}) copy-start(f32[128]{0:T(128)} %param.13) | copy-start | bytes 1540
  127.6 33.6 %all-to-all-start.1 = ((bf16[8,2,64,128]{3,2,1,0:T(8,128)(2,1)}), bf16[8,2,64,128]{3,2,1,0:T(8,128)(2,1)}, u32[]{:S(2)}, u32[]{:S(2)}) async-start(bf16[8,2,64,128]{3,2,1,0:T(8,128)(2,1)} %copy.36), calls=%async_computation.1 | async-start | bytes 524288 | tf_op jit(solution)/shard_map/all_to_all | solution.py:207
  131.6 76.4 %reduce-scatter.2.cloned.1.call-start = ((), (), s32[]{:S(2)}) async-start(), calls=%async_computation.5 | async-start | bytes 1179648 | tf_op jit(solution)/shard_map/reduce_scatter | solution.py:231
  137.8 11.4 %copy-start.4 = (s32[1,8]{1,0:T(1,128)S(1)}, s32[1,8]{1,0:T(1,128)}, u32[]{:S(2)}) copy-start(s32[1,8]{1,0:T(1,128)} %param.15) | copy-start | bytes 100
  145.1 0.7 copy-start
  145.8 21.1 %collective-permute-start = (bf16[2,1024,128]{2,1,0:T(8,128)(2,1)}, bf16[2,1024,128]{2,1,0:T(8,128)(2,1)S(1)}, u32[]{:S(2)}, u32[]{:S(2)}) collective-permute-start(bf16[2,1024,128]{2,1,0:T(8,128)(2,1)} %get-tuple-element.10.kv_ref), channel_id=1, source_target_pairs={{0,16},{1,17},{2,18},{3,19},{4,20},{5,21},{6,22},{7,23},{8,24},{9,... | collective-permute-start | bytes 1572872 | tf_op jit(solution)/shard_map/ppermute | solution.py:224
  162.2 1.0 copy-start.1
  180.4 27.5 %copy-start.3 = (bf16[1,128,3072]{2,1,0:T(8,128)(2,1)S(1)}, bf16[1,128,3072]{2,1,0:T(8,128)(2,1)}, u32[]{:S(2)}) copy-start(bf16[1,128,3072]{2,1,0:T(8,128)(2,1)} %param.8) | copy-start | bytes 2359300
Sparse Core Ops, SparseCore 0:
  11.6 117.4 all-gather.2
  185.4 22.5 reduce-scatter.1

commit v2 on v0

--- a/solution.py
+++ b/solution.py
@@ -1,21 +1,14 @@
 import jax
 import jax.numpy as jnp
 from jax import lax
+from jax.experimental import pallas as pl
+from jax.experimental.pallas import tpu as pltpu
 from jax.sharding import PartitionSpec as P
 
 HEAD_DIM = 128
 GRID_W = 64
 TILE = 128
-
-
-def passed_along(x, axis, by):
-    size = lax.axis_size(axis)
-    pairs = [(i, i + by) for i in range(size) if 0 <= i + by < size]
-    return lax.ppermute(x, axis, pairs)
-
-
-def rms_rows(x, gain):
-    return x * lax.rsqrt(jnp.mean(x * x, axis=-1, keepdims=True) + 1e-06) * gain
+VMEM_LIMIT = 48 * 1024 * 1024
 
 
 def axis_freqs(width):
@@ -39,6 +32,259 @@
     return (jnp.cos(angles), jnp.sin(angles))
 
 
+def layer_norm(tokens, mods):
+    mean = jnp.mean(tokens, axis=-1, keepdims=True)
+    var = jnp.mean((tokens - mean) ** 2, axis=-1, keepdims=True)
+    return ((tokens - mean) * lax.rsqrt(var + 1e-06) * (1.0 + mods[1]) + mods[0]).astype(
+        jnp.bfloat16
+    )
+
+
+def normed_rotated(x, gain, cosine, sine):
+    x = x * lax.rsqrt(jnp.mean(x * x, axis=-1, keepdims=True) + 1e-06) * gain
+    even = lax.broadcasted_iota(jnp.int32, x.shape, 1) % 2 == 0
+    other = jnp.where(even, pltpu.roll(x, HEAD_DIM - 1, 1), pltpu.roll(x, 1, 1))
+    return (x * cosine + other * sine).astype(jnp.bfloat16)
+
+
+def gather_weights(into, section, mine, peer, kinds):
+    sources, _, half, _ = mine.shape
+    for ref, at in ((mine, section), (peer, 1 - section)):
+        for s in range(sources):
+            rows = pl.ds(pl.multiple_of(s * 2 * half + at * half, half), half)
+            for place, kind in enumerate(kinds):
+                into[rows, place * HEAD_DIM : (place + 1) * HEAD_DIM] = ref[s, kind]
+
+
+def kv_kernel(section_ref, x_ref, mine, peer, cos_ref, sin_ref, gain_ref, kv_ref, w_ref):
+    @pl.when(pl.program_id(0) == 0)
+    def _():
+        gather_weights(w_ref, section_ref[0], mine, peer, (1, 2))
+
+    both = jnp.dot(x_ref[...], w_ref[...], preferred_element_type=jnp.float32)
+    kv_ref[0] = normed_rotated(both[:, :HEAD_DIM], gain_ref[1:2, :], cos_ref[...], sin_ref[...])
+    kv_ref[1] = both[:, HEAD_DIM:].astype(jnp.bfloat16)
+
+
+def weights_of(query, keys):
+    scores = lax.dot_general(
+        query, keys, (((1,), (1,)), ((), ())), preferred_element_type=jnp.float32
+    )
+    return jnp.exp(scores * (1.0 / HEAD_DIM**0.5))
+
+
+def own_kernel(
+    section_ref, x_ref, mine, peer, cos_ref, sin_ref, gain_ref, kv_ref, text_ref,
+    q_ref, num_ref, den_ref, w_ref,
+):
+    @pl.when(pl.program_id(0) == 0)
+    def _():
+        gather_weights(w_ref, section_ref[0], mine, peer, (0,))
+
+    query = jnp.dot(x_ref[...], w_ref[...], preferred_element_type=jnp.float32)
+    query = normed_rotated(query, gain_ref[0:1, :], cos_ref[...], sin_ref[...])
+    q_ref[...] = query
+    num = jnp.zeros(num_ref.shape, jnp.float32)
+    den = jnp.zeros((num_ref.shape[0], 1), jnp.float32)
+    count = text_ref.shape[1] // 2 - 8
+    text_k = text_ref[:, :count, :].reshape(-1, HEAD_DIM)
+    text_v = text_ref[:, count : 2 * count, :].reshape(-1, HEAD_DIM)
+    for keys, values in ((kv_ref[0], kv_ref[1]), (text_k, text_v)):
+        weights = weights_of(query, keys)
+        den = den + jnp.sum(weights, axis=-1, keepdims=True)
+        num = num + jnp.dot(weights.astype(jnp.bfloat16), values, preferred_element_type=jnp.float32)
+    num_ref[...] = num
+    den_ref[...] = jnp.broadcast_to(den, den_ref.shape)
+
+
+def cond_kernel(section_ref, keep_ref, q_ref, cond_ref, num_ref, den_ref, out_ref):
+    section = section_ref[0]
+
+    @pl.when(section == 0)
+    def _():
+        out_ref[...] = (num_ref[...] / den_ref[...]).astype(jnp.bfloat16)
+
+    @pl.when(section != 0)
+    def _():
+        weights = weights_of(q_ref[...], cond_ref[0])
+        rows, keys = weights.shape
+        weights = weights.reshape(rows // TILE, TILE, keys) * keep_ref[0][:, None, :]
+        weights = weights.reshape(rows, keys)
+        den = den_ref[...] + jnp.sum(weights, axis=-1, keepdims=True)
+        num = num_ref[...] + jnp.dot(
+            weights.astype(jnp.bfloat16), cond_ref[1], preferred_element_type=jnp.float32
+        )
+        out_ref[...] = (num / den).astype(jnp.bfloat16)
+
+
+BLOCK = 256
+
+
+def whole(array):
+    return pl.BlockSpec(array.shape, lambda i, *_: (0,) * array.ndim)
+
+
+def by_rows(width):
+    return pl.BlockSpec((BLOCK, width), lambda i, *_: (i, 0))
+
+
+def call(kernel, name, grid, in_specs, out_specs, out_shape, scratch, flops, moved, exps, args):
+    return pl.pallas_call(
+        kernel,
+        grid_spec=pltpu.PrefetchScalarGridSpec(
+            num_scalar_prefetch=1,
+            grid=grid,
+            in_specs=in_specs,
+            out_specs=out_specs,
+            scratch_shapes=scratch,
+        ),
+        out_shape=out_shape,
+        compiler_params=pltpu.CompilerParams(vmem_limit_bytes=VMEM_LIMIT),
+        cost_estimate=pl.CostEstimate(flops=flops, bytes_accessed=moved, transcendentals=exps),
+        name=name,
+    )(*args)
+
+
+def project_kv(section, x, mine, peer, cosine, sine, gains):
+    rows, depth = x.shape
+    return call(
+        kv_kernel, "project_kv", (rows // BLOCK,),
+        [
+            by_rows(depth), whole(mine), whole(peer), by_rows(HEAD_DIM), by_rows(HEAD_DIM),
+            whole(gains),
+        ],
+        pl.BlockSpec((2, BLOCK, HEAD_DIM), lambda i, *_: (0, i, 0)),
+        jax.ShapeDtypeStruct((2, rows, HEAD_DIM), jnp.bfloat16),
+        [pltpu.VMEM((depth, 2 * HEAD_DIM), jnp.bfloat16)],
+        4 * rows * depth * HEAD_DIM, 2 * (x.size + 2 * mine.size), 0,
+        (section, x, mine, peer, cosine, sine, gains),
+    )
+
+
+def attend_own(section, x, mine, peer, cosine, sine, gains, kv, text):
+    rows, depth = x.shape
+    keys = rows + text.shape[0] * (text.shape[1] // 2 - 8)
+    return call(
+        own_kernel, "attend_own", (rows // BLOCK,),
+        [
+            by_rows(depth), whole(mine), whole(peer), by_rows(HEAD_DIM), by_rows(HEAD_DIM),
+            whole(gains), whole(kv), whole(text),
+        ],
+        [by_rows(HEAD_DIM)] * 3,
+        [
+            jax.ShapeDtypeStruct((rows, HEAD_DIM), jnp.bfloat16),
+            jax.ShapeDtypeStruct((rows, HEAD_DIM), jnp.float32),
+            jax.ShapeDtypeStruct((rows, HEAD_DIM), jnp.float32),
+        ],
+        [pltpu.VMEM((depth, HEAD_DIM), jnp.bfloat16)],
+        2 * rows * depth * HEAD_DIM + 4 * rows * keys * HEAD_DIM,
+        2 * (x.size + 2 * mine.size), rows * keys,
+        (section, x, mine, peer, cosine, sine, gains, kv, text),
+    )
+
+
+def attend_cond(section, keep, query, cond, num, den):
+    rows, keys = query.shape[0], cond.shape[1]
+    keep = keep.reshape(rows // BLOCK, BLOCK // TILE, keys)
+    return call(
+        cond_kernel, "attend_cond", (rows // BLOCK,),
+        [
+            pl.BlockSpec((1, BLOCK // TILE, keys), lambda i, *_: (i, 0, 0)),
+            by_rows(HEAD_DIM), whole(cond), by_rows(HEAD_DIM), by_rows(HEAD_DIM),
+        ],
+        by_rows(HEAD_DIM),
+        jax.ShapeDtypeStruct((rows, HEAD_DIM), jnp.bfloat16),
+        [],
+        4 * rows * keys * HEAD_DIM, 2 * cond.size + 10 * query.size, rows * keys,
+        (section, keep, query, cond, num, den),
+    )
+
+
+def sent_kernel(half_ref, attn_ref, w_ref, out_ref):
+    attn = jnp.concatenate([attn_ref[s] for s in range(attn_ref.shape[0])], axis=1)
+    out_ref[...] = jnp.dot(attn, w_ref[...], preferred_element_type=jnp.float32).astype(jnp.bfloat16)
+
+
+def kept_kernel(half_ref, attn_ref, w_ref, image_ref, gate_ref, out_ref):
+    attn = jnp.concatenate([attn_ref[s] for s in range(attn_ref.shape[0])], axis=1)
+    branch = jnp.dot(attn, w_ref[...], preferred_element_type=jnp.float32)
+    out_ref[...] = image_ref[...].astype(jnp.float32) + gate_ref[...] * branch
+
+
+def project_out(half, attn, w_out, image=None, gate=None):
+    sources, rows, _ = attn.shape
+    depth, width = w_out.shape[0], w_out.shape[1] // 2
+    block = 512
+    steps = width // block
+
+    def columns(height):
+        return pl.BlockSpec((height, block), lambda i, half: (0, half[0] * steps + i))
+
+    kept = image is not None
+    return call(
+        kept_kernel if kept else sent_kernel, "out_kept" if kept else "out_sent", (steps,),
+        [whole(attn), columns(depth)] + ([columns(rows), columns(1)] if kept else []),
+        pl.BlockSpec((rows, block), lambda i, half: (0, i)),
+        jax.ShapeDtypeStruct((rows, width), jnp.float32 if kept else jnp.bfloat16),
+        [],
+        2 * rows * depth * width, 2 * depth * width, 0,
+        (half, attn, w_out) + ((image, gate) if kept else ()),
+    )
+
+
+def head_body(image, text_kv, modulation, w_qkv, w_out, q_gain, k_gain, region_mask):
+    seq = lax.axis_size("seq")
+    img_rows = image.shape[1]
+    depth = w_qkv.shape[0]
+    rows = img_rows * seq
+    section = lax.axis_index("section")
+    tp = lax.axis_index("tp")
+    mods = modulation[0]
+    section_at = section.astype(jnp.int32).reshape(1)
+
+    half = depth // 2
+    w_half = lax.dynamic_slice_in_dim(w_qkv.transpose(1, 0, 2), section * half, half, 1)
+    w_half = w_half.reshape(3, half, seq, HEAD_DIM).transpose(2, 0, 1, 3)
+    mine = lax.all_to_all(w_half, "seq", 0, 0)
+    peer = lax.ppermute(mine, "section", [(0, 1), (1, 0)])
+
+    part = img_rows // lax.axis_size("tp")
+    tokens = lax.dynamic_slice_in_dim(image[0], tp * part, part, 0).astype(jnp.float32)
+    x = lax.all_gather(layer_norm(tokens, mods), ("seq", "tp"), axis=0, tiled=True)
+
+    text = text_kv[0].reshape(-1, 2, seq, HEAD_DIM).transpose(2, 1, 0, 3)
+    text = text.reshape(seq, -1, HEAD_DIM)
+    mask = region_mask.astype(jnp.bfloat16)
+    mask = jnp.pad(mask, ((0, 16 - mask.shape[0]), (0, HEAD_DIM - mask.shape[1])))
+    text = lax.all_to_all(
+        jnp.concatenate([text, jnp.broadcast_to(mask, (seq,) + mask.shape)], axis=1), "seq", 0, 0
+    )
+    keep = text[:, -16 : -16 + region_mask.shape[0], : region_mask.shape[1]].astype(jnp.float32)
+    keep = jnp.repeat(keep.reshape(-1, region_mask.shape[1]), TILE, axis=1)
+
+    time_index = (section == 0).astype(jnp.float32)
+    cosine, sine = rope_tables(jnp.arange(rows, dtype=jnp.int32), time_index)
+    cosine = jnp.repeat(cosine, 2, axis=-1)
+    sine = jnp.stack([-sine, sine], axis=-1).reshape(rows, HEAD_DIM)
+    gains = jnp.stack([q_gain, k_gain])
+    kv = project_kv(section_at, x, mine, peer, cosine, sine, gains)
+    cond = lax.ppermute(kv, "section", [(0, 1)])
+    query, num, den = attend_own(section_at, x, mine, peer, cosine, sine, gains, kv, text)
+    attn = attend_cond(section_at, keep, query, cond, num, den)
+
+    attn = lax.all_to_all(attn.reshape(seq, img_rows, HEAD_DIM), "seq", 0, 0)
+    tp_at = tp.astype(jnp.int32).reshape(1)
+    gate = mods[2:3]
+    other = lax.ppermute(project_out(1 - tp_at, attn, w_out), "tp", [(0, 1), (1, 0)])
+    kept = project_out(tp_at, attn, w_out, image[0], gate)
+    gate = lax.dynamic_slice_in_dim(gate, tp * other.shape[1], other.shape[1], 1)
+    return (kept + gate * other.astype(jnp.float32)).astype(jnp.bfloat16)[None]
+
+
+def rms_rows(x, gain):
+    return x * lax.rsqrt(jnp.mean(x * x, axis=-1, keepdims=True) + 1e-06) * gain
+
+
 def apply_rope(x, cosine, sine):
     rows, heads_here = (x.shape[0], x.shape[1])
     pairs = x.reshape(rows, heads_here, HEAD_DIM // 2, 2)
@@ -69,17 +315,13 @@
     return (num, den)
 
 
-def body(image, text_kv, modulation, w_qkv, w_out, q_gain, k_gain, region_mask):
+def token_body(image, text_kv, modulation, w_qkv, w_out, q_gain, k_gain, region_mask):
     img_rows = image.shape[1]
     width_local = w_qkv.shape[2]
     heads_local = width_local // HEAD_DIM
     tokens = image[0].astype(jnp.float32)
     mods = modulation[0]
-    mean = jnp.mean(tokens, axis=-1, keepdims=True)
-    var = jnp.mean((tokens - mean) ** 2, axis=-1, keepdims=True)
-    normed = ((tokens - mean) * lax.rsqrt(var + 1e-06) * (1.0 + mods[1]) + mods[0]).astype(
-        jnp.bfloat16
-    )
+    normed = layer_norm(tokens, mods)
     qkv = jnp.einsum(
         "td,dcf->tcf",
         normed,
@@ -106,7 +348,7 @@
         jnp.zeros((heads_local, img_rows), jnp.float32),
     )
     carry = attend_piece(init, lax.all_gather(own_kv, "seq", axis=0, tiled=True), query, None)
-    cond_local = passed_along(image_kv, "section", 1)
+    cond_local = lax.ppermute(image_kv, "section", [(0, 1)])
     keep = jnp.repeat(jnp.repeat(local_mask, TILE, axis=0), TILE, axis=1) > 0
     carry = attend_piece(carry, lax.all_gather(cond_local, "seq", axis=0, tiled=True), query, keep)
     num, den = carry
@@ -122,6 +364,22 @@
     gate = lax.dynamic_slice_in_dim(mods[2], offset, cols, 0)
     out = residual + gate[None, :] * branch
     return out.astype(jnp.bfloat16)[None]
+
+
+def body(*arrays):
+    image, w_qkv, region_mask = arrays[0], arrays[3], arrays[7]
+    one_head_each = (
+        w_qkv.shape[2] // HEAD_DIM == lax.axis_size("seq")
+        and lax.axis_size("section") == 2
+        and lax.axis_size("tp") == 2
+        and w_qkv.shape[0] % 32 == 0
+        and image.shape[1] % 32 == 0
+        and image.shape[1] * lax.axis_size("seq") % BLOCK == 0
+        and arrays[4].shape[1] % 1024 == 0
+        and region_mask.shape[0] <= 16
+        and region_mask.shape[1] <= HEAD_DIM
+    )
+    return (head_body if one_head_each else token_body)(*arrays)
 
 
 def solution(mesh):

time: 371 us -> 164 us (0.44)
  waiting for transfers between devices: 294 us -> 69.4 us
  matrix products: 27.6 us -> 0 us
  Pallas kernels: 0 us -> 23.4 us
  starting transfers between devices: 3.71 us -> 21.2 us
    all_gather x3 -> x1, waiting for transfers between devices: 266 us -> 3.42 us  [head_body(): lax.all_gather(layer_norm(tokens, mods), ('seq', 'tp'), axis=0, tiled=True)]
    all_to_all x0 -> x3, waiting for transfers between devices: none -> 48.1 us  [the longest x1 38.4 us: head_body(): mine = lax.all_to_all(w_half, 'seq', 0, 0)]
    dot_general x6 -> x0, matrix products: 27.6 us -> none  [the longest x2 9.48 us: attend_piece(): jnp.einsum('qhd,khd->hqk', query, piece_k, preferred_element_type=jnp.flo...]
    pallas_call x0 -> x5, Pallas kernels: none -> 23.4 us  [call(): pl.pallas_call(kernel, grid_spec=pltpu.PrefetchScalarGridSpec(num_scalar_...]
    reduce_scatter x1 -> x0, waiting for transfers between devices: 16.1 us -> none  [body(): lax.psum_scatter(term.astype(jnp.bfloat16), 'tp', scatter_dimension=1, ti...]
    all_to_all x0 -> x3, starting transfers between devices: none -> 13.9 us  [the longest x1 6.46 us: head_body(): mine = lax.all_to_all(w_half, 'seq', 0, 0)]
    unnamed x23 -> x18, local copies, waits for them, and re-layouts: 12.8 us -> 4.19 us
    reshape x0 -> x4, local copies, waits for them, and re-layouts: none -> 8.58 us  [the longest x2 4.31 us: head_body(): cosine = jnp.repeat(cosine, 2, axis=-1)]
  transfers between devices with their start and end apart: 5 -> 7, of which waited for: 5 -> 5; matrix products, arithmetic and copies ran while one was open for 5% -> 14% of each run, Pallas kernels for 0% -> 11%
where the time goes in v2:
time: 164 us; the launch traced here: 162 us
  waiting for transfers between devices  69.4 us (42%)
  Pallas kernels  23.4 us (14%)
  local copies, waits for them, and re-layouts  22.3 us (14%)
  starting transfers between devices  21.2 us (13%)
  between operations  13.6 us (8%)
  other arithmetic  12.4 us (8%)
    all_to_all x1, waiting for transfers between devices, head_body(): mine = lax.all_to_all(w_half, 'seq', 0, 0)  38.4 us
    pallas_call x5, Pallas kernels, call(): pl.pallas_call(kernel, grid_spec=pltpu.PrefetchScalarGridSpec(num_scalar_...  23.4 us
    ppermute x1, waiting for transfers between devices, head_body(): peer = lax.ppermute(mine, 'section', [(0, 1), (1, 0)])  11.8 us
    all_to_all x1, waiting for transfers between devices, head_body(): attn = lax.all_to_all(attn.reshape(seq, img_rows, HEAD_DIM), 'seq', 0, 0)  9.64 us
    all_to_all x1, starting transfers between devices, head_body(): mine = lax.all_to_all(w_half, 'seq', 0, 0)  6.46 us
    ppermute x1, waiting for transfers between devices, head_body(): lax.ppermute(project_out(1 - tp_at, attn, w_out), 'tp', [(0, 1), (1, 0)])  6.1 us
    reshape x2, local copies, waits for them, and re-layouts, head_body(): cosine = jnp.repeat(cosine, 2, axis=-1)  4.31 us
    reshape x2, local copies, waits for them, and re-layouts, head_body(): sine = jnp.stack([-sine, sine], axis=-1).reshape(rows, HEAD_DIM)  4.28 us
  transfers between devices with their start and end apart: 7, of which 5 were waited for; matrix products, arithmetic and copies ran while one was open for 14% of the time, Pallas kernels for 11%

profile of v2, /device:TPU:0, one launch (start us, length us, event | category | flops | bytes accessed | tf_op | source)
XLA Modules:
  0.0 162.2 jit_solution(15919681855754476043)
XLA Ops:
  10.5 1.9 %fusion.6 = bf16[64,3072]{1,0:T(8,128)(2,1)} fusion(f32[3072]{0:T(1024)S(1)} %bitcast.51, f32[3072]{0:T(1024)S(1)} %bitcast.50, f32[64]{0:T(128)S(1)} %add_rsqrt_fusion, f32[64]{0:T(128)S(1)} %broadcast_multiply_fusion.2, bf16[1,128,3072]{2,1,0:T(8,128)(2,1)} %param.8, s32[]{:T(128)S(6)} %select_n.33), kind=kLoop, calls=%fused_computation.10 | loop fusion | flops 1179648 | bytes 811524 | tf_op jit(solution)/shard_map/convert_element_type | solution.py:38
  13.8 6.5 %all-to-all-start.1 = ((bf16[8,3,192,128]{3,2,1,0:T(8,128)(2,1)}), bf16[8,3,192,128]{3,2,1,0:T(8,128)(2,1)S(1)}, u32[]{:S(2)}, u32[]{:S(2)}) async-start(bf16[8,3,192,128]{3,2,1,0:T(8,128)(2,1)} %bitcast_bitcast_fusion), calls=%async_computation.1 | async-start | bytes 2359296 | tf_op jit(solution)/shard_map/all_to_all | solution.py:248
  20.3 1.8 %reshape_squeeze.3 = bf16[64,2,8,128]{3,2,1,0:T(8,128)(2,1)} reshape(bf16[1,64,2,1024]{3,2,1,0:T(2,128)(2,1)} %param.9) | data formatting | bytes 524288 | tf_op jit(solution)/shard_map/reshape;squeeze | solution.py:255
  23.9 38.4 %all-to-all-done.1.mine = bf16[8,3,192,128]{3,2,1,0:T(8,128)(2,1)S(1)} async-done(((bf16[8,3,192,128]{3,2,1,0:T(8,128)(2,1)}), bf16[8,3,192,128]{3,2,1,0:T(8,128)(2,1)S(1)}, u32[]{:S(2)}, u32[]{:S(2)}) %all-to-all-start.1) | async-done | bytes 1179680 | tf_op jit(solution)/shard_map/all_to_all | solution.py:248
  62.3 4.1 %all-to-all-start = ((bf16[8,144,128]{2,1,0:T(8,128)(2,1)}), bf16[8,144,128]{2,1,0:T(8,128)(2,1)}, u32[]{:S(2)}, u32[]{:S(2)}) async-start(bf16[8,144,128]{2,1,0:T(8,128)(2,1)} %pad_maximum_fusion.1), calls=%async_computation | async-start | bytes 589824 | tf_op jit(solution)/shard_map/all_to_all | solution.py:259
  66.4 1.6 collective-permute-start
  68.1 1.6 maximum_cosine_fusion
  71.8 2.3 %reshape.231 = f32[1024,128]{0,1:T(8,128)} reshape(f32[1024,64,2]{0,2,1:T(2,128)} %copy.13) | data formatting | bytes 1048576 | tf_op jit(solution)/shard_map/reshape | solution.py:268
  74.0 2.0 %copy.17.sin_ref = f32[1024,128]{1,0:T(8,128)} copy(f32[1024,128]{0,1:T(8,128)} %reshape.231) | data formatting | bytes 1048576 | tf_op jit(solution)/shard_map/reshape | solution.py:268
  76.0 2.0 %broadcast_in_dim.10 = f32[1024,64,2]{0,2,1:T(2,128)} broadcast(f32[1024,64]{0,1:T(8,128)} %maximum_cosine_fusion), dimensions={0,1} | broadcast | bytes 786432 | tf_op jit(solution)/shard_map/broadcast_in_dim | solution.py:267
  78.0 2.3 %reshape.230 = f32[1024,128]{0,1:T(8,128)} reshape(f32[1024,64,2]{0,2,1:T(2,128)} %broadcast_in_dim.10) | data formatting | bytes 1048576 | tf_op jit(solution)/shard_map/reshape | solution.py:267
  80.3 2.0 %copy.16.cos_ref = f32[1024,128]{1,0:T(8,128)} copy(f32[1024,128]{0,1:T(8,128)} %reshape.230) | data formatting | bytes 1048576 | tf_op jit(solution)/shard_map/reshape | solution.py:267
  83.0 11.8 %collective-permute-done.peer = bf16[8,3,192,128]{3,2,1,0:T(8,128)(2,1)} collective-permute-done((bf16[8,3,192,128]{3,2,1,0:T(8,128)(2,1)S(1)}, bf16[8,3,192,128]{3,2,1,0:T(8,128)(2,1)}, u32[]{:S(2)}, u32[]{:S(2)}) %collective-permute-start) | collective-permute-done | bytes 1179680 | tf_op jit(solution)/shard_map/ppermute | solution.py:249
  94.8 3.4 %all-gather.2.cloned.1.call-done.x_ref = bf16[1024,3072]{1,0:T(8,128)(2,1)} async-done(((bf16[64,3072]{1,0:T(8,128)(2,1)}), bf16[1024,3072]{1,0:T(8,128)(2,1)}) %all-gather.2.cloned.1.call-update) | async-done | bytes 6291472 | tf_op jit(solution)/shard_map/all_gather | solution.py:253
  100.3 6.5 %project_kv.1.kv_ref = bf16[2,1024,128]{2,1,0:T(8,128)(2,1)} custom-call(s32[1]{0:T(128)} %bitcast.1.section_ref, bf16[1024,3072]{1,0:T(8,128)(2,1)} %all-gather.2.cloned.1.call-done.x_ref, bf16[8,3,192,128]{3,2,1,0:T(8,128)(2,1)S(1)} %all-to-all-done.1.mine, bf16[8,3,192,128]{3,2,1,0:T(8,128)(2,1)} %collective-permute-done.peer, f32[1024,128]{1,0:T(8,128)S(1)} %copy-done.4, ...), custom_call_target="tpu_custom_call" | custom-call | flops 1610612736 | bytes 8650752 | tf_op jit(solution)/shard_map/project_kv/pallas_call | solution.py:132
  106.8 4.2 %collective-permute-start.1 = (bf16[2,1024,128]{2,1,0:T(8,128)(2,1)}, bf16[2,1024,128]{2,1,0:T(8,128)(2,1)}, u32[]{:S(2)}, u32[]{:S(2)}) collective-permute-start(bf16[2,1024,128]{2,1,0:T(8,128)(2,1)} %project_kv.1.kv_ref), channel_id=1, source_target_pairs={{0,16},{1,17},{2,18},{3,19},{4,20},{5,21},{6,22},{7,23},{8,24},{9,... | collective-permute-start | bytes 1572872 | tf_op jit(solution)/shard_map/ppermute | solution.py:271
  115.9 7.4 %attend_own.1 = (bf16[1024,128]{1,0:T(8,128)(2,1)S(1)}, f32[1024,128]{1,0:T(8,128)S(1)}, f32[1024,128]{1,0:T(8,128)S(1)}) custom-call(s32[1]{0:T(128)} %bitcast.1.section_ref, bf16[1024,3072]{1,0:T(8,128)(2,1)} %all-gather.2.cloned.1.call-done.x_ref, bf16[8,3,192,128]{3,2,1,0:T(8,128)(2,1)S(1)} %all-to-all-done.1.mine, ...), custom_call_target="tpu_custom_call" | custom-call | flops 1610612736 | bytes 8650752 | tf_op jit(solution)/shard_map/attend_own/pallas_call | solution.py:132
  123.3 2.4 %attend_cond.1 = bf16[1024,128]{1,0:T(8,128)(2,1)} custom-call(s32[1]{0:T(128)} %bitcast.1.section_ref, f32[4,2,1024]{2,1,0:T(2,128)S(1)} %copy-done.6, bf16[1024,128]{1,0:T(8,128)(2,1)S(1)} %get-tuple-element.8.q_ref, bf16[2,1024,128]{2,1,0:T(8,128)(2,1)} %collective-permute-done.1.cond_ref, f32[1024,128]{1,0:T(8,128)S(1)} %get-tuple-element.9.num_ref, ...), custom_call_target="tpu_custom_call" | custom-call | flops 536870912 | bytes 1835008 | tf_op jit(solution)/shard_map/attend_cond/pallas_call | solution.py:132
  125.8 3.4 %all-to-all-start.2 = ((bf16[8,128,128]{2,1,0:T(8,128)(2,1)}), bf16[8,128,128]{2,1,0:T(8,128)(2,1)S(1)}, u32[]{:S(2)}, u32[]{:S(2)}) async-start(bf16[8,128,128]{2,1,0:T(8,128)(2,1)} %bitcast.14), calls=%async_computation.2 | async-start | bytes 524288 | tf_op jit(solution)/shard_map/all_to_all | solution.py:275
  129.2 9.6 %all-to-all-done.2.attn_ref = bf16[8,128,128]{2,1,0:T(8,128)(2,1)S(1)} async-done(((bf16[8,128,128]{2,1,0:T(8,128)(2,1)}), bf16[8,128,128]{2,1,0:T(8,128)(2,1)S(1)}, u32[]{:S(2)}, u32[]{:S(2)}) %all-to-all-start.2) | async-done | bytes 262176 | tf_op jit(solution)/shard_map/all_to_all | solution.py:275
  138.9 3.8 %out_sent.1 = bf16[128,1536]{1,0:T(8,128)(2,1)} custom-call(s32[1]{0:T(128)S(6)} %sub.26.half_ref, bf16[8,128,128]{2,1,0:T(8,128)(2,1)S(1)} %all-to-all-done.2.attn_ref, bf16[1024,3072]{1,0:T(8,128)(2,1)} %w_ref.3), custom_call_target="tpu_custom_call" | custom-call | flops 402653184 | bytes 3145728 | tf_op jit(solution)/shard_map/out_sent/pallas_call | solution.py:132
  144.2 3.2 %out_kept.1 = f32[128,1536]{1,0:T(8,128)S(1)} custom-call(s32[1]{0:T(128)} %bitcast.half_ref, bf16[8,128,128]{2,1,0:T(8,128)(2,1)S(1)} %all-to-all-done.2.attn_ref, bf16[1024,3072]{1,0:T(8,128)(2,1)} %w_ref.3, bf16[128,3072]{1,0:T(8,128)(2,1)S(1)} %bitcast.48, f32[1,3072]{1,0:T(1,128)S(1)} %get-tuple-element.14.gate_ref), custom_call_target="tpu_custom_call" | custom-call | flops 402653184 | bytes 3145728 | tf_op jit(solution)/shard_map/out_kept/pallas_call | solution.py:132
  147.4 6.1 %collective-permute-done.2 = bf16[128,1536]{1,0:T(8,128)(2,1)} collective-permute-done((bf16[128,1536]{1,0:T(8,128)(2,1)}, bf16[128,1536]{1,0:T(8,128)(2,1)}, u32[]{:S(2)}, u32[]{:S(2)}) %collective-permute-start.2) | collective-permute-done | bytes 393248 | tf_op jit(solution)/shard_map/ppermute | solution.py:278
  153.5 1.9 %fusion.7 = bf16[1,128,1536]{2,1,0:T(8,128)(2,1)} fusion(f32[128,1536]{1,0:T(8,128)S(1)} %out_kept.1, bf16[128,1536]{1,0:T(8,128)(2,1)} %collective-permute-done.2, f32[1536]{0:T(1024)S(1)} %dynamic-slice_reduce_fusion), kind=kLoop, calls=%fused_computation.13 | loop fusion | flops 786432 | bytes 1579008 | tf_op jit(solution)/shard_map/broadcast_in_dim | solution.py:281
  (47 shorter events, 18.5 us)
Async XLA Ops:
  6.5 5.9 %copy-start = (bf16[384,3,1024]{2,0,1:T(8,128)(2,1)S(1)}, bf16[384,3,1024]{2,0,1:T(8,128)(2,1)}, u32[]{:S(2)}) copy-start(bf16[384,3,1024]{2,0,1:T(8,128)(2,1)} %param.11) | copy-start | bytes 7077892
  6.5 91.7 %all-gather.2.cloned.1.call-start = ((), (), s32[]{:S(2)}) async-start(), calls=%async_computation.3 | async-start | bytes 6684672 | tf_op jit(solution)/shard_map/all_gather | solution.py:253
  13.8 9.3 %copy-start.8 = (s32[1,8]{1,0:T(1,128)S(1)}, s32[1,8]{1,0:T(1,128)}, u32[]{:S(2)}) copy-start(s32[1,8]{1,0:T(1,128)} %param.15) | copy-start | bytes 100
  13.8 48.5 %all-to-all-start.1 = ((bf16[8,3,192,128]{3,2,1,0:T(8,128)(2,1)}), bf16[8,3,192,128]{3,2,1,0:T(8,128)(2,1)S(1)}, u32[]{:S(2)}, u32[]{:S(2)}) async-start(bf16[8,3,192,128]{3,2,1,0:T(8,128)(2,1)} %bitcast_bitcast_fusion), calls=%async_computation.1 | async-start | bytes 2359296 | tf_op jit(solution)/shard_map/all_to_all | solution.py:248
  62.3 48.7 %all-to-all-start = ((bf16[8,144,128]{2,1,0:T(8,128)(2,1)}), bf16[8,144,128]{2,1,0:T(8,128)(2,1)}, u32[]{:S(2)}, u32[]{:S(2)}) async-start(bf16[8,144,128]{2,1,0:T(8,128)(2,1)} %pad_maximum_fusion.1), calls=%async_computation | async-start | bytes 589824 | tf_op jit(solution)/shard_map/all_to_all | solution.py:259
  66.4 28.4 %collective-permute-start = (bf16[8,3,192,128]{3,2,1,0:T(8,128)(2,1)S(1)}, bf16[8,3,192,128]{3,2,1,0:T(8,128)(2,1)}, u32[]{:S(2)}, u32[]{:S(2)}) collective-permute-start(bf16[8,3,192,128]{3,2,1,0:T(8,128)(2,1)S(1)} %all-to-all-done.1.mine), channel_id=1, source_target_pairs={{0,16},{16,0},{1,17},{17,1},{2,18},{18,2},{3,19},{19,3},{4,20},{20... | collective-permute-start | bytes 3538952 | tf_op jit(solution)/shard_map/ppermute | solution.py:249
  98.2 1.0 copy-start.2
  99.2 1.0 copy-start.4
  106.8 16.5 %collective-permute-start.1 = (bf16[2,1024,128]{2,1,0:T(8,128)(2,1)}, bf16[2,1024,128]{2,1,0:T(8,128)(2,1)}, u32[]{:S(2)}, u32[]{:S(2)}) collective-permute-start(bf16[2,1024,128]{2,1,0:T(8,128)(2,1)} %project_kv.1.kv_ref), channel_id=1, source_target_pairs={{0,16},{1,17},{2,18},{3,19},{4,20},{5,21},{6,22},{7,23},{8,24},{9,... | collective-permute-start | bytes 1572872 | tf_op jit(solution)/shard_map/ppermute | solution.py:271
  113.8 1.0 copy-start.3
  114.8 1.0 copy-start.5
  115.9 7.4 %copy-start.6 = (f32[4,2,1024]{2,1,0:T(2,128)S(1)}, f32[4,2,1024]{2,1,0:T(2,128)}, u32[]{:S(2)}) copy-start(f32[4,2,1024]{2,1,0:T(2,128)} %reshape_reshape.3.keep_ref) | copy-start | bytes 98308
  125.8 13.1 %all-to-all-start.2 = ((bf16[8,128,128]{2,1,0:T(8,128)(2,1)}), bf16[8,128,128]{2,1,0:T(8,128)(2,1)S(1)}, u32[]{:S(2)}, u32[]{:S(2)}) async-start(bf16[8,128,128]{2,1,0:T(8,128)(2,1)} %bitcast.14), calls=%async_computation.2 | async-start | bytes 524288 | tf_op jit(solution)/shard_map/all_to_all | solution.py:275
  129.2 15.0 %copy-start.7 = (f32[1,1,3072]{2,0,1:T(1,128)S(1)}, f32[1,1,3072]{2,0,1:T(1,128)}, u32[]{:S(2)}) copy-start(f32[1,1,3072]{2,0,1:T(1,128)} %get-tuple-element.13) | copy-start | bytes 36868
  129.2 15.0 %copy-start.1 = (bf16[1,128,3072]{2,1,0:T(8,128)(2,1)S(1)}, bf16[1,128,3072]{2,1,0:T(8,128)(2,1)}, u32[]{:S(2)}) copy-start(bf16[1,128,3072]{2,1,0:T(8,128)(2,1)} %param.8) | copy-start | bytes 2359300
  142.7 10.8 %collective-permute-start.2 = (bf16[128,1536]{1,0:T(8,128)(2,1)}, bf16[128,1536]{1,0:T(8,128)(2,1)}, u32[]{:S(2)}, u32[]{:S(2)}) collective-permute-start(bf16[128,1536]{1,0:T(8,128)(2,1)} %out_sent.1), channel_id=1, source_target_pairs={{0,1},{1,0},{2,3},{3,2},{4,5},{5,4},{6,7},{7,6},{8,9},{9,8},{10,11... | collective-permute-start | bytes 1179656 | tf_op jit(solution)/shard_map/ppermute | solution.py:278
Sparse Core Ops, SparseCore 0:
  12.6 85.5 all-gather.1

commit v3 on v0

--- a/solution.py
+++ b/solution.py
@@ -1,21 +1,14 @@
 import jax
 import jax.numpy as jnp
 from jax import lax
+from jax.experimental import pallas as pl
+from jax.experimental.pallas import tpu as pltpu
 from jax.sharding import PartitionSpec as P
 
 HEAD_DIM = 128
 GRID_W = 64
 TILE = 128
-
-
-def passed_along(x, axis, by):
-    size = lax.axis_size(axis)
-    pairs = [(i, i + by) for i in range(size) if 0 <= i + by < size]
-    return lax.ppermute(x, axis, pairs)
-
-
-def rms_rows(x, gain):
-    return x * lax.rsqrt(jnp.mean(x * x, axis=-1, keepdims=True) + 1e-06) * gain
+VMEM_LIMIT = 30 * 1024 * 1024
 
 
 def axis_freqs(width):
@@ -39,6 +32,362 @@
     return (jnp.cos(angles), jnp.sin(angles))
 
 
+def layer_norm(tokens, mods):
+    mean = jnp.mean(tokens, axis=-1, keepdims=True)
+    var = jnp.mean((tokens - mean) ** 2, axis=-1, keepdims=True)
+    return ((tokens - mean) * lax.rsqrt(var + 1e-06) * (1.0 + mods[1:2]) + mods[0:1]).astype(
+        jnp.bfloat16
+    )
+
+
+CHUNKS = 2
+BLOCK = 256
+VMEM = pl.BlockSpec(memory_space=pltpu.VMEM)
+SMEM = pl.BlockSpec(memory_space=pltpu.SMEM)
+
+
+def call(kernel, name, out_shape, flops, moved, exps, **spec):
+    return pl.pallas_call(
+        kernel,
+        out_shape=out_shape,
+        compiler_params=pltpu.CompilerParams(vmem_limit_bytes=VMEM_LIMIT),
+        cost_estimate=pl.CostEstimate(flops=flops, bytes_accessed=moved, transcendentals=exps),
+        name=name,
+        **spec,
+    )
+
+
+def norm_kernel(tp_ref, image_ref, mods_ref, *out_refs):
+    normed = layer_norm(image_ref[...].astype(jnp.float32), mods_ref[...])
+    rows = normed.shape[0] // len(out_refs)
+    for c, out_ref in enumerate(out_refs):
+        out_ref[...] = normed[c * rows : (c + 1) * rows]
+
+
+def norm_part(tp, parts, image, mods):
+    rows, depth = image.shape
+    part = rows // parts
+    small = pl.BlockSpec((part // CHUNKS, depth), lambda i, tp: (0, 0))
+    return call(
+        norm_kernel, "norm_part",
+        [jax.ShapeDtypeStruct((part // CHUNKS, depth), jnp.bfloat16)] * CHUNKS,
+        10 * part * depth, 4 * part * depth, 0,
+        grid_spec=pltpu.PrefetchScalarGridSpec(
+            num_scalar_prefetch=1,
+            grid=(1,),
+            in_specs=[
+                pl.BlockSpec((part, depth), lambda i, tp: (tp[0], 0)),
+                pl.BlockSpec(mods.shape, lambda i, tp: (0, 0)),
+            ],
+            out_specs=[small] * CHUNKS,
+        ),
+    )(tp, image, mods)
+
+
+def normed_rotated(x, gain, cosine, sine):
+    x = x * lax.rsqrt(jnp.mean(x * x, axis=-1, keepdims=True) + 1e-06) * gain
+    even = lax.broadcasted_iota(jnp.int32, x.shape, 1) % 2 == 0
+    other = jnp.where(even, pltpu.roll(x, HEAD_DIM - 1, 1), pltpu.roll(x, 1, 1))
+    return (x * cosine + other * sine).astype(jnp.bfloat16)
+
+
+def project_kernel(kinds, section_ref, x_ref, mine, peer, cos_ref, sin_ref, gain_ref, *refs):
+    out_refs, acc_ref = refs[:-1], refs[-1]
+    step = pl.program_id(0)
+    half = peer.shape[1] // 3
+    first = section_ref[0] == 0
+
+    def piece(s, kind):
+        at = slice(kind * half, (kind + 1) * half)
+        a, b = mine[s, at, :], peer[s, at, :]
+        return jnp.concatenate([jnp.where(first, a, b), jnp.where(first, b, a)], axis=0)
+
+    w = jnp.concatenate(
+        [
+            jnp.concatenate([piece(s, kind) for s in range(mine.shape[0])], axis=0)
+            for kind in kinds
+        ],
+        axis=1,
+    )
+    part = jnp.dot(x_ref[...], w, preferred_element_type=jnp.float32)
+
+    @pl.when(step == 0)
+    def _():
+        acc_ref[...] = part
+
+    @pl.when(step > 0)
+    def _():
+        acc_ref[...] += part
+
+    @pl.when(step == pl.num_programs(0) - 1)
+    def _():
+        for place, kind in enumerate(kinds):
+            value = acc_ref[:, place * HEAD_DIM : (place + 1) * HEAD_DIM]
+            if kind < 2:
+                value = normed_rotated(
+                    value, gain_ref[kind : kind + 1, :], cos_ref[...], sin_ref[...]
+                )
+            if kind == 0:
+                out_refs[0][...] = value
+            else:
+                out_refs[-1][kind - 1] = value.astype(jnp.bfloat16)
+
+
+def project(kinds, section, x, mine, peer, cosine, sine, gains):
+    rows, depth = x.shape
+    sources = mine.shape[0]
+    steps = 4
+    out_shape, out_specs = [], []
+    if 0 in kinds:
+        out_shape.append(jax.ShapeDtypeStruct((rows, HEAD_DIM), jnp.bfloat16))
+        out_specs.append(pl.BlockSpec((rows, HEAD_DIM), lambda k, s: (0, 0)))
+    if 1 in kinds:
+        out_shape.append(jax.ShapeDtypeStruct((2, rows, HEAD_DIM), jnp.bfloat16))
+        out_specs.append(pl.BlockSpec((2, rows, HEAD_DIM), lambda k, s: (0, 0, 0)))
+
+    def pieces(array):
+        return pl.BlockSpec((sources // steps,) + array.shape[1:], lambda k, s: (k, 0, 0))
+
+    return call(
+        lambda *refs: project_kernel(kinds, *refs), "project_" + "".join("qkv"[k] for k in kinds),
+        out_shape,
+        2 * len(kinds) * rows * depth * HEAD_DIM, 2 * (x.size + mine.size + peer.size), 0,
+        grid_spec=pltpu.PrefetchScalarGridSpec(
+            num_scalar_prefetch=1,
+            grid=(steps,),
+            in_specs=[
+                pl.BlockSpec((rows, depth // steps), lambda k, s: (0, k)),
+                pieces(mine),
+                pieces(peer),
+                pl.BlockSpec((rows, HEAD_DIM), lambda k, s: (0, 0)),
+                pl.BlockSpec((rows, HEAD_DIM), lambda k, s: (0, 0)),
+                pl.BlockSpec((2, HEAD_DIM), lambda k, s: (0, 0)),
+            ],
+            out_specs=out_specs,
+            scratch_shapes=[pltpu.VMEM((rows, len(kinds) * HEAD_DIM), jnp.float32)],
+        ),
+    )(section, x, mine, peer, cosine, sine, gains)
+
+
+def weights_of(query, keys):
+    scores = lax.dot_general(
+        query, keys, (((1,), (1,)), ((), ())), preferred_element_type=jnp.float32
+    )
+    return jnp.exp(scores * (1.0 / HEAD_DIM**0.5))
+
+
+def summed(weights, values):
+    den = jnp.sum(weights, axis=-1, keepdims=True)
+    num = jnp.dot(weights.astype(jnp.bfloat16), values, preferred_element_type=jnp.float32)
+    return num, den
+
+
+def kept_weights(query, cond_ref, keep):
+    weights = weights_of(query, cond_ref[0])
+    rows, keys = weights.shape
+    tiles = keep.shape[0]
+    return (weights.reshape(tiles, rows // tiles, keys) * keep[:, None, :]).reshape(rows, keys)
+
+
+def own_kernel(section_ref, keep_ref, qa, qb, kva, kvb, text, conda, num_ref, den_ref):
+    rows = qa.shape[0]
+    tiles = keep_ref.shape[0] * BLOCK // rows
+    for c, q_ref in enumerate((qa, qb)):
+        for b in range(rows // BLOCK):
+            query = q_ref[b * BLOCK : (b + 1) * BLOCK, :]
+            at = pl.ds(c * rows + b * BLOCK, BLOCK)
+            num, den = 0.0, 0.0
+            for ref in (kva, kvb, text):
+                more = summed(weights_of(query, ref[0]), ref[1])
+                num, den = num + more[0], den + more[1]
+            num_ref[at, :] = num
+            den_ref[at, :] = jnp.broadcast_to(den, num.shape)
+
+    @pl.when(section_ref[0] != 0)
+    def _():
+        for c, q_ref in enumerate((qa, qb)):
+            for b in range(rows // BLOCK):
+                query = q_ref[b * BLOCK : (b + 1) * BLOCK, :]
+                at = pl.ds(c * rows + b * BLOCK, BLOCK)
+                keep = keep_ref[b * tiles : (b + 1) * tiles, :]
+                num, den = summed(kept_weights(query, conda, keep), conda[1])
+                num_ref[at, :] += num
+                den_ref[at, :] += jnp.broadcast_to(den, num.shape)
+
+
+def cond_kernel(section_ref, keep_ref, qa, qb, condb, num_ref, den_ref, out_ref):
+    rows = qa.shape[0]
+    tiles = keep_ref.shape[0] * BLOCK // rows
+
+    def store(c, b, num, den):
+        value = (num / den).astype(jnp.bfloat16).reshape(tiles, -1, HEAD_DIM)
+        out_ref[b * tiles : (b + 1) * tiles, c] = value
+
+    @pl.when(section_ref[0] == 0)
+    def _():
+        for c in range(CHUNKS):
+            for b in range(rows // BLOCK):
+                at = pl.ds(c * rows + b * BLOCK, BLOCK)
+                store(c, b, num_ref[at, :], den_ref[at, :])
+
+    @pl.when(section_ref[0] != 0)
+    def _():
+        for c, q_ref in enumerate((qa, qb)):
+            for b in range(rows // BLOCK):
+                query = q_ref[b * BLOCK : (b + 1) * BLOCK, :]
+                at = pl.ds(c * rows + b * BLOCK, BLOCK)
+                keep = keep_ref[b * tiles : (b + 1) * tiles, :]
+                num, den = summed(kept_weights(query, condb, keep), condb[1])
+                store(c, b, num_ref[at, :] + num, den_ref[at, :] + den)
+
+
+def attend_own(section, keep, queries, kvs, text, cond):
+    rows = 2 * queries[0].shape[0]
+    keys = rows + text.shape[1] + cond.shape[1]
+    return call(
+        own_kernel, "attend_own", [jax.ShapeDtypeStruct((rows, HEAD_DIM), jnp.float32)] * 2,
+        4 * rows * keys * HEAD_DIM, 2 * rows * HEAD_DIM * 10, rows * keys,
+        in_specs=[SMEM] + [VMEM] * 7,
+        out_specs=[VMEM] * 2,
+    )(section, keep, *queries, *kvs, text, cond)
+
+
+def attend_cond(section, keep, queries, cond, num, den):
+    rows, seq = num.shape[0], keep.shape[0]
+    keys = cond.shape[1]
+    return call(
+        cond_kernel, "attend_cond",
+        jax.ShapeDtypeStruct((seq, CHUNKS, rows // seq // CHUNKS, HEAD_DIM), jnp.bfloat16),
+        4 * rows * keys * HEAD_DIM, 2 * rows * HEAD_DIM * 8, rows * keys,
+        in_specs=[SMEM] + [VMEM] * 6,
+        out_specs=VMEM,
+    )(section, keep, *queries, cond, num, den)
+
+
+def token_rows(attn_ref):
+    heads, chunks, held, _ = attn_ref.shape
+    parts = 2
+    piece = held // parts
+    return jnp.concatenate(
+        [
+            jnp.concatenate(
+                [
+                    attn_ref[h, c, t * piece : (t + 1) * piece, :]
+                    for t in range(parts)
+                    for c in range(chunks)
+                ],
+                axis=0,
+            )
+            for h in range(heads)
+        ],
+        axis=1,
+    )
+
+
+def sent_kernel(half_ref, attn_ref, w_ref, out_ref):
+    branch = jnp.dot(token_rows(attn_ref), w_ref[...], preferred_element_type=jnp.float32)
+    out_ref[...] = branch.astype(jnp.bfloat16)
+
+
+def kept_kernel(half_ref, attn_ref, w_ref, image_ref, gate_ref, out_ref):
+    branch = jnp.dot(token_rows(attn_ref), w_ref[...], preferred_element_type=jnp.float32)
+    out_ref[...] = image_ref[...].astype(jnp.float32) + gate_ref[...] * branch
+
+
+def project_out(half, attn, w_out, image=None, gate=None):
+    rows = attn.shape[1] * attn.shape[2]
+    depth, width = w_out.shape[0], w_out.shape[1] // 2
+    block = 512
+    steps = width // block
+
+    def columns(height):
+        return pl.BlockSpec((height, block), lambda i, half: (0, half[0] * steps + i))
+
+    kept = image is not None
+    return call(
+        kept_kernel if kept else sent_kernel, "out_kept" if kept else "out_sent",
+        jax.ShapeDtypeStruct((rows, width), jnp.float32 if kept else jnp.bfloat16),
+        2 * rows * depth * width, 2 * depth * width, 0,
+        grid_spec=pltpu.PrefetchScalarGridSpec(
+            num_scalar_prefetch=1,
+            grid=(steps,),
+            in_specs=[pl.BlockSpec(attn.shape, lambda i, half: (0, 0, 0, 0)), columns(depth)]
+            + ([columns(rows), columns(1)] if kept else []),
+            out_specs=pl.BlockSpec((rows, block), lambda i, half: (0, i)),
+        ),
+    )(half, attn, w_out, *((image, gate) if kept else ()))
+
+
+def lane_tables(rows_index, time_index):
+    first = HEAD_DIM // 8
+    rest = (HEAD_DIM - first) // 2
+    freqs = jnp.concatenate([axis_freqs(first), axis_freqs(rest), axis_freqs(rest)])
+    freqs = jnp.repeat(freqs, 2)[None]
+    lane = jnp.arange(HEAD_DIM, dtype=jnp.int32)[None]
+    row_pos = (rows_index // GRID_W).astype(jnp.float32)[:, None]
+    col_pos = (rows_index % GRID_W).astype(jnp.float32)[:, None]
+    ids = jnp.where(lane < first, time_index, jnp.where(lane < first + rest, row_pos, col_pos))
+    angles = ids * freqs
+    return jnp.cos(angles), jnp.sin(angles) * jnp.where(lane % 2 == 0, -1.0, 1.0)
+
+
+def head_body(image, text_kv, modulation, w_qkv, w_out, q_gain, k_gain, region_mask):
+    seq = lax.axis_size("seq")
+    parts = lax.axis_size("tp")
+    img_rows = image.shape[1]
+    depth = w_qkv.shape[0]
+    section = lax.axis_index("section")
+    tp = lax.axis_index("tp")
+    mods = modulation[0]
+    section_at = section.astype(jnp.int32).reshape(1)
+    tp_at = tp.astype(jnp.int32).reshape(1)
+
+    piece = img_rows // parts // CHUNKS
+    normed = norm_part(tp_at, parts, image[0], mods)
+    xs = [lax.all_gather(n, ("seq", "tp"), axis=0, tiled=True) for n in normed]
+
+    half = depth // 2
+    w_half = lax.dynamic_slice_in_dim(w_qkv.transpose(1, 0, 2), section * half, half, 1)
+    w_half = w_half.reshape(3, half, seq, HEAD_DIM).transpose(2, 0, 1, 3).reshape(seq, -1, HEAD_DIM)
+    text = text_kv[0].reshape(-1, 2, seq, HEAD_DIM).transpose(2, 0, 1, 3).reshape(seq, -1, HEAD_DIM)
+    mask = jnp.pad(
+        region_mask.astype(jnp.bfloat16), ((0, 15), (0, HEAD_DIM - region_mask.shape[1]))
+    )
+    mask = jnp.broadcast_to(mask, (seq,) + mask.shape)
+    mine = lax.all_to_all(jnp.concatenate([w_half, text, mask], axis=1), "seq", 0, 0)
+    w_rows = 3 * half
+    peer = lax.ppermute(mine[:, :w_rows], "section", [(0, 1), (1, 0)])
+    text = mine[:, w_rows:-16].reshape(-1, 2, HEAD_DIM).transpose(1, 0, 2)
+    keep = mine[:, -16, : region_mask.shape[1]].astype(jnp.float32)
+    keep = jnp.repeat(keep, parts * piece, axis=1)
+
+    time_index = (section == 0).astype(jnp.float32)
+    index = jnp.arange(seq * parts * piece, dtype=jnp.int32)
+    index = index // piece * (CHUNKS * piece) + index % piece
+    tables = [lane_tables(index + c * piece, time_index) for c in range(CHUNKS)]
+    gains = jnp.stack([q_gain, k_gain])
+
+    q_a, kv_a = project((0, 1, 2), section_at, xs[0], mine, peer, *tables[0], gains)
+    cond_a = lax.ppermute(kv_a, "section", [(0, 1)])
+    (kv_b,) = project((1, 2), section_at, xs[1], mine, peer, *tables[1], gains)
+    cond_b = lax.ppermute(kv_b, "section", [(0, 1)])
+    (q_b,) = project((0,), section_at, xs[1], mine, peer, *tables[1], gains)
+    queries = (q_a, q_b)
+    num, den = attend_own(section_at, keep, queries, (kv_a, kv_b), text, cond_a)
+    attn = attend_cond(section_at, keep, queries, cond_b, num, den)
+
+    attn = lax.all_to_all(attn, "seq", 0, 0)
+    gate = mods[2:3]
+    other = lax.ppermute(project_out(1 - tp_at, attn, w_out), "tp", [(0, 1), (1, 0)])
+    kept = project_out(tp_at, attn, w_out, image[0], gate)
+    gate = lax.dynamic_slice_in_dim(gate, tp * other.shape[1], other.shape[1], 1)
+    return (kept + gate * other.astype(jnp.float32)).astype(jnp.bfloat16)[None]
+
+
+def rms_rows(x, gain):
+    return x * lax.rsqrt(jnp.mean(x * x, axis=-1, keepdims=True) + 1e-06) * gain
+
+
 def apply_rope(x, cosine, sine):
     rows, heads_here = (x.shape[0], x.shape[1])
     pairs = x.reshape(rows, heads_here, HEAD_DIM // 2, 2)
@@ -69,17 +418,13 @@
     return (num, den)
 
 
-def body(image, text_kv, modulation, w_qkv, w_out, q_gain, k_gain, region_mask):
+def token_body(image, text_kv, modulation, w_qkv, w_out, q_gain, k_gain, region_mask):
     img_rows = image.shape[1]
     width_local = w_qkv.shape[2]
     heads_local = width_local // HEAD_DIM
     tokens = image[0].astype(jnp.float32)
     mods = modulation[0]
-    mean = jnp.mean(tokens, axis=-1, keepdims=True)
-    var = jnp.mean((tokens - mean) ** 2, axis=-1, keepdims=True)
-    normed = ((tokens - mean) * lax.rsqrt(var + 1e-06) * (1.0 + mods[1]) + mods[0]).astype(
-        jnp.bfloat16
-    )
+    normed = layer_norm(tokens, mods)
     qkv = jnp.einsum(
         "td,dcf->tcf",
         normed,
@@ -106,7 +451,7 @@
         jnp.zeros((heads_local, img_rows), jnp.float32),
     )
     carry = attend_piece(init, lax.all_gather(own_kv, "seq", axis=0, tiled=True), query, None)
-    cond_local = passed_along(image_kv, "section", 1)
+    cond_local = lax.ppermute(image_kv, "section", [(0, 1)])
     keep = jnp.repeat(jnp.repeat(local_mask, TILE, axis=0), TILE, axis=1) > 0
     carry = attend_piece(carry, lax.all_gather(cond_local, "seq", axis=0, tiled=True), query, keep)
     num, den = carry
@@ -122,6 +467,24 @@
     gate = lax.dynamic_slice_in_dim(mods[2], offset, cols, 0)
     out = residual + gate[None, :] * branch
     return out.astype(jnp.bfloat16)[None]
+
+
+def body(*arrays):
+    image, w_qkv, region_mask = arrays[0], arrays[3], arrays[7]
+    seq = lax.axis_size("seq")
+    one_head_each = (
+        w_qkv.shape[2] // HEAD_DIM == seq
+        and seq % 4 == 0
+        and lax.axis_size("section") == 2
+        and lax.axis_size("tp") == 2
+        and w_qkv.shape[0] % 128 == 0
+        and image.shape[1] == TILE
+        and image.shape[1] * seq % (2 * BLOCK) == 0
+        and arrays[1].shape[1] % 16 == 0
+        and arrays[4].shape[1] % 1024 == 0
+        and region_mask.shape[1] <= HEAD_DIM
+    )
+    return (head_body if one_head_each else token_body)(*arrays)
 
 
 def solution(mesh):

time: 371 us -> 180 us (0.49)
  waiting for transfers between devices: 294 us -> 40.6 us
  blocking collectives: 0 us -> 60.8 us
  matrix products: 27.6 us -> 0 us
  Pallas kernels: 0 us -> 17.6 us
  starting transfers between devices: 3.71 us -> 13.7 us
  local copies, waits for them, and re-layouts: 23.1 us -> 28.6 us
  other arithmetic: 8.76 us -> 4.15 us
    all_gather x3 -> x2, waiting for transfers between devices: 266 us -> 0.96 us  [head_body(): xs = [lax.all_gather(n, ('seq', 'tp'), axis=0, tiled=True) for n in normed]]
    all_to_all x0 -> x1, blocking collectives: none -> 60.8 us  [head_body(): lax.all_to_all(jnp.concatenate([w_half, text, mask], axis=1), 'seq', 0, 0)]
    dot_general x6 -> x0, matrix products: 27.6 us -> none  [the longest x2 9.48 us: attend_piece(): jnp.einsum('qhd,khd->hqk', query, piece_k, preferred_element_type=jnp.flo...]
    ppermute x1 -> x4, waiting for transfers between devices: 11.6 us -> 29.2 us  [the longest x1 21.4 us: head_body(): peer = lax.ppermute(mine[:, :w_rows], 'section', [(0, 1), (1, 0)])]
    pallas_call x0 -> x8, Pallas kernels: none -> 17.6 us  [the longest x3 8.61 us: project(): call(lambda *refs: project_kernel(kinds, *refs), 'project_' + ''.join(('q...]
    reduce_scatter x1 -> x0, waiting for transfers between devices: 16.1 us -> none  [body(): lax.psum_scatter(term.astype(jnp.bfloat16), 'tp', scatter_dimension=1, ti...]
    unnamed x23 -> x51, local copies, waits for them, and re-layouts: 12.8 us -> 23.2 us
    all_to_all x0 -> x1, waiting for transfers between devices: none -> 9.73 us  [head_body(): attn = lax.all_to_all(attn, 'seq', 0, 0)]
  transfers between devices with their start and end apart: 5 -> 7, of which waited for: 5 -> 4; matrix products, arithmetic and copies ran while one was open for 5% -> 5% of each run, Pallas kernels for 0% -> 8%
where the time goes in v3:
time: 180 us; the launch traced here: 179 us
  blocking collectives  60.8 us (34%)
  waiting for transfers between devices  40.6 us (23%)
  local copies, waits for them, and re-layouts  28.6 us (16%)
  Pallas kernels  17.6 us (10%)
  starting transfers between devices  13.7 us (8%)
  between operations  13.7 us (8%)
  other arithmetic  4.15 us (2%)
    all_to_all x1, blocking collectives, head_body(): lax.all_to_all(jnp.concatenate([w_half, text, mask], axis=1), 'seq', 0, 0)  60.8 us
    unnamed x51, local copies, waits for them, and re-layouts  23.2 us
    ppermute x1, waiting for transfers between devices, head_body(): peer = lax.ppermute(mine[:, :w_rows], 'section', [(0, 1), (1, 0)])  21.4 us
    all_to_all x1, waiting for transfers between devices, head_body(): attn = lax.all_to_all(attn, 'seq', 0, 0)  9.73 us
    pallas_call x3, Pallas kernels, project(): call(lambda *refs: project_kernel(kinds, *refs), 'project_' + ''.join(('q...  8.61 us
    ppermute x1, waiting for transfers between devices, head_body(): lax.ppermute(project_out(1 - tp_at, attn, w_out), 'tp', [(0, 1), (1, 0)])  7.84 us
    ppermute x1, starting transfers between devices, head_body(): cond_a = lax.ppermute(kv_a, 'section', [(0, 1)])  4.1 us
    ppermute x1, starting transfers between devices, head_body(): cond_b = lax.ppermute(kv_b, 'section', [(0, 1)])  4.07 us
  transfers between devices with their start and end apart: 7, of which 4 were waited for; matrix products, arithmetic and copies ran while one was open for 5% of the time, Pallas kernels for 8%

profile of v3, /device:TPU:0, one launch (start us, length us, event | category | flops | bytes accessed | tf_op | source)
XLA Modules:
  0.0 179.2 jit_solution(824481231737306206)
XLA Ops:
  12.3 60.8 %all_to_all.10.refs_2_ = bf16[8,720,128]{2,1,0:T(8,128)(2,1)S(1)} all-to-all(bf16[8,720,128]{2,1,0:T(8,128)(2,1)S(1)} %pad_maximum_fusion), channel_id=1, replica_groups=mesh['section'=2,'seq'=8,'tp'=2] {'seq'}, dimensions={0} | all-to-all | bytes 2949120 | tf_op jit(solution)/shard_map/all_to_all | solution.py:357
  75.5 1.5 collective-permute-start
  78.8 3.1 %sine_multiply_fusion = (f32[512,128]{1,0:T(8,128)}, f32[512,128]{1,0:T(8,128)}, f32[512,128]{1,0:T(8,128)}, f32[512,128]{1,0:T(8,128)}) fusion(f32[512]{0:T(512)S(1)} %get-tuple-element.28, f32[512]{0:T(512)S(1)} %get-tuple-element.27, f32[128]{0:T(128)S(1)} %compare_select_fusion, f32[128]{0:T(128)S(1)} %mul.86, f32[]{:T(128)S(6)} %convert_element_type.63, ...), kind=kLoop, calls=%fused_computation.6 | loop fusion | flops 524288 | bytes 1058052 | tf_op jit(solution)/shard_map/mul | solution.py:331
  81.8 21.4 %collective-permute-done.refs_3_ = bf16[8,576,128]{2,1,0:T(8,128)(2,1)S(1)} collective-permute-done((bf16[8,576,128]{2,1,0:T(8,128)(2,1)}, bf16[8,576,128]{2,1,0:T(8,128)(2,1)S(1)}, u32[]{:S(2)}, u32[]{:S(2)}) %collective-permute-start) | collective-permute-done | bytes 1179680 | tf_op jit(solution)/shard_map/ppermute | solution.py:359
  103.2 1.8 %copy-done.2 = bf16[8,720,128]{2,1,0:T(8,128)(2,1)S(1)} copy-done((bf16[8,720,128]{2,1,0:T(8,128)(2,1)S(1)}, bf16[8,720,128]{2,1,0:T(8,128)(2,1)}, u32[]{:S(2)}) %copy-start.2) | copy-done | bytes 1474584
  105.0 1.9 %copy-done.13 = bf16[512,3072]{1,0:T(8,128)(2,1)S(1)} copy-done((bf16[512,3072]{1,0:T(8,128)(2,1)S(1)}, bf16[512,3072]{1,0:T(8,128)(2,1)}, u32[]{:S(2)}) %copy-start.13) | copy-done | bytes 3145752
  108.8 4.2 %project_qkv.1 = (bf16[512,128]{1,0:T(8,128)(2,1)S(1)}, bf16[2,512,128]{2,1,0:T(8,128)(2,1)}) custom-call(s32[1]{0:T(128)} %bitcast.1.refs_0_.section_ref, bf16[512,3072]{1,0:T(8,128)(2,1)S(1)} %copy-done.13, bf16[8,720,128]{2,1,0:T(8,128)(2,1)S(1)} %copy-done.2, bf16[8,576,128]{2,1,0:T(8,128)(2,1)S(1)} %collective-permute-done.refs_3_, ...), custom_call_target="tpu_custom_call" | custom-call | flops 1207959552 | bytes 5799936 | tf_op jit(solution)/shard_map/project_qkv/pallas_call | solution.py:151
  113.6 4.1 %collective-permute-start.2 = (bf16[2,512,128]{2,1,0:T(8,128)(2,1)}, bf16[2,512,128]{2,1,0:T(8,128)(2,1)}, u32[]{:S(2)}, u32[]{:S(2)}) collective-permute-start(bf16[2,512,128]{2,1,0:T(8,128)(2,1)} %get-tuple-element.14.kva), channel_id=1, source_target_pairs={{0,16},{1,17},{2,18},{3,19},{4,20},{5,21},{6,22},{7,23},{8,24},{9,... | collective-permute-start | bytes 786440 | tf_op jit(solution)/shard_map/ppermute | solution.py:371
  118.7 1.4 copy-done.3
  120.0 1.9 %copy-done.6 = bf16[512,3072]{1,0:T(8,128)(2,1)S(1)} copy-done((bf16[512,3072]{1,0:T(8,128)(2,1)S(1)}, bf16[512,3072]{1,0:T(8,128)(2,1)}, u32[]{:S(2)}) %copy-start.6) | copy-done | bytes 3145752
  121.9 1.3 copy-done.9
  125.1 2.3 %project_kv.1.kvb = bf16[2,512,128]{2,1,0:T(8,128)(2,1)S(1)} custom-call(s32[1]{0:T(128)} %bitcast.1.refs_0_.section_ref, bf16[512,3072]{1,0:T(8,128)(2,1)S(1)} %copy-done.6, bf16[8,720,128]{2,1,0:T(8,128)(2,1)S(1)} %copy-done.3, bf16[8,576,128]{2,1,0:T(8,128)(2,1)S(1)} %copy-done.9, f32[512,128]{1,0:T(8,128)S(1)} %copy-done.16, f32[512,128]{1,0:T(8,128)S(1)} %copy-done.14, ...), custom_call_target="tpu_custom_call" | custom-call | flops 805306368 | bytes 5799936 | tf_op jit(solution)/shard_map/project_kv/pallas_call | solution.py:151
  127.4 4.1 %collective-permute-start.1 = (bf16[2,512,128]{2,1,0:T(8,128)(2,1)S(1)}, bf16[2,512,128]{2,1,0:T(8,128)(2,1)}, u32[]{:S(2)}, u32[]{:S(2)}) collective-permute-start(bf16[2,512,128]{2,1,0:T(8,128)(2,1)S(1)} %project_kv.1.kvb), channel_id=1, source_target_pairs={{0,16},{1,17},{2,18},{3,19},{4,20},{5,21},{6,22},{7,23},{8,24},{9,... | collective-permute-start | bytes 786440 | tf_op jit(solution)/shard_map/ppermute | solution.py:373
  131.7 1.4 copy-done.4
  133.1 1.9 %copy-done.7 = bf16[512,3072]{1,0:T(8,128)(2,1)S(1)} copy-done((bf16[512,3072]{1,0:T(8,128)(2,1)S(1)}, bf16[512,3072]{1,0:T(8,128)(2,1)}, u32[]{:S(2)}) %copy-start.7) | copy-done | bytes 3145752
  134.9 1.3 copy-done.10
  136.2 2.1 %project_q.1.qb = bf16[512,128]{1,0:T(8,128)(2,1)S(1)} custom-call(s32[1]{0:T(128)} %bitcast.1.refs_0_.section_ref, bf16[512,3072]{1,0:T(8,128)(2,1)S(1)} %copy-done.7, bf16[8,720,128]{2,1,0:T(8,128)(2,1)S(1)} %copy-done.4, bf16[8,576,128]{2,1,0:T(8,128)(2,1)S(1)} %copy-done.10, f32[512,128]{1,0:T(8,128)S(1)} %copy-done.17, f32[512,128]{1,0:T(8,128)S(1)} %copy-done.15, ...), custom_call_target="tpu_custom_call" | custom-call | flops 402653184 | bytes 5799936 | tf_op jit(solution)/shard_map/project_q/pallas_call | solution.py:151
  138.4 3.6 %attend_own.1 = (f32[1024,128]{1,0:T(8,128)S(1)}, f32[1024,128]{1,0:T(8,128)S(1)}) custom-call(s32[1]{0:T(128)} %bitcast.1.refs_0_.section_ref, f32[8,512]{1,0:T(8,128)S(1)} %reshape.146.keep_ref, bf16[512,128]{1,0:T(8,128)(2,1)S(1)} %copy-done.21, bf16[512,128]{1,0:T(8,128)(2,1)S(1)} %project_q.1.qb, bf16[2,512,128]{2,1,0:T(8,128)(2,1)} %get-tuple-element.14.kva, ...), custom_call_target="tpu_custom_call" | custom-call | flops 1073741824 | bytes 2621440 | tf_op jit(solution)/shard_map/attend_own/pallas_call | solution.py:247
  142.0 1.7 attend_cond.1
  143.7 3.4 %all-to-all-start.1 = ((bf16[8,2,64,128]{3,2,1,0:T(8,128)(2,1)}), bf16[8,2,64,128]{3,2,1,0:T(8,128)(2,1)S(1)}, u32[]{:S(2)}, u32[]{:S(2)}) async-start(bf16[8,2,64,128]{3,2,1,0:T(8,128)(2,1)} %attend_cond.1), calls=%async_computation.1 | async-start | bytes 524288 | tf_op jit(solution)/shard_map/all_to_all | solution.py:379
  147.1 9.7 %all-to-all-done.1.attn_ref = bf16[8,2,64,128]{3,2,1,0:T(8,128)(2,1)S(1)} async-done(((bf16[8,2,64,128]{3,2,1,0:T(8,128)(2,1)}), bf16[8,2,64,128]{3,2,1,0:T(8,128)(2,1)S(1)}, u32[]{:S(2)}, u32[]{:S(2)}) %all-to-all-start.1) | async-done | bytes 262176 | tf_op jit(solution)/shard_map/all_to_all | solution.py:379
  156.9 2.8 %copy-done.5 = bf16[1024,3072]{1,0:T(8,128)(2,1)S(1)} copy-done((bf16[1024,3072]{1,0:T(8,128)(2,1)S(1)}, bf16[1024,3072]{1,0:T(8,128)(2,1)}, u32[]{:S(2)}) %copy-start.5) | copy-done | bytes 6291480
  162.3 1.3 out_kept.1
  163.6 7.8 %collective-permute-done.3 = bf16[128,1536]{1,0:T(8,128)(2,1)S(1)} collective-permute-done((bf16[128,1536]{1,0:T(8,128)(2,1)S(1)}, bf16[128,1536]{1,0:T(8,128)(2,1)S(1)}, u32[]{:S(2)}, u32[]{:S(2)}) %collective-permute-start.3) | collective-permute-done | bytes 393248 | tf_op jit(solution)/shard_map/ppermute | solution.py:381
  (80 shorter events, 18.9 us)
Async XLA Ops:
  6.5 5.3 %copy-start = (bf16[384,3,1024]{2,0,1:T(8,128)(2,1)S(1)}, bf16[384,3,1024]{2,0,1:T(8,128)(2,1)}, u32[]{:S(2)}) copy-start(bf16[384,3,1024]{2,0,1:T(8,128)(2,1)} %param.11) | copy-start | bytes 7077892
  6.5 5.3 %copy-start.24 = (s32[1,8]{1,0:T(1,128)S(1)}, s32[1,8]{1,0:T(1,128)}, u32[]{:S(2)}) copy-start(s32[1,8]{1,0:T(1,128)} %param.15) | copy-start | bytes 100
  6.5 96.6 %all-gather.3.cloned.1.call-start = ((), (), s32[]{:S(2)}) async-start(), calls=%async_computation.2 | async-start | bytes 3342336 | tf_op jit(solution)/shard_map/all_gather | solution.py:347
  9.7 108.9 %all-gather.5.cloned.1.call-start = ((), (), s32[]{:S(2)}) async-start(), calls=%async_computation.3 | async-start | bytes 3342336 | tf_op jit(solution)/shard_map/all_gather | solution.py:347
  73.1 5.5 %copy-start.22 = (f32[128]{0:T(128)S(1)}, f32[128]{0:T(128)}, u32[]{:S(2)}) copy-start(f32[128]{0:T(128)} %param.14) | copy-start | bytes 1540
  73.1 5.6 %copy-start.23 = (f32[128]{0:T(128)S(1)}, f32[128]{0:T(128)}, u32[]{:S(2)}) copy-start(f32[128]{0:T(128)} %param.13) | copy-start | bytes 1540
  75.5 27.7 %collective-permute-start = (bf16[8,576,128]{2,1,0:T(8,128)(2,1)}, bf16[8,576,128]{2,1,0:T(8,128)(2,1)S(1)}, u32[]{:S(2)}, u32[]{:S(2)}) collective-permute-start(bf16[8,576,128]{2,1,0:T(8,128)(2,1)} %slice.21), channel_id=1, source_target_pairs={{0,16},{16,0},{1,17},{17,1},{2,18},{18,2},{3,19},{19,3},{4,20},{20... | collective-permute-start | bytes 3538952 | tf_op jit(solution)/shard_map/ppermute | solution.py:359
  103.2 9.8 %copy-start.8 = (bf16[8,576,128]{2,1,0:T(8,128)(2,1)}, bf16[8,576,128]{2,1,0:T(8,128)(2,1)S(1)}, u32[]{:S(2)}) copy-start(bf16[8,576,128]{2,1,0:T(8,128)(2,1)S(1)} %collective-permute-done.refs_3_) | copy-start | bytes 3538948
  103.2 1.8 %copy-start.2 = (bf16[8,720,128]{2,1,0:T(8,128)(2,1)S(1)}, bf16[8,720,128]{2,1,0:T(8,128)(2,1)}, u32[]{:S(2)}) copy-start(bf16[8,720,128]{2,1,0:T(8,128)(2,1)} %copy-done.1) | copy-start | bytes 4423684
  105.0 1.9 %copy-start.13 = (bf16[512,3072]{1,0:T(8,128)(2,1)S(1)}, bf16[512,3072]{1,0:T(8,128)(2,1)}, u32[]{:S(2)}) copy-start(bf16[512,3072]{1,0:T(8,128)(2,1)} %all-gather.3.cloned.1.call-done.refs_1_) | copy-start | bytes 9437188
  113.6 24.8 %collective-permute-start.2 = (bf16[2,512,128]{2,1,0:T(8,128)(2,1)}, bf16[2,512,128]{2,1,0:T(8,128)(2,1)}, u32[]{:S(2)}, u32[]{:S(2)}) collective-permute-start(bf16[2,512,128]{2,1,0:T(8,128)(2,1)} %get-tuple-element.14.kva), channel_id=1, source_target_pairs={{0,16},{1,17},{2,18},{3,19},{4,20},{5,21},{6,22},{7,23},{8,24},{9,... | collective-permute-start | bytes 786440 | tf_op jit(solution)/shard_map/ppermute | solution.py:371
  118.7 1.4 copy-start.3
  120.0 1.9 %copy-start.6 = (bf16[512,3072]{1,0:T(8,128)(2,1)S(1)}, bf16[512,3072]{1,0:T(8,128)(2,1)}, u32[]{:S(2)}) copy-start(bf16[512,3072]{1,0:T(8,128)(2,1)} %all-gather.5.cloned.1.call-done.refs_1_) | copy-start | bytes 9437188
  125.1 6.5 %slice-start = ((bf16[8,720,128]{2,1,0:T(8,128)(2,1)}), bf16[8,128,128]{2,1,0:T(8,128)(2,1)S(1)}, s32[]{:S(2)}) async-start(bf16[8,720,128]{2,1,0:T(8,128)(2,1)} %copy-done.1), calls=%async_computation.4 | async-start | bytes 524288 | tf_op jit(solution)/shard_map/slice | solution.py:360
  125.1 6.6 %copy-start.15 = (f32[512,128]{1,0:T(8,128)S(1)}, f32[512,128]{1,0:T(8,128)}, u32[]{:S(2)}) copy-start(f32[512,128]{1,0:T(8,128)} %get-tuple-element.19.refs_5_) | copy-start | bytes 786436
  125.1 6.6 %copy-start.17 = (f32[512,128]{1,0:T(8,128)S(1)}, f32[512,128]{1,0:T(8,128)}, u32[]{:S(2)}) copy-start(f32[512,128]{1,0:T(8,128)} %get-tuple-element.20.refs_4_) | copy-start | bytes 786436
  127.4 14.6 %collective-permute-start.1 = (bf16[2,512,128]{2,1,0:T(8,128)(2,1)S(1)}, bf16[2,512,128]{2,1,0:T(8,128)(2,1)}, u32[]{:S(2)}, u32[]{:S(2)}) collective-permute-start(bf16[2,512,128]{2,1,0:T(8,128)(2,1)S(1)} %project_kv.1.kvb), channel_id=1, source_target_pairs={{0,16},{1,17},{2,18},{3,19},{4,20},{5,21},{6,22},{7,23},{8,24},{9,... | collective-permute-start | bytes 786440 | tf_op jit(solution)/shard_map/ppermute | solution.py:373
  131.7 1.4 copy-start.4
  133.1 1.9 %copy-start.7 = (bf16[512,3072]{1,0:T(8,128)(2,1)S(1)}, bf16[512,3072]{1,0:T(8,128)(2,1)}, u32[]{:S(2)}) copy-start(bf16[512,3072]{1,0:T(8,128)(2,1)} %all-gather.5.cloned.1.call-done.refs_1_) | copy-start | bytes 9437188
  136.2 2.2 %copy-start.21 = (bf16[512,128]{1,0:T(8,128)(2,1)S(1)}, bf16[512,128]{1,0:T(8,128)(2,1)}, u32[]{:S(2)}) copy-start(bf16[512,128]{1,0:T(8,128)(2,1)} %copy-done.20) | copy-start | bytes 393220
  143.7 13.2 %all-to-all-start.1 = ((bf16[8,2,64,128]{3,2,1,0:T(8,128)(2,1)}), bf16[8,2,64,128]{3,2,1,0:T(8,128)(2,1)S(1)}, u32[]{:S(2)}, u32[]{:S(2)}) async-start(bf16[8,2,64,128]{3,2,1,0:T(8,128)(2,1)} %attend_cond.1), calls=%async_computation.1 | async-start | bytes 524288 | tf_op jit(solution)/shard_map/all_to_all | solution.py:379
  156.9 2.8 %copy-start.5 = (bf16[1024,3072]{1,0:T(8,128)(2,1)S(1)}, bf16[1024,3072]{1,0:T(8,128)(2,1)}, u32[]{:S(2)}) copy-start(bf16[1024,3072]{1,0:T(8,128)(2,1)} %w_ref.3) | copy-start | bytes 18874372
  159.7 2.6 %copy-start.12 = (bf16[1,128,3072]{2,1,0:T(8,128)(2,1)S(1)}, bf16[1,128,3072]{2,1,0:T(8,128)(2,1)}, u32[]{:S(2)}) copy-start(bf16[1,128,3072]{2,1,0:T(8,128)(2,1)} %param.8) | copy-start | bytes 2359300
  160.9 10.6 %collective-permute-start.3 = (bf16[128,1536]{1,0:T(8,128)(2,1)S(1)}, bf16[128,1536]{1,0:T(8,128)(2,1)S(1)}, u32[]{:S(2)}, u32[]{:S(2)}) collective-permute-start(bf16[128,1536]{1,0:T(8,128)(2,1)S(1)} %out_sent.1), channel_id=1, source_target_pairs={{0,1},{1,0},{2,3},{3,2},{4,5},{5,4},{6,7},{7,6},{8,9},{9,8},{10,11... | collective-permute-start | bytes 1179656 | tf_op jit(solution)/shard_map/ppermute | solution.py:381
  (9 other events, 9.3 us)
Sparse Core Ops, SparseCore 0:
  9.9 62.8 all-gather.2
  75.0 43.6 all-gather.4

commit v4 on v3

--- a/solution.py
+++ b/solution.py
@@ -8,7 +8,7 @@
 HEAD_DIM = 128
 GRID_W = 64
 TILE = 128
-VMEM_LIMIT = 30 * 1024 * 1024
+VMEM_LIMIT = 56 * 1024 * 1024
 
 
 def axis_freqs(width):
@@ -40,47 +40,44 @@
     )
 
 
-CHUNKS = 2
-BLOCK = 256
 VMEM = pl.BlockSpec(memory_space=pltpu.VMEM)
 SMEM = pl.BlockSpec(memory_space=pltpu.SMEM)
 
 
-def call(kernel, name, out_shape, flops, moved, exps, **spec):
+def call(kernel, name, out_shape, flops, moved, exps, limit=VMEM_LIMIT, **spec):
     return pl.pallas_call(
         kernel,
         out_shape=out_shape,
-        compiler_params=pltpu.CompilerParams(vmem_limit_bytes=VMEM_LIMIT),
+        compiler_params=pltpu.CompilerParams(vmem_limit_bytes=limit),
         cost_estimate=pl.CostEstimate(flops=flops, bytes_accessed=moved, transcendentals=exps),
         name=name,
         **spec,
     )
 
 
-def norm_kernel(tp_ref, image_ref, mods_ref, *out_refs):
+def norm_kernel(tp_ref, image_ref, mods_ref, shared_ref, direct_ref):
     normed = layer_norm(image_ref[...].astype(jnp.float32), mods_ref[...])
-    rows = normed.shape[0] // len(out_refs)
-    for c, out_ref in enumerate(out_refs):
-        out_ref[...] = normed[c * rows : (c + 1) * rows]
-
-
-def norm_part(tp, parts, image, mods):
+    half = direct_ref.shape[0]
+    piece = shared_ref.shape[0]
+    direct_ref[...] = normed[half:]
+    for t in range(half // piece):
+
+        @pl.when(tp_ref[0] == t)
+        def _(t=t):
+            shared_ref[...] = normed[t * piece : (t + 1) * piece]
+
+
+def norm_tokens(tp, image, mods):
     rows, depth = image.shape
-    part = rows // parts
-    small = pl.BlockSpec((part // CHUNKS, depth), lambda i, tp: (0, 0))
     return call(
-        norm_kernel, "norm_part",
-        [jax.ShapeDtypeStruct((part // CHUNKS, depth), jnp.bfloat16)] * CHUNKS,
-        10 * part * depth, 4 * part * depth, 0,
-        grid_spec=pltpu.PrefetchScalarGridSpec(
-            num_scalar_prefetch=1,
-            grid=(1,),
-            in_specs=[
-                pl.BlockSpec((part, depth), lambda i, tp: (tp[0], 0)),
-                pl.BlockSpec(mods.shape, lambda i, tp: (0, 0)),
-            ],
-            out_specs=[small] * CHUNKS,
-        ),
+        norm_kernel, "norm_tokens",
+        [
+            jax.ShapeDtypeStruct((rows // 4, depth), jnp.bfloat16),
+            jax.ShapeDtypeStruct((rows // 2, depth), jnp.bfloat16),
+        ],
+        10 * rows * depth, 4 * rows * depth, 0,
+        in_specs=[SMEM, VMEM, VMEM],
+        out_specs=[VMEM, VMEM],
     )(tp, image, mods)
 
 
@@ -91,21 +88,25 @@
     return (x * cosine + other * sine).astype(jnp.bfloat16)
 
 
-def project_kernel(kinds, section_ref, x_ref, mine, peer, cos_ref, sin_ref, gain_ref, *refs):
-    out_refs, acc_ref = refs[:-1], refs[-1]
+def project_kernel(kinds, counts, section_ref, x_ref, cos_ref, sin_ref, gain_ref, *refs):
+    pairs = [refs[2 * i : 2 * i + 2] for i in range(len(counts))]
+    out_refs, acc_ref = refs[2 * len(counts) : -1], refs[-1]
     step = pl.program_id(0)
-    half = peer.shape[1] // 3
     first = section_ref[0] == 0
 
-    def piece(s, kind):
-        at = slice(kind * half, (kind + 1) * half)
+    def piece(mine, peer, s, place):
+        half = peer.shape[1] // place[1]
+        at = slice(place[0] * half, (place[0] + 1) * half)
         a, b = mine[s, at, :], peer[s, at, :]
         return jnp.concatenate([jnp.where(first, a, b), jnp.where(first, b, a)], axis=0)
 
     w = jnp.concatenate(
         [
-            jnp.concatenate([piece(s, kind) for s in range(mine.shape[0])], axis=0)
-            for kind in kinds
+            jnp.concatenate(
+                [piece(mine, peer, s, (k, count)) for s in range(mine.shape[0])], axis=0
+            )
+            for (mine, peer), count in zip(pairs, counts)
+            for k in range(count)
         ],
         axis=1,
     )
@@ -128,45 +129,45 @@
                     value, gain_ref[kind : kind + 1, :], cos_ref[...], sin_ref[...]
                 )
             if kind == 0:
-                out_refs[0][...] = value
+                out_refs[-1][...] = value
             else:
-                out_refs[-1][kind - 1] = value.astype(jnp.bfloat16)
-
-
-def project(kinds, section, x, mine, peer, cosine, sine, gains):
+                out_refs[0][kind - 1] = value.astype(jnp.bfloat16)
+
+
+def project(kinds, section, x, tables, gains, *pairs):
     rows, depth = x.shape
-    sources = mine.shape[0]
+    sources = pairs[0][0].shape[0]
     steps = 4
     out_shape, out_specs = [], []
+    if 1 in kinds:
+        out_shape.append(jax.ShapeDtypeStruct((2, rows, HEAD_DIM), jnp.bfloat16))
+        out_specs.append(pl.BlockSpec((2, rows, HEAD_DIM), lambda k, s: (0, 0, 0)))
     if 0 in kinds:
         out_shape.append(jax.ShapeDtypeStruct((rows, HEAD_DIM), jnp.bfloat16))
         out_specs.append(pl.BlockSpec((rows, HEAD_DIM), lambda k, s: (0, 0)))
-    if 1 in kinds:
-        out_shape.append(jax.ShapeDtypeStruct((2, rows, HEAD_DIM), jnp.bfloat16))
-        out_specs.append(pl.BlockSpec((2, rows, HEAD_DIM), lambda k, s: (0, 0, 0)))
 
     def pieces(array):
         return pl.BlockSpec((sources // steps,) + array.shape[1:], lambda k, s: (k, 0, 0))
 
+    half = depth // sources // 2
+    counts = [peer.shape[1] // half for _, peer in pairs]
+    weights = [array for pair in pairs for array in pair]
+    table = pl.BlockSpec((rows, HEAD_DIM), lambda k, s: (0, 0))
     return call(
-        lambda *refs: project_kernel(kinds, *refs), "project_" + "".join("qkv"[k] for k in kinds),
+        lambda *refs: project_kernel(kinds, counts, *refs),
+        "project_" + "".join("qkv"[k] for k in kinds),
         out_shape,
-        2 * len(kinds) * rows * depth * HEAD_DIM, 2 * (x.size + mine.size + peer.size), 0,
+        2 * len(kinds) * rows * depth * HEAD_DIM, 2 * (x.size + sum(w.size for w in weights)), 0,
         grid_spec=pltpu.PrefetchScalarGridSpec(
             num_scalar_prefetch=1,
             grid=(steps,),
-            in_specs=[
-                pl.BlockSpec((rows, depth // steps), lambda k, s: (0, k)),
-                pieces(mine),
-                pieces(peer),
-                pl.BlockSpec((rows, HEAD_DIM), lambda k, s: (0, 0)),
-                pl.BlockSpec((rows, HEAD_DIM), lambda k, s: (0, 0)),
-                pl.BlockSpec((2, HEAD_DIM), lambda k, s: (0, 0)),
-            ],
+            in_specs=[pl.BlockSpec((rows, depth // steps), lambda k, s: (0, k))]
+            + [table, table, pl.BlockSpec((2, HEAD_DIM), lambda k, s: (0, 0))]
+            + [pieces(w) for w in weights],
             out_specs=out_specs,
             scratch_shapes=[pltpu.VMEM((rows, len(kinds) * HEAD_DIM), jnp.float32)],
         ),
-    )(section, x, mine, peer, cosine, sine, gains)
+    )(section, x, *tables, gains, *weights)
 
 
 def weights_of(query, keys):
@@ -189,56 +190,57 @@
     return (weights.reshape(tiles, rows // tiles, keys) * keep[:, None, :]).reshape(rows, keys)
 
 
+def query_blocks(qa, qb, tiles):
+    rows = qa.shape[0]
+    for b in range(2):
+        piece = rows // 2 // tiles
+        yield qa, b * rows // 2, b * rows // 2, slice(0, tiles), slice(b * piece, (b + 1) * piece)
+    piece = rows // tiles
+    for b in range(2):
+        at = slice(b * tiles // 2, (b + 1) * tiles // 2)
+        yield qb, b * rows // 2, rows + b * rows // 2, at, slice(piece, 2 * piece)
+
+
 def own_kernel(section_ref, keep_ref, qa, qb, kva, kvb, text, conda, num_ref, den_ref):
-    rows = qa.shape[0]
-    tiles = keep_ref.shape[0] * BLOCK // rows
-    for c, q_ref in enumerate((qa, qb)):
-        for b in range(rows // BLOCK):
-            query = q_ref[b * BLOCK : (b + 1) * BLOCK, :]
-            at = pl.ds(c * rows + b * BLOCK, BLOCK)
-            num, den = 0.0, 0.0
-            for ref in (kva, kvb, text):
-                more = summed(weights_of(query, ref[0]), ref[1])
-                num, den = num + more[0], den + more[1]
-            num_ref[at, :] = num
-            den_ref[at, :] = jnp.broadcast_to(den, num.shape)
+    size = qa.shape[0] // 2
+    for q_ref, start, place, _, _ in query_blocks(qa, qb, keep_ref.shape[0]):
+        query = q_ref[start : start + size, :]
+        num, den = 0.0, 0.0
+        for ref in (kva, kvb, text):
+            more = summed(weights_of(query, ref[0]), ref[1])
+            num, den = num + more[0], den + more[1]
+        num_ref[place : place + size, :] = num
+        den_ref[place : place + size, :] = jnp.broadcast_to(den, num.shape)
 
     @pl.when(section_ref[0] != 0)
     def _():
-        for c, q_ref in enumerate((qa, qb)):
-            for b in range(rows // BLOCK):
-                query = q_ref[b * BLOCK : (b + 1) * BLOCK, :]
-                at = pl.ds(c * rows + b * BLOCK, BLOCK)
-                keep = keep_ref[b * tiles : (b + 1) * tiles, :]
-                num, den = summed(kept_weights(query, conda, keep), conda[1])
-                num_ref[at, :] += num
-                den_ref[at, :] += jnp.broadcast_to(den, num.shape)
+        for q_ref, start, place, tiles, _ in query_blocks(qa, qb, keep_ref.shape[0]):
+            query = q_ref[start : start + size, :]
+            num, den = summed(kept_weights(query, conda, keep_ref[tiles, :]), conda[1])
+            num_ref[place : place + size, :] += num
+            den_ref[place : place + size, :] += jnp.broadcast_to(den, num.shape)
 
 
 def cond_kernel(section_ref, keep_ref, qa, qb, condb, num_ref, den_ref, out_ref):
-    rows = qa.shape[0]
-    tiles = keep_ref.shape[0] * BLOCK // rows
-
-    def store(c, b, num, den):
-        value = (num / den).astype(jnp.bfloat16).reshape(tiles, -1, HEAD_DIM)
-        out_ref[b * tiles : (b + 1) * tiles, c] = value
+    size = qa.shape[0] // 2
+
+    def store(tiles, shard_rows, num, den):
+        value = (num / den).astype(jnp.bfloat16)
+        out_ref[tiles, shard_rows, :] = value.reshape(tiles.stop - tiles.start, -1, HEAD_DIM)
 
     @pl.when(section_ref[0] == 0)
     def _():
-        for c in range(CHUNKS):
-            for b in range(rows // BLOCK):
-                at = pl.ds(c * rows + b * BLOCK, BLOCK)
-                store(c, b, num_ref[at, :], den_ref[at, :])
+        for _, _, place, tiles, shard_rows in query_blocks(qa, qb, keep_ref.shape[0]):
+            at = slice(place, place + size)
+            store(tiles, shard_rows, num_ref[at, :], den_ref[at, :])
 
     @pl.when(section_ref[0] != 0)
     def _():
-        for c, q_ref in enumerate((qa, qb)):
-            for b in range(rows // BLOCK):
-                query = q_ref[b * BLOCK : (b + 1) * BLOCK, :]
-                at = pl.ds(c * rows + b * BLOCK, BLOCK)
-                keep = keep_ref[b * tiles : (b + 1) * tiles, :]
-                num, den = summed(kept_weights(query, condb, keep), condb[1])
-                store(c, b, num_ref[at, :] + num, den_ref[at, :] + den)
+        for q_ref, start, place, tiles, shard_rows in query_blocks(qa, qb, keep_ref.shape[0]):
+            query = q_ref[start : start + size, :]
+            at = slice(place, place + size)
+            num, den = summed(kept_weights(query, condb, keep_ref[tiles, :]), condb[1])
+            store(tiles, shard_rows, num_ref[at, :] + num, den_ref[at, :] + den)
 
 
 def attend_own(section, keep, queries, kvs, text, cond):
@@ -257,7 +259,7 @@
     keys = cond.shape[1]
     return call(
         cond_kernel, "attend_cond",
-        jax.ShapeDtypeStruct((seq, CHUNKS, rows // seq // CHUNKS, HEAD_DIM), jnp.bfloat16),
+        jax.ShapeDtypeStruct((seq, rows // seq, HEAD_DIM), jnp.bfloat16),
         4 * rows * keys * HEAD_DIM, 2 * rows * HEAD_DIM * 8, rows * keys,
         in_specs=[SMEM] + [VMEM] * 6,
         out_specs=VMEM,
@@ -265,23 +267,7 @@
 
 
 def token_rows(attn_ref):
-    heads, chunks, held, _ = attn_ref.shape
-    parts = 2
-    piece = held // parts
-    return jnp.concatenate(
-        [
-            jnp.concatenate(
-                [
-                    attn_ref[h, c, t * piece : (t + 1) * piece, :]
-                    for t in range(parts)
-                    for c in range(chunks)
-                ],
-                axis=0,
-            )
-            for h in range(heads)
-        ],
-        axis=1,
-    )
+    return jnp.concatenate([attn_ref[h] for h in range(attn_ref.shape[0])], axis=1)
 
 
 def sent_kernel(half_ref, attn_ref, w_ref, out_ref):
@@ -295,7 +281,7 @@
 
 
 def project_out(half, attn, w_out, image=None, gate=None):
-    rows = attn.shape[1] * attn.shape[2]
+    rows = attn.shape[1]
     depth, width = w_out.shape[0], w_out.shape[1] // 2
     block = 512
     steps = width // block
@@ -307,11 +293,11 @@
     return call(
         kept_kernel if kept else sent_kernel, "out_kept" if kept else "out_sent",
         jax.ShapeDtypeStruct((rows, width), jnp.float32 if kept else jnp.bfloat16),
-        2 * rows * depth * width, 2 * depth * width, 0,
+        2 * rows * depth * width, 2 * depth * width, 0, 24 * 1024 * 1024,
         grid_spec=pltpu.PrefetchScalarGridSpec(
             num_scalar_prefetch=1,
             grid=(steps,),
-            in_specs=[pl.BlockSpec(attn.shape, lambda i, half: (0, 0, 0, 0)), columns(depth)]
+            in_specs=[pl.BlockSpec(attn.shape, lambda i, half: (0, 0, 0)), columns(depth)]
             + ([columns(rows), columns(1)] if kept else []),
             out_specs=pl.BlockSpec((rows, block), lambda i, half: (0, i)),
         ),
@@ -333,52 +319,69 @@
 
 def head_body(image, text_kv, modulation, w_qkv, w_out, q_gain, k_gain, region_mask):
     seq = lax.axis_size("seq")
-    parts = lax.axis_size("tp")
     img_rows = image.shape[1]
     depth = w_qkv.shape[0]
     section = lax.axis_index("section")
     tp = lax.axis_index("tp")
+    core = lax.axis_index("seq") % 2
     mods = modulation[0]
     section_at = section.astype(jnp.int32).reshape(1)
     tp_at = tp.astype(jnp.int32).reshape(1)
-
-    piece = img_rows // parts // CHUNKS
-    normed = norm_part(tp_at, parts, image[0], mods)
-    xs = [lax.all_gather(n, ("seq", "tp"), axis=0, tiled=True) for n in normed]
+    both = [(0, 1), (1, 0)]
 
     half = depth // 2
     w_half = lax.dynamic_slice_in_dim(w_qkv.transpose(1, 0, 2), section * half, half, 1)
-    w_half = w_half.reshape(3, half, seq, HEAD_DIM).transpose(2, 0, 1, 3).reshape(seq, -1, HEAD_DIM)
+    w_half = w_half.reshape(3, half, seq, HEAD_DIM).transpose(2, 0, 1, 3)
     text = text_kv[0].reshape(-1, 2, seq, HEAD_DIM).transpose(2, 0, 1, 3).reshape(seq, -1, HEAD_DIM)
     mask = jnp.pad(
         region_mask.astype(jnp.bfloat16), ((0, 15), (0, HEAD_DIM - region_mask.shape[1]))
     )
     mask = jnp.broadcast_to(mask, (seq,) + mask.shape)
-    mine = lax.all_to_all(jnp.concatenate([w_half, text, mask], axis=1), "seq", 0, 0)
-    w_rows = 3 * half
-    peer = lax.ppermute(mine[:, :w_rows], "section", [(0, 1), (1, 0)])
-    text = mine[:, w_rows:-16].reshape(-1, 2, HEAD_DIM).transpose(1, 0, 2)
-    keep = mine[:, -16, : region_mask.shape[1]].astype(jnp.float32)
-    keep = jnp.repeat(keep, parts * piece, axis=1)
+    kv_mine = lax.all_to_all(w_half[:, 1:].reshape(seq, -1, HEAD_DIM), "seq", 0, 0)
+    kv_peer = lax.ppermute(kv_mine, "section", both)
+    q_mine = lax.all_to_all(jnp.concatenate([w_half[:, 0], text, mask], axis=1), "seq", 0, 0)
+    q_peer = lax.ppermute(q_mine[:, :half], "section", both)
+    text = q_mine[:, half:-16].reshape(-1, 2, HEAD_DIM).transpose(1, 0, 2)
+    keep = q_mine[:, -16, : region_mask.shape[1]].astype(jnp.float32)
+
+    shared, direct = norm_tokens(tp_at, image[0], mods)
+    ours = lax.all_gather(shared, "seq", axis=0, tiled=True)
+    count = ours.shape[0] // 2
+    theirs = lax.ppermute(lax.dynamic_slice_in_dim(ours, core * count, count, 0), "tp", both)
+    swapped = lax.ppermute(theirs, "seq", [(s, s ^ 1) for s in range(seq)])
+    theirs = jnp.concatenate(
+        [jnp.where(core == 0, theirs, swapped), jnp.where(core == 0, swapped, theirs)], axis=0
+    )
+    x_a = jnp.concatenate(
+        [jnp.where(tp == 0, ours, theirs), jnp.where(tp == 0, theirs, ours)], axis=0
+    )
+    x_b = lax.all_gather(direct, "seq", axis=0, tiled=True)
 
     time_index = (section == 0).astype(jnp.float32)
-    index = jnp.arange(seq * parts * piece, dtype=jnp.int32)
-    index = index // piece * (CHUNKS * piece) + index % piece
-    tables = [lane_tables(index + c * piece, time_index) for c in range(CHUNKS)]
+    index = jnp.arange(x_a.shape[0], dtype=jnp.int32)
+    piece = img_rows // 4
+    index_a = index // piece % seq * img_rows + index // (seq * piece) * piece + index % piece
+    index_b = index // (2 * piece) * img_rows + 2 * piece + index % (2 * piece)
+    tables_a = lane_tables(index_a, time_index)
+    tables_b = lane_tables(index_b, time_index)
     gains = jnp.stack([q_gain, k_gain])
-
-    q_a, kv_a = project((0, 1, 2), section_at, xs[0], mine, peer, *tables[0], gains)
+    keep_a = jnp.tile(jnp.repeat(keep, piece, axis=1), (1, 2))
+    keep_b = jnp.repeat(keep, 2 * piece, axis=1)
+
+    kv_pair, q_pair = (kv_mine, kv_peer), (q_mine, q_peer)
+    (kv_a,) = project((1, 2), section_at, x_a, tables_a, gains, kv_pair)
     cond_a = lax.ppermute(kv_a, "section", [(0, 1)])
-    (kv_b,) = project((1, 2), section_at, xs[1], mine, peer, *tables[1], gains)
+    (q_a,) = project((0,), section_at, x_a, tables_a, gains, q_pair)
+    (kv_b,) = project((1, 2), section_at, x_b, tables_b, gains, kv_pair)
     cond_b = lax.ppermute(kv_b, "section", [(0, 1)])
-    (q_b,) = project((0,), section_at, xs[1], mine, peer, *tables[1], gains)
+    (q_b,) = project((0,), section_at, x_b, tables_b, gains, q_pair)
     queries = (q_a, q_b)
-    num, den = attend_own(section_at, keep, queries, (kv_a, kv_b), text, cond_a)
-    attn = attend_cond(section_at, keep, queries, cond_b, num, den)
+    num, den = attend_own(section_at, keep_a, queries, (kv_a, kv_b), text, cond_a)
+    attn = attend_cond(section_at, keep_b, queries, cond_b, num, den)
 
     attn = lax.all_to_all(attn, "seq", 0, 0)
     gate = mods[2:3]
-    other = lax.ppermute(project_out(1 - tp_at, attn, w_out), "tp", [(0, 1), (1, 0)])
+    other = lax.ppermute(project_out(1 - tp_at, attn, w_out), "tp", both)
     kept = project_out(tp_at, attn, w_out, image[0], gate)
     gate = lax.dynamic_slice_in_dim(gate, tp * other.shape[1], other.shape[1], 1)
     return (kept + gate * other.astype(jnp.float32)).astype(jnp.bfloat16)[None]
@@ -479,10 +482,9 @@
         and lax.axis_size("tp") == 2
         and w_qkv.shape[0] % 128 == 0
         and image.shape[1] == TILE
-        and image.shape[1] * seq % (2 * BLOCK) == 0
+        and region_mask.shape == (1, seq)
         and arrays[1].shape[1] % 16 == 0
         and arrays[4].shape[1] % 1024 == 0
-        and region_mask.shape[1] <= HEAD_DIM
     )
     return (head_body if one_head_each else token_body)(*arrays)
 

time: 180 us -> 195 us (1.083)
  blocking collectives: 60.8 us -> 0 us
  waiting for transfers between devices: 40.6 us -> 95.8 us
  Pallas kernels: 17.6 us -> 32.3 us
  starting transfers between devices: 13.7 us -> 25.2 us
  local copies, waits for them, and re-layouts: 28.6 us -> 17.9 us
  other arithmetic: 4.15 us -> 9.66 us
    all_to_all x1 -> x0, blocking collectives: 60.8 us -> none  [head_body(): lax.all_to_all(jnp.concatenate([w_half, text, mask], axis=1), 'seq', 0, 0)]
    all_gather x2, waiting for transfers between devices: 0.96 us -> 32 us  [the longest x1 32 us: head_body(): ours = lax.all_gather(shared, 'seq', axis=0, tiled=True)]
    all_to_all x0 -> x2, waiting for transfers between devices: none -> 21.4 us  [the longest x1 21.4 us: head_body(): lax.all_to_all(w_half[:, 1:].reshape(seq, -1, HEAD_DIM), 'seq', 0, 0)]
    pallas_call x5 -> x6, Pallas kernels: 11.4 us -> 24.9 us  [the longest x4 20.1 us: project(): call(lambda *refs: project_kernel(kinds, counts, *refs), 'project_' + ''....]
    unnamed x51 -> x27, local copies, waits for them, and re-layouts: 23.2 us -> 9.89 us
    all_to_all x0 -> x2, starting transfers between devices: none -> 10.5 us  [the longest x1 6.33 us: head_body(): lax.all_to_all(jnp.concatenate([w_half[:, 0], text, mask], axis=1), 'seq'...]
    ppermute x2 -> x5, starting transfers between devices: 2.11 us -> 5.29 us  [the longest x1 1.47 us: head_body(): lax.ppermute(lax.dynamic_slice_in_dim(ours, core * count, count, 0), 'tp'...]
    ppermute x2 -> x5, waiting for transfers between devices: 29.2 us -> 32 us  [the longest x1 14.4 us: head_body(): kv_peer = lax.ppermute(kv_mine, 'section', both)]
  transfers between devices with their start and end apart: 7 -> 12, of which waited for: 4 -> 6; matrix products, arithmetic and copies ran while one was open for 5% -> 9% of each run, Pallas kernels for 8% -> 14%
where the time goes in v4:
time: 195 us; the launch traced here: 194 us
  waiting for transfers between devices  95.8 us (49%)
  Pallas kernels  32.3 us (17%)
  starting transfers between devices  25.2 us (13%)
  local copies, waits for them, and re-layouts  17.9 us (9%)
  between operations  13.7 us (7%)
  other arithmetic  9.66 us (5%)
    all_gather x1, waiting for transfers between devices, head_body(): ours = lax.all_gather(shared, 'seq', axis=0, tiled=True)  32 us
    all_to_all x1, waiting for transfers between devices, head_body(): lax.all_to_all(w_half[:, 1:].reshape(seq, -1, HEAD_DIM), 'seq', 0, 0)  21.4 us
    pallas_call x4, Pallas kernels, project(): call(lambda *refs: project_kernel(kinds, counts, *refs), 'project_' + ''....  20.1 us
    ppermute x1, waiting for transfers between devices, head_body(): kv_peer = lax.ppermute(kv_mine, 'section', both)  14.4 us
    ppermute x1, waiting for transfers between devices, head_body(): lax.ppermute(lax.dynamic_slice_in_dim(ours, core * count, count, 0), 'tp'...  13 us
    unnamed x27, local copies, waits for them, and re-layouts  9.89 us
    all_to_all x1, waiting for transfers between devices, head_body(): attn = lax.all_to_all(attn, 'seq', 0, 0)  9.66 us
    all_to_all x1, starting transfers between devices, head_body(): lax.all_to_all(jnp.concatenate([w_half[:, 0], text, mask], axis=1), 'seq'...  6.33 us
  transfers between devices with their start and end apart: 12, of which 6 were waited for; matrix products, arithmetic and copies ran while one was open for 9% of the time, Pallas kernels for 14%

profile of v4, /device:TPU:0, one launch (start us, length us, event | category | flops | bytes accessed | tf_op | source)
XLA Modules:
  0.0 194.4 jit_solution(10853264191026202222)
XLA Ops:
  6.6 1.5 copy.21
  8.1 2.6 %norm_tokens.1 = (bf16[32,3072]{1,0:T(8,128)(2,1)}, bf16[64,3072]{1,0:T(8,128)(2,1)}) custom-call(s32[1]{0:T(128)} %bitcast.tp_ref.half_ref, bf16[128,3072]{1,0:T(8,128)(2,1)} %bitcast.32, f32[3,3072]{1,0:T(4,128)} %bitcast.38), custom_call_target="tpu_custom_call" | custom-call | flops 3932160 | bytes 1572864 | tf_op jit(solution)/shard_map/norm_tokens/pallas_call | solution.py:72
  14.2 6.3 %all-to-all-start = ((bf16[8,336,128]{2,1,0:T(8,128)(2,1)}), bf16[8,336,128]{2,1,0:T(8,128)(2,1)S(1)}, u32[]{:S(2)}, u32[]{:S(2)}) async-start(bf16[8,336,128]{2,1,0:T(8,128)(2,1)} %pad_maximum_fusion.2), calls=%async_computation | async-start | bytes 1376256 | tf_op jit(solution)/shard_map/all_to_all | solution.py:342
  20.6 32.0 %all-gather.3.cloned.1.call-done = bf16[256,3072]{1,0:T(8,128)(2,1)} async-done(((bf16[32,3072]{1,0:T(8,128)(2,1)}), bf16[256,3072]{1,0:T(8,128)(2,1)}) %all-gather.3.cloned.1.call-update) | async-done | bytes 1572880 | tf_op jit(solution)/shard_map/all_gather | solution.py:348
  52.6 2.2 %constant_dynamic-slice_fusion = bf16[128,3072]{1,0:T(8,128)(2,1)} fusion(bf16[256,3072]{1,0:T(8,128)(2,1)} %all-gather.3.cloned.1.call-done, s32[]{:T(128)S(6)} %select_n.182), kind=kLoop, calls=%fused_computation.78 | loop fusion | bytes 1572868 | tf_op jit(solution)/shard_map/dynamic_slice | solution.py:350
  57.3 4.2 %all-to-all-start.1 = ((bf16[8,384,128]{2,1,0:T(8,128)(2,1)}), bf16[8,384,128]{2,1,0:T(8,128)(2,1)}, u32[]{:S(2)}, u32[]{:S(2)}) async-start(bf16[8,384,128]{2,1,0:T(8,128)(2,1)} %bitcast.34), calls=%async_computation.1 | async-start | bytes 1572864 | tf_op jit(solution)/shard_map/all_to_all | solution.py:340
  61.8 13.0 %collective-permute-done = bf16[128,3072]{1,0:T(8,128)(2,1)} collective-permute-done((bf16[128,3072]{1,0:T(8,128)(2,1)}, bf16[128,3072]{1,0:T(8,128)(2,1)}, u32[]{:S(2)}, u32[]{:S(2)}) %collective-permute-start) | collective-permute-done | bytes 786464 | tf_op jit(solution)/shard_map/ppermute | solution.py:350
  75.4 3.1 %sine_multiply_fusion = (f32[512,128]{1,0:T(8,128)}, f32[512,128]{1,0:T(8,128)}, f32[512,128]{1,0:T(8,128)}, f32[512,128]{1,0:T(8,128)}) fusion(f32[512]{0:T(512)S(1)} %get-tuple-element.28, f32[512]{0:T(512)S(1)} %get-tuple-element.27, f32[128]{0:T(128)S(1)} %compare_select_fusion, f32[128]{0:T(128)S(1)} %mul.100, f32[]{:T(128)S(6)} %convert_element_type.63, ...), kind=kLoop, calls=%fused_computation.13 | loop fusion | flops 524288 | bytes 1058052 | tf_op jit(solution)/shard_map/mul | solution.py:317
  80.8 21.4 %all-to-all-done.1.refs_5_ = bf16[8,384,128]{2,1,0:T(8,128)(2,1)} async-done(((bf16[8,384,128]{2,1,0:T(8,128)(2,1)}), bf16[8,384,128]{2,1,0:T(8,128)(2,1)}, u32[]{:S(2)}, u32[]{:S(2)}) %all-to-all-start.1) | async-done | bytes 786464 | tf_op jit(solution)/shard_map/all_to_all | solution.py:340
  105.7 1.9 pad_maximum_fusion.refs_1_
  107.6 14.4 %collective-permute-done.3.refs_6_ = bf16[8,384,128]{2,1,0:T(8,128)(2,1)S(1)} collective-permute-done((bf16[8,384,128]{2,1,0:T(8,128)(2,1)}, bf16[8,384,128]{2,1,0:T(8,128)(2,1)S(1)}, u32[]{:S(2)}, u32[]{:S(2)}) %collective-permute-start.3) | collective-permute-done | bytes 786464 | tf_op jit(solution)/shard_map/ppermute | solution.py:341
  122.9 5.1 %project_kv.3.kva = bf16[2,512,128]{2,1,0:T(8,128)(2,1)} custom-call(s32[1]{0:T(128)} %bitcast.1.refs_0_.section_ref, bf16[512,3072]{1,0:T(8,128)(2,1)} %pad_maximum_fusion.refs_1_, f32[512,128]{1,0:T(8,128)} %get-tuple-element.23.refs_2_, f32[512,128]{1,0:T(8,128)} %get-tuple-element.24.refs_3_, f32[2,128]{1,0:T(2,128)} %pad_maximum_fusion.3.refs_4_, ...), custom_call_target="tpu_custom_call" | custom-call | flops 805306368 | bytes 4718592 | tf_op jit(solution)/shard_map/project_kv/pallas_call | solution.py:156
  128.1 3.9 %collective-permute-start.5 = (bf16[2,512,128]{2,1,0:T(8,128)(2,1)}, bf16[2,512,128]{2,1,0:T(8,128)(2,1)}, u32[]{:S(2)}, u32[]{:S(2)}) collective-permute-start(bf16[2,512,128]{2,1,0:T(8,128)(2,1)} %project_kv.3.kva), channel_id=1, source_target_pairs={{0,16},{1,17},{2,18},{3,19},{4,20},{5,21},{6,22},{7,23},{8,24},{9,... | collective-permute-start | bytes 786440 | tf_op jit(solution)/shard_map/ppermute | solution.py:373
  132.0 5.1 %project_kv.2.kvb = bf16[2,512,128]{2,1,0:T(8,128)(2,1)} custom-call(s32[1]{0:T(128)} %bitcast.1.refs_0_.section_ref, bf16[512,3072]{1,0:T(8,128)(2,1)} %all-gather.5.cloned.1.call-done.refs_1_, f32[512,128]{1,0:T(8,128)} %get-tuple-element.20.refs_2_, f32[512,128]{1,0:T(8,128)} %get-tuple-element.19.refs_3_, f32[2,128]{1,0:T(2,128)} %pad_maximum_fusion.3.refs_4_, ...), custom_call_target="tpu_custom_call" | custom-call | flops 805306368 | bytes 4718592 | tf_op jit(solution)/shard_map/project_kv/pallas_call | solution.py:156
  137.1 2.0 %collective-permute-start.4 = (bf16[2,512,128]{2,1,0:T(8,128)(2,1)}, bf16[2,512,128]{2,1,0:T(8,128)(2,1)}, u32[]{:S(2)}, u32[]{:S(2)}) collective-permute-start(bf16[2,512,128]{2,1,0:T(8,128)(2,1)} %project_kv.2.kvb), channel_id=1, source_target_pairs={{0,16},{1,17},{2,18},{3,19},{4,20},{5,21},{6,22},{7,23},{8,24},{9,... | collective-permute-start | bytes 786440 | tf_op jit(solution)/shard_map/ppermute | solution.py:376
  141.5 4.9 %project_q.2.qa = bf16[512,128]{1,0:T(8,128)(2,1)} custom-call(s32[1]{0:T(128)} %bitcast.1.refs_0_.section_ref, bf16[512,3072]{1,0:T(8,128)(2,1)} %pad_maximum_fusion.refs_1_, f32[512,128]{1,0:T(8,128)} %get-tuple-element.23.refs_2_, f32[512,128]{1,0:T(8,128)} %get-tuple-element.24.refs_3_, f32[2,128]{1,0:T(2,128)} %pad_maximum_fusion.3.refs_4_, ...), custom_call_target="tpu_custom_call" | custom-call | flops 402653184 | bytes 4227072 | tf_op jit(solution)/shard_map/project_q/pallas_call | solution.py:156
  146.4 4.9 %project_q.3.qb = bf16[512,128]{1,0:T(8,128)(2,1)} custom-call(s32[1]{0:T(128)} %bitcast.1.refs_0_.section_ref, bf16[512,3072]{1,0:T(8,128)(2,1)} %all-gather.5.cloned.1.call-done.refs_1_, f32[512,128]{1,0:T(8,128)} %get-tuple-element.20.refs_2_, f32[512,128]{1,0:T(8,128)} %get-tuple-element.19.refs_3_, f32[2,128]{1,0:T(2,128)} %pad_maximum_fusion.3.refs_4_, ...), custom_call_target="tpu_custom_call" | custom-call | flops 402653184 | bytes 4227072 | tf_op jit(solution)/shard_map/project_q/pallas_call | solution.py:156
  152.0 4.8 %attend_own.1 = (f32[1024,128]{1,0:T(8,128)}, f32[1024,128]{1,0:T(8,128)}) custom-call(s32[1]{0:T(128)} %bitcast.1.refs_0_.section_ref, f32[8,512]{1,0:T(8,128)} %bitcast.41, bf16[512,128]{1,0:T(8,128)(2,1)} %project_q.2.qa, bf16[512,128]{1,0:T(8,128)(2,1)} %project_q.3.qb, bf16[2,512,128]{2,1,0:T(8,128)(2,1)} %project_kv.3.kva, ...), custom_call_target="tpu_custom_call" | custom-call | flops 1073741824 | bytes 2621440 | tf_op jit(solution)/shard_map/attend_own/pallas_call | solution.py:249
  156.8 2.2 %attend_cond.1 = bf16[8,128,128]{2,1,0:T(8,128)(2,1)} custom-call(s32[1]{0:T(128)} %bitcast.1.refs_0_.section_ref, f32[8,512]{1,0:T(8,128)} %reshape.189.keep_ref, bf16[512,128]{1,0:T(8,128)(2,1)} %project_q.2.qa, bf16[512,128]{1,0:T(8,128)(2,1)} %project_q.3.qb, bf16[2,512,128]{2,1,0:T(8,128)(2,1)} %collective-permute-done.4.condb, ...), custom_call_target="tpu_custom_call" | custom-call | flops 268435456 | bytes 2097152 | tf_op jit(solution)/shard_map/attend_cond/pallas_call | solution.py:260
  159.0 3.4 %all-to-all-start.2 = ((bf16[8,128,128]{2,1,0:T(8,128)(2,1)}), bf16[8,128,128]{2,1,0:T(8,128)(2,1)S(1)}, u32[]{:S(2)}, u32[]{:S(2)}) async-start(bf16[8,128,128]{2,1,0:T(8,128)(2,1)} %attend_cond.1), calls=%async_computation.2 | async-start | bytes 524288 | tf_op jit(solution)/shard_map/all_to_all | solution.py:382
  162.5 9.7 %all-to-all-done.2.attn_ref = bf16[8,128,128]{2,1,0:T(8,128)(2,1)S(1)} async-done(((bf16[8,128,128]{2,1,0:T(8,128)(2,1)}), bf16[8,128,128]{2,1,0:T(8,128)(2,1)S(1)}, u32[]{:S(2)}, u32[]{:S(2)}) %all-to-all-start.2) | async-done | bytes 262176 | tf_op jit(solution)/shard_map/all_to_all | solution.py:382
  172.1 2.8 %copy-done.1 = bf16[1024,3072]{1,0:T(8,128)(2,1)S(1)} copy-done((bf16[1024,3072]{1,0:T(8,128)(2,1)S(1)}, bf16[1024,3072]{1,0:T(8,128)(2,1)}, u32[]{:S(2)}) %copy-start.1) | copy-done | bytes 6291480
  178.0 2.8 %copy-done.2 = bf16[1024,3072]{1,0:T(8,128)(2,1)S(1)} copy-done((bf16[1024,3072]{1,0:T(8,128)(2,1)S(1)}, bf16[1024,3072]{1,0:T(8,128)(2,1)}, u32[]{:S(2)}) %copy-start.2) | copy-done | bytes 6291480
  182.1 4.6 %collective-permute-done.6 = bf16[128,1536]{1,0:T(8,128)(2,1)S(1)} collective-permute-done((bf16[128,1536]{1,0:T(8,128)(2,1)S(1)}, bf16[128,1536]{1,0:T(8,128)(2,1)S(1)}, u32[]{:S(2)}, u32[]{:S(2)}) %collective-permute-start.6) | collective-permute-done | bytes 393248 | tf_op jit(solution)/shard_map/ppermute | solution.py:384
  (76 shorter events, 21.8 us)
Async XLA Ops:
  6.5 5.3 %copy-start = (bf16[384,3,1024]{2,0,1:T(8,128)(2,1)S(1)}, bf16[384,3,1024]{2,0,1:T(8,128)(2,1)}, u32[]{:S(2)}) copy-start(bf16[384,3,1024]{2,0,1:T(8,128)(2,1)} %param.11) | copy-start | bytes 7077892
  6.5 4.9 %copy-start.9 = (bf16[1,64,2,1024]{3,2,1,0:T(2,128)(2,1)S(1)}, bf16[1,64,2,1024]{3,2,1,0:T(2,128)(2,1)}, u32[]{:S(2)}) copy-start(bf16[1,64,2,1024]{3,2,1,0:T(2,128)(2,1)} %param.9) | copy-start | bytes 786436
  6.5 5.3 %copy-start.12 = (s32[1,8]{1,0:T(1,128)S(1)}, s32[1,8]{1,0:T(1,128)}, u32[]{:S(2)}) copy-start(s32[1,8]{1,0:T(1,128)} %param.15) | copy-start | bytes 100
  6.5 46.1 %all-gather.3.cloned.1.call-start = ((), (), s32[]{:S(2)}) async-start(), calls=%async_computation.3 | async-start | bytes 1769472 | tf_op jit(solution)/shard_map/all_gather | solution.py:348
  10.7 121.3 %all-gather.5.cloned.1.call-start = ((), (), s32[]{:S(2)}) async-start(), calls=%async_computation.4 | async-start | bytes 3538944 | tf_op jit(solution)/shard_map/all_gather | solution.py:358
  12.2 1.1 copy-start.5
  14.2 43.0 %all-to-all-start = ((bf16[8,336,128]{2,1,0:T(8,128)(2,1)}), bf16[8,336,128]{2,1,0:T(8,128)(2,1)S(1)}, u32[]{:S(2)}, u32[]{:S(2)}) async-start(bf16[8,336,128]{2,1,0:T(8,128)(2,1)} %pad_maximum_fusion.2), calls=%async_computation | async-start | bytes 1376256 | tf_op jit(solution)/shard_map/all_to_all | solution.py:342
  52.6 3.7 %slice-start = ((bf16[8,3,192,128]{3,2,0,1:T(8,128)(2,1)}), bf16[8,2,192,128]{3,2,0,1:T(8,128)(2,1)S(1)}, s32[]{:S(2)}) async-start(bf16[8,3,192,128]{3,2,0,1:T(8,128)(2,1)} %copy-done.5), calls=%async_computation.5 | async-start | bytes 1572864 | tf_op jit(solution)/shard_map/slice | solution.py:340
  54.8 20.0 %collective-permute-start = (bf16[128,3072]{1,0:T(8,128)(2,1)}, bf16[128,3072]{1,0:T(8,128)(2,1)}, u32[]{:S(2)}, u32[]{:S(2)}) collective-permute-start(bf16[128,3072]{1,0:T(8,128)(2,1)} %constant_dynamic-slice_fusion), channel_id=1, source_target_pairs={{0,1},{1,0},{2,3},{3,2},{4,5},{5,4},{6,7},{7,6},{8,9},{9,8},{10,11... | collective-permute-start | bytes 2359304 | tf_op jit(solution)/shard_map/ppermute | solution.py:350
  56.3 18.5 %copy-start.10 = (f32[128]{0:T(128)S(1)}, f32[128]{0:T(128)}, u32[]{:S(2)}) copy-start(f32[128]{0:T(128)} %param.14) | copy-start | bytes 1540
  56.3 18.5 %copy-start.11 = (f32[128]{0:T(128)S(1)}, f32[128]{0:T(128)}, u32[]{:S(2)}) copy-start(f32[128]{0:T(128)} %param.13) | copy-start | bytes 1540
  57.3 82.0 %copy-start.4 = (bf16[8,336,128]{2,1,0:T(8,128)(2,1)}, bf16[8,336,128]{2,1,0:T(8,128)(2,1)S(1)}, u32[]{:S(2)}) copy-start(bf16[8,336,128]{2,1,0:T(8,128)(2,1)S(1)} %all-to-all-done.refs_5_) | copy-start | bytes 2064388
  57.3 44.9 %all-to-all-start.1 = ((bf16[8,384,128]{2,1,0:T(8,128)(2,1)}), bf16[8,384,128]{2,1,0:T(8,128)(2,1)}, u32[]{:S(2)}, u32[]{:S(2)}) async-start(bf16[8,384,128]{2,1,0:T(8,128)(2,1)} %bitcast.34), calls=%async_computation.1 | async-start | bytes 1572864 | tf_op jit(solution)/shard_map/all_to_all | solution.py:340
  74.8 28.7 %collective-permute-start.1 = (bf16[128,3072]{1,0:T(8,128)(2,1)}, bf16[128,3072]{1,0:T(8,128)(2,1)}, u32[]{:S(2)}, u32[]{:S(2)}) collective-permute-start(bf16[128,3072]{1,0:T(8,128)(2,1)} %collective-permute-done), channel_id=1, source_target_pairs={{0,2},{2,0},{4,6},{6,4},{8,10},{10,8},{12,14},{14,12},{1,3},{3,1},... | collective-permute-start | bytes 2359304 | tf_op jit(solution)/shard_map/ppermute | solution.py:351
  79.3 61.4 %collective-permute-start.2 = (bf16[8,192,128]{2,1,0:T(8,128)(2,1)}, bf16[8,192,128]{2,1,0:T(8,128)(2,1)S(1)}, u32[]{:S(2)}, u32[]{:S(2)}) collective-permute-start(bf16[8,192,128]{2,1,0:T(8,128)(2,1)} %slice.30), channel_id=1, source_target_pairs={{0,16},{16,0},{1,17},{17,1},{2,18},{18,2},{3,19},{19,3},{4,20},{20... | collective-permute-start | bytes 1179656 | tf_op jit(solution)/shard_map/ppermute | solution.py:343
  102.2 2.8 %copy-start.6 = (bf16[256,3072]{1,0:T(8,128)(2,1)S(1)}, bf16[256,3072]{1,0:T(8,128)(2,1)}, u32[]{:S(2)}) copy-start(bf16[256,3072]{1,0:T(8,128)(2,1)} %all-gather.3.cloned.1.call-done) | copy-start | bytes 4718596
  102.2 19.8 %collective-permute-start.3 = (bf16[8,384,128]{2,1,0:T(8,128)(2,1)}, bf16[8,384,128]{2,1,0:T(8,128)(2,1)S(1)}, u32[]{:S(2)}, u32[]{:S(2)}) collective-permute-start(bf16[8,384,128]{2,1,0:T(8,128)(2,1)} %all-to-all-done.1.refs_5_), channel_id=1, source_target_pairs={{0,16},{16,0},{1,17},{17,1},{2,18},{18,2},{3,19},{19,3},{4,20},{20... | collective-permute-start | bytes 2359304 | tf_op jit(solution)/shard_map/ppermute | solution.py:341
  128.1 23.3 %collective-permute-start.5 = (bf16[2,512,128]{2,1,0:T(8,128)(2,1)}, bf16[2,512,128]{2,1,0:T(8,128)(2,1)}, u32[]{:S(2)}, u32[]{:S(2)}) collective-permute-start(bf16[2,512,128]{2,1,0:T(8,128)(2,1)} %project_kv.3.kva), channel_id=1, source_target_pairs={{0,16},{1,17},{2,18},{3,19},{4,20},{5,21},{6,22},{7,23},{8,24},{9,... | collective-permute-start | bytes 786440 | tf_op jit(solution)/shard_map/ppermute | solution.py:373
  137.1 19.8 %collective-permute-start.4 = (bf16[2,512,128]{2,1,0:T(8,128)(2,1)}, bf16[2,512,128]{2,1,0:T(8,128)(2,1)}, u32[]{:S(2)}, u32[]{:S(2)}) collective-permute-start(bf16[2,512,128]{2,1,0:T(8,128)(2,1)} %project_kv.2.kvb), channel_id=1, source_target_pairs={{0,16},{1,17},{2,18},{3,19},{4,20},{5,21},{6,22},{7,23},{8,24},{9,... | collective-permute-start | bytes 786440 | tf_op jit(solution)/shard_map/ppermute | solution.py:376
  159.0 13.1 %all-to-all-start.2 = ((bf16[8,128,128]{2,1,0:T(8,128)(2,1)}), bf16[8,128,128]{2,1,0:T(8,128)(2,1)S(1)}, u32[]{:S(2)}, u32[]{:S(2)}) async-start(bf16[8,128,128]{2,1,0:T(8,128)(2,1)} %attend_cond.1), calls=%async_computation.2 | async-start | bytes 524288 | tf_op jit(solution)/shard_map/all_to_all | solution.py:382
  172.1 2.8 %copy-start.1 = (bf16[1024,3072]{1,0:T(8,128)(2,1)S(1)}, bf16[1024,3072]{1,0:T(8,128)(2,1)}, u32[]{:S(2)}) copy-start(bf16[1024,3072]{1,0:T(8,128)(2,1)} %w_ref.3) | copy-start | bytes 18874372
  174.9 3.1 %copy-start.3 = (bf16[1,128,3072]{2,1,0:T(8,128)(2,1)S(1)}, bf16[1,128,3072]{2,1,0:T(8,128)(2,1)}, u32[]{:S(2)}) copy-start(bf16[1,128,3072]{2,1,0:T(8,128)(2,1)} %param.8) | copy-start | bytes 2359300
  176.2 10.6 %collective-permute-start.6 = (bf16[128,1536]{1,0:T(8,128)(2,1)S(1)}, bf16[128,1536]{1,0:T(8,128)(2,1)S(1)}, u32[]{:S(2)}, u32[]{:S(2)}) collective-permute-start(bf16[128,1536]{1,0:T(8,128)(2,1)S(1)} %out_sent.1), channel_id=1, source_target_pairs={{0,1},{1,0},{2,3},{3,2},{4,5},{5,4},{6,7},{7,6},{8,9},{9,8},{10,11... | collective-permute-start | bytes 1179656 | tf_op jit(solution)/shard_map/ppermute | solution.py:384
  178.0 2.8 %copy-start.2 = (bf16[1024,3072]{1,0:T(8,128)(2,1)S(1)}, bf16[1024,3072]{1,0:T(8,128)(2,1)}, u32[]{:S(2)}) copy-start(bf16[1024,3072]{1,0:T(8,128)(2,1)} %w_ref.3) | copy-start | bytes 18874372
  (2 other events, 1.7 us)
Sparse Core Ops, SparseCore 0:
  10.8 41.7 all-gather.2
  54.2 53.9 all-gather.4

commit v5 on v4

--- a/solution.py
+++ b/solution.py
@@ -8,7 +8,7 @@
 HEAD_DIM = 128
 GRID_W = 64
 TILE = 128
-VMEM_LIMIT = 56 * 1024 * 1024
+VMEM_LIMIT = 20 * 1024 * 1024
 
 
 def axis_freqs(width):
@@ -55,16 +55,18 @@
     )
 
 
-def norm_kernel(tp_ref, image_ref, mods_ref, shared_ref, direct_ref):
-    normed = layer_norm(image_ref[...].astype(jnp.float32), mods_ref[...])
-    half = direct_ref.shape[0]
-    piece = shared_ref.shape[0]
-    direct_ref[...] = normed[half:]
-    for t in range(half // piece):
+def norm_kernel(tp_ref, image_ref, mods_ref, full_ref, part_ref):
+    mods = jnp.concatenate([mods_ref[0], mods_ref[1]], axis=0)
+    normed = layer_norm(image_ref[...].astype(jnp.float32), mods)
+    part = part_ref.shape[0]
+    for t in range(2):
 
         @pl.when(tp_ref[0] == t)
         def _(t=t):
-            shared_ref[...] = normed[t * piece : (t + 1) * piece]
+            ours, theirs = normed[t * part : (t + 1) * part], normed[(1 - t) * part : (2 - t) * part]
+            full_ref[:part, :] = ours
+            full_ref[part:, :] = theirs
+            part_ref[...] = ours
 
 
 def norm_tokens(tp, image, mods):
@@ -72,7 +74,7 @@
     return call(
         norm_kernel, "norm_tokens",
         [
-            jax.ShapeDtypeStruct((rows // 4, depth), jnp.bfloat16),
+            jax.ShapeDtypeStruct((rows, depth), jnp.bfloat16),
             jax.ShapeDtypeStruct((rows // 2, depth), jnp.bfloat16),
         ],
         10 * rows * depth, 4 * rows * depth, 0,
@@ -88,29 +90,26 @@
     return (x * cosine + other * sine).astype(jnp.bfloat16)
 
 
-def project_kernel(kinds, counts, section_ref, x_ref, cos_ref, sin_ref, gain_ref, *refs):
-    pairs = [refs[2 * i : 2 * i + 2] for i in range(len(counts))]
-    out_refs, acc_ref = refs[2 * len(counts) : -1], refs[-1]
+def project_kernel(kinds, pieces, section_ref, mine, peer, cos_ref, sin_ref, gain_ref, *refs):
+    x_refs, out_refs, acc_ref = refs[:pieces], refs[pieces:-1], refs[-1]
     step = pl.program_id(0)
+    half = peer.shape[1] // 3
     first = section_ref[0] == 0
 
-    def piece(mine, peer, s, place):
-        half = peer.shape[1] // place[1]
-        at = slice(place[0] * half, (place[0] + 1) * half)
+    def rows_of(s, kind):
+        at = slice(kind * half, (kind + 1) * half)
         a, b = mine[s, at, :], peer[s, at, :]
         return jnp.concatenate([jnp.where(first, a, b), jnp.where(first, b, a)], axis=0)
 
     w = jnp.concatenate(
         [
-            jnp.concatenate(
-                [piece(mine, peer, s, (k, count)) for s in range(mine.shape[0])], axis=0
-            )
-            for (mine, peer), count in zip(pairs, counts)
-            for k in range(count)
+            jnp.concatenate([rows_of(s, kind) for s in range(mine.shape[0])], axis=0)
+            for kind in kinds
         ],
         axis=1,
     )
-    part = jnp.dot(x_ref[...], w, preferred_element_type=jnp.float32)
+    x = jnp.concatenate([ref[...] for ref in x_refs], axis=0)
+    part = jnp.dot(x, w, preferred_element_type=jnp.float32)
 
     @pl.when(step == 0)
     def _():
@@ -129,45 +128,37 @@
                     value, gain_ref[kind : kind + 1, :], cos_ref[...], sin_ref[...]
                 )
             if kind == 0:
-                out_refs[-1][...] = value
+                out_refs[0][...] = value
             else:
                 out_refs[0][kind - 1] = value.astype(jnp.bfloat16)
 
 
-def project(kinds, section, x, tables, gains, *pairs):
-    rows, depth = x.shape
-    sources = pairs[0][0].shape[0]
+def project(kinds, section, pieces, mine, peer, cosine, sine, gains):
+    depth = pieces[0].shape[1]
+    rows = sum(p.shape[0] for p in pieces)
+    sources = mine.shape[0]
     steps = 4
-    out_shape, out_specs = [], []
-    if 1 in kinds:
-        out_shape.append(jax.ShapeDtypeStruct((2, rows, HEAD_DIM), jnp.bfloat16))
-        out_specs.append(pl.BlockSpec((2, rows, HEAD_DIM), lambda k, s: (0, 0, 0)))
-    if 0 in kinds:
-        out_shape.append(jax.ShapeDtypeStruct((rows, HEAD_DIM), jnp.bfloat16))
-        out_specs.append(pl.BlockSpec((rows, HEAD_DIM), lambda k, s: (0, 0)))
-
-    def pieces(array):
+    shape = (rows, HEAD_DIM) if kinds == (0,) else (2, rows, HEAD_DIM)
+
+    def weights(array):
         return pl.BlockSpec((sources // steps,) + array.shape[1:], lambda k, s: (k, 0, 0))
 
-    half = depth // sources // 2
-    counts = [peer.shape[1] // half for _, peer in pairs]
-    weights = [array for pair in pairs for array in pair]
     table = pl.BlockSpec((rows, HEAD_DIM), lambda k, s: (0, 0))
     return call(
-        lambda *refs: project_kernel(kinds, counts, *refs),
+        lambda *refs: project_kernel(kinds, len(pieces), *refs),
         "project_" + "".join("qkv"[k] for k in kinds),
-        out_shape,
-        2 * len(kinds) * rows * depth * HEAD_DIM, 2 * (x.size + sum(w.size for w in weights)), 0,
+        jax.ShapeDtypeStruct(shape, jnp.bfloat16),
+        2 * len(kinds) * rows * depth * HEAD_DIM, 2 * (rows * depth + mine.size + peer.size), 0,
         grid_spec=pltpu.PrefetchScalarGridSpec(
             num_scalar_prefetch=1,
             grid=(steps,),
-            in_specs=[pl.BlockSpec((rows, depth // steps), lambda k, s: (0, k))]
+            in_specs=[weights(mine), weights(peer)]
             + [table, table, pl.BlockSpec((2, HEAD_DIM), lambda k, s: (0, 0))]
-            + [pieces(w) for w in weights],
-            out_specs=out_specs,
+            + [pl.BlockSpec((p.shape[0], depth // steps), lambda k, s: (0, k)) for p in pieces],
+            out_specs=pl.BlockSpec(shape, lambda k, s: (0,) * len(shape)),
             scratch_shapes=[pltpu.VMEM((rows, len(kinds) * HEAD_DIM), jnp.float32)],
         ),
-    )(section, x, *tables, gains, *weights)
+    )(section, mine, peer, cosine, sine, gains, *pieces)
 
 
 def weights_of(query, keys):
@@ -186,84 +177,83 @@
 def kept_weights(query, cond_ref, keep):
     weights = weights_of(query, cond_ref[0])
     rows, keys = weights.shape
-    tiles = keep.shape[0]
-    return (weights.reshape(tiles, rows // tiles, keys) * keep[:, None, :]).reshape(rows, keys)
-
-
-def query_blocks(qa, qb, tiles):
-    rows = qa.shape[0]
-    for b in range(2):
-        piece = rows // 2 // tiles
-        yield qa, b * rows // 2, b * rows // 2, slice(0, tiles), slice(b * piece, (b + 1) * piece)
-    piece = rows // tiles
-    for b in range(2):
-        at = slice(b * tiles // 2, (b + 1) * tiles // 2)
-        yield qb, b * rows // 2, rows + b * rows // 2, at, slice(piece, 2 * piece)
-
-
-def own_kernel(section_ref, keep_ref, qa, qb, kva, kvb, text, conda, num_ref, den_ref):
-    size = qa.shape[0] // 2
-    for q_ref, start, place, _, _ in query_blocks(qa, qb, keep_ref.shape[0]):
-        query = q_ref[start : start + size, :]
+    groups = keep.shape[0]
+    return (weights.reshape(groups, rows // groups, keys) * keep[:, None, :]).reshape(rows, keys)
+
+
+BLOCK = 256
+
+
+def own_kernel(section_ref, keep_ref, q_ref, kva, kvb, text, conda, num_ref, den_ref):
+    rows = q_ref.shape[0]
+    groups = keep_ref.shape[0] * BLOCK // rows
+    for b in range(rows // BLOCK):
+        at = slice(b * BLOCK, (b + 1) * BLOCK)
         num, den = 0.0, 0.0
         for ref in (kva, kvb, text):
-            more = summed(weights_of(query, ref[0]), ref[1])
+            more = summed(weights_of(q_ref[at, :], ref[0]), ref[1])
             num, den = num + more[0], den + more[1]
-        num_ref[place : place + size, :] = num
-        den_ref[place : place + size, :] = jnp.broadcast_to(den, num.shape)
+        num_ref[at, :] = num
+        den_ref[at, :] = jnp.broadcast_to(den, num.shape)
 
     @pl.when(section_ref[0] != 0)
     def _():
-        for q_ref, start, place, tiles, _ in query_blocks(qa, qb, keep_ref.shape[0]):
-            query = q_ref[start : start + size, :]
-            num, den = summed(kept_weights(query, conda, keep_ref[tiles, :]), conda[1])
-            num_ref[place : place + size, :] += num
-            den_ref[place : place + size, :] += jnp.broadcast_to(den, num.shape)
-
-
-def cond_kernel(section_ref, keep_ref, qa, qb, condb, num_ref, den_ref, out_ref):
-    size = qa.shape[0] // 2
-
-    def store(tiles, shard_rows, num, den):
+        for b in range(rows // BLOCK):
+            at = slice(b * BLOCK, (b + 1) * BLOCK)
+            keep = keep_ref[b * groups : (b + 1) * groups, :]
+            num, den = summed(kept_weights(q_ref[at, :], conda, keep), conda[1])
+            num_ref[at, :] += num
+            den_ref[at, :] += jnp.broadcast_to(den, num.shape)
+
+
+def cond_kernel(section_ref, place_ref, keep_ref, q_ref, condb, num_ref, den_ref, out_ref):
+    rows = q_ref.shape[0]
+    groups = keep_ref.shape[0] * BLOCK // rows
+    size = BLOCK // groups
+
+    def store(b, num, den):
         value = (num / den).astype(jnp.bfloat16)
-        out_ref[tiles, shard_rows, :] = value.reshape(tiles.stop - tiles.start, -1, HEAD_DIM)
+        for g in range(groups):
+            shard, part = place_ref[0, b * groups + g], place_ref[1, b * groups + g]
+            at = pl.ds(pl.multiple_of(part * size, size), size)
+            out_ref[shard, at, :] = value[g * size : (g + 1) * size]
 
     @pl.when(section_ref[0] == 0)
     def _():
-        for _, _, place, tiles, shard_rows in query_blocks(qa, qb, keep_ref.shape[0]):
-            at = slice(place, place + size)
-            store(tiles, shard_rows, num_ref[at, :], den_ref[at, :])
+        for b in range(rows // BLOCK):
+            at = slice(b * BLOCK, (b + 1) * BLOCK)
+            store(b, num_ref[at, :], den_ref[at, :])
 
     @pl.when(section_ref[0] != 0)
     def _():
-        for q_ref, start, place, tiles, shard_rows in query_blocks(qa, qb, keep_ref.shape[0]):
-            query = q_ref[start : start + size, :]
-            at = slice(place, place + size)
-            num, den = summed(kept_weights(query, condb, keep_ref[tiles, :]), condb[1])
-            store(tiles, shard_rows, num_ref[at, :] + num, den_ref[at, :] + den)
-
-
-def attend_own(section, keep, queries, kvs, text, cond):
-    rows = 2 * queries[0].shape[0]
+        for b in range(rows // BLOCK):
+            at = slice(b * BLOCK, (b + 1) * BLOCK)
+            keep = keep_ref[b * groups : (b + 1) * groups, :]
+            num, den = summed(kept_weights(q_ref[at, :], condb, keep), condb[1])
+            store(b, num_ref[at, :] + num, den_ref[at, :] + den)
+
+
+def attend_own(section, keep, query, kvs, text, cond):
+    rows = query.shape[0]
     keys = rows + text.shape[1] + cond.shape[1]
     return call(
         own_kernel, "attend_own", [jax.ShapeDtypeStruct((rows, HEAD_DIM), jnp.float32)] * 2,
         4 * rows * keys * HEAD_DIM, 2 * rows * HEAD_DIM * 10, rows * keys,
-        in_specs=[SMEM] + [VMEM] * 7,
+        in_specs=[SMEM] + [VMEM] * 6,
         out_specs=[VMEM] * 2,
-    )(section, keep, *queries, *kvs, text, cond)
-
-
-def attend_cond(section, keep, queries, cond, num, den):
-    rows, seq = num.shape[0], keep.shape[0]
+    )(section, keep, query, *kvs, text, cond)
+
+
+def attend_cond(section, place, keep, query, cond, num, den, seq):
+    rows = num.shape[0]
     keys = cond.shape[1]
     return call(
         cond_kernel, "attend_cond",
         jax.ShapeDtypeStruct((seq, rows // seq, HEAD_DIM), jnp.bfloat16),
         4 * rows * keys * HEAD_DIM, 2 * rows * HEAD_DIM * 8, rows * keys,
-        in_specs=[SMEM] + [VMEM] * 6,
+        in_specs=[SMEM, SMEM] + [VMEM] * 5,
         out_specs=VMEM,
-    )(section, keep, *queries, cond, num, den)
+    )(section, place, keep, query, cond, num, den)
 
 
 def token_rows(attn_ref):
@@ -293,7 +283,7 @@
     return call(
         kept_kernel if kept else sent_kernel, "out_kept" if kept else "out_sent",
         jax.ShapeDtypeStruct((rows, width), jnp.float32 if kept else jnp.bfloat16),
-        2 * rows * depth * width, 2 * depth * width, 0, 24 * 1024 * 1024,
+        2 * rows * depth * width, 2 * depth * width, 0,
         grid_spec=pltpu.PrefetchScalarGridSpec(
             num_scalar_prefetch=1,
             grid=(steps,),
@@ -317,13 +307,17 @@
     return jnp.cos(angles), jnp.sin(angles) * jnp.where(lane % 2 == 0, -1.0, 1.0)
 
 
+def z_pairs(seq, pairs):
+    return [(2 * a + core, 2 * b + core) for a, b in pairs for core in range(2)]
+
+
 def head_body(image, text_kv, modulation, w_qkv, w_out, q_gain, k_gain, region_mask):
     seq = lax.axis_size("seq")
     img_rows = image.shape[1]
     depth = w_qkv.shape[0]
     section = lax.axis_index("section")
     tp = lax.axis_index("tp")
-    core = lax.axis_index("seq") % 2
+    chip, core = lax.axis_index("seq") // 2, lax.axis_index("seq") % 2
     mods = modulation[0]
     section_at = section.astype(jnp.int32).reshape(1)
     tp_at = tp.astype(jnp.int32).reshape(1)
@@ -331,53 +325,62 @@
 
     half = depth // 2
     w_half = lax.dynamic_slice_in_dim(w_qkv.transpose(1, 0, 2), section * half, half, 1)
-    w_half = w_half.reshape(3, half, seq, HEAD_DIM).transpose(2, 0, 1, 3)
+    w_half = w_half.reshape(3, half, seq, HEAD_DIM).transpose(2, 0, 1, 3).reshape(seq, -1, HEAD_DIM)
     text = text_kv[0].reshape(-1, 2, seq, HEAD_DIM).transpose(2, 0, 1, 3).reshape(seq, -1, HEAD_DIM)
     mask = jnp.pad(
         region_mask.astype(jnp.bfloat16), ((0, 15), (0, HEAD_DIM - region_mask.shape[1]))
     )
     mask = jnp.broadcast_to(mask, (seq,) + mask.shape)
-    kv_mine = lax.all_to_all(w_half[:, 1:].reshape(seq, -1, HEAD_DIM), "seq", 0, 0)
-    kv_peer = lax.ppermute(kv_mine, "section", both)
-    q_mine = lax.all_to_all(jnp.concatenate([w_half[:, 0], text, mask], axis=1), "seq", 0, 0)
-    q_peer = lax.ppermute(q_mine[:, :half], "section", both)
-    text = q_mine[:, half:-16].reshape(-1, 2, HEAD_DIM).transpose(1, 0, 2)
-    keep = q_mine[:, -16, : region_mask.shape[1]].astype(jnp.float32)
-
-    shared, direct = norm_tokens(tp_at, image[0], mods)
-    ours = lax.all_gather(shared, "seq", axis=0, tiled=True)
-    count = ours.shape[0] // 2
-    theirs = lax.ppermute(lax.dynamic_slice_in_dim(ours, core * count, count, 0), "tp", both)
-    swapped = lax.ppermute(theirs, "seq", [(s, s ^ 1) for s in range(seq)])
-    theirs = jnp.concatenate(
-        [jnp.where(core == 0, theirs, swapped), jnp.where(core == 0, swapped, theirs)], axis=0
-    )
-    x_a = jnp.concatenate(
-        [jnp.where(tp == 0, ours, theirs), jnp.where(tp == 0, theirs, ours)], axis=0
-    )
-    x_b = lax.all_gather(direct, "seq", axis=0, tiled=True)
-
-    time_index = (section == 0).astype(jnp.float32)
-    index = jnp.arange(x_a.shape[0], dtype=jnp.int32)
-    piece = img_rows // 4
-    index_a = index // piece % seq * img_rows + index // (seq * piece) * piece + index % piece
-    index_b = index // (2 * piece) * img_rows + 2 * piece + index % (2 * piece)
-    tables_a = lane_tables(index_a, time_index)
-    tables_b = lane_tables(index_b, time_index)
+    mine = lax.all_to_all(jnp.concatenate([w_half, text, mask], axis=1), "seq", 0, 0)
+    peer = lax.ppermute(mine[:, : 3 * half], "section", both)
+    text = mine[:, 3 * half : -16].reshape(-1, 2, HEAD_DIM).transpose(1, 0, 2)
+    keep = mine[:, -16, : region_mask.shape[1]].astype(jnp.float32)
+
+    full, part = norm_tokens(tp_at, image[0], modulation.transpose(1, 0, 2))
+
+    def along_z(x, pairs):
+        return lax.ppermute(x, "seq", z_pairs(seq, pairs))
+
+    near = along_z(part, [(0, 1), (1, 0), (2, 3), (3, 2)])
+    middle = along_z(part, [(1, 2), (2, 1)])
+    far = along_z(near, [(1, 2), (2, 1)])
+    middle_end = along_z(middle, [(1, 0), (2, 3)])
+    far_end = along_z(far, [(1, 0), (2, 3)])
+    inner = (chip == 1) | (chip == 2)
+    third = jnp.where(inner, middle, middle_end)
+    fourth = jnp.where(inner, far, far_end)
+    groups = [full]
+    for came in (near, third, fourth):
+        groups.append(jnp.concatenate([came, lax.ppermute(came, "tp", both)], axis=0))
+    pieces = [
+        (g, lax.ppermute(g, "seq", [(s, s ^ 1) for s in range(seq)])) for g in groups
+    ]
+
+    upper = chip >= 2
+    chips = jnp.stack([chip, chip ^ 1, jnp.where(upper, 1, 2), jnp.where(upper, 0, 3)])
+    cores = jnp.stack([core, 1 - core])
+    parts = jnp.stack([tp, 1 - tp])
+    shards = chips[:, None, None] * 2 + cores[None, :, None] + 0 * parts[None, None, :]
+    parts = parts[None, None, :] + 0 * shards
+    shards, parts = shards.reshape(-1).astype(jnp.int32), parts.reshape(-1).astype(jnp.int32)
+    size = img_rows // 2
+    first_row = shards * img_rows + parts * size
+    rows_index = (first_row[:, None] + jnp.arange(size, dtype=jnp.int32)[None]).reshape(-1)
+    cosine, sine = lane_tables(rows_index, (section == 0).astype(jnp.float32))
     gains = jnp.stack([q_gain, k_gain])
-    keep_a = jnp.tile(jnp.repeat(keep, piece, axis=1), (1, 2))
-    keep_b = jnp.repeat(keep, 2 * piece, axis=1)
-
-    kv_pair, q_pair = (kv_mine, kv_peer), (q_mine, q_peer)
-    (kv_a,) = project((1, 2), section_at, x_a, tables_a, gains, kv_pair)
+    chosen = (shards[:, None] == jnp.arange(seq)[None]).astype(jnp.float32)
+    keep = jnp.repeat(chosen @ keep @ chosen.T, size, axis=1)
+
+    rows = rows_index.shape[0] // 2
+    a, b = list(pieces[0] + pieces[1]), list(pieces[2] + pieces[3])
+    kv_a = project((1, 2), section_at, a, mine, peer, cosine[:rows], sine[:rows], gains)
     cond_a = lax.ppermute(kv_a, "section", [(0, 1)])
-    (q_a,) = project((0,), section_at, x_a, tables_a, gains, q_pair)
-    (kv_b,) = project((1, 2), section_at, x_b, tables_b, gains, kv_pair)
+    kv_b = project((1, 2), section_at, b, mine, peer, cosine[rows:], sine[rows:], gains)
     cond_b = lax.ppermute(kv_b, "section", [(0, 1)])
-    (q_b,) = project((0,), section_at, x_b, tables_b, gains, q_pair)
-    queries = (q_a, q_b)
-    num, den = attend_own(section_at, keep_a, queries, (kv_a, kv_b), text, cond_a)
-    attn = attend_cond(section_at, keep_b, queries, cond_b, num, den)
+    query = project((0,), section_at, a + b, mine, peer, cosine, sine, gains)
+    num, den = attend_own(section_at, keep[:, :rows], query, (kv_a, kv_b), text, cond_a)
+    place = jnp.stack([shards, parts])
+    attn = attend_cond(section_at, place, keep[:, rows:], query, cond_b, num, den, seq)
 
     attn = lax.all_to_all(attn, "seq", 0, 0)
     gate = mods[2:3]
@@ -476,8 +479,7 @@
     image, w_qkv, region_mask = arrays[0], arrays[3], arrays[7]
     seq = lax.axis_size("seq")
     one_head_each = (
-        w_qkv.shape[2] // HEAD_DIM == seq
-        and seq % 4 == 0
+        w_qkv.shape[2] // HEAD_DIM == seq == 8
         and lax.axis_size("section") == 2
         and lax.axis_size("tp") == 2
         and w_qkv.shape[0] % 128 == 0

time: 195 us -> 161 us (0.83)
  waiting for transfers between devices: 95.8 us -> 68.8 us
  between operations: 13.7 us -> 0.41 us
  Pallas kernels: 32.3 us -> 22.4 us
  local copies, waits for them, and re-layouts: 17.9 us -> 25.1 us
  other arithmetic: 9.66 us -> 13.8 us
  starting transfers between devices: 25.2 us -> 28.3 us
    all_gather x2 -> x0, waiting for transfers between devices: 32 us -> none  [the longest x1 32 us: head_body(): ours = lax.all_gather(shared, 'seq', axis=0, tiled=True)]
    ppermute x4 -> x13, waiting for transfers between devices: 27.3 us -> 54 us  [the longest x5 40 us: along_z(): return lax.ppermute(x, 'seq', z_pairs(seq, pairs))]
    all_to_all x2 -> x1, waiting for transfers between devices: 21.4 us -> 0.01 us  [head_body(): lax.all_to_all(jnp.concatenate([w_half, text, mask], axis=1), 'seq', 0, 0)]
    ppermute x4 -> x13, starting transfers between devices: 4.24 us -> 14.5 us  [the longest x5 7.7 us: along_z(): return lax.ppermute(x, 'seq', z_pairs(seq, pairs))]
    pallas_call x5 -> x4, Pallas kernels: 22.7 us -> 15.9 us  [the longest x3 14.4 us: project(): call(lambda *refs: project_kernel(kinds, len(pieces), *refs), 'project_'...]
    all_to_all x2 -> x1, starting transfers between devices: 10.5 us -> 5.06 us  [head_body(): lax.all_to_all(jnp.concatenate([w_half, text, mask], axis=1), 'seq', 0, 0)]
    slice x5, local copies, waits for them, and re-layouts: 1.8 us -> 5.72 us  [the longest x1 2.37 us: head_body(): peer = lax.ppermute(mine[:, :3 * half], 'section', both)]
    unnamed x27 -> x47, local copies, waits for them, and re-layouts: 9.89 us -> 12.5 us
  transfers between devices with their start and end apart: 12 -> 18, of which waited for: 6 -> 6; matrix products, arithmetic and copies ran while one was open for 9% -> 18% of each run, Pallas kernels for 14% -> 11%
where the time goes in v5:
time: 161 us; the launch traced here: 160 us
  waiting for transfers between devices  68.8 us (43%)
  starting transfers between devices  28.3 us (18%)
  local copies, waits for them, and re-layouts  25.1 us (16%)
  Pallas kernels  22.4 us (14%)
  other arithmetic  13.8 us (9%)
    ppermute x5, waiting for transfers between devices, along_z(): return lax.ppermute(x, 'seq', z_pairs(seq, pairs))  40 us
    pallas_call x3, Pallas kernels, project(): call(lambda *refs: project_kernel(kinds, len(pieces), *refs), 'project_'...  14.4 us
    unnamed x47, local copies, waits for them, and re-layouts  12.5 us
    ppermute x1, waiting for transfers between devices, head_body(): peer = lax.ppermute(mine[:, :3 * half], 'section', both)  12.2 us
    all_to_all x1, waiting for transfers between devices, head_body(): attn = lax.all_to_all(attn, 'seq', 0, 0)  9.66 us
    ppermute x5, starting transfers between devices, along_z(): return lax.ppermute(x, 'seq', z_pairs(seq, pairs))  7.7 us
    ppermute x1, waiting for transfers between devices, head_body(): other = lax.ppermute(project_out(1 - tp_at, attn, w_out), 'tp', both)  5.12 us
    all_to_all x1, starting transfers between devices, head_body(): lax.all_to_all(jnp.concatenate([w_half, text, mask], axis=1), 'seq', 0, 0)  5.06 us
  transfers between devices with their start and end apart: 18, of which 6 were waited for; matrix products, arithmetic and copies ran while one was open for 18% of the time, Pallas kernels for 11%

profile of v5, /device:TPU:0, one launch (start us, length us, event | category | flops | bytes accessed | tf_op | source)
XLA Modules:
  0.0 159.8 jit_solution(6064397965432889549)
XLA Ops:
  2.1 1.6 norm_tokens.1
  3.6 3.0 %collective-permute-start.2 = (bf16[64,3072]{1,0:T(8,128)(2,1)S(1)}, bf16[64,3072]{1,0:T(8,128)(2,1)}, u32[]{:S(2)}, u32[]{:S(2)}) collective-permute-start(bf16[64,3072]{1,0:T(8,128)(2,1)S(1)} %get-tuple-element.10), channel_id=1, source_target_pairs={{0,4},{2,6},{4,0},{6,2},{8,12},{10,14},{12,8},{14,10},{1,5},{3,7},... | collective-permute-start | bytes 1179656 | tf_op jit(solution)/shard_map/ppermute | solution.py:342
  11.0 5.1 %all-to-all-start = ((bf16[8,720,128]{2,1,0:T(8,128)(2,1)}), bf16[8,720,128]{2,1,0:T(8,128)(2,1)}, u32[]{:S(2)}, u32[]{:S(2)}) async-start(bf16[8,720,128]{2,1,0:T(8,128)(2,1)} %pad_maximum_fusion), calls=%async_computation | async-start | bytes 2949120 | tf_op jit(solution)/shard_map/all_to_all | solution.py:334
  25.6 1.8 %constant_dynamic-update-slice_fusion.1 = bf16[128,3072]{1,0:T(8,128)(2,1)} fusion(bf16[64,3072]{1,0:T(8,128)(2,1)} %collective-permute-done.2), kind=kLoop, calls=%fused_computation.18 | loop fusion | bytes 786432
  28.7 18.0 %collective-permute-done.6 = bf16[64,3072]{1,0:T(8,128)(2,1)S(1)} collective-permute-done((bf16[64,3072]{1,0:T(8,128)(2,1)}, bf16[64,3072]{1,0:T(8,128)(2,1)S(1)}, u32[]{:S(2)}, u32[]{:S(2)}) %collective-permute-start.6) | collective-permute-done | bytes 393248 | tf_op jit(solution)/shard_map/ppermute | solution.py:342
  49.0 22.0 %collective-permute-done.10 = bf16[64,3072]{1,0:T(8,128)(2,1)S(1)} collective-permute-done((bf16[64,3072]{1,0:T(8,128)(2,1)S(1)}, bf16[64,3072]{1,0:T(8,128)(2,1)S(1)}, u32[]{:S(2)}, u32[]{:S(2)}) %collective-permute-start.10) | collective-permute-done | bytes 393248 | tf_op jit(solution)/shard_map/ppermute | solution.py:342
  74.2 2.4 %slice.46 = bf16[8,576,128]{2,1,0:T(8,128)(2,1)} slice(bf16[8,720,128]{2,1,0:T(8,128)(2,1)} %all-to-all-done.refs_1_), slice={[0:8], [0:576], [0:128]} | slice | bytes 2359296 | tf_op jit(solution)/shard_map/slice | solution.py:335
  76.5 1.6 collective-permute-start
  78.1 2.1 %pad_maximum_fusion.1.refs_10_.refs_6_ = bf16[128,3072]{1,0:T(8,128)(2,1)} fusion(bf16[64,3072]{1,0:T(8,128)(2,1)} %collective-permute-done.7, bf16[64,3072]{1,0:T(8,128)(2,1)} %broadcast_select_fusion.1), kind=kLoop, calls=%fused_computation.5 | loop fusion | flops 1572864 | bytes 1572864 | tf_op jit(solution)/shard_map/concatenate | solution.py:354
  80.4 1.8 %collective-permute-done.11 = bf16[64,3072]{1,0:T(8,128)(2,1)} collective-permute-done((bf16[64,3072]{1,0:T(8,128)(2,1)}, bf16[64,3072]{1,0:T(8,128)(2,1)}, u32[]{:S(2)}, u32[]{:S(2)}) %collective-permute-start.11) | collective-permute-done | bytes 393248 | tf_op jit(solution)/shard_map/ppermute | solution.py:354
  82.2 2.1 %pad_maximum_fusion.2.refs_12_.refs_8_ = bf16[128,3072]{1,0:T(8,128)(2,1)} fusion(bf16[64,3072]{1,0:T(8,128)(2,1)} %collective-permute-done.11, bf16[64,3072]{1,0:T(8,128)(2,1)} %broadcast_select_fusion), kind=kLoop, calls=%fused_computation.6 | loop fusion | flops 1572864 | bytes 1572864 | tf_op jit(solution)/shard_map/concatenate | solution.py:354
  84.4 1.9 %sine_multiply_fusion = (f32[1024,128]{1,0:T(8,128)S(1)}, f32[1024,128]{1,0:T(8,128)S(1)}) fusion(f32[128]{0:T(128)S(1)} %copy-done.16, f32[128]{0:T(128)S(1)} %copy-done.15, f32[1024]{0:T(1024)S(1)} %get-tuple-element.26, f32[1024]{0:T(1024)S(1)} %get-tuple-element.25, f32[]{:T(128)S(6)} %convert_element_type.40, pred[128]{0:T(512)(128)(4,1)S(1)} %copy-done.17, ...), kind=kLoop, calls=%fused_computation.8 | loop fusion | flops 524288 | bytes 1058052 | tf_op jit(solution)/shard_map/mul | solution.py:307
  91.3 1.6 %reshape.188 = f32[16,1024]{1,0:T(8,128)} reshape(f32[16,16,64]{2,1,0:T(8,128)} %broadcast_in_dim.66) | data formatting | bytes 131072 | tf_op jit(solution)/shard_map/reshape | solution.py:372
  93.0 12.2 %collective-permute-done.refs_2_ = bf16[8,576,128]{2,1,0:T(8,128)(2,1)S(1)} collective-permute-done((bf16[8,576,128]{2,1,0:T(8,128)(2,1)}, bf16[8,576,128]{2,1,0:T(8,128)(2,1)S(1)}, u32[]{:S(2)}, u32[]{:S(2)}) %collective-permute-start) | collective-permute-done | bytes 1179680 | tf_op jit(solution)/shard_map/ppermute | solution.py:335
  107.1 4.3 %project_kv.3.kva = bf16[2,512,128]{2,1,0:T(8,128)(2,1)S(1)} custom-call(s32[1]{0:T(128)} %bitcast.1.refs_0_.section_ref, bf16[8,720,128]{2,1,0:T(8,128)(2,1)} %all-to-all-done.refs_1_, bf16[8,576,128]{2,1,0:T(8,128)(2,1)S(1)} %collective-permute-done.refs_2_, f32[512,128]{1,0:T(8,128)S(1)} %copy-done.12, f32[512,128]{1,0:T(8,128)S(1)} %copy-done.11, ...), custom_call_target="tpu_custom_call" | custom-call | flops 805306368 | bytes 5799936 | tf_op jit(solution)/shard_map/project_kv/pallas_call | solution.py:147
  111.4 3.4 %collective-permute-start.14 = (bf16[2,512,128]{2,1,0:T(8,128)(2,1)S(1)}, bf16[2,512,128]{2,1,0:T(8,128)(2,1)S(1)}, u32[]{:S(2)}, u32[]{:S(2)}) collective-permute-start(bf16[2,512,128]{2,1,0:T(8,128)(2,1)S(1)} %project_kv.3.kva), channel_id=1, source_target_pairs={{0,16},{1,17},{2,18},{3,19},{4,20},{5,21},{6,22},{7,23},{8,24},{9,... | collective-permute-start | bytes 786440 | tf_op jit(solution)/shard_map/ppermute | solution.py:377
  114.9 4.4 %project_kv.2.kvb = bf16[2,512,128]{2,1,0:T(8,128)(2,1)S(1)} custom-call(s32[1]{0:T(128)} %bitcast.1.refs_0_.section_ref, bf16[8,720,128]{2,1,0:T(8,128)(2,1)} %all-to-all-done.refs_1_, bf16[8,576,128]{2,1,0:T(8,128)(2,1)S(1)} %collective-permute-done.refs_2_, f32[512,128]{1,0:T(8,128)S(1)} %copy-done.10, f32[512,128]{1,0:T(8,128)S(1)} %copy-done.9, ...), custom_call_target="tpu_custom_call" | custom-call | flops 805306368 | bytes 5799936 | tf_op jit(solution)/shard_map/project_kv/pallas_call | solution.py:147
  121.6 5.7 %project_q.1.q_ref = bf16[1024,128]{1,0:T(8,128)(2,1)S(1)} custom-call(s32[1]{0:T(128)} %bitcast.1.refs_0_.section_ref, bf16[8,720,128]{2,1,0:T(8,128)(2,1)} %all-to-all-done.refs_1_, bf16[8,576,128]{2,1,0:T(8,128)(2,1)S(1)} %collective-permute-done.refs_2_, f32[1024,128]{1,0:T(8,128)S(1)} %copy-done.6, f32[1024,128]{1,0:T(8,128)S(1)} %copy-done.4, ...), custom_call_target="tpu_custom_call" | custom-call | flops 805306368 | bytes 8945664 | tf_op jit(solution)/shard_map/project_q/pallas_call | solution.py:147
  127.4 2.5 %attend_own.1 = (f32[1024,128]{1,0:T(8,128)S(1)}, f32[1024,128]{1,0:T(8,128)S(1)}) custom-call(s32[1]{0:T(128)} %bitcast.1.refs_0_.section_ref, f32[16,512]{1,0:T(8,128)S(1)} %get-tuple-element.19.keep_ref, bf16[1024,128]{1,0:T(8,128)(2,1)S(1)} %project_q.1.q_ref, bf16[2,512,128]{2,1,0:T(8,128)(2,1)S(1)} %project_kv.3.kva, ...), custom_call_target="tpu_custom_call" | custom-call | flops 1073741824 | bytes 2621440 | tf_op jit(solution)/shard_map/attend_own/pallas_call | solution.py:239
  131.3 3.4 %all-to-all-start.1 = ((bf16[8,128,128]{2,1,0:T(8,128)(2,1)}), bf16[8,128,128]{2,1,0:T(8,128)(2,1)S(1)}, u32[]{:S(2)}, u32[]{:S(2)}) async-start(bf16[8,128,128]{2,1,0:T(8,128)(2,1)} %attend_cond.1), calls=%async_computation.1 | async-start | bytes 524288 | tf_op jit(solution)/shard_map/all_to_all | solution.py:385
  134.7 9.7 %all-to-all-done.1.attn_ref = bf16[8,128,128]{2,1,0:T(8,128)(2,1)S(1)} async-done(((bf16[8,128,128]{2,1,0:T(8,128)(2,1)}), bf16[8,128,128]{2,1,0:T(8,128)(2,1)S(1)}, u32[]{:S(2)}, u32[]{:S(2)}) %all-to-all-start.1) | async-done | bytes 262176 | tf_op jit(solution)/shard_map/all_to_all | solution.py:385
  144.4 2.8 %copy-done.1 = bf16[1024,3072]{1,0:T(8,128)(2,1)S(1)} copy-done((bf16[1024,3072]{1,0:T(8,128)(2,1)S(1)}, bf16[1024,3072]{1,0:T(8,128)(2,1)}, u32[]{:S(2)}) %copy-start.1) | copy-done | bytes 6291480
  149.7 2.8 %copy-done.2 = bf16[1024,3072]{1,0:T(8,128)(2,1)S(1)} copy-done((bf16[1024,3072]{1,0:T(8,128)(2,1)S(1)}, bf16[1024,3072]{1,0:T(8,128)(2,1)}, u32[]{:S(2)}) %copy-start.2) | copy-done | bytes 6291480
  153.8 5.1 %collective-permute-done.15 = bf16[128,1536]{1,0:T(8,128)(2,1)S(1)} collective-permute-done((bf16[128,1536]{1,0:T(8,128)(2,1)S(1)}, bf16[128,1536]{1,0:T(8,128)(2,1)S(1)}, u32[]{:S(2)}, u32[]{:S(2)}) %collective-permute-start.15) | collective-permute-done | bytes 393248 | tf_op jit(solution)/shard_map/ppermute | solution.py:387
  (117 shorter events, 38.2 us)
Async XLA Ops:
  0.0 9.4 %copy-start = (bf16[384,3,1024]{2,0,1:T(8,128)(2,1)S(1)}, bf16[384,3,1024]{2,0,1:T(8,128)(2,1)}, u32[]{:S(2)}) copy-start(bf16[384,3,1024]{2,0,1:T(8,128)(2,1)} %param.11) | copy-start | bytes 7077892
  0.0 9.4 %copy-start.22 = (s32[1,8]{1,0:T(1,128)S(1)}, s32[1,8]{1,0:T(1,128)}, u32[]{:S(2)}) copy-start(s32[1,8]{1,0:T(1,128)} %param.15) | copy-start | bytes 100
  3.6 16.9 %collective-permute-start.2 = (bf16[64,3072]{1,0:T(8,128)(2,1)S(1)}, bf16[64,3072]{1,0:T(8,128)(2,1)}, u32[]{:S(2)}, u32[]{:S(2)}) collective-permute-start(bf16[64,3072]{1,0:T(8,128)(2,1)S(1)} %get-tuple-element.10), channel_id=1, source_target_pairs={{0,4},{2,6},{4,0},{6,2},{8,12},{10,14},{12,8},{14,10},{1,5},{3,7},... | collective-permute-start | bytes 1179656 | tf_op jit(solution)/shard_map/ppermute | solution.py:342
  6.7 14.5 %collective-permute-start.5 = (bf16[64,3072]{1,0:T(8,128)(2,1)S(1)}, bf16[64,3072]{1,0:T(8,128)(2,1)}, u32[]{:S(2)}, u32[]{:S(2)}) collective-permute-start(bf16[64,3072]{1,0:T(8,128)(2,1)S(1)} %get-tuple-element.10), channel_id=1, source_target_pairs={{4,8},{6,10},{8,4},{10,6},{5,9},{7,11},{9,5},{11,7},{20,24},{22,26... | collective-permute-start | bytes 1179656 | tf_op jit(solution)/shard_map/ppermute | solution.py:342
  11.0 8.5 %copy-start.20 = (f32[128]{0:T(128)S(1)}, f32[128]{0:T(128)}, u32[]{:S(2)}) copy-start(f32[128]{0:T(128)} %param.14) | copy-start | bytes 1540
  11.0 8.5 %copy-start.21 = (f32[128]{0:T(128)S(1)}, f32[128]{0:T(128)}, u32[]{:S(2)}) copy-start(f32[128]{0:T(128)} %param.13) | copy-start | bytes 1540
  11.0 63.1 %all-to-all-start = ((bf16[8,720,128]{2,1,0:T(8,128)(2,1)}), bf16[8,720,128]{2,1,0:T(8,128)(2,1)}, u32[]{:S(2)}, u32[]{:S(2)}) async-start(bf16[8,720,128]{2,1,0:T(8,128)(2,1)} %pad_maximum_fusion), calls=%async_computation | async-start | bytes 2949120 | tf_op jit(solution)/shard_map/all_to_all | solution.py:334
  16.1 76.9 %collective-permute-start.1 = (bf16[128,3072]{1,0:T(8,128)(2,1)}, bf16[128,3072]{1,0:T(8,128)(2,1)}, u32[]{:S(2)}, u32[]{:S(2)}) collective-permute-start(bf16[128,3072]{1,0:T(8,128)(2,1)} %get-tuple-element.9.refs_6_), channel_id=1, source_target_pairs={{0,2},{2,0},{4,6},{6,4},{8,10},{10,8},{12,14},{14,12},{1,3},{3,1},... | collective-permute-start | bytes 2359304 | tf_op jit(solution)/shard_map/ppermute | solution.py:356
  20.5 6.9 %collective-permute-start.9 = (bf16[64,3072]{1,0:T(8,128)(2,1)}, bf16[64,3072]{1,0:T(8,128)(2,1)S(1)}, u32[]{:S(2)}, u32[]{:S(2)}) collective-permute-start(bf16[64,3072]{1,0:T(8,128)(2,1)} %collective-permute-done.2), channel_id=1, source_target_pairs={{4,8},{6,10},{8,4},{10,6},{5,9},{7,11},{9,5},{11,7},{20,24},{22,26... | collective-permute-start | bytes 1179656 | tf_op jit(solution)/shard_map/ppermute | solution.py:342
  21.2 25.5 %collective-permute-start.6 = (bf16[64,3072]{1,0:T(8,128)(2,1)}, bf16[64,3072]{1,0:T(8,128)(2,1)S(1)}, u32[]{:S(2)}, u32[]{:S(2)}) collective-permute-start(bf16[64,3072]{1,0:T(8,128)(2,1)} %collective-permute-done.5), channel_id=1, source_target_pairs={{4,0},{6,2},{8,12},{10,14},{5,1},{7,3},{9,13},{11,15},{20,16},{22,... | collective-permute-start | bytes 1179656 | tf_op jit(solution)/shard_map/ppermute | solution.py:342
  24.1 49.3 %collective-permute-start.3 = (bf16[64,3072]{1,0:T(8,128)(2,1)}, bf16[64,3072]{1,0:T(8,128)(2,1)S(1)}, u32[]{:S(2)}, u32[]{:S(2)}) collective-permute-start(bf16[64,3072]{1,0:T(8,128)(2,1)} %collective-permute-done.2), channel_id=1, source_target_pairs={{0,1},{1,0},{2,3},{3,2},{4,5},{5,4},{6,7},{7,6},{8,9},{9,8},{10,11... | collective-permute-start | bytes 1179656 | tf_op jit(solution)/shard_map/ppermute | solution.py:354
  27.4 43.5 %collective-permute-start.10 = (bf16[64,3072]{1,0:T(8,128)(2,1)S(1)}, bf16[64,3072]{1,0:T(8,128)(2,1)S(1)}, u32[]{:S(2)}, u32[]{:S(2)}) collective-permute-start(bf16[64,3072]{1,0:T(8,128)(2,1)S(1)} %collective-permute-done.9), channel_id=1, source_target_pairs={{4,0},{6,2},{8,12},{10,14},{5,1},{7,3},{9,13},{11,15},{20,16},{22,... | collective-permute-start | bytes 1179656 | tf_op jit(solution)/shard_map/ppermute | solution.py:342
  47.5 30.6 %collective-permute-start.7 = (bf16[64,3072]{1,0:T(8,128)(2,1)}, bf16[64,3072]{1,0:T(8,128)(2,1)}, u32[]{:S(2)}, u32[]{:S(2)}) collective-permute-start(bf16[64,3072]{1,0:T(8,128)(2,1)} %broadcast_select_fusion.1), channel_id=1, source_target_pairs={{0,1},{1,0},{2,3},{3,2},{4,5},{5,4},{6,7},{7,6},{8,9},{9,8},{10,11... | collective-permute-start | bytes 1179656 | tf_op jit(solution)/shard_map/ppermute | solution.py:354
  71.8 10.4 %collective-permute-start.11 = (bf16[64,3072]{1,0:T(8,128)(2,1)}, bf16[64,3072]{1,0:T(8,128)(2,1)}, u32[]{:S(2)}, u32[]{:S(2)}) collective-permute-start(bf16[64,3072]{1,0:T(8,128)(2,1)} %broadcast_select_fusion), channel_id=1, source_target_pairs={{0,1},{1,0},{2,3},{3,2},{4,5},{5,4},{6,7},{7,6},{8,9},{9,8},{10,11... | collective-permute-start | bytes 1179656 | tf_op jit(solution)/shard_map/ppermute | solution.py:354
  74.1 18.8 %collective-permute-start.4 = (bf16[128,3072]{1,0:T(8,128)(2,1)}, bf16[128,3072]{1,0:T(8,128)(2,1)}, u32[]{:S(2)}, u32[]{:S(2)}) collective-permute-start(bf16[128,3072]{1,0:T(8,128)(2,1)} %constant_dynamic-update-slice_fusion.refs_8_), channel_id=1, source_target_pairs={{0,2},{2,0},{4,6},{6,4},{8,10},{10,8},{12,14},{14,12},{1,3},{3,1},... | collective-permute-start | bytes 2359304 | tf_op jit(solution)/shard_map/ppermute | solution.py:356
  76.5 7.8 %copy-start.17 = (pred[128]{0:T(512)(128)(4,1)S(1)}, pred[128]{0:T(512)(128)(4,1)}, u32[]{:S(2)}) copy-start(pred[128]{0:T(512)(128)(4,1)} %iota_compare_fusion.3) | copy-start | bytes 388
  76.5 7.8 %copy-start.18 = (pred[128]{0:T(512)(128)(4,1)S(1)}, pred[128]{0:T(512)(128)(4,1)}, u32[]{:S(2)}) copy-start(pred[128]{0:T(512)(128)(4,1)} %iota_compare_fusion.4) | copy-start | bytes 388
  76.5 28.7 %collective-permute-start = (bf16[8,576,128]{2,1,0:T(8,128)(2,1)}, bf16[8,576,128]{2,1,0:T(8,128)(2,1)S(1)}, u32[]{:S(2)}, u32[]{:S(2)}) collective-permute-start(bf16[8,576,128]{2,1,0:T(8,128)(2,1)} %slice.46), channel_id=1, source_target_pairs={{0,16},{16,0},{1,17},{17,1},{2,18},{18,2},{3,19},{19,3},{4,20},{20... | collective-permute-start | bytes 3538952 | tf_op jit(solution)/shard_map/ppermute | solution.py:335
  80.2 34.7 %collective-permute-start.8 = (bf16[128,3072]{1,0:T(8,128)(2,1)}, bf16[128,3072]{1,0:T(8,128)(2,1)}, u32[]{:S(2)}, u32[]{:S(2)}) collective-permute-start(bf16[128,3072]{1,0:T(8,128)(2,1)} %pad_maximum_fusion.1.refs_10_.refs_6_), channel_id=1, source_target_pairs={{0,2},{2,0},{4,6},{6,4},{8,10},{10,8},{12,14},{14,12},{1,3},{3,1},... | collective-permute-start | bytes 2359304 | tf_op jit(solution)/shard_map/ppermute | solution.py:356
  84.3 30.5 %collective-permute-start.12 = (bf16[128,3072]{1,0:T(8,128)(2,1)}, bf16[128,3072]{1,0:T(8,128)(2,1)}, u32[]{:S(2)}, u32[]{:S(2)}) collective-permute-start(bf16[128,3072]{1,0:T(8,128)(2,1)} %pad_maximum_fusion.2.refs_12_.refs_8_), channel_id=1, source_target_pairs={{0,2},{2,0},{4,6},{6,4},{8,10},{10,8},{12,14},{14,12},{1,3},{3,1},... | collective-permute-start | bytes 2359304 | tf_op jit(solution)/shard_map/ppermute | solution.py:356
  111.4 16.0 %collective-permute-start.14 = (bf16[2,512,128]{2,1,0:T(8,128)(2,1)S(1)}, bf16[2,512,128]{2,1,0:T(8,128)(2,1)S(1)}, u32[]{:S(2)}, u32[]{:S(2)}) collective-permute-start(bf16[2,512,128]{2,1,0:T(8,128)(2,1)S(1)} %project_kv.3.kva), channel_id=1, source_target_pairs={{0,16},{1,17},{2,18},{3,19},{4,20},{5,21},{6,22},{7,23},{8,24},{9,... | collective-permute-start | bytes 786440 | tf_op jit(solution)/shard_map/ppermute | solution.py:377
  119.3 10.7 %collective-permute-start.13 = (bf16[2,512,128]{2,1,0:T(8,128)(2,1)S(1)}, bf16[2,512,128]{2,1,0:T(8,128)(2,1)S(1)}, u32[]{:S(2)}, u32[]{:S(2)}) collective-permute-start(bf16[2,512,128]{2,1,0:T(8,128)(2,1)S(1)} %project_kv.2.kvb), channel_id=1, source_target_pairs={{0,16},{1,17},{2,18},{3,19},{4,20},{5,21},{6,22},{7,23},{8,24},{9,... | collective-permute-start | bytes 786440 | tf_op jit(solution)/shard_map/ppermute | solution.py:379
  131.3 13.1 %all-to-all-start.1 = ((bf16[8,128,128]{2,1,0:T(8,128)(2,1)}), bf16[8,128,128]{2,1,0:T(8,128)(2,1)S(1)}, u32[]{:S(2)}, u32[]{:S(2)}) async-start(bf16[8,128,128]{2,1,0:T(8,128)(2,1)} %attend_cond.1), calls=%async_computation.1 | async-start | bytes 524288 | tf_op jit(solution)/shard_map/all_to_all | solution.py:385
  148.4 10.6 %collective-permute-start.15 = (bf16[128,1536]{1,0:T(8,128)(2,1)S(1)}, bf16[128,1536]{1,0:T(8,128)(2,1)S(1)}, u32[]{:S(2)}, u32[]{:S(2)}) collective-permute-start(bf16[128,1536]{1,0:T(8,128)(2,1)S(1)} %out_sent.1), channel_id=1, source_target_pairs={{0,1},{1,0},{2,3},{3,2},{4,5},{5,4},{6,7},{7,6},{8,9},{9,8},{10,11... | collective-permute-start | bytes 1179656 | tf_op jit(solution)/shard_map/ppermute | solution.py:387
  (17 other events, 64.9 us)

commit v6 on v5

--- a/solution.py
+++ b/solution.py
@@ -90,20 +90,25 @@
     return (x * cosine + other * sine).astype(jnp.bfloat16)
 
 
-def project_kernel(kinds, pieces, section_ref, mine, peer, cos_ref, sin_ref, gain_ref, *refs):
-    x_refs, out_refs, acc_ref = refs[:pieces], refs[pieces:-1], refs[-1]
+def project_kernel(kinds, section_ref, *refs):
+    weight_refs, (cos_ref, sin_ref, gain_ref) = refs[:3], refs[3:6]
+    outputs = 2 if kinds == (0, 1, 2) else 1
+    x_refs, out_refs, acc_ref = refs[6 : -1 - outputs], refs[-1 - outputs : -1], refs[-1]
     step = pl.program_id(0)
-    half = peer.shape[1] // 3
     first = section_ref[0] == 0
 
     def rows_of(s, kind):
-        at = slice(kind * half, (kind + 1) * half)
-        a, b = mine[s, at, :], peer[s, at, :]
-        return jnp.concatenate([jnp.where(first, a, b), jnp.where(first, b, a)], axis=0)
+        mine, peer, direct = (
+            ref[s, kind * (ref.shape[1] // 3) : (kind + 1) * (ref.shape[1] // 3), :]
+            for ref in weight_refs
+        )
+        return jnp.concatenate(
+            [jnp.where(first, mine, peer), jnp.where(first, peer, mine), direct], axis=0
+        )
 
     w = jnp.concatenate(
         [
-            jnp.concatenate([rows_of(s, kind) for s in range(mine.shape[0])], axis=0)
+            jnp.concatenate([rows_of(s, kind) for s in range(weight_refs[0].shape[0])], axis=0)
             for kind in kinds
         ],
         axis=1,
@@ -130,35 +135,38 @@
             if kind == 0:
                 out_refs[0][...] = value
             else:
-                out_refs[0][kind - 1] = value.astype(jnp.bfloat16)
-
-
-def project(kinds, section, pieces, mine, peer, cosine, sine, gains):
+                out_refs[-1][kind - 1] = value.astype(jnp.bfloat16)
+
+
+def project(kinds, chunk, section, pieces, weights, cosine, sine, gains):
     depth = pieces[0].shape[1]
     rows = sum(p.shape[0] for p in pieces)
-    sources = mine.shape[0]
+    sources = weights[0].shape[0]
     steps = 4
-    shape = (rows, HEAD_DIM) if kinds == (0,) else (2, rows, HEAD_DIM)
-
-    def weights(array):
-        return pl.BlockSpec((sources // steps,) + array.shape[1:], lambda k, s: (k, 0, 0))
-
-    table = pl.BlockSpec((rows, HEAD_DIM), lambda k, s: (0, 0))
+    out_shape, out_specs = [], []
+    for shape in ((rows, HEAD_DIM),) * (0 in kinds) + ((2, rows, HEAD_DIM),) * (1 in kinds):
+        out_shape.append(jax.ShapeDtypeStruct(shape, jnp.bfloat16))
+        out_specs.append(pl.BlockSpec(shape, lambda k, s, n=len(shape): (0,) * n))
+    table = pl.BlockSpec((rows, HEAD_DIM), lambda k, s: (chunk, 0))
     return call(
-        lambda *refs: project_kernel(kinds, len(pieces), *refs),
+        lambda *refs: project_kernel(kinds, *refs),
         "project_" + "".join("qkv"[k] for k in kinds),
-        jax.ShapeDtypeStruct(shape, jnp.bfloat16),
-        2 * len(kinds) * rows * depth * HEAD_DIM, 2 * (rows * depth + mine.size + peer.size), 0,
+        out_shape,
+        2 * len(kinds) * rows * depth * HEAD_DIM,
+        2 * (rows * depth + sum(w.size for w in weights)), 0,
         grid_spec=pltpu.PrefetchScalarGridSpec(
             num_scalar_prefetch=1,
             grid=(steps,),
-            in_specs=[weights(mine), weights(peer)]
+            in_specs=[
+                pl.BlockSpec((sources // steps,) + w.shape[1:], lambda k, s: (k, 0, 0))
+                for w in weights
+            ]
             + [table, table, pl.BlockSpec((2, HEAD_DIM), lambda k, s: (0, 0))]
             + [pl.BlockSpec((p.shape[0], depth // steps), lambda k, s: (0, k)) for p in pieces],
-            out_specs=pl.BlockSpec(shape, lambda k, s: (0,) * len(shape)),
+            out_specs=out_specs,
             scratch_shapes=[pltpu.VMEM((rows, len(kinds) * HEAD_DIM), jnp.float32)],
         ),
-    )(section, mine, peer, cosine, sine, gains, *pieces)
+    )(section, *weights, cosine, sine, gains, *pieces)
 
 
 def weights_of(query, keys):
@@ -184,32 +192,39 @@
 BLOCK = 256
 
 
-def own_kernel(section_ref, keep_ref, q_ref, kva, kvb, text, conda, num_ref, den_ref):
-    rows = q_ref.shape[0]
-    groups = keep_ref.shape[0] * BLOCK // rows
-    for b in range(rows // BLOCK):
+def query_blocks(q_refs):
+    for c, ref in enumerate(q_refs):
+        for b in range(ref.shape[0] // BLOCK):
+            yield ref[b * BLOCK : (b + 1) * BLOCK, :], c * (ref.shape[0] // BLOCK) + b
+
+
+def own_kernel(section_ref, keep_ref, qa, qb, kva, kvb, text, conda, num_ref, den_ref):
+    groups = keep_ref.shape[0] * BLOCK // num_ref.shape[0]
+    keys = conda.shape[1]
+    for query, b in query_blocks((qa, qb)):
         at = slice(b * BLOCK, (b + 1) * BLOCK)
         num, den = 0.0, 0.0
         for ref in (kva, kvb, text):
-            more = summed(weights_of(q_ref[at, :], ref[0]), ref[1])
+            more = summed(weights_of(query, ref[0]), ref[1])
             num, den = num + more[0], den + more[1]
         num_ref[at, :] = num
         den_ref[at, :] = jnp.broadcast_to(den, num.shape)
 
     @pl.when(section_ref[0] != 0)
     def _():
-        for b in range(rows // BLOCK):
+        for query, b in query_blocks((qa, qb)):
             at = slice(b * BLOCK, (b + 1) * BLOCK)
-            keep = keep_ref[b * groups : (b + 1) * groups, :]
-            num, den = summed(kept_weights(q_ref[at, :], conda, keep), conda[1])
+            keep = keep_ref[b * groups : (b + 1) * groups, :keys]
+            num, den = summed(kept_weights(query, conda, keep), conda[1])
             num_ref[at, :] += num
             den_ref[at, :] += jnp.broadcast_to(den, num.shape)
 
 
-def cond_kernel(section_ref, place_ref, keep_ref, q_ref, condb, num_ref, den_ref, out_ref):
-    rows = q_ref.shape[0]
+def cond_kernel(section_ref, place_ref, keep_ref, qa, qb, condb, num_ref, den_ref, out_ref):
+    rows = num_ref.shape[0]
     groups = keep_ref.shape[0] * BLOCK // rows
     size = BLOCK // groups
+    keys = condb.shape[1]
 
     def store(b, num, den):
         value = (num / den).astype(jnp.bfloat16)
@@ -226,72 +241,85 @@
 
     @pl.when(section_ref[0] != 0)
     def _():
-        for b in range(rows // BLOCK):
+        for query, b in query_blocks((qa, qb)):
             at = slice(b * BLOCK, (b + 1) * BLOCK)
-            keep = keep_ref[b * groups : (b + 1) * groups, :]
-            num, den = summed(kept_weights(q_ref[at, :], condb, keep), condb[1])
+            keep = keep_ref[b * groups : (b + 1) * groups, -keys:]
+            num, den = summed(kept_weights(query, condb, keep), condb[1])
             store(b, num_ref[at, :] + num, den_ref[at, :] + den)
 
 
-def attend_own(section, keep, query, kvs, text, cond):
-    rows = query.shape[0]
+def attend_own(section, keep, queries, kvs, text, cond):
+    rows = 2 * queries[0].shape[0]
     keys = rows + text.shape[1] + cond.shape[1]
     return call(
         own_kernel, "attend_own", [jax.ShapeDtypeStruct((rows, HEAD_DIM), jnp.float32)] * 2,
         4 * rows * keys * HEAD_DIM, 2 * rows * HEAD_DIM * 10, rows * keys,
-        in_specs=[SMEM] + [VMEM] * 6,
+        in_specs=[SMEM] + [VMEM] * 7,
         out_specs=[VMEM] * 2,
-    )(section, keep, query, *kvs, text, cond)
-
-
-def attend_cond(section, place, keep, query, cond, num, den, seq):
+    )(section, keep, *queries, *kvs, text, cond)
+
+
+def attend_cond(section, place, keep, queries, cond, num, den, seq):
     rows = num.shape[0]
     keys = cond.shape[1]
     return call(
         cond_kernel, "attend_cond",
         jax.ShapeDtypeStruct((seq, rows // seq, HEAD_DIM), jnp.bfloat16),
         4 * rows * keys * HEAD_DIM, 2 * rows * HEAD_DIM * 8, rows * keys,
-        in_specs=[SMEM, SMEM] + [VMEM] * 5,
+        in_specs=[SMEM, SMEM] + [VMEM] * 6,
         out_specs=VMEM,
-    )(section, place, keep, query, cond, num, den)
+    )(section, place, keep, *queries, cond, num, den)
 
 
 def token_rows(attn_ref):
     return jnp.concatenate([attn_ref[h] for h in range(attn_ref.shape[0])], axis=1)
 
 
-def sent_kernel(half_ref, attn_ref, w_ref, out_ref):
+def load_kernel(half_ref, w_ref, sent_ref, kept_ref, sems):
+    width = sent_ref.shape[1]
+    copies = []
+    for i, out_ref in enumerate((sent_ref, kept_ref)):
+        half = half_ref[0] if i else 1 - half_ref[0]
+        columns = pl.ds(pl.multiple_of(half * width, width), width)
+        copies.append(pltpu.make_async_copy(w_ref.at[:, columns], out_ref, sems.at[i]))
+    for copy in copies:
+        copy.start()
+    for copy in copies:
+        copy.wait()
+
+
+def load_out(half, w_out):
+    shape = jax.ShapeDtypeStruct((w_out.shape[0], w_out.shape[1] // 2), w_out.dtype)
+    return call(
+        load_kernel, "load_out", [shape] * 2, 0, 4 * w_out.size, 0,
+        in_specs=[SMEM, pl.BlockSpec(memory_space=pl.ANY)],
+        out_specs=[VMEM, VMEM],
+        scratch_shapes=[pltpu.SemaphoreType.DMA((2,))],
+    )(half, w_out)
+
+
+def sent_kernel(attn_ref, w_ref, out_ref):
     branch = jnp.dot(token_rows(attn_ref), w_ref[...], preferred_element_type=jnp.float32)
     out_ref[...] = branch.astype(jnp.bfloat16)
 
 
-def kept_kernel(half_ref, attn_ref, w_ref, image_ref, gate_ref, out_ref):
+def kept_kernel(attn_ref, w_ref, image_ref, gate_ref, out_ref):
     branch = jnp.dot(token_rows(attn_ref), w_ref[...], preferred_element_type=jnp.float32)
     out_ref[...] = image_ref[...].astype(jnp.float32) + gate_ref[...] * branch
 
 
-def project_out(half, attn, w_out, image=None, gate=None):
+def project_out(attn, w, image=None, gate=None):
     rows = attn.shape[1]
-    depth, width = w_out.shape[0], w_out.shape[1] // 2
-    block = 512
-    steps = width // block
-
-    def columns(height):
-        return pl.BlockSpec((height, block), lambda i, half: (0, half[0] * steps + i))
-
+    depth, width = w.shape
     kept = image is not None
+    args = (attn, w) + ((image, gate) if kept else ())
     return call(
         kept_kernel if kept else sent_kernel, "out_kept" if kept else "out_sent",
         jax.ShapeDtypeStruct((rows, width), jnp.float32 if kept else jnp.bfloat16),
         2 * rows * depth * width, 2 * depth * width, 0,
-        grid_spec=pltpu.PrefetchScalarGridSpec(
-            num_scalar_prefetch=1,
-            grid=(steps,),
-            in_specs=[pl.BlockSpec(attn.shape, lambda i, half: (0, 0, 0)), columns(depth)]
-            + ([columns(rows), columns(1)] if kept else []),
-            out_specs=pl.BlockSpec((rows, block), lambda i, half: (0, i)),
-        ),
-    )(half, attn, w_out, *((image, gate) if kept else ()))
+        in_specs=[VMEM] * len(args),
+        out_specs=VMEM,
+    )(*args)
 
 
 def lane_tables(rows_index, time_index):
@@ -323,23 +351,22 @@
     tp_at = tp.astype(jnp.int32).reshape(1)
     both = [(0, 1), (1, 0)]
 
-    half = depth // 2
-    w_half = lax.dynamic_slice_in_dim(w_qkv.transpose(1, 0, 2), section * half, half, 1)
-    w_half = w_half.reshape(3, half, seq, HEAD_DIM).transpose(2, 0, 1, 3).reshape(seq, -1, HEAD_DIM)
-    text = text_kv[0].reshape(-1, 2, seq, HEAD_DIM).transpose(2, 0, 1, 3).reshape(seq, -1, HEAD_DIM)
-    mask = jnp.pad(
-        region_mask.astype(jnp.bfloat16), ((0, 15), (0, HEAD_DIM - region_mask.shape[1]))
-    )
-    mask = jnp.broadcast_to(mask, (seq,) + mask.shape)
-    mine = lax.all_to_all(jnp.concatenate([w_half, text, mask], axis=1), "seq", 0, 0)
-    peer = lax.ppermute(mine[:, : 3 * half], "section", both)
-    text = mine[:, 3 * half : -16].reshape(-1, 2, HEAD_DIM).transpose(1, 0, 2)
-    keep = mine[:, -16, : region_mask.shape[1]].astype(jnp.float32)
+    rows3 = w_qkv.transpose(1, 0, 2)
+    half = depth * 3 // 8
+
+    def for_heads(rows):
+        return rows.reshape(3, -1, seq, HEAD_DIM).transpose(2, 0, 1, 3).reshape(seq, -1, HEAD_DIM)
+
+    mine = for_heads(lax.dynamic_slice_in_dim(rows3, section * half, half, 1))
+    mine = lax.all_to_all(mine, "seq", 0, 0)
 
     full, part = norm_tokens(tp_at, image[0], modulation.transpose(1, 0, 2))
 
     def along_z(x, pairs):
         return lax.ppermute(x, "seq", z_pairs(seq, pairs))
+
+    def to_core(x):
+        return lax.ppermute(x, "seq", [(s, s ^ 1) for s in range(seq)])
 
     near = along_z(part, [(0, 1), (1, 0), (2, 3), (3, 2)])
     middle = along_z(part, [(1, 2), (2, 1)])
@@ -349,12 +376,28 @@
     inner = (chip == 1) | (chip == 2)
     third = jnp.where(inner, middle, middle_end)
     fourth = jnp.where(inner, far, far_end)
-    groups = [full]
-    for came in (near, third, fourth):
-        groups.append(jnp.concatenate([came, lax.ppermute(came, "tp", both)], axis=0))
-    pieces = [
-        (g, lax.ppermute(g, "seq", [(s, s ^ 1) for s in range(seq)])) for g in groups
-    ]
+    pieces = [(full, to_core(full))]
+    for came in (near, third):
+        group = jnp.concatenate([came, lax.ppermute(came, "tp", both)], axis=0)
+        pieces.append((group, to_core(group)))
+    fourth, mine = lax.optimization_barrier((fourth, mine))
+    passed = lax.ppermute(fourth, "tp", both)
+    pieces.append((fourth, passed, to_core(fourth), to_core(passed)))
+
+    peer = lax.ppermute(mine, "section", both)
+    text = text_kv[0].reshape(-1, 2, seq, HEAD_DIM).transpose(2, 0, 1, 3).reshape(seq, -1, HEAD_DIM)
+    mask = jnp.pad(
+        region_mask.astype(jnp.bfloat16), ((0, 15), (0, HEAD_DIM - region_mask.shape[1]))
+    )
+    mask = jnp.broadcast_to(mask, (seq,) + mask.shape)
+    direct = jnp.concatenate([for_heads(rows3[:, 2 * half :]), text, mask], axis=1)
+    direct, mine = lax.optimization_barrier((direct, mine))
+    direct = lax.all_to_all(direct, "seq", 0, 0)
+    w_sent, w_kept = load_out(tp_at, w_out)
+    direct, w_sent, w_kept = lax.optimization_barrier((direct, w_sent, w_kept))
+    text = direct[:, -16 - 2 * text_kv.shape[1] : -16].reshape(-1, 2, HEAD_DIM).transpose(1, 0, 2)
+    keep = direct[:, -16, : region_mask.shape[1]].astype(jnp.float32)
+    direct = direct[:, : 3 * (depth - 2 * half)]
 
     upper = chip >= 2
     chips = jnp.stack([chip, chip ^ 1, jnp.where(upper, 1, 2), jnp.where(upper, 0, 3)])
@@ -371,22 +414,24 @@
     chosen = (shards[:, None] == jnp.arange(seq)[None]).astype(jnp.float32)
     keep = jnp.repeat(chosen @ keep @ chosen.T, size, axis=1)
 
-    rows = rows_index.shape[0] // 2
-    a, b = list(pieces[0] + pieces[1]), list(pieces[2] + pieces[3])
-    kv_a = project((1, 2), section_at, a, mine, peer, cosine[:rows], sine[:rows], gains)
+    a, b = pieces[0] + pieces[1], pieces[2] + pieces[3]
+    weights = (mine, peer, direct)
+    q_a, kv_a = project((0, 1, 2), 0, section_at, a, weights, cosine, sine, gains)
     cond_a = lax.ppermute(kv_a, "section", [(0, 1)])
-    kv_b = project((1, 2), section_at, b, mine, peer, cosine[rows:], sine[rows:], gains)
+    (kv_b,) = project((1, 2), 1, section_at, b, weights, cosine, sine, gains)
     cond_b = lax.ppermute(kv_b, "section", [(0, 1)])
-    query = project((0,), section_at, a + b, mine, peer, cosine, sine, gains)
-    num, den = attend_own(section_at, keep[:, :rows], query, (kv_a, kv_b), text, cond_a)
+    (q_b,) = project((0,), 1, section_at, b, weights, cosine, sine, gains)
+    queries = (q_a, q_b)
+    num, den = attend_own(section_at, keep, queries, (kv_a, kv_b), text, cond_a)
     place = jnp.stack([shards, parts])
-    attn = attend_cond(section_at, place, keep[:, rows:], query, cond_b, num, den, seq)
+    attn = attend_cond(section_at, place, keep, queries, cond_b, num, den, seq)
 
     attn = lax.all_to_all(attn, "seq", 0, 0)
-    gate = mods[2:3]
-    other = lax.ppermute(project_out(1 - tp_at, attn, w_out), "tp", both)
-    kept = project_out(tp_at, attn, w_out, image[0], gate)
-    gate = lax.dynamic_slice_in_dim(gate, tp * other.shape[1], other.shape[1], 1)
+    other = lax.ppermute(project_out(attn, w_sent), "tp", both)
+    cols = other.shape[1]
+    gate = lax.dynamic_slice_in_dim(mods[2:3], tp * cols, cols, 1)
+    residual = lax.dynamic_slice_in_dim(image[0], tp * cols, cols, 1)
+    kept = project_out(attn, w_kept, residual, gate)
     return (kept + gate * other.astype(jnp.float32)).astype(jnp.bfloat16)[None]
 
 

time: 161 us -> 151 us (0.938)
  waiting for transfers between devices: 68.8 us -> 43.7 us
  blocking collectives: 0 us -> 13.5 us
  other arithmetic: 13.8 us -> 8.34 us
  starting transfers between devices: 28.3 us -> 31.9 us
  local copies, waits for them, and re-layouts: 25.1 us -> 27.8 us
    all_to_all x0 -> x1, blocking collectives: none -> 13.5 us  [head_body(): attn = lax.all_to_all(attn, 'seq', 0, 0)]
    ppermute x5, waiting for transfers between devices: 40 us -> 30.5 us  [along_z(): return lax.ppermute(x, 'seq', z_pairs(seq, pairs))]
    all_to_all x2, waiting for transfers between devices: 9.66 us -> 0.82 us  [the longest x1 0.82 us: head_body(): direct = lax.all_to_all(direct, 'seq', 0, 0)]
    ppermute x9 -> x10, waiting for transfers between devices: 19.2 us -> 12.4 us  [the longest x1 6.91 us: head_body(): other = lax.ppermute(project_out(attn, w_sent), 'tp', both)]
    reshape x2 -> x3, local copies, waits for them, and re-layouts: 0.36 us -> 4.41 us  [the longest x2 3.43 us: for_heads(): rows.reshape(3, -1, seq, HEAD_DIM).transpose(2, 0, 1, 3)]
    ppermute x1, starting transfers between devices: 1.31 us -> 4.1 us  [head_body(): cond_b = lax.ppermute(kv_b, 'section', [(0, 1)])]
    concatenate x3 -> x2, other arithmetic: 5.37 us -> 2.92 us  [the longest x1 1.95 us: head_body(): group = jnp.concatenate([came, lax.ppermute(came, 'tp', both)], axis=0)]
    slice x6 -> x4, local copies, waits for them, and re-layouts: 6.44 us -> 4.22 us  [the longest x1 1.69 us: head_body(): direct[:, -16 - 2 * text_kv.shape[1]:-16].reshape(-1, 2, HEAD_DIM)]
  transfers between devices with their start and end apart: 18 -> 19, of which waited for: 6 -> 5; matrix products, arithmetic and copies ran while one was open for 18% -> 15% of each run, Pallas kernels for 11% -> 13%
where the time goes in v6:
time: 151 us; the launch traced here: 149 us
  waiting for transfers between devices  43.7 us (29%)
  starting transfers between devices  31.9 us (21%)
  local copies, waits for them, and re-layouts  27.8 us (18%)
  Pallas kernels  23.5 us (16%)
  blocking collectives  13.5 us (9%)
  other arithmetic  8.34 us (6%)
    ppermute x5, waiting for transfers between devices, along_z(): return lax.ppermute(x, 'seq', z_pairs(seq, pairs))  30.5 us
    pallas_call x3, Pallas kernels, project(): call(lambda *refs: project_kernel(kinds, *refs), 'project_' + ''.join(('q...  14.1 us
    all_to_all x1, blocking collectives, head_body(): attn = lax.all_to_all(attn, 'seq', 0, 0)  13.5 us
    unnamed x37, local copies, waits for them, and re-layouts  13.5 us
    ppermute x5, starting transfers between devices, along_z(): return lax.ppermute(x, 'seq', z_pairs(seq, pairs))  6.96 us
    ppermute x1, waiting for transfers between devices, head_body(): other = lax.ppermute(project_out(attn, w_sent), 'tp', both)  6.91 us
    all_to_all x1, starting transfers between devices, head_body(): mine = lax.all_to_all(mine, 'seq', 0, 0)  5.65 us
    ppermute x1, waiting for transfers between devices, head_body(): passed = lax.ppermute(fourth, 'tp', both)  5.45 us
  transfers between devices with their start and end apart: 19, of which 5 were waited for; matrix products, arithmetic and copies ran while one was open for 15% of the time, Pallas kernels for 13%

profile of v6, /device:TPU:0, one launch (start us, length us, event | category | flops | bytes accessed | tf_op | source)
XLA Modules:
  0.0 149.4 jit_solution(10847335291395478759)
XLA Ops:
  1.9 1.7 %norm_tokens.1 = (bf16[128,3072]{1,0:T(8,128)(2,1)}, bf16[64,3072]{1,0:T(8,128)(2,1)S(1)}) custom-call(s32[1]{0:T(128)} %bitcast.7.tp_ref.half_ref, bf16[128,3072]{1,0:T(8,128)(2,1)S(1)} %bitcast.48, f32[3,1,3072]{2,1,0:T(1,128)S(1)} %bitcast.50), custom_call_target="tpu_custom_call" | custom-call | flops 3932160 | bytes 1572864 | tf_op jit(solution)/shard_map/norm_tokens/pallas_call | solution.py:74
  3.6 3.0 %collective-permute-start = (bf16[64,3072]{1,0:T(8,128)(2,1)S(1)}, bf16[64,3072]{1,0:T(8,128)(2,1)S(1)}, u32[]{:S(2)}, u32[]{:S(2)}) collective-permute-start(bf16[64,3072]{1,0:T(8,128)(2,1)S(1)} %get-tuple-element.20), channel_id=1, source_target_pairs={{0,4},{2,6},{4,0},{6,2},{8,12},{10,14},{12,8},{14,10},{1,5},{3,7},... | collective-permute-start | bytes 1179656 | tf_op jit(solution)/shard_map/ppermute | solution.py:366
  7.3 2.2 %copy_bitcast_fusion = bf16[3,144,8,128]{3,1,0,2:T(8,128)(2,1)} fusion(bf16[384,3,1024]{2,0,1:T(8,128)(2,1)} %param.11, s32[]{:T(128)S(6)} %select_n.90), kind=kLoop, calls=%fused_computation.2 | loop fusion | bytes 1769476 | tf_op jit(solution)/shard_map/reshape | solution.py:358
  9.5 5.7 %all-to-all-start = ((bf16[8,432,128]{2,1,0:T(8,128)(2,1)}), bf16[8,432,128]{2,1,0:T(8,128)(2,1)S(1)}, u32[]{:S(2)}, u32[]{:S(2)}) async-start(bf16[8,432,128]{2,1,0:T(8,128)(2,1)} %bitcast.18), calls=%async_computation | async-start | bytes 1769472 | tf_op jit(solution)/shard_map/all_to_all | solution.py:361
  24.9 16.2 %collective-permute-done.8 = bf16[64,3072]{1,0:T(8,128)(2,1)} collective-permute-done((bf16[64,3072]{1,0:T(8,128)(2,1)S(1)}, bf16[64,3072]{1,0:T(8,128)(2,1)}, u32[]{:S(2)}, u32[]{:S(2)}) %collective-permute-start.8) | collective-permute-done | bytes 393248 | tf_op jit(solution)/shard_map/ppermute | solution.py:366
  42.2 1.6 %collective-permute-start.9 = (bf16[64,3072]{1,0:T(8,128)(2,1)S(1)}, bf16[64,3072]{1,0:T(8,128)(2,1)}, u32[]{:S(2)}, u32[]{:S(2)}) collective-permute-start(bf16[64,3072]{1,0:T(8,128)(2,1)S(1)} %broadcast_select_fusion), channel_id=1, source_target_pairs={{0,1},{1,0},{2,3},{3,2},{4,5},{5,4},{6,7},{7,6},{8,9},{9,8},{10,11... | collective-permute-start | bytes 1179656 | tf_op jit(solution)/shard_map/ppermute | solution.py:381
  43.8 14.2 %collective-permute-done.2 = bf16[64,3072]{1,0:T(8,128)(2,1)S(1)} collective-permute-done((bf16[64,3072]{1,0:T(8,128)(2,1)S(1)}, bf16[64,3072]{1,0:T(8,128)(2,1)S(1)}, u32[]{:S(2)}, u32[]{:S(2)}) %collective-permute-start.2) | collective-permute-done | bytes 393248 | tf_op jit(solution)/shard_map/ppermute | solution.py:366
  58.1 4.2 %all-to-all-start.1 = ((bf16[8,432,128]{2,1,0:T(8,128)(2,1)}), bf16[8,432,128]{2,1,0:T(8,128)(2,1)}, u32[]{:S(2)}, u32[]{:S(2)}) async-start(bf16[8,432,128]{2,1,0:T(8,128)(2,1)} %pad_maximum_fusion), calls=%async_computation.1 | async-start | bytes 1769472 | tf_op jit(solution)/shard_map/all_to_all | solution.py:395
  67.3 2.0 %pad_maximum_fusion.1.refs_7_ = bf16[128,3072]{1,0:T(8,128)(2,1)} fusion(bf16[64,3072]{1,0:T(8,128)(2,1)} %collective-permute-done.9, bf16[64,3072]{1,0:T(8,128)(2,1)S(1)} %broadcast_select_fusion), kind=kLoop, calls=%fused_computation.5 | loop fusion | flops 1572864 | bytes 1572864 | tf_op jit(solution)/shard_map/concatenate | solution.py:381
  69.2 5.4 %collective-permute-done.11.refs_10_ = bf16[64,3072]{1,0:T(8,128)(2,1)} collective-permute-done((bf16[64,3072]{1,0:T(8,128)(2,1)S(1)}, bf16[64,3072]{1,0:T(8,128)(2,1)}, u32[]{:S(2)}, u32[]{:S(2)}) %collective-permute-start.11) | collective-permute-done | bytes 393248 | tf_op jit(solution)/shard_map/ppermute | solution.py:384
  75.4 2.8 %copy-done = bf16[1024,3072]{1,0:T(8,128)(2,1)S(1)} copy-done((bf16[1024,3072]{1,0:T(8,128)(2,1)S(1)}, bf16[1024,3072]{1,0:T(8,128)(2,1)}, u32[]{:S(2)}) %copy-start) | copy-done | bytes 6291480
  79.1 1.6 %copy-done.4 = bf16[1024,1536]{1,0:T(8,128)(2,1)} copy-done((bf16[1024,1536]{1,0:T(8,128)(2,1)}, bf16[1024,1536]{1,0:T(8,128)(2,1)S(1)}, u32[]{:S(2)}) %copy-start.4) | copy-done | bytes 3145752
  80.7 1.7 %copy-done.6 = bf16[1024,1536]{1,0:T(8,128)(2,1)} copy-done((bf16[1024,1536]{1,0:T(8,128)(2,1)}, bf16[1024,1536]{1,0:T(8,128)(2,1)S(1)}, u32[]{:S(2)}) %copy-start.6) | copy-done | bytes 3145752
  82.7 1.9 %sine_multiply_fusion = (f32[1024,128]{1,0:T(8,128)S(1)}, f32[1024,128]{1,0:T(8,128)S(1)}) fusion(f32[128]{0:T(128)S(1)} %compare_select_fusion, f32[128]{0:T(128)S(1)} %mul.77, f32[1024]{0:T(1024)S(1)} %get-tuple-element.42, f32[1024]{0:T(1024)S(1)} %get-tuple-element.41, f32[]{:T(128)S(6)} %convert_element_type.40, pred[128]{0:T(512)(128)(4,1)S(1)} %get-tuple-element.43, ...), kind=kLoop, calls=%fused_computation.9 | loop fusion | flops 524288 | bytes 1058052 | tf_op jit(solution)/shard_map/mul | solution.py:335
  87.3 1.7 %slice.19 = bf16[8,128,128]{2,1,0:T(8,128)(2,1)} slice(bf16[8,432,128]{2,1,0:T(8,128)(2,1)} %all-to-all-done.1), slice={[0:8], [288:416], [0:128]} | slice | bytes 524288 | tf_op jit(solution)/shard_map/slice | solution.py:398
  91.0 4.6 %project_kv.1.kvb = bf16[2,512,128]{2,1,0:T(8,128)(2,1)} custom-call(s32[1]{0:T(128)} %bitcast.refs_0_.section_ref, bf16[8,432,128]{2,1,0:T(8,128)(2,1)S(1)} %all-to-all-done.refs_1_, bf16[8,432,128]{2,1,0:T(8,128)(2,1)S(1)} %collective-permute-done.3.refs_2_, bf16[8,288,128]{2,1,0:T(8,128)(2,1)S(1)} %slice.18.refs_3_, ...), custom_call_target="tpu_custom_call" | custom-call | flops 805306368 | bytes 5505024 | tf_op jit(solution)/shard_map/project_kv/pallas_call | solution.py:151
  95.6 4.1 %collective-permute-start.14 = (bf16[2,512,128]{2,1,0:T(8,128)(2,1)}, bf16[2,512,128]{2,1,0:T(8,128)(2,1)}, u32[]{:S(2)}, u32[]{:S(2)}) collective-permute-start(bf16[2,512,128]{2,1,0:T(8,128)(2,1)} %project_kv.1.kvb), channel_id=1, source_target_pairs={{0,16},{1,17},{2,18},{3,19},{4,20},{5,21},{6,22},{7,23},{8,24},{9,... | collective-permute-start | bytes 786440 | tf_op jit(solution)/shard_map/ppermute | solution.py:422
  99.7 5.7 %project_qkv.1 = (bf16[512,128]{1,0:T(8,128)(2,1)S(1)}, bf16[2,512,128]{2,1,0:T(8,128)(2,1)}) custom-call(s32[1]{0:T(128)} %bitcast.refs_0_.section_ref, bf16[8,432,128]{2,1,0:T(8,128)(2,1)S(1)} %all-to-all-done.refs_1_, bf16[8,432,128]{2,1,0:T(8,128)(2,1)S(1)} %collective-permute-done.3.refs_2_, bf16[8,288,128]{2,1,0:T(8,128)(2,1)S(1)} %slice.18.refs_3_, ...), custom_call_target="tpu_custom_call" | custom-call | flops 1207959552 | bytes 5505024 | tf_op jit(solution)/shard_map/project_qkv/pallas_call | solution.py:151
  106.0 2.0 %collective-permute-start.15 = (bf16[2,512,128]{2,1,0:T(8,128)(2,1)}, bf16[2,512,128]{2,1,0:T(8,128)(2,1)}, u32[]{:S(2)}, u32[]{:S(2)}) collective-permute-start(bf16[2,512,128]{2,1,0:T(8,128)(2,1)} %get-tuple-element.30.kva), channel_id=1, source_target_pairs={{0,16},{1,17},{2,18},{3,19},{4,20},{5,21},{6,22},{7,23},{8,24},{9,... | collective-permute-start | bytes 786440 | tf_op jit(solution)/shard_map/ppermute | solution.py:420
  113.0 3.8 %project_q.1.qb = bf16[512,128]{1,0:T(8,128)(2,1)S(1)} custom-call(s32[1]{0:T(128)} %bitcast.refs_0_.section_ref, bf16[8,432,128]{2,1,0:T(8,128)(2,1)S(1)} %all-to-all-done.refs_1_, bf16[8,432,128]{2,1,0:T(8,128)(2,1)S(1)} %collective-permute-done.3.refs_2_, bf16[8,288,128]{2,1,0:T(8,128)(2,1)S(1)} %slice.18.refs_3_, ...), custom_call_target="tpu_custom_call" | custom-call | flops 402653184 | bytes 5505024 | tf_op jit(solution)/shard_map/project_q/pallas_call | solution.py:151
  116.9 4.0 %attend_own.1 = (f32[1024,128]{1,0:T(8,128)S(1)}, f32[1024,128]{1,0:T(8,128)S(1)}) custom-call(s32[1]{0:T(128)} %bitcast.refs_0_.section_ref, f32[16,1024]{1,0:T(8,128)S(1)} %reshape.194.keep_ref, bf16[512,128]{1,0:T(8,128)(2,1)S(1)} %copy-done.13, bf16[512,128]{1,0:T(8,128)(2,1)S(1)} %project_q.1.qb, bf16[2,512,128]{2,1,0:T(8,128)(2,1)} %get-tuple-element.30.kva, ...), custom_call_target="tpu_custom_call" | custom-call | flops 1073741824 | bytes 2621440 | tf_op jit(solution)/shard_map/attend_own/pallas_call | solution.py:254
  121.9 13.5 %all_to_all.15.attn_ref = bf16[8,128,128]{2,1,0:T(8,128)(2,1)S(1)} all-to-all(bf16[8,128,128]{2,1,0:T(8,128)(2,1)S(1)} %attend_cond.1), channel_id=1, replica_groups=mesh['section'=2,'seq'=8,'tp'=2] {'seq'}, dimensions={0} | all-to-all | bytes 524288 | tf_op jit(solution)/shard_map/all_to_all | solution.py:429
  140.7 6.9 %collective-permute-done.16 = bf16[128,1536]{1,0:T(8,128)(2,1)} collective-permute-done((bf16[128,1536]{1,0:T(8,128)(2,1)}, bf16[128,1536]{1,0:T(8,128)(2,1)}, u32[]{:S(2)}, u32[]{:S(2)}) %collective-permute-start.16) | collective-permute-done | bytes 393248 | tf_op jit(solution)/shard_map/ppermute | solution.py:430
  147.6 1.8 %fusion.4 = bf16[1,128,1536]{2,1,0:T(8,128)(2,1)} fusion(f32[128,1536]{1,0:T(8,128)S(1)} %out_kept.1, bf16[128,1536]{1,0:T(8,128)(2,1)} %collective-permute-done.16, f32[1536]{0:T(1024)S(1)} %get-tuple-element.37), kind=kLoop, calls=%fused_computation.12 | loop fusion | flops 786432 | bytes 1579008 | tf_op jit(solution)/shard_map/broadcast_in_dim | solution.py:435
  (109 shorter events, 36.6 us)
Async XLA Ops:
  3.6 14.0 %collective-permute-start = (bf16[64,3072]{1,0:T(8,128)(2,1)S(1)}, bf16[64,3072]{1,0:T(8,128)(2,1)S(1)}, u32[]{:S(2)}, u32[]{:S(2)}) collective-permute-start(bf16[64,3072]{1,0:T(8,128)(2,1)S(1)} %get-tuple-element.20), channel_id=1, source_target_pairs={{0,4},{2,6},{4,0},{6,2},{8,12},{10,14},{12,8},{14,10},{1,5},{3,7},... | collective-permute-start | bytes 1179656 | tf_op jit(solution)/shard_map/ppermute | solution.py:366
  6.6 11.6 %collective-permute-start.7 = (bf16[64,3072]{1,0:T(8,128)(2,1)S(1)}, bf16[64,3072]{1,0:T(8,128)(2,1)S(1)}, u32[]{:S(2)}, u32[]{:S(2)}) collective-permute-start(bf16[64,3072]{1,0:T(8,128)(2,1)S(1)} %get-tuple-element.20), channel_id=1, source_target_pairs={{4,8},{6,10},{8,4},{10,6},{5,9},{7,11},{9,5},{11,7},{20,24},{22,26... | collective-permute-start | bytes 1179656 | tf_op jit(solution)/shard_map/ppermute | solution.py:366
  7.3 12.5 %copy-start.17 = (s32[1,8]{1,0:T(1,128)S(1)}, s32[1,8]{1,0:T(1,128)}, u32[]{:S(2)}) copy-start(s32[1,8]{1,0:T(1,128)} %param.15) | copy-start | bytes 100
  9.5 48.6 %all-to-all-start = ((bf16[8,432,128]{2,1,0:T(8,128)(2,1)}), bf16[8,432,128]{2,1,0:T(8,128)(2,1)S(1)}, u32[]{:S(2)}, u32[]{:S(2)}) async-start(bf16[8,432,128]{2,1,0:T(8,128)(2,1)} %bitcast.18), calls=%async_computation | async-start | bytes 1769472 | tf_op jit(solution)/shard_map/all_to_all | solution.py:361
  15.2 84.5 %collective-permute-start.4 = (bf16[128,3072]{1,0:T(8,128)(2,1)}, bf16[128,3072]{1,0:T(8,128)(2,1)}, u32[]{:S(2)}, u32[]{:S(2)}) collective-permute-start(bf16[128,3072]{1,0:T(8,128)(2,1)} %get-tuple-element.27.refs_7_), channel_id=1, source_target_pairs={{0,2},{2,0},{4,6},{6,4},{8,10},{10,8},{12,14},{14,12},{1,3},{3,1},... | collective-permute-start | bytes 2359304 | tf_op jit(solution)/shard_map/ppermute | solution.py:369
  17.5 6.1 %collective-permute-start.1 = (bf16[64,3072]{1,0:T(8,128)(2,1)S(1)}, bf16[64,3072]{1,0:T(8,128)(2,1)S(1)}, u32[]{:S(2)}, u32[]{:S(2)}) collective-permute-start(bf16[64,3072]{1,0:T(8,128)(2,1)S(1)} %collective-permute-done), channel_id=1, source_target_pairs={{4,8},{6,10},{8,4},{10,6},{5,9},{7,11},{9,5},{11,7},{20,24},{22,26... | collective-permute-start | bytes 1179656 | tf_op jit(solution)/shard_map/ppermute | solution.py:366
  18.2 22.9 %collective-permute-start.8 = (bf16[64,3072]{1,0:T(8,128)(2,1)S(1)}, bf16[64,3072]{1,0:T(8,128)(2,1)}, u32[]{:S(2)}, u32[]{:S(2)}) collective-permute-start(bf16[64,3072]{1,0:T(8,128)(2,1)S(1)} %collective-permute-done.7), channel_id=1, source_target_pairs={{4,0},{6,2},{8,12},{10,14},{5,1},{7,3},{9,13},{11,15},{20,16},{22,... | collective-permute-start | bytes 1179656 | tf_op jit(solution)/shard_map/ppermute | solution.py:366
  22.1 42.6 %collective-permute-start.5 = (bf16[64,3072]{1,0:T(8,128)(2,1)S(1)}, bf16[64,3072]{1,0:T(8,128)(2,1)S(1)}, u32[]{:S(2)}, u32[]{:S(2)}) collective-permute-start(bf16[64,3072]{1,0:T(8,128)(2,1)S(1)} %collective-permute-done), channel_id=1, source_target_pairs={{0,1},{1,0},{2,3},{3,2},{4,5},{5,4},{6,7},{7,6},{8,9},{9,8},{10,11... | collective-permute-start | bytes 1179656 | tf_op jit(solution)/shard_map/ppermute | solution.py:381
  23.6 34.4 %collective-permute-start.2 = (bf16[64,3072]{1,0:T(8,128)(2,1)S(1)}, bf16[64,3072]{1,0:T(8,128)(2,1)S(1)}, u32[]{:S(2)}, u32[]{:S(2)}) collective-permute-start(bf16[64,3072]{1,0:T(8,128)(2,1)S(1)} %collective-permute-done.1), channel_id=1, source_target_pairs={{4,0},{6,2},{8,12},{10,14},{5,1},{7,3},{9,13},{11,15},{20,16},{22,... | collective-permute-start | bytes 1179656 | tf_op jit(solution)/shard_map/ppermute | solution.py:366
  42.2 24.9 %collective-permute-start.9 = (bf16[64,3072]{1,0:T(8,128)(2,1)S(1)}, bf16[64,3072]{1,0:T(8,128)(2,1)}, u32[]{:S(2)}, u32[]{:S(2)}) collective-permute-start(bf16[64,3072]{1,0:T(8,128)(2,1)S(1)} %broadcast_select_fusion), channel_id=1, source_target_pairs={{0,1},{1,0},{2,3},{3,2},{4,5},{5,4},{6,7},{7,6},{8,9},{9,8},{10,11... | collective-permute-start | bytes 1179656 | tf_op jit(solution)/shard_map/ppermute | solution.py:381
  58.1 11.1 %copy-start.1 = (bf16[64,3072]{1,0:T(8,128)(2,1)}, bf16[64,3072]{1,0:T(8,128)(2,1)S(1)}, u32[]{:S(2)}) copy-start(bf16[64,3072]{1,0:T(8,128)(2,1)S(1)} %broadcast_select_fusion.1.refs_9_) | copy-start | bytes 1179652
  58.1 27.3 %all-to-all-start.1 = ((bf16[8,432,128]{2,1,0:T(8,128)(2,1)}), bf16[8,432,128]{2,1,0:T(8,128)(2,1)}, u32[]{:S(2)}, u32[]{:S(2)}) async-start(bf16[8,432,128]{2,1,0:T(8,128)(2,1)} %pad_maximum_fusion), calls=%async_computation.1 | async-start | bytes 1769472 | tf_op jit(solution)/shard_map/all_to_all | solution.py:395
  63.2 11.5 %collective-permute-start.11 = (bf16[64,3072]{1,0:T(8,128)(2,1)S(1)}, bf16[64,3072]{1,0:T(8,128)(2,1)}, u32[]{:S(2)}, u32[]{:S(2)}) collective-permute-start(bf16[64,3072]{1,0:T(8,128)(2,1)S(1)} %broadcast_select_fusion.1.refs_9_), channel_id=1, source_target_pairs={{0,1},{1,0},{2,3},{3,2},{4,5},{5,4},{6,7},{7,6},{8,9},{9,8},{10,11... | collective-permute-start | bytes 1179656 | tf_op jit(solution)/shard_map/ppermute | solution.py:384
  65.5 34.2 %collective-permute-start.6 = (bf16[128,3072]{1,0:T(8,128)(2,1)}, bf16[128,3072]{1,0:T(8,128)(2,1)}, u32[]{:S(2)}, u32[]{:S(2)}) collective-permute-start(bf16[128,3072]{1,0:T(8,128)(2,1)} %constant_dynamic-update-slice_fusion.refs_9_), channel_id=1, source_target_pairs={{0,2},{2,0},{4,6},{6,4},{8,10},{10,8},{12,14},{14,12},{1,3},{3,1},... | collective-permute-start | bytes 2359304 | tf_op jit(solution)/shard_map/ppermute | solution.py:369
  65.6 23.4 %collective-permute-start.3 = (bf16[8,432,128]{2,1,0:T(8,128)(2,1)S(1)}, bf16[8,432,128]{2,1,0:T(8,128)(2,1)S(1)}, u32[]{:S(2)}, u32[]{:S(2)}) collective-permute-start(bf16[8,432,128]{2,1,0:T(8,128)(2,1)S(1)} %all-to-all-done.refs_1_), channel_id=1, source_target_pairs={{0,16},{16,0},{1,17},{17,1},{2,18},{18,2},{3,19},{19,3},{4,20},{20... | collective-permute-start | bytes 2654216 | tf_op jit(solution)/shard_map/ppermute | solution.py:387
  67.1 7.7 %collective-permute-start.12 = (bf16[64,3072]{1,0:T(8,128)(2,1)S(1)}, bf16[64,3072]{1,0:T(8,128)(2,1)S(1)}, u32[]{:S(2)}, u32[]{:S(2)}) collective-permute-start(bf16[64,3072]{1,0:T(8,128)(2,1)S(1)} %broadcast_select_fusion.1.refs_9_), channel_id=1, source_target_pairs={{0,2},{2,0},{4,6},{6,4},{8,10},{10,8},{12,14},{14,12},{1,3},{3,1},... | collective-permute-start | bytes 1179656 | tf_op jit(solution)/shard_map/ppermute | solution.py:369
  74.7 14.3 %collective-permute-start.10 = (bf16[128,3072]{1,0:T(8,128)(2,1)}, bf16[128,3072]{1,0:T(8,128)(2,1)}, u32[]{:S(2)}, u32[]{:S(2)}) collective-permute-start(bf16[128,3072]{1,0:T(8,128)(2,1)} %pad_maximum_fusion.1.refs_7_), channel_id=1, source_target_pairs={{0,2},{2,0},{4,6},{6,4},{8,10},{10,8},{12,14},{14,12},{1,3},{3,1},... | collective-permute-start | bytes 2359304 | tf_op jit(solution)/shard_map/ppermute | solution.py:369
  74.8 14.2 %collective-permute-start.13 = (bf16[64,3072]{1,0:T(8,128)(2,1)}, bf16[64,3072]{1,0:T(8,128)(2,1)}, u32[]{:S(2)}, u32[]{:S(2)}) collective-permute-start(bf16[64,3072]{1,0:T(8,128)(2,1)} %collective-permute-done.11.refs_10_), channel_id=1, source_target_pairs={{0,2},{2,0},{4,6},{6,4},{8,10},{10,8},{12,14},{14,12},{1,3},{3,1},... | collective-permute-start | bytes 1179656 | tf_op jit(solution)/shard_map/ppermute | solution.py:369
  78.2 4.4 %copy-start.16 = (f32[128]{0:T(128)S(1)}, f32[128]{0:T(128)}, u32[]{:S(2)}) copy-start(f32[128]{0:T(128)} %param.13) | copy-start | bytes 1540
  95.6 25.3 %collective-permute-start.14 = (bf16[2,512,128]{2,1,0:T(8,128)(2,1)}, bf16[2,512,128]{2,1,0:T(8,128)(2,1)}, u32[]{:S(2)}, u32[]{:S(2)}) collective-permute-start(bf16[2,512,128]{2,1,0:T(8,128)(2,1)} %project_kv.1.kvb), channel_id=1, source_target_pairs={{0,16},{1,17},{2,18},{3,19},{4,20},{5,21},{6,22},{7,23},{8,24},{9,... | collective-permute-start | bytes 786440 | tf_op jit(solution)/shard_map/ppermute | solution.py:422
  106.0 10.9 %collective-permute-start.15 = (bf16[2,512,128]{2,1,0:T(8,128)(2,1)}, bf16[2,512,128]{2,1,0:T(8,128)(2,1)}, u32[]{:S(2)}, u32[]{:S(2)}) collective-permute-start(bf16[2,512,128]{2,1,0:T(8,128)(2,1)} %get-tuple-element.30.kva), channel_id=1, source_target_pairs={{0,16},{1,17},{2,18},{3,19},{4,20},{5,21},{6,22},{7,23},{8,24},{9,... | collective-permute-start | bytes 786440 | tf_op jit(solution)/shard_map/ppermute | solution.py:420
  116.9 18.6 %copy-start.7 = (bf16[1024,1536]{1,0:T(8,128)(2,1)S(1)}, bf16[1024,1536]{1,0:T(8,128)(2,1)}, u32[]{:S(2)}) copy-start(bf16[1024,1536]{1,0:T(8,128)(2,1)} %copy-done.6) | copy-start | bytes 9437188
  135.5 4.6 %copy-start.5 = (bf16[1024,1536]{1,0:T(8,128)(2,1)S(1)}, bf16[1024,1536]{1,0:T(8,128)(2,1)}, u32[]{:S(2)}) copy-start(bf16[1024,1536]{1,0:T(8,128)(2,1)} %copy-done.4) | copy-start | bytes 9437188
  136.8 10.8 %collective-permute-start.16 = (bf16[128,1536]{1,0:T(8,128)(2,1)}, bf16[128,1536]{1,0:T(8,128)(2,1)}, u32[]{:S(2)}, u32[]{:S(2)}) collective-permute-start(bf16[128,1536]{1,0:T(8,128)(2,1)} %out_sent.1), channel_id=1, source_target_pairs={{0,1},{1,0},{2,3},{3,2},{4,5},{5,4},{6,7},{7,6},{8,9},{9,8},{10,11... | collective-permute-start | bytes 1179656 | tf_op jit(solution)/shard_map/ppermute | solution.py:430
  (13 other events, 25.2 us)

commit v7 on v5

--- a/solution.py
+++ b/solution.py
@@ -90,75 +90,80 @@
     return (x * cosine + other * sine).astype(jnp.bfloat16)
 
 
-def project_kernel(kinds, pieces, section_ref, mine, peer, cos_ref, sin_ref, gain_ref, *refs):
-    x_refs, out_refs, acc_ref = refs[:pieces], refs[pieces:-1], refs[-1]
-    step = pl.program_id(0)
-    half = peer.shape[1] // 3
+def copy_all(pairs, sems):
+    copies = [pltpu.make_async_copy(s, d, sems.at[i]) for i, (s, d) in enumerate(pairs)]
+    for copy in copies:
+        copy.start()
+    for copy in copies:
+        copy.wait()
+
+
+def pack_kernel(*refs):
+    x_refs, out_ref, sems = refs[:-2], refs[-2], refs[-1]
+    at, pairs = 0, []
+    for ref in x_refs:
+        pairs.append((ref, out_ref.at[pl.ds(at, ref.shape[0]), :]))
+        at += ref.shape[0]
+    copy_all(pairs, sems)
+
+
+def pack(pieces):
+    rows, depth = sum(p.shape[0] for p in pieces), pieces[0].shape[1]
+    return call(
+        pack_kernel, "pack_tokens", jax.ShapeDtypeStruct((rows, depth), jnp.bfloat16),
+        0, 4 * rows * depth, 0,
+        in_specs=[pl.BlockSpec(memory_space=pl.ANY)] * len(pieces),
+        out_specs=VMEM,
+        scratch_shapes=[pltpu.SemaphoreType.DMA((len(pieces),))],
+    )(*pieces)
+
+
+def first_kv_kernel(section_ref, x_ref, mine, peer, cos_ref, sin_ref, gain_ref, kv_ref, w_ref):
     first = section_ref[0] == 0
-
-    def rows_of(s, kind):
-        at = slice(kind * half, (kind + 1) * half)
-        a, b = mine[s, at, :], peer[s, at, :]
-        return jnp.concatenate([jnp.where(first, a, b), jnp.where(first, b, a)], axis=0)
-
-    w = jnp.concatenate(
+    sources, held, _ = mine.shape
+    half = held // 2
+    for s in range(sources):
+        for kind in range(2):
+            at = slice(kind * half, (kind + 1) * half)
+            lanes = slice(kind * HEAD_DIM, (kind + 1) * HEAD_DIM)
+            a, b = mine[s, at, :], peer[s, at, :]
+            w_ref[2 * s * half : (2 * s + 1) * half, lanes] = jnp.where(first, a, b)
+            w_ref[(2 * s + 1) * half : (2 * s + 2) * half, lanes] = jnp.where(first, b, a)
+    kv_kernel(0, x_ref, w_ref, cos_ref, sin_ref, gain_ref, kv_ref)
+
+
+def kv_kernel(chunk, x_ref, w_ref, cos_ref, sin_ref, gain_ref, kv_ref):
+    both = jnp.dot(x_ref[...], w_ref[...], preferred_element_type=jnp.float32)
+    at = slice(chunk * x_ref.shape[0], (chunk + 1) * x_ref.shape[0])
+    kv_ref[0] = normed_rotated(
+        both[:, :HEAD_DIM], gain_ref[1:2, :], cos_ref[at, :], sin_ref[at, :]
+    )
+    kv_ref[1] = both[:, HEAD_DIM:].astype(jnp.bfloat16)
+
+
+def first_kv(section, x, mine, peer, cosine, sine, gains):
+    rows, depth = x.shape
+    return call(
+        first_kv_kernel, "first_kv",
         [
-            jnp.concatenate([rows_of(s, kind) for s in range(mine.shape[0])], axis=0)
-            for kind in kinds
+            jax.ShapeDtypeStruct((2, rows, HEAD_DIM), jnp.bfloat16),
+            jax.ShapeDtypeStruct((depth, 2 * HEAD_DIM), jnp.bfloat16),
         ],
-        axis=1,
-    )
-    x = jnp.concatenate([ref[...] for ref in x_refs], axis=0)
-    part = jnp.dot(x, w, preferred_element_type=jnp.float32)
-
-    @pl.when(step == 0)
-    def _():
-        acc_ref[...] = part
-
-    @pl.when(step > 0)
-    def _():
-        acc_ref[...] += part
-
-    @pl.when(step == pl.num_programs(0) - 1)
-    def _():
-        for place, kind in enumerate(kinds):
-            value = acc_ref[:, place * HEAD_DIM : (place + 1) * HEAD_DIM]
-            if kind < 2:
-                value = normed_rotated(
-                    value, gain_ref[kind : kind + 1, :], cos_ref[...], sin_ref[...]
-                )
-            if kind == 0:
-                out_refs[0][...] = value
-            else:
-                out_refs[0][kind - 1] = value.astype(jnp.bfloat16)
-
-
-def project(kinds, section, pieces, mine, peer, cosine, sine, gains):
-    depth = pieces[0].shape[1]
-    rows = sum(p.shape[0] for p in pieces)
-    sources = mine.shape[0]
-    steps = 4
-    shape = (rows, HEAD_DIM) if kinds == (0,) else (2, rows, HEAD_DIM)
-
-    def weights(array):
-        return pl.BlockSpec((sources // steps,) + array.shape[1:], lambda k, s: (k, 0, 0))
-
-    table = pl.BlockSpec((rows, HEAD_DIM), lambda k, s: (0, 0))
-    return call(
-        lambda *refs: project_kernel(kinds, len(pieces), *refs),
-        "project_" + "".join("qkv"[k] for k in kinds),
-        jax.ShapeDtypeStruct(shape, jnp.bfloat16),
-        2 * len(kinds) * rows * depth * HEAD_DIM, 2 * (rows * depth + mine.size + peer.size), 0,
-        grid_spec=pltpu.PrefetchScalarGridSpec(
-            num_scalar_prefetch=1,
-            grid=(steps,),
-            in_specs=[weights(mine), weights(peer)]
-            + [table, table, pl.BlockSpec((2, HEAD_DIM), lambda k, s: (0, 0))]
-            + [pl.BlockSpec((p.shape[0], depth // steps), lambda k, s: (0, k)) for p in pieces],
-            out_specs=pl.BlockSpec(shape, lambda k, s: (0,) * len(shape)),
-            scratch_shapes=[pltpu.VMEM((rows, len(kinds) * HEAD_DIM), jnp.float32)],
-        ),
-    )(section, mine, peer, cosine, sine, gains, *pieces)
+        4 * rows * depth * HEAD_DIM, 2 * (x.size + 4 * mine.size), 0,
+        in_specs=[SMEM] + [VMEM] * 6,
+        out_specs=[VMEM, VMEM],
+    )(section, x, mine, peer, cosine, sine, gains)
+
+
+def second_kv(x, w, cosine, sine, gains):
+    rows, depth = x.shape
+    return call(
+        lambda *refs: kv_kernel(1, *refs), "second_kv",
+        jax.ShapeDtypeStruct((2, rows, HEAD_DIM), jnp.bfloat16),
+        4 * rows * depth * HEAD_DIM, 2 * (x.size + w.size), 0,
+        in_specs=[VMEM] * 5,
+        out_specs=VMEM,
+    )(x, w, cosine, sine, gains)
 
 
 def weights_of(query, keys):
@@ -184,31 +189,65 @@
 BLOCK = 256
 
 
-def own_kernel(section_ref, keep_ref, q_ref, kva, kvb, text, conda, num_ref, den_ref):
-    rows = q_ref.shape[0]
-    groups = keep_ref.shape[0] * BLOCK // rows
-    for b in range(rows // BLOCK):
-        at = slice(b * BLOCK, (b + 1) * BLOCK)
-        num, den = 0.0, 0.0
-        for ref in (kva, kvb, text):
-            more = summed(weights_of(q_ref[at, :], ref[0]), ref[1])
-            num, den = num + more[0], den + more[1]
-        num_ref[at, :] = num
-        den_ref[at, :] = jnp.broadcast_to(den, num.shape)
+def own_kernel(
+    xa, xb, direct, cos_ref, sin_ref, gain_ref, rows_ref, keys_ref, kva, kvb,
+    q_ref, num_ref, den_ref, keep_ref,
+):
+    depth = xa.shape[1]
+    sources, held, _ = direct.shape
+    w = direct[:, : depth // sources, :].reshape(depth, HEAD_DIM)
+    count = (held - 16 - depth // sources) // 2
+    at = depth // sources
+    text = (
+        direct[:, at : at + count, :].reshape(-1, HEAD_DIM),
+        direct[:, at + count : at + 2 * count, :].reshape(-1, HEAD_DIM),
+    )
+    for c, x_ref in enumerate((xa, xb)):
+        for b in range(x_ref.shape[0] // BLOCK):
+            start = c * x_ref.shape[0] + b * BLOCK
+            at = slice(start, start + BLOCK)
+            query = jnp.dot(
+                x_ref[b * BLOCK : (b + 1) * BLOCK, :], w, preferred_element_type=jnp.float32
+            )
+            query = normed_rotated(query, gain_ref[0:1, :], cos_ref[at, :], sin_ref[at, :])
+            q_ref[at, :] = query
+            num, den = 0.0, 0.0
+            for keys, values in ((kva[0], kva[1]), (kvb[0], kvb[1]), text):
+                more = summed(weights_of(query, keys), values)
+                num, den = num + more[0], den + more[1]
+            num_ref[at, :] = num
+            den_ref[at, :] = jnp.broadcast_to(den, num.shape)
+    mask = jnp.concatenate(
+        [direct[s, held - 16 : held, :].astype(jnp.float32)[:1] for s in range(sources)], axis=0
+    )
+    mask = jnp.dot(rows_ref[...], mask, preferred_element_type=jnp.float32)
+    keep_ref[...] = jnp.dot(mask, keys_ref[...], preferred_element_type=jnp.float32)
+
+
+def cond_sum(keep_ref, q_ref, cond, chunk, b):
+    groups = keep_ref.shape[0] * BLOCK // q_ref.shape[0]
+    keys = cond.shape[1]
+    keep = keep_ref[b * groups : (b + 1) * groups, chunk * keys : (chunk + 1) * keys]
+    return summed(kept_weights(q_ref[b * BLOCK : (b + 1) * BLOCK, :], cond, keep), cond[1])
+
+
+def first_cond_kernel(section_ref, keep_ref, q_ref, cond, num_in, den_in, num_ref, den_ref):
+    @pl.when(section_ref[0] == 0)
+    def _():
+        num_ref[...] = num_in[...]
+        den_ref[...] = den_in[...]
 
     @pl.when(section_ref[0] != 0)
     def _():
-        for b in range(rows // BLOCK):
+        for b in range(num_ref.shape[0] // BLOCK):
             at = slice(b * BLOCK, (b + 1) * BLOCK)
-            keep = keep_ref[b * groups : (b + 1) * groups, :]
-            num, den = summed(kept_weights(q_ref[at, :], conda, keep), conda[1])
-            num_ref[at, :] += num
-            den_ref[at, :] += jnp.broadcast_to(den, num.shape)
-
-
-def cond_kernel(section_ref, place_ref, keep_ref, q_ref, condb, num_ref, den_ref, out_ref):
-    rows = q_ref.shape[0]
-    groups = keep_ref.shape[0] * BLOCK // rows
+            num, den = cond_sum(keep_ref, q_ref, cond, 0, b)
+            num_ref[at, :] = num_in[at, :] + num
+            den_ref[at, :] = den_in[at, :] + den
+
+
+def second_cond_kernel(section_ref, place_ref, keep_ref, q_ref, cond, num_ref, den_ref, out_ref):
+    groups = keep_ref.shape[0] * BLOCK // num_ref.shape[0]
     size = BLOCK // groups
 
     def store(b, num, den):
@@ -220,35 +259,49 @@
 
     @pl.when(section_ref[0] == 0)
     def _():
-        for b in range(rows // BLOCK):
+        for b in range(num_ref.shape[0] // BLOCK):
             at = slice(b * BLOCK, (b + 1) * BLOCK)
             store(b, num_ref[at, :], den_ref[at, :])
 
     @pl.when(section_ref[0] != 0)
     def _():
-        for b in range(rows // BLOCK):
+        for b in range(num_ref.shape[0] // BLOCK):
             at = slice(b * BLOCK, (b + 1) * BLOCK)
-            keep = keep_ref[b * groups : (b + 1) * groups, :]
-            num, den = summed(kept_weights(q_ref[at, :], condb, keep), condb[1])
+            num, den = cond_sum(keep_ref, q_ref, cond, 1, b)
             store(b, num_ref[at, :] + num, den_ref[at, :] + den)
 
 
-def attend_own(section, keep, query, kvs, text, cond):
-    rows = query.shape[0]
-    keys = rows + text.shape[1] + cond.shape[1]
-    return call(
-        own_kernel, "attend_own", [jax.ShapeDtypeStruct((rows, HEAD_DIM), jnp.float32)] * 2,
-        4 * rows * keys * HEAD_DIM, 2 * rows * HEAD_DIM * 10, rows * keys,
-        in_specs=[SMEM] + [VMEM] * 6,
+def attend_own(xs, direct, cosine, sine, gains, row_tiles, key_tiles, kvs):
+    rows, depth = 2 * xs[0].shape[0], xs[0].shape[1]
+    keys = rows + 512
+    return call(
+        own_kernel, "attend_own",
+        [
+            jax.ShapeDtypeStruct((rows, HEAD_DIM), jnp.bfloat16),
+            jax.ShapeDtypeStruct((rows, HEAD_DIM), jnp.float32),
+            jax.ShapeDtypeStruct((rows, HEAD_DIM), jnp.float32),
+            jax.ShapeDtypeStruct((row_tiles.shape[0], rows), jnp.float32),
+        ],
+        2 * rows * HEAD_DIM * (2 * keys + depth), 2 * rows * depth, rows * keys,
+        in_specs=[VMEM] * 10,
+        out_specs=[VMEM] * 4,
+    )(*xs, direct, cosine, sine, gains, row_tiles, key_tiles, *kvs)
+
+
+def attend_first(section, keep, query, cond, num, den):
+    rows, keys = num.shape[0], cond.shape[1]
+    return call(
+        first_cond_kernel, "attend_first", [jax.ShapeDtypeStruct(num.shape, jnp.float32)] * 2,
+        4 * rows * keys * HEAD_DIM, 2 * rows * HEAD_DIM * 8, rows * keys,
+        in_specs=[SMEM] + [VMEM] * 5,
         out_specs=[VMEM] * 2,
-    )(section, keep, query, *kvs, text, cond)
-
-
-def attend_cond(section, place, keep, query, cond, num, den, seq):
-    rows = num.shape[0]
-    keys = cond.shape[1]
-    return call(
-        cond_kernel, "attend_cond",
+    )(section, keep, query, cond, num, den)
+
+
+def attend_second(section, place, keep, query, cond, num, den, seq):
+    rows, keys = num.shape[0], cond.shape[1]
+    return call(
+        second_cond_kernel, "attend_second",
         jax.ShapeDtypeStruct((seq, rows // seq, HEAD_DIM), jnp.bfloat16),
         4 * rows * keys * HEAD_DIM, 2 * rows * HEAD_DIM * 8, rows * keys,
         in_specs=[SMEM, SMEM] + [VMEM] * 5,
@@ -260,38 +313,47 @@
     return jnp.concatenate([attn_ref[h] for h in range(attn_ref.shape[0])], axis=1)
 
 
-def sent_kernel(half_ref, attn_ref, w_ref, out_ref):
+def load_kernel(half_ref, w_ref, sent_ref, kept_ref, sems):
+    width = sent_ref.shape[1]
+    pairs = []
+    for half, out_ref in ((1 - half_ref[0], sent_ref), (half_ref[0], kept_ref)):
+        columns = pl.ds(pl.multiple_of(half * width, width), width)
+        pairs.append((w_ref.at[:, columns], out_ref))
+    copy_all(pairs, sems)
+
+
+def load_out(half, w_out):
+    shape = jax.ShapeDtypeStruct((w_out.shape[0], w_out.shape[1] // 2), w_out.dtype)
+    return call(
+        load_kernel, "load_out", [shape] * 2, 0, 4 * w_out.size, 0,
+        in_specs=[SMEM, pl.BlockSpec(memory_space=pl.ANY)],
+        out_specs=[VMEM, VMEM],
+        scratch_shapes=[pltpu.SemaphoreType.DMA((2,))],
+    )(half, w_out)
+
+
+def sent_kernel(attn_ref, w_ref, out_ref):
     branch = jnp.dot(token_rows(attn_ref), w_ref[...], preferred_element_type=jnp.float32)
     out_ref[...] = branch.astype(jnp.bfloat16)
 
 
-def kept_kernel(half_ref, attn_ref, w_ref, image_ref, gate_ref, out_ref):
+def kept_kernel(attn_ref, w_ref, image_ref, gate_ref, out_ref):
     branch = jnp.dot(token_rows(attn_ref), w_ref[...], preferred_element_type=jnp.float32)
     out_ref[...] = image_ref[...].astype(jnp.float32) + gate_ref[...] * branch
 
 
-def project_out(half, attn, w_out, image=None, gate=None):
+def project_out(attn, w, image=None, gate=None):
     rows = attn.shape[1]
-    depth, width = w_out.shape[0], w_out.shape[1] // 2
-    block = 512
-    steps = width // block
-
-    def columns(height):
-        return pl.BlockSpec((height, block), lambda i, half: (0, half[0] * steps + i))
-
+    depth, width = w.shape
     kept = image is not None
+    args = (attn, w) + ((image, gate) if kept else ())
     return call(
         kept_kernel if kept else sent_kernel, "out_kept" if kept else "out_sent",
         jax.ShapeDtypeStruct((rows, width), jnp.float32 if kept else jnp.bfloat16),
         2 * rows * depth * width, 2 * depth * width, 0,
-        grid_spec=pltpu.PrefetchScalarGridSpec(
-            num_scalar_prefetch=1,
-            grid=(steps,),
-            in_specs=[pl.BlockSpec(attn.shape, lambda i, half: (0, 0, 0)), columns(depth)]
-            + ([columns(rows), columns(1)] if kept else []),
-            out_specs=pl.BlockSpec((rows, block), lambda i, half: (0, i)),
-        ),
-    )(half, attn, w_out, *((image, gate) if kept else ()))
+        in_specs=[VMEM] * len(args),
+        out_specs=VMEM,
+    )(*args)
 
 
 def lane_tables(rows_index, time_index):
@@ -322,39 +384,6 @@
     section_at = section.astype(jnp.int32).reshape(1)
     tp_at = tp.astype(jnp.int32).reshape(1)
     both = [(0, 1), (1, 0)]
-
-    half = depth // 2
-    w_half = lax.dynamic_slice_in_dim(w_qkv.transpose(1, 0, 2), section * half, half, 1)
-    w_half = w_half.reshape(3, half, seq, HEAD_DIM).transpose(2, 0, 1, 3).reshape(seq, -1, HEAD_DIM)
-    text = text_kv[0].reshape(-1, 2, seq, HEAD_DIM).transpose(2, 0, 1, 3).reshape(seq, -1, HEAD_DIM)
-    mask = jnp.pad(
-        region_mask.astype(jnp.bfloat16), ((0, 15), (0, HEAD_DIM - region_mask.shape[1]))
-    )
-    mask = jnp.broadcast_to(mask, (seq,) + mask.shape)
-    mine = lax.all_to_all(jnp.concatenate([w_half, text, mask], axis=1), "seq", 0, 0)
-    peer = lax.ppermute(mine[:, : 3 * half], "section", both)
-    text = mine[:, 3 * half : -16].reshape(-1, 2, HEAD_DIM).transpose(1, 0, 2)
-    keep = mine[:, -16, : region_mask.shape[1]].astype(jnp.float32)
-
-    full, part = norm_tokens(tp_at, image[0], modulation.transpose(1, 0, 2))
-
-    def along_z(x, pairs):
-        return lax.ppermute(x, "seq", z_pairs(seq, pairs))
-
-    near = along_z(part, [(0, 1), (1, 0), (2, 3), (3, 2)])
-    middle = along_z(part, [(1, 2), (2, 1)])
-    far = along_z(near, [(1, 2), (2, 1)])
-    middle_end = along_z(middle, [(1, 0), (2, 3)])
-    far_end = along_z(far, [(1, 0), (2, 3)])
-    inner = (chip == 1) | (chip == 2)
-    third = jnp.where(inner, middle, middle_end)
-    fourth = jnp.where(inner, far, far_end)
-    groups = [full]
-    for came in (near, third, fourth):
-        groups.append(jnp.concatenate([came, lax.ppermute(came, "tp", both)], axis=0))
-    pieces = [
-        (g, lax.ppermute(g, "seq", [(s, s ^ 1) for s in range(seq)])) for g in groups
-    ]
 
     upper = chip >= 2
     chips = jnp.stack([chip, chip ^ 1, jnp.where(upper, 1, 2), jnp.where(upper, 0, 3)])
@@ -368,25 +397,76 @@
     rows_index = (first_row[:, None] + jnp.arange(size, dtype=jnp.int32)[None]).reshape(-1)
     cosine, sine = lane_tables(rows_index, (section == 0).astype(jnp.float32))
     gains = jnp.stack([q_gain, k_gain])
-    chosen = (shards[:, None] == jnp.arange(seq)[None]).astype(jnp.float32)
-    keep = jnp.repeat(chosen @ keep @ chosen.T, size, axis=1)
-
-    rows = rows_index.shape[0] // 2
-    a, b = list(pieces[0] + pieces[1]), list(pieces[2] + pieces[3])
-    kv_a = project((1, 2), section_at, a, mine, peer, cosine[:rows], sine[:rows], gains)
+    row_tiles = (shards[:, None] == jnp.arange(seq)[None]).astype(jnp.float32)
+    key_tiles = jnp.arange(HEAD_DIM)[:, None] == jnp.repeat(shards, size)[None]
+    key_tiles = key_tiles.astype(jnp.float32)
+    place = jnp.stack([shards, parts])
+
+    rows3 = w_qkv.transpose(1, 0, 2)
+    half = depth // 2
+
+    def for_heads(rows):
+        rows = rows.reshape(rows.shape[0], -1, seq, HEAD_DIM).transpose(2, 0, 1, 3)
+        return rows.reshape(seq, -1, HEAD_DIM)
+
+    mine = for_heads(lax.dynamic_slice_in_dim(rows3[1:], section * half, half, 1))
+    mine = lax.all_to_all(mine, "seq", 0, 0)
+
+    full, part = norm_tokens(tp_at, image[0], modulation.transpose(1, 0, 2))
+
+    def along_z(x, pairs):
+        return lax.ppermute(x, "seq", z_pairs(seq, pairs))
+
+    def to_core(x):
+        return lax.ppermute(x, "seq", [(s, s ^ 1) for s in range(seq)])
+
+    def shared(came):
+        passed = lax.ppermute(came, "tp", both)
+        return [came, passed, to_core(came), to_core(passed)]
+
+    near = along_z(part, [(0, 1), (1, 0), (2, 3), (3, 2)])
+    middle = along_z(part, [(1, 2), (2, 1)])
+    far = along_z(near, [(1, 2), (2, 1)])
+    middle_end = along_z(middle, [(1, 0), (2, 3)])
+    far_end = along_z(far, [(1, 0), (2, 3)])
+    inner = (chip == 1) | (chip == 2)
+    third = jnp.where(inner, middle, middle_end)
+    x_a = pack([full, to_core(full)] + shared(near))
+    third, mine = lax.optimization_barrier((third, mine))
+    peer = lax.ppermute(mine, "section", both)
+
+    text = text_kv[0].reshape(-1, 2, seq, HEAD_DIM).transpose(2, 1, 0, 3).reshape(seq, -1, HEAD_DIM)
+    mask = jnp.pad(
+        region_mask.astype(jnp.bfloat16), ((0, 15), (0, HEAD_DIM - region_mask.shape[1]))
+    )
+    mask = jnp.broadcast_to(mask, (seq,) + mask.shape)
+    direct = jnp.concatenate([for_heads(rows3[:1]), text, mask], axis=1)
+    direct, mine = lax.optimization_barrier((direct, mine))
+    direct = lax.all_to_all(direct, "seq", 0, 0)
+
+    fourth = jnp.where(inner, far, far_end)
+    w_sent, w_kept = load_out(tp_at, w_out)
+    cols = w_sent.shape[1]
+    gate = lax.dynamic_slice_in_dim(mods[2:3], tp * cols, cols, 1)
+    residual = lax.dynamic_slice_in_dim(image[0], tp * cols, cols, 1)
+    early = (cosine, sine, gains, row_tiles, key_tiles, place, gate, residual, w_sent, w_kept, x_a)
+    fourth, early = lax.optimization_barrier((fourth, early))
+    cosine, sine, gains, row_tiles, key_tiles, place, gate, residual, w_sent, w_kept, x_a = early
+    x_b = pack(shared(third) + shared(fourth))
+
+    kv_a, w_kv = first_kv(section_at, x_a, mine, peer, cosine, sine, gains)
     cond_a = lax.ppermute(kv_a, "section", [(0, 1)])
-    kv_b = project((1, 2), section_at, b, mine, peer, cosine[rows:], sine[rows:], gains)
+    kv_b = second_kv(x_b, w_kv, cosine, sine, gains)
     cond_b = lax.ppermute(kv_b, "section", [(0, 1)])
-    query = project((0,), section_at, a + b, mine, peer, cosine, sine, gains)
-    num, den = attend_own(section_at, keep[:, :rows], query, (kv_a, kv_b), text, cond_a)
-    place = jnp.stack([shards, parts])
-    attn = attend_cond(section_at, place, keep[:, rows:], query, cond_b, num, den, seq)
+    query, num, den, keep = attend_own(
+        (x_a, x_b), direct, cosine, sine, gains, row_tiles, key_tiles, (kv_a, kv_b)
+    )
+    num, den = attend_first(section_at, keep, query, cond_a, num, den)
+    attn = attend_second(section_at, place, keep, query, cond_b, num, den, seq)
 
     attn = lax.all_to_all(attn, "seq", 0, 0)
-    gate = mods[2:3]
-    other = lax.ppermute(project_out(1 - tp_at, attn, w_out), "tp", both)
-    kept = project_out(tp_at, attn, w_out, image[0], gate)
-    gate = lax.dynamic_slice_in_dim(gate, tp * other.shape[1], other.shape[1], 1)
+    other = lax.ppermute(project_out(attn, w_sent), "tp", both)
+    kept = project_out(attn, w_kept, residual, gate)
     return (kept + gate * other.astype(jnp.float32)).astype(jnp.bfloat16)[None]
 
 

time: 161 us -> 150 us (0.932)
  waiting for transfers between devices: 68.8 us -> 30.7 us
  blocking collectives: 0 us -> 14.5 us
  local copies, waits for them, and re-layouts: 25.1 us -> 37.5 us
  starting transfers between devices: 28.3 us -> 34.2 us
  Pallas kernels: 22.4 us -> 19.6 us
  other arithmetic: 13.8 us -> 11.6 us
    ppermute x5, waiting for transfers between devices: 40 us -> 6.19 us  [along_z(): return lax.ppermute(x, 'seq', z_pairs(seq, pairs))]
    all_to_all x0 -> x1, blocking collectives: none -> 14.5 us  [head_body(): attn = lax.all_to_all(attn, 'seq', 0, 0)]
    unnamed x47 -> x75, local copies, waits for them, and re-layouts: 12.5 us -> 23.3 us
    all_to_all x2, waiting for transfers between devices: 9.66 us -> 0.01 us  [the longest x1 0.01 us: head_body(): mine = lax.all_to_all(mine, 'seq', 0, 0)]
    ppermute x9 -> x12, waiting for transfers between devices: 19.2 us -> 24.5 us  [the longest x3 16.8 us: shared(): passed = lax.ppermute(came, 'tp', both)]
    pallas_call x4 -> x7, Pallas kernels: 15.7 us -> 10.4 us  [the longest x1 3.44 us: first_kv(): call(first_kv_kernel, 'first_kv', [jax.ShapeDtypeStruct((2, rows, HEAD_DI...]
    concatenate x3 -> x1, other arithmetic: 5.37 us -> 1.06 us  [head_body(): direct = jnp.concatenate([for_heads(rows3[:1]), text, mask], axis=1)]
    pallas_call x1, Pallas kernels: 2.54 us -> 6.54 us  [attend_own(): call(own_kernel, 'attend_own', [jax.ShapeDtypeStruct((rows, HEAD_DIM), jn...]
  transfers between devices with their start and end apart: 18 -> 21, of which waited for: 6 -> 5; matrix products, arithmetic and copies ran while one was open for 18% -> 19% of each run, Pallas kernels for 11% -> 11%
where the time goes in v7:
time: 150 us; the launch traced here: 148 us
  local copies, waits for them, and re-layouts  37.5 us (25%)
  starting transfers between devices  34.2 us (23%)
  waiting for transfers between devices  30.7 us (20%)
  Pallas kernels  19.6 us (13%)
  blocking collectives  14.5 us (10%)
  other arithmetic  11.6 us (8%)
    unnamed x75, local copies, waits for them, and re-layouts  23.3 us
    ppermute x3, waiting for transfers between devices, shared(): passed = lax.ppermute(came, 'tp', both)  16.8 us
    all_to_all x1, blocking collectives, head_body(): attn = lax.all_to_all(attn, 'seq', 0, 0)  14.5 us
    ppermute x5, starting transfers between devices, along_z(): return lax.ppermute(x, 'seq', z_pairs(seq, pairs))  8.51 us
    ppermute x1, waiting for transfers between devices, head_body(): other = lax.ppermute(project_out(attn, w_sent), 'tp', both)  7.67 us
    all_to_all x1, starting transfers between devices, head_body(): direct = lax.all_to_all(direct, 'seq', 0, 0)  7.07 us
    pallas_call x1, Pallas kernels, attend_own(): call(own_kernel, 'attend_own', [jax.ShapeDtypeStruct((rows, HEAD_DIM), jn...  6.54 us
    ppermute x5, waiting for transfers between devices, along_z(): return lax.ppermute(x, 'seq', z_pairs(seq, pairs))  6.19 us
  transfers between devices with their start and end apart: 21, of which 5 were waited for; matrix products, arithmetic and copies ran while one was open for 19% of the time, Pallas kernels for 11%

profile of v7, /device:TPU:0, one launch (start us, length us, event | category | flops | bytes accessed | tf_op | source)
XLA Modules:
  0.0 148.5 jit_solution(2215306531505783195)
XLA Ops:
  2.6 3.1 %collective-permute-start = (bf16[64,3072]{1,0:T(8,128)(2,1)S(1)}, bf16[64,3072]{1,0:T(8,128)(2,1)S(1)}, u32[]{:S(2)}, u32[]{:S(2)}) collective-permute-start(bf16[64,3072]{1,0:T(8,128)(2,1)S(1)} %get-tuple-element.33), channel_id=1, source_target_pairs={{0,4},{2,6},{4,0},{6,2},{8,12},{10,14},{12,8},{14,10},{1,5},{3,7},... | collective-permute-start | bytes 1179656 | tf_op jit(solution)/shard_map/ppermute | solution.py:418
  7.1 4.3 %copy.10 = bf16[384,3,1024]{0,2,1:T(8,128)(2,1)} copy(bf16[384,3,1024]{2,0,1:T(8,128)(2,1)} %param.11) | data formatting | bytes 4718592 | tf_op args[3]
  11.4 2.7 %slice.13 = bf16[2,384,1024]{1,2,0:T(8,128)(2,1)} slice(bf16[3,384,1024]{1,2,0:T(8,128)(2,1)} %bitcast.34), slice={[1:3], [0:384], [0:1024]} | slice | bytes 3145728 | tf_op jit(solution)/shard_map/slice | solution.py:412
  14.1 2.8 %constant_dynamic-slice_fusion = bf16[2,192,1024]{1,2,0:T(8,128)(2,1)} fusion(bf16[2,384,1024]{1,2,0:T(8,128)(2,1)} %slice.13, s32[]{:T(128)S(6)} %select_n.98), kind=kLoop, calls=%fused_computation.30 | loop fusion | bytes 1572868 | tf_op jit(solution)/shard_map/dynamic_slice | solution.py:412
  17.0 2.3 %copy.12 = bf16[8,2,192,128]{3,2,1,0:T(8,128)(2,1)} copy(bf16[8,2,192,128]{2,3,0,1:T(8,128)(2,1)} %bitcast.36) | data formatting | bytes 1572864 | tf_op jit(solution)/shard_map/transpose | solution.py:409
  19.3 5.1 %all-to-all-start = ((bf16[8,384,128]{2,1,0:T(8,128)(2,1)}), bf16[8,384,128]{2,1,0:T(8,128)(2,1)}, u32[]{:S(2)}, u32[]{:S(2)}) async-start(bf16[8,384,128]{2,1,0:T(8,128)(2,1)} %bitcast.37), calls=%async_computation | async-start | bytes 1572864 | tf_op jit(solution)/shard_map/all_to_all | solution.py:413
  38.1 3.2 %sine_multiply_fusion = (f32[1024,128]{1,0:T(8,128)}, f32[1024,128]{1,0:T(8,128)}) fusion(f32[128]{0:T(128)S(1)} %copy-done.34, f32[128]{0:T(128)S(1)} %copy-done.30, f32[1024]{0:T(1024)S(1)} %get-tuple-element.66, f32[1024]{0:T(1024)S(1)} %get-tuple-element.65, f32[]{:T(128)S(6)} %convert_element_type.43, pred[128]{0:T(512)(128)(4,1)S(1)} %copy-done.32, ...), kind=kLoop, calls=%fused_computation.3 | loop fusion | flops 524288 | bytes 1058052 | tf_op jit(solution)/shard_map/mul | solution.py:369
  44.1 5.9 %collective-permute-done.8 = bf16[64,3072]{1,0:T(8,128)(2,1)} collective-permute-done((bf16[64,3072]{1,0:T(8,128)(2,1)}, bf16[64,3072]{1,0:T(8,128)(2,1)}, u32[]{:S(2)}, u32[]{:S(2)}) %collective-permute-start.8) | collective-permute-done | bytes 393248 | tf_op jit(solution)/shard_map/ppermute | solution.py:418
  51.1 7.1 %all-to-all-start.1 = ((bf16[8,528,128]{2,1,0:T(8,128)(2,1)}), bf16[8,528,128]{2,1,0:T(8,128)(2,1)}, u32[]{:S(2)}, u32[]{:S(2)}) async-start(bf16[8,528,128]{2,1,0:T(8,128)(2,1)} %pad_maximum_fusion), calls=%async_computation.1 | async-start | bytes 2162688 | tf_op jit(solution)/shard_map/all_to_all | solution.py:445
  58.4 2.8 %copy-done.6 = bf16[1024,3072]{1,0:T(8,128)(2,1)S(1)} copy-done((bf16[1024,3072]{1,0:T(8,128)(2,1)S(1)}, bf16[1024,3072]{1,0:T(8,128)(2,1)}, u32[]{:S(2)}) %copy-start.6) | copy-done | bytes 6291480
  62.0 1.6 %copy-done.7 = bf16[1024,1536]{1,0:T(8,128)(2,1)} copy-done((bf16[1024,1536]{1,0:T(8,128)(2,1)}, bf16[1024,1536]{1,0:T(8,128)(2,1)S(1)}, u32[]{:S(2)}) %copy-start.7) | copy-done | bytes 3145752
  63.6 1.7 %copy-done.9 = bf16[1024,1536]{1,0:T(8,128)(2,1)} copy-done((bf16[1024,1536]{1,0:T(8,128)(2,1)}, bf16[1024,1536]{1,0:T(8,128)(2,1)S(1)}, u32[]{:S(2)}) %copy-start.9) | copy-done | bytes 3145752
  73.3 1.6 %collective-permute-start.12 = (bf16[64,3072]{1,0:T(8,128)(2,1)S(1)}, bf16[64,3072]{1,0:T(8,128)(2,1)S(1)}, u32[]{:S(2)}, u32[]{:S(2)}) collective-permute-start(bf16[64,3072]{1,0:T(8,128)(2,1)S(1)} %broadcast_select_fusion.1.refs_4_), channel_id=1, source_target_pairs={{0,1},{1,0},{2,3},{3,2},{4,5},{5,4},{6,7},{7,6},{8,9},{9,8},{10,11... | collective-permute-start | bytes 1179656 | tf_op jit(solution)/shard_map/ppermute | solution.py:424
  75.9 9.4 %collective-permute-done.12.refs_5_ = bf16[64,3072]{1,0:T(8,128)(2,1)S(1)} collective-permute-done((bf16[64,3072]{1,0:T(8,128)(2,1)S(1)}, bf16[64,3072]{1,0:T(8,128)(2,1)S(1)}, u32[]{:S(2)}, u32[]{:S(2)}) %collective-permute-start.12) | collective-permute-done | bytes 393248 | tf_op jit(solution)/shard_map/ppermute | solution.py:424
  85.3 7.4 %collective-permute-done.9.refs_1_ = bf16[64,3072]{1,0:T(8,128)(2,1)S(1)} collective-permute-done((bf16[64,3072]{1,0:T(8,128)(2,1)S(1)}, bf16[64,3072]{1,0:T(8,128)(2,1)S(1)}, u32[]{:S(2)}, u32[]{:S(2)}) %collective-permute-start.9) | collective-permute-done | bytes 393248 | tf_op jit(solution)/shard_map/ppermute | solution.py:424
  92.7 3.4 %first_kv.1 = (bf16[2,512,128]{2,1,0:T(8,128)(2,1)}, bf16[3072,256]{1,0:T(8,128)(2,1)S(1)}) custom-call(s32[1]{0:T(128)} %bitcast.section_ref, bf16[512,3072]{1,0:T(8,128)(2,1)S(1)} %pack_tokens.2.x_ref.xa, bf16[8,384,128]{2,1,0:T(8,128)(2,1)} %all-to-all-done.mine, bf16[8,384,128]{2,1,0:T(8,128)(2,1)S(1)} %collective-permute-done.15.peer, ...), custom_call_target="tpu_custom_call" | custom-call | flops 805306368 | bytes 6291456 | tf_op jit(solution)/shard_map/first_kv/pallas_call | solution.py:146
  96.2 3.9 %collective-permute-start.17 = (bf16[2,512,128]{2,1,0:T(8,128)(2,1)}, bf16[2,512,128]{2,1,0:T(8,128)(2,1)}, u32[]{:S(2)}, u32[]{:S(2)}) collective-permute-start(bf16[2,512,128]{2,1,0:T(8,128)(2,1)} %get-tuple-element.49.kva), channel_id=1, source_target_pairs={{0,16},{1,17},{2,18},{3,19},{4,20},{5,21},{6,22},{7,23},{8,24},{9,... | collective-permute-start | bytes 786440 | tf_op jit(solution)/shard_map/ppermute | solution.py:458
  100.1 1.6 %pack_tokens.3.refs_0_.xb = bf16[512,3072]{1,0:T(8,128)(2,1)S(1)} custom-call(bf16[64,3072]{1,0:T(8,128)(2,1)S(1)} %broadcast_select_fusion.refs_0_, bf16[64,3072]{1,0:T(8,128)(2,1)S(1)} %collective-permute-done.9.refs_1_, bf16[64,3072]{1,0:T(8,128)(2,1)S(1)} %collective-permute-done.10.refs_2_, bf16[64,3072]{1,0:T(8,128)(2,1)S(1)} %collective-permute-done.11.refs_3_, ...), custom_call_target="tpu_custom_call" | custom-call | bytes 6291456 | tf_op jit(solution)/shard_map/pack_tokens/pallas_call | solution.py:112
  103.4 2.0 %collective-permute-start.16 = (bf16[2,512,128]{2,1,0:T(8,128)(2,1)S(1)}, bf16[2,512,128]{2,1,0:T(8,128)(2,1)}, u32[]{:S(2)}, u32[]{:S(2)}) collective-permute-start(bf16[2,512,128]{2,1,0:T(8,128)(2,1)S(1)} %second_kv.1.kvb), channel_id=1, source_target_pairs={{0,16},{1,17},{2,18},{3,19},{4,20},{5,21},{6,22},{7,23},{8,24},{9,... | collective-permute-start | bytes 786440 | tf_op jit(solution)/shard_map/ppermute | solution.py:460
  105.4 1.9 %copy-done.1 = bf16[512,3072]{1,0:T(8,128)(2,1)S(1)} copy-done((bf16[512,3072]{1,0:T(8,128)(2,1)S(1)}, bf16[512,3072]{1,0:T(8,128)(2,1)}, u32[]{:S(2)}) %copy-start.1) | copy-done | bytes 3145752
  111.1 6.5 %attend_own.1 = (bf16[1024,128]{1,0:T(8,128)(2,1)S(1)}, f32[1024,128]{1,0:T(8,128)S(1)}, f32[1024,128]{1,0:T(8,128)S(1)}, f32[16,1024]{1,0:T(8,128)S(1)}) custom-call(bf16[512,3072]{1,0:T(8,128)(2,1)S(1)} %pack_tokens.2.x_ref.xa, bf16[512,3072]{1,0:T(8,128)(2,1)S(1)} %copy-done.1, bf16[8,528,128]{2,1,0:T(8,128)(2,1)} %all-to-all-done.1.direct, ...), custom_call_target="tpu_custom_call" | custom-call | flops 1610612736 | bytes 6291456 | tf_op jit(solution)/shard_map/attend_own/pallas_call | solution.py:277
  119.9 14.5 %all_to_all.15.attn_ref = bf16[8,128,128]{2,1,0:T(8,128)(2,1)S(1)} all-to-all(bf16[8,128,128]{2,1,0:T(8,128)(2,1)S(1)} %attend_second.1), channel_id=1, replica_groups=mesh['section'=2,'seq'=8,'tp'=2] {'seq'}, dimensions={0} | all-to-all | bytes 524288 | tf_op jit(solution)/shard_map/all_to_all | solution.py:467
  139.0 7.7 %collective-permute-done.18 = bf16[128,1536]{1,0:T(8,128)(2,1)} collective-permute-done((bf16[128,1536]{1,0:T(8,128)(2,1)}, bf16[128,1536]{1,0:T(8,128)(2,1)}, u32[]{:S(2)}, u32[]{:S(2)}) %collective-permute-start.18) | collective-permute-done | bytes 393248 | tf_op jit(solution)/shard_map/ppermute | solution.py:468
  146.6 1.9 %fusion.2 = bf16[1,128,1536]{2,1,0:T(8,128)(2,1)} fusion(f32[128,1536]{1,0:T(8,128)S(1)} %out_kept.1, bf16[128,1536]{1,0:T(8,128)(2,1)} %collective-permute-done.18, f32[1536]{0:T(1024)S(1)} %reduce), kind=kLoop, calls=%fused_computation.7 | loop fusion | flops 786432 | bytes 1579008 | tf_op jit(solution)/shard_map/broadcast_in_dim | solution.py:470
  (152 shorter events, 43.6 us)
Async XLA Ops:
  2.6 26.0 %collective-permute-start = (bf16[64,3072]{1,0:T(8,128)(2,1)S(1)}, bf16[64,3072]{1,0:T(8,128)(2,1)S(1)}, u32[]{:S(2)}, u32[]{:S(2)}) collective-permute-start(bf16[64,3072]{1,0:T(8,128)(2,1)S(1)} %get-tuple-element.33), channel_id=1, source_target_pairs={{0,4},{2,6},{4,0},{6,2},{8,12},{10,14},{12,8},{14,10},{1,5},{3,7},... | collective-permute-start | bytes 1179656 | tf_op jit(solution)/shard_map/ppermute | solution.py:418
  5.7 24.4 %collective-permute-start.7 = (bf16[64,3072]{1,0:T(8,128)(2,1)S(1)}, bf16[64,3072]{1,0:T(8,128)(2,1)}, u32[]{:S(2)}, u32[]{:S(2)}) collective-permute-start(bf16[64,3072]{1,0:T(8,128)(2,1)S(1)} %get-tuple-element.33), channel_id=1, source_target_pairs={{4,8},{6,10},{8,4},{10,6},{5,9},{7,11},{9,5},{11,7},{20,24},{22,26... | collective-permute-start | bytes 1179656 | tf_op jit(solution)/shard_map/ppermute | solution.py:418
  7.1 61.1 %collective-permute-start.3 = (bf16[128,3072]{1,0:T(8,128)(2,1)S(1)}, bf16[128,3072]{1,0:T(8,128)(2,1)S(1)}, u32[]{:S(2)}, u32[]{:S(2)}) collective-permute-start(bf16[128,3072]{1,0:T(8,128)(2,1)S(1)} %get-tuple-element.36.refs_0_), channel_id=1, source_target_pairs={{0,2},{2,0},{4,6},{6,4},{8,10},{10,8},{12,14},{14,12},{1,3},{3,1},... | collective-permute-start | bytes 2359304 | tf_op jit(solution)/shard_map/ppermute | solution.py:421
  19.3 31.8 %all-to-all-start = ((bf16[8,384,128]{2,1,0:T(8,128)(2,1)}), bf16[8,384,128]{2,1,0:T(8,128)(2,1)}, u32[]{:S(2)}, u32[]{:S(2)}) async-start(bf16[8,384,128]{2,1,0:T(8,128)(2,1)} %bitcast.37), calls=%async_computation | async-start | bytes 1572864 | tf_op jit(solution)/shard_map/all_to_all | solution.py:413
  28.6 37.3 %copy-start.19 = (bf16[64,3072]{1,0:T(8,128)(2,1)}, bf16[64,3072]{1,0:T(8,128)(2,1)S(1)}, u32[]{:S(2)}) copy-start(bf16[64,3072]{1,0:T(8,128)(2,1)S(1)} %collective-permute-done.refs_2_) | copy-start | bytes 1179652
  28.6 14.2 %collective-permute-start.1 = (bf16[64,3072]{1,0:T(8,128)(2,1)S(1)}, bf16[64,3072]{1,0:T(8,128)(2,1)}, u32[]{:S(2)}, u32[]{:S(2)}) collective-permute-start(bf16[64,3072]{1,0:T(8,128)(2,1)S(1)} %collective-permute-done.refs_2_), channel_id=1, source_target_pairs={{4,8},{6,10},{8,4},{10,6},{5,9},{7,11},{9,5},{11,7},{20,24},{22,26... | collective-permute-start | bytes 1179656 | tf_op jit(solution)/shard_map/ppermute | solution.py:418
  30.1 20.0 %collective-permute-start.8 = (bf16[64,3072]{1,0:T(8,128)(2,1)}, bf16[64,3072]{1,0:T(8,128)(2,1)}, u32[]{:S(2)}, u32[]{:S(2)}) collective-permute-start(bf16[64,3072]{1,0:T(8,128)(2,1)} %collective-permute-done.7), channel_id=1, source_target_pairs={{4,0},{6,2},{8,12},{10,14},{5,1},{7,3},{9,13},{11,15},{20,16},{22,... | collective-permute-start | bytes 1179656 | tf_op jit(solution)/shard_map/ppermute | solution.py:418
  41.3 25.2 %collective-permute-start.4 = (bf16[64,3072]{1,0:T(8,128)(2,1)S(1)}, bf16[64,3072]{1,0:T(8,128)(2,1)S(1)}, u32[]{:S(2)}, u32[]{:S(2)}) collective-permute-start(bf16[64,3072]{1,0:T(8,128)(2,1)S(1)} %collective-permute-done.refs_2_), channel_id=1, source_target_pairs={{0,1},{1,0},{2,3},{3,2},{4,5},{5,4},{6,7},{7,6},{8,9},{9,8},{10,11... | collective-permute-start | bytes 1179656 | tf_op jit(solution)/shard_map/ppermute | solution.py:424
  42.8 25.3 %collective-permute-start.2 = (bf16[64,3072]{1,0:T(8,128)(2,1)}, bf16[64,3072]{1,0:T(8,128)(2,1)S(1)}, u32[]{:S(2)}, u32[]{:S(2)}) collective-permute-start(bf16[64,3072]{1,0:T(8,128)(2,1)} %collective-permute-done.1), channel_id=1, source_target_pairs={{4,0},{6,2},{8,12},{10,14},{5,1},{7,3},{9,13},{11,15},{20,16},{22,... | collective-permute-start | bytes 1179656 | tf_op jit(solution)/shard_map/ppermute | solution.py:418
  51.1 54.3 %all-to-all-start.1 = ((bf16[8,528,128]{2,1,0:T(8,128)(2,1)}), bf16[8,528,128]{2,1,0:T(8,128)(2,1)}, u32[]{:S(2)}, u32[]{:S(2)}) async-start(bf16[8,528,128]{2,1,0:T(8,128)(2,1)} %pad_maximum_fusion), calls=%async_computation.1 | async-start | bytes 2162688 | tf_op jit(solution)/shard_map/all_to_all | solution.py:445
  65.9 35.8 %copy-start.24 = (f32[2,128]{1,0:T(2,128)}, f32[2,128]{1,0:T(2,128)S(1)}, u32[]{:S(2)}) copy-start(f32[2,128]{1,0:T(2,128)S(1)} %pad_maximum_fusion.1.gain_ref.refs_4_) | copy-start | bytes 3076
  65.9 2.3 %collective-permute-start.5 = (bf16[64,3072]{1,0:T(8,128)(2,1)S(1)}, bf16[64,3072]{1,0:T(8,128)(2,1)S(1)}, u32[]{:S(2)}, u32[]{:S(2)}) collective-permute-start(bf16[64,3072]{1,0:T(8,128)(2,1)S(1)} %collective-permute-done.refs_2_), channel_id=1, source_target_pairs={{0,2},{2,0},{4,6},{6,4},{8,10},{10,8},{12,14},{14,12},{1,3},{3,1},... | collective-permute-start | bytes 1179656 | tf_op jit(solution)/shard_map/ppermute | solution.py:421
  66.5 2.7 %collective-permute-start.6 = (bf16[64,3072]{1,0:T(8,128)(2,1)S(1)}, bf16[64,3072]{1,0:T(8,128)(2,1)S(1)}, u32[]{:S(2)}, u32[]{:S(2)}) collective-permute-start(bf16[64,3072]{1,0:T(8,128)(2,1)S(1)} %collective-permute-done.4.refs_3_), channel_id=1, source_target_pairs={{0,2},{2,0},{4,6},{6,4},{8,10},{10,8},{12,14},{14,12},{1,3},{3,1},... | collective-permute-start | bytes 1179656 | tf_op jit(solution)/shard_map/ppermute | solution.py:421
  66.6 26.1 %collective-permute-start.15 = (bf16[8,384,128]{2,1,0:T(8,128)(2,1)}, bf16[8,384,128]{2,1,0:T(8,128)(2,1)S(1)}, u32[]{:S(2)}, u32[]{:S(2)}) collective-permute-start(bf16[8,384,128]{2,1,0:T(8,128)(2,1)} %all-to-all-done.mine), channel_id=1, source_target_pairs={{0,16},{16,0},{1,17},{17,1},{2,18},{18,2},{3,19},{19,3},{4,20},{20... | collective-permute-start | bytes 2359304 | tf_op jit(solution)/shard_map/ppermute | solution.py:436
  68.2 24.5 %copy-start.2 = (f32[1024,128]{1,0:T(8,128)S(1)}, f32[1024,128]{1,0:T(8,128)}, u32[]{:S(2)}) copy-start(f32[1024,128]{1,0:T(8,128)} %get-tuple-element.44.sin_ref.refs_3_) | copy-start | bytes 1572868
  73.3 12.1 %collective-permute-start.12 = (bf16[64,3072]{1,0:T(8,128)(2,1)S(1)}, bf16[64,3072]{1,0:T(8,128)(2,1)S(1)}, u32[]{:S(2)}, u32[]{:S(2)}) collective-permute-start(bf16[64,3072]{1,0:T(8,128)(2,1)S(1)} %broadcast_select_fusion.1.refs_4_), channel_id=1, source_target_pairs={{0,1},{1,0},{2,3},{3,2},{4,5},{5,4},{6,7},{7,6},{8,9},{9,8},{10,11... | collective-permute-start | bytes 1179656 | tf_op jit(solution)/shard_map/ppermute | solution.py:424
  74.8 17.9 %collective-permute-start.9 = (bf16[64,3072]{1,0:T(8,128)(2,1)S(1)}, bf16[64,3072]{1,0:T(8,128)(2,1)S(1)}, u32[]{:S(2)}, u32[]{:S(2)}) collective-permute-start(bf16[64,3072]{1,0:T(8,128)(2,1)S(1)} %broadcast_select_fusion.refs_0_), channel_id=1, source_target_pairs={{0,1},{1,0},{2,3},{3,2},{4,5},{5,4},{6,7},{7,6},{8,9},{9,8},{10,11... | collective-permute-start | bytes 1179656 | tf_op jit(solution)/shard_map/ppermute | solution.py:424
  75.3 24.8 %collective-permute-start.13 = (bf16[64,3072]{1,0:T(8,128)(2,1)S(1)}, bf16[64,3072]{1,0:T(8,128)(2,1)S(1)}, u32[]{:S(2)}, u32[]{:S(2)}) collective-permute-start(bf16[64,3072]{1,0:T(8,128)(2,1)S(1)} %broadcast_select_fusion.1.refs_4_), channel_id=1, source_target_pairs={{0,2},{2,0},{4,6},{6,4},{8,10},{10,8},{12,14},{14,12},{1,3},{3,1},... | collective-permute-start | bytes 1179656 | tf_op jit(solution)/shard_map/ppermute | solution.py:421
  75.3 24.8 %collective-permute-start.10 = (bf16[64,3072]{1,0:T(8,128)(2,1)S(1)}, bf16[64,3072]{1,0:T(8,128)(2,1)S(1)}, u32[]{:S(2)}, u32[]{:S(2)}) collective-permute-start(bf16[64,3072]{1,0:T(8,128)(2,1)S(1)} %broadcast_select_fusion.refs_0_), channel_id=1, source_target_pairs={{0,2},{2,0},{4,6},{6,4},{8,10},{10,8},{12,14},{14,12},{1,3},{3,1},... | collective-permute-start | bytes 1179656 | tf_op jit(solution)/shard_map/ppermute | solution.py:421
  85.3 14.8 %collective-permute-start.14 = (bf16[64,3072]{1,0:T(8,128)(2,1)S(1)}, bf16[64,3072]{1,0:T(8,128)(2,1)S(1)}, u32[]{:S(2)}, u32[]{:S(2)}) collective-permute-start(bf16[64,3072]{1,0:T(8,128)(2,1)S(1)} %collective-permute-done.12.refs_5_), channel_id=1, source_target_pairs={{0,2},{2,0},{4,6},{6,4},{8,10},{10,8},{12,14},{14,12},{1,3},{3,1},... | collective-permute-start | bytes 1179656 | tf_op jit(solution)/shard_map/ppermute | solution.py:421
  92.7 7.4 %collective-permute-start.11 = (bf16[64,3072]{1,0:T(8,128)(2,1)S(1)}, bf16[64,3072]{1,0:T(8,128)(2,1)S(1)}, u32[]{:S(2)}, u32[]{:S(2)}) collective-permute-start(bf16[64,3072]{1,0:T(8,128)(2,1)S(1)} %collective-permute-done.9.refs_1_), channel_id=1, source_target_pairs={{0,2},{2,0},{4,6},{6,4},{8,10},{10,8},{12,14},{14,12},{1,3},{3,1},... | collective-permute-start | bytes 1179656 | tf_op jit(solution)/shard_map/ppermute | solution.py:421
  96.2 21.5 %collective-permute-start.17 = (bf16[2,512,128]{2,1,0:T(8,128)(2,1)}, bf16[2,512,128]{2,1,0:T(8,128)(2,1)}, u32[]{:S(2)}, u32[]{:S(2)}) collective-permute-start(bf16[2,512,128]{2,1,0:T(8,128)(2,1)} %get-tuple-element.49.kva), channel_id=1, source_target_pairs={{0,16},{1,17},{2,18},{3,19},{4,20},{5,21},{6,22},{7,23},{8,24},{9,... | collective-permute-start | bytes 786440 | tf_op jit(solution)/shard_map/ppermute | solution.py:458
  103.4 15.4 %collective-permute-start.16 = (bf16[2,512,128]{2,1,0:T(8,128)(2,1)S(1)}, bf16[2,512,128]{2,1,0:T(8,128)(2,1)}, u32[]{:S(2)}, u32[]{:S(2)}) collective-permute-start(bf16[2,512,128]{2,1,0:T(8,128)(2,1)S(1)} %second_kv.1.kvb), channel_id=1, source_target_pairs={{0,16},{1,17},{2,18},{3,19},{4,20},{5,21},{6,22},{7,23},{8,24},{9,... | collective-permute-start | bytes 786440 | tf_op jit(solution)/shard_map/ppermute | solution.py:460
  135.8 10.8 %collective-permute-start.18 = (bf16[128,1536]{1,0:T(8,128)(2,1)}, bf16[128,1536]{1,0:T(8,128)(2,1)}, u32[]{:S(2)}, u32[]{:S(2)}) collective-permute-start(bf16[128,1536]{1,0:T(8,128)(2,1)} %out_sent.1), channel_id=1, source_target_pairs={{0,1},{1,0},{2,3},{3,2},{4,5},{5,4},{6,7},{7,6},{8,9},{9,8},{10,11... | collective-permute-start | bytes 1179656 | tf_op jit(solution)/shard_map/ppermute | solution.py:468
  (34 other events, 213.0 us)

commit v8 on v7

--- a/solution.py
+++ b/solution.py
@@ -8,7 +8,7 @@
 HEAD_DIM = 128
 GRID_W = 64
 TILE = 128
-VMEM_LIMIT = 20 * 1024 * 1024
+VMEM_LIMIT = 56 * 1024 * 1024
 
 
 def axis_freqs(width):
@@ -42,6 +42,7 @@
 
 VMEM = pl.BlockSpec(memory_space=pltpu.VMEM)
 SMEM = pl.BlockSpec(memory_space=pltpu.SMEM)
+ANY = pl.BlockSpec(memory_space=pl.ANY)
 
 
 def call(kernel, name, out_shape, flops, moved, exps, limit=VMEM_LIMIT, **spec):
@@ -55,7 +56,25 @@
     )
 
 
-def norm_kernel(tp_ref, image_ref, mods_ref, full_ref, part_ref):
+def started(pairs, sems, first=0):
+    copies = [pltpu.make_async_copy(s, d, sems.at[first + i]) for i, (s, d) in enumerate(pairs)]
+    for copy in copies:
+        copy.start()
+    return copies
+
+
+def finished(copies):
+    for copy in copies:
+        copy.wait()
+
+
+def norm_kernel(tp_ref, image_hbm, mods_hbm, full_ref, part_ref, image_ref, mods_ref, sems):
+    rows = image_ref.shape[0] // 4
+    pairs = [
+        (image_hbm.at[pl.ds(i * rows, rows), :], image_ref.at[pl.ds(i * rows, rows), :])
+        for i in range(4)
+    ]
+    finished(started(pairs + [(mods_hbm, mods_ref)], sems))
     mods = jnp.concatenate([mods_ref[0], mods_ref[1]], axis=0)
     normed = layer_norm(image_ref[...].astype(jnp.float32), mods)
     part = part_ref.shape[0]
@@ -78,9 +97,69 @@
             jax.ShapeDtypeStruct((rows // 2, depth), jnp.bfloat16),
         ],
         10 * rows * depth, 4 * rows * depth, 0,
-        in_specs=[SMEM, VMEM, VMEM],
+        in_specs=[SMEM, ANY, ANY],
         out_specs=[VMEM, VMEM],
+        scratch_shapes=[
+            pltpu.VMEM(image.shape, image.dtype),
+            pltpu.VMEM(mods.shape, mods.dtype),
+            pltpu.SemaphoreType.DMA((5,)),
+        ],
     )(tp, image, mods)
+
+
+def kv_weights_kernel(section_ref, w_ref, out_ref, sems):
+    heads, held, _ = out_ref.shape
+    half = held // 2
+    rows = pl.ds(pl.multiple_of(section_ref[0] * half, half), half)
+    finished(
+        started(
+            [
+                (
+                    w_ref.at[1 + kind, rows, pl.ds(s * HEAD_DIM, HEAD_DIM)],
+                    out_ref.at[s, pl.ds(kind * half, half), :],
+                )
+                for s in range(heads)
+                for kind in range(2)
+            ],
+            sems,
+        )
+    )
+
+
+def kv_weights(section, w):
+    _, depth, width = w.shape
+    shape = (width // HEAD_DIM, depth, HEAD_DIM)
+    return call(
+        kv_weights_kernel, "kv_weights", jax.ShapeDtypeStruct(shape, w.dtype),
+        0, 4 * depth * width, 0,
+        in_specs=[SMEM, ANY],
+        out_specs=ANY,
+        scratch_shapes=[pltpu.SemaphoreType.DMA((2 * shape[0],))],
+    )(section, w)
+
+
+def direct_kernel(w_ref, text_ref, mask_ref, out_ref, sems):
+    heads = out_ref.shape[0]
+    depth, count, last = w_ref.shape[1], text_ref.shape[1], mask_ref.shape[0]
+    pairs = []
+    for s in range(heads):
+        lanes = pl.ds(s * HEAD_DIM, HEAD_DIM)
+        pairs.append((w_ref.at[0, :, lanes], out_ref.at[s, pl.ds(0, depth), :]))
+        pairs.append((text_ref.at[s], out_ref.at[s, pl.ds(depth, count), :]))
+        pairs.append((mask_ref, out_ref.at[s, pl.ds(depth + count, last), :]))
+    finished(started(pairs, sems))
+
+
+def direct_rows(w, text, mask):
+    heads, count, _ = text.shape
+    shape = (heads, w.shape[1] + count + mask.shape[0], HEAD_DIM)
+    return call(
+        direct_kernel, "direct_rows", jax.ShapeDtypeStruct(shape, w.dtype),
+        0, 4 * heads * shape[1] * HEAD_DIM, 0,
+        in_specs=[ANY, ANY, ANY],
+        out_specs=ANY,
+        scratch_shapes=[pltpu.SemaphoreType.DMA((3 * heads,))],
+    )(w, text, mask)
 
 
 def normed_rotated(x, gain, cosine, sine):
@@ -90,38 +169,45 @@
     return (x * cosine + other * sine).astype(jnp.bfloat16)
 
 
-def copy_all(pairs, sems):
-    copies = [pltpu.make_async_copy(s, d, sems.at[i]) for i, (s, d) in enumerate(pairs)]
-    for copy in copies:
-        copy.start()
-    for copy in copies:
-        copy.wait()
-
-
-def pack_kernel(*refs):
-    x_refs, out_ref, sems = refs[:-2], refs[-2], refs[-1]
+def table_of(tabs_ref, which, start, rows):
+    groups = tabs_ref.shape[1] - GRID_W
+    columns = tabs_ref[which, groups:, :]
+    lane = lax.broadcasted_iota(jnp.int32, columns.shape, 1)
+    first = HEAD_DIM // 8
+    by_row = lane < first + (HEAD_DIM - first) // 2
+    return jnp.concatenate(
+        [
+            jnp.where(by_row, tabs_ref[which, g : g + 1, :], columns)
+            for g in range(start // GRID_W, (start + rows) // GRID_W)
+        ],
+        axis=0,
+    )
+
+
+def piece_copies(piece_refs, x_ref):
     at, pairs = 0, []
-    for ref in x_refs:
-        pairs.append((ref, out_ref.at[pl.ds(at, ref.shape[0]), :]))
+    for ref in piece_refs:
+        pairs.append((ref, x_ref.at[pl.ds(at, ref.shape[0]), :]))
         at += ref.shape[0]
-    copy_all(pairs, sems)
-
-
-def pack(pieces):
-    rows, depth = sum(p.shape[0] for p in pieces), pieces[0].shape[1]
-    return call(
-        pack_kernel, "pack_tokens", jax.ShapeDtypeStruct((rows, depth), jnp.bfloat16),
-        0, 4 * rows * depth, 0,
-        in_specs=[pl.BlockSpec(memory_space=pl.ANY)] * len(pieces),
-        out_specs=VMEM,
-        scratch_shapes=[pltpu.SemaphoreType.DMA((len(pieces),))],
-    )(*pieces)
-
-
-def first_kv_kernel(section_ref, x_ref, mine, peer, cos_ref, sin_ref, gain_ref, kv_ref, w_ref):
-    first = section_ref[0] == 0
+    return pairs
+
+
+def kv_kernel(chunk, section_ref, tabs_ref, gain_ref, mine_hbm, peer_a, peer_b, *refs):
+    piece_refs, (kv_ref, x_ref, mine, peer, w_ref, sems) = refs[:-6], refs[-6:]
     sources, held, _ = mine.shape
     half = held // 2
+    some = sources // 2
+    weights = started(
+        [
+            (mine_hbm, mine),
+            (peer_a, peer.at[pl.ds(0, some)]),
+            (peer_b, peer.at[pl.ds(some, some)]),
+        ],
+        sems,
+    )
+    tokens = started(piece_copies(piece_refs, x_ref), sems, 3)
+    finished(weights)
+    first = section_ref[0] == 0
     for s in range(sources):
         for kind in range(2):
             at = slice(kind * half, (kind + 1) * half)
@@ -129,41 +215,35 @@
             a, b = mine[s, at, :], peer[s, at, :]
             w_ref[2 * s * half : (2 * s + 1) * half, lanes] = jnp.where(first, a, b)
             w_ref[(2 * s + 1) * half : (2 * s + 2) * half, lanes] = jnp.where(first, b, a)
-    kv_kernel(0, x_ref, w_ref, cos_ref, sin_ref, gain_ref, kv_ref)
-
-
-def kv_kernel(chunk, x_ref, w_ref, cos_ref, sin_ref, gain_ref, kv_ref):
+    finished(tokens)
     both = jnp.dot(x_ref[...], w_ref[...], preferred_element_type=jnp.float32)
-    at = slice(chunk * x_ref.shape[0], (chunk + 1) * x_ref.shape[0])
+    rows = x_ref.shape[0]
     kv_ref[0] = normed_rotated(
-        both[:, :HEAD_DIM], gain_ref[1:2, :], cos_ref[at, :], sin_ref[at, :]
+        both[:, :HEAD_DIM],
+        gain_ref[1:2, :],
+        table_of(tabs_ref, 0, chunk * rows, rows),
+        table_of(tabs_ref, 1, chunk * rows, rows),
     )
     kv_ref[1] = both[:, HEAD_DIM:].astype(jnp.bfloat16)
 
 
-def first_kv(section, x, mine, peer, cosine, sine, gains):
-    rows, depth = x.shape
-    return call(
-        first_kv_kernel, "first_kv",
-        [
-            jax.ShapeDtypeStruct((2, rows, HEAD_DIM), jnp.bfloat16),
-            jax.ShapeDtypeStruct((depth, 2 * HEAD_DIM), jnp.bfloat16),
-        ],
-        4 * rows * depth * HEAD_DIM, 2 * (x.size + 4 * mine.size), 0,
-        in_specs=[SMEM] + [VMEM] * 6,
-        out_specs=[VMEM, VMEM],
-    )(section, x, mine, peer, cosine, sine, gains)
-
-
-def second_kv(x, w, cosine, sine, gains):
-    rows, depth = x.shape
-    return call(
-        lambda *refs: kv_kernel(1, *refs), "second_kv",
+def project_kv(chunk, section, tabs, gains, mine, peers, pieces):
+    depth = pieces[0].shape[1]
+    rows = sum(p.shape[0] for p in pieces)
+    return call(
+        lambda *refs: kv_kernel(chunk, *refs), "project_kv" + "ab"[chunk],
         jax.ShapeDtypeStruct((2, rows, HEAD_DIM), jnp.bfloat16),
-        4 * rows * depth * HEAD_DIM, 2 * (x.size + w.size), 0,
-        in_specs=[VMEM] * 5,
+        4 * rows * depth * HEAD_DIM, 2 * (rows * depth + 2 * mine.size), 0,
+        in_specs=[SMEM, VMEM, VMEM] + [ANY] * (3 + len(pieces)),
         out_specs=VMEM,
-    )(x, w, cosine, sine, gains)
+        scratch_shapes=[
+            pltpu.VMEM((rows, depth), jnp.bfloat16),
+            pltpu.VMEM(mine.shape, jnp.bfloat16),
+            pltpu.VMEM(mine.shape, jnp.bfloat16),
+            pltpu.VMEM((depth, 2 * HEAD_DIM), jnp.bfloat16),
+            pltpu.SemaphoreType.DMA((3 + len(pieces),)),
+        ],
+    )(section, tabs, gains, mine, *peers, *pieces)
 
 
 def weights_of(query, keys):
@@ -189,39 +269,50 @@
 BLOCK = 256
 
 
-def own_kernel(
-    xa, xb, direct, cos_ref, sin_ref, gain_ref, rows_ref, keys_ref, kva, kvb,
-    q_ref, num_ref, den_ref, keep_ref,
-):
-    depth = xa.shape[1]
+def own_kernel(tabs_ref, gain_ref, rows_ref, keys_ref, kva, kvb, direct_hbm, *refs):
+    piece_refs = refs[:-7]
+    q_ref, num_ref, den_ref, keep_ref, x_ref, direct, sems = refs[-7:]
+    rows, depth = x_ref.shape
     sources, held, _ = direct.shape
-    w = direct[:, : depth // sources, :].reshape(depth, HEAD_DIM)
-    count = (held - 16 - depth // sources) // 2
-    at = depth // sources
+    copies = started(
+        [(direct_hbm.at[s], direct.at[s]) for s in range(sources)]
+        + piece_copies(piece_refs, x_ref),
+        sems,
+    )
+    finished(copies)
+    wide = depth // sources
+    w = direct[:, :wide, :].reshape(depth, HEAD_DIM)
+    count = (held - 16 - wide) // 2
     text = (
-        direct[:, at : at + count, :].reshape(-1, HEAD_DIM),
-        direct[:, at + count : at + 2 * count, :].reshape(-1, HEAD_DIM),
-    )
-    for c, x_ref in enumerate((xa, xb)):
-        for b in range(x_ref.shape[0] // BLOCK):
-            start = c * x_ref.shape[0] + b * BLOCK
-            at = slice(start, start + BLOCK)
-            query = jnp.dot(
-                x_ref[b * BLOCK : (b + 1) * BLOCK, :], w, preferred_element_type=jnp.float32
-            )
-            query = normed_rotated(query, gain_ref[0:1, :], cos_ref[at, :], sin_ref[at, :])
-            q_ref[at, :] = query
-            num, den = 0.0, 0.0
-            for keys, values in ((kva[0], kva[1]), (kvb[0], kvb[1]), text):
-                more = summed(weights_of(query, keys), values)
-                num, den = num + more[0], den + more[1]
-            num_ref[at, :] = num
-            den_ref[at, :] = jnp.broadcast_to(den, num.shape)
+        direct[:, wide : wide + count, :].reshape(-1, HEAD_DIM),
+        direct[:, wide + count : wide + 2 * count, :].reshape(-1, HEAD_DIM),
+    )
+    for b in range(rows // BLOCK):
+        at = slice(b * BLOCK, (b + 1) * BLOCK)
+        query = jnp.dot(x_ref[at, :], w, preferred_element_type=jnp.float32)
+        query = normed_rotated(
+            query,
+            gain_ref[0:1, :],
+            table_of(tabs_ref, 0, b * BLOCK, BLOCK),
+            table_of(tabs_ref, 1, b * BLOCK, BLOCK),
+        )
+        q_ref[at, :] = query
+        num, den = 0.0, 0.0
+        for keys, values in ((kva[0], kva[1]), (kvb[0], kvb[1]), text):
+            more = summed(weights_of(query, keys), values)
+            num, den = num + more[0], den + more[1]
+        num_ref[at, :] = num
+        den_ref[at, :] = jnp.broadcast_to(den, num.shape)
     mask = jnp.concatenate(
         [direct[s, held - 16 : held, :].astype(jnp.float32)[:1] for s in range(sources)], axis=0
     )
     mask = jnp.dot(rows_ref[...], mask, preferred_element_type=jnp.float32)
-    keep_ref[...] = jnp.dot(mask, keys_ref[...], preferred_element_type=jnp.float32)
+    mask = jnp.dot(mask, keys_ref[...], preferred_element_type=jnp.float32)
+    size = rows // keep_ref.shape[0]
+    for g in range(keep_ref.shape[0]):
+        keep_ref[:, g * size : (g + 1) * size] = jnp.broadcast_to(
+            mask[:, g : g + 1], (keep_ref.shape[0], size)
+        )
 
 
 def cond_sum(keep_ref, q_ref, cond, chunk, b):
@@ -271,9 +362,10 @@
             store(b, num_ref[at, :] + num, den_ref[at, :] + den)
 
 
-def attend_own(xs, direct, cosine, sine, gains, row_tiles, key_tiles, kvs):
-    rows, depth = 2 * xs[0].shape[0], xs[0].shape[1]
-    keys = rows + 512
+def attend_own(tabs, gains, row_tiles, key_tiles, kvs, direct, pieces):
+    depth = pieces[0].shape[1]
+    rows = sum(p.shape[0] for p in pieces)
+    keys = rows + rows // 2
     return call(
         own_kernel, "attend_own",
         [
@@ -283,9 +375,14 @@
             jax.ShapeDtypeStruct((row_tiles.shape[0], rows), jnp.float32),
         ],
         2 * rows * HEAD_DIM * (2 * keys + depth), 2 * rows * depth, rows * keys,
-        in_specs=[VMEM] * 10,
+        in_specs=[VMEM] * 6 + [ANY] * (1 + len(pieces)),
         out_specs=[VMEM] * 4,
-    )(*xs, direct, cosine, sine, gains, row_tiles, key_tiles, *kvs)
+        scratch_shapes=[
+            pltpu.VMEM((rows, depth), jnp.bfloat16),
+            pltpu.VMEM(direct.shape, jnp.bfloat16),
+            pltpu.SemaphoreType.DMA((direct.shape[0] + len(pieces),)),
+        ],
+    )(tabs, gains, row_tiles, key_tiles, *kvs, direct, *pieces)
 
 
 def attend_first(section, keep, query, cond, num, den):
@@ -313,60 +410,57 @@
     return jnp.concatenate([attn_ref[h] for h in range(attn_ref.shape[0])], axis=1)
 
 
-def load_kernel(half_ref, w_ref, sent_ref, kept_ref, sems):
-    width = sent_ref.shape[1]
-    pairs = []
-    for half, out_ref in ((1 - half_ref[0], sent_ref), (half_ref[0], kept_ref)):
-        columns = pl.ds(pl.multiple_of(half * width, width), width)
-        pairs.append((w_ref.at[:, columns], out_ref))
-    copy_all(pairs, sems)
-
-
-def load_out(half, w_out):
-    shape = jax.ShapeDtypeStruct((w_out.shape[0], w_out.shape[1] // 2), w_out.dtype)
-    return call(
-        load_kernel, "load_out", [shape] * 2, 0, 4 * w_out.size, 0,
-        in_specs=[SMEM, pl.BlockSpec(memory_space=pl.ANY)],
-        out_specs=[VMEM, VMEM],
-        scratch_shapes=[pltpu.SemaphoreType.DMA((2,))],
-    )(half, w_out)
-
-
-def sent_kernel(attn_ref, w_ref, out_ref):
-    branch = jnp.dot(token_rows(attn_ref), w_ref[...], preferred_element_type=jnp.float32)
+def product(half, attn_ref, w_hbm, w_ref, sems):
+    depth, width = w_ref.shape
+    rows = depth // sems.shape[0]
+    columns = pl.ds(pl.multiple_of(half * width, width), width)
+    finished(
+        started(
+            [
+                (w_hbm.at[pl.ds(i * rows, rows), columns], w_ref.at[pl.ds(i * rows, rows), :])
+                for i in range(sems.shape[0])
+            ],
+            sems,
+        )
+    )
+    return jnp.dot(token_rows(attn_ref), w_ref[...], preferred_element_type=jnp.float32)
+
+
+def sent_kernel(half_ref, attn_ref, w_hbm, out_ref, w_ref, sems):
+    branch = product(1 - half_ref[0], attn_ref, w_hbm, w_ref, sems)
     out_ref[...] = branch.astype(jnp.bfloat16)
 
 
-def kept_kernel(attn_ref, w_ref, image_ref, gate_ref, out_ref):
-    branch = jnp.dot(token_rows(attn_ref), w_ref[...], preferred_element_type=jnp.float32)
+def kept_kernel(half_ref, attn_ref, w_hbm, image_ref, gate_ref, out_ref, w_ref, sems):
+    branch = product(half_ref[0], attn_ref, w_hbm, w_ref, sems)
     out_ref[...] = image_ref[...].astype(jnp.float32) + gate_ref[...] * branch
 
 
-def project_out(attn, w, image=None, gate=None):
+def project_out(half, attn, w, image=None, gate=None):
     rows = attn.shape[1]
-    depth, width = w.shape
+    depth, width = w.shape[0], w.shape[1] // 2
     kept = image is not None
-    args = (attn, w) + ((image, gate) if kept else ())
+    more = (image, gate) if kept else ()
     return call(
         kept_kernel if kept else sent_kernel, "out_kept" if kept else "out_sent",
         jax.ShapeDtypeStruct((rows, width), jnp.float32 if kept else jnp.bfloat16),
         2 * rows * depth * width, 2 * depth * width, 0,
-        in_specs=[VMEM] * len(args),
+        in_specs=[SMEM, VMEM, ANY] + [VMEM] * len(more),
         out_specs=VMEM,
-    )(*args)
-
-
-def lane_tables(rows_index, time_index):
+        scratch_shapes=[pltpu.VMEM((depth, width), w.dtype), pltpu.SemaphoreType.DMA((8,))],
+    )(half, attn, w, *more)
+
+
+def lane_tables(row_ids, time_index):
     first = HEAD_DIM // 8
     rest = (HEAD_DIM - first) // 2
     freqs = jnp.concatenate([axis_freqs(first), axis_freqs(rest), axis_freqs(rest)])
     freqs = jnp.repeat(freqs, 2)[None]
     lane = jnp.arange(HEAD_DIM, dtype=jnp.int32)[None]
-    row_pos = (rows_index // GRID_W).astype(jnp.float32)[:, None]
-    col_pos = (rows_index % GRID_W).astype(jnp.float32)[:, None]
-    ids = jnp.where(lane < first, time_index, jnp.where(lane < first + rest, row_pos, col_pos))
-    angles = ids * freqs
-    return jnp.cos(angles), jnp.sin(angles) * jnp.where(lane % 2 == 0, -1.0, 1.0)
+    rows = jnp.where(lane < first, time_index, row_ids.astype(jnp.float32)[:, None])
+    columns = jnp.broadcast_to(jnp.arange(GRID_W, dtype=jnp.float32)[:, None], (GRID_W, HEAD_DIM))
+    angles = jnp.concatenate([rows, columns], axis=0) * freqs
+    return jnp.stack([jnp.cos(angles), jnp.sin(angles) * jnp.where(lane % 2 == 0, -1.0, 1.0)])
 
 
 def z_pairs(seq, pairs):
@@ -393,24 +487,16 @@
     parts = parts[None, None, :] + 0 * shards
     shards, parts = shards.reshape(-1).astype(jnp.int32), parts.reshape(-1).astype(jnp.int32)
     size = img_rows // 2
-    first_row = shards * img_rows + parts * size
-    rows_index = (first_row[:, None] + jnp.arange(size, dtype=jnp.int32)[None]).reshape(-1)
-    cosine, sine = lane_tables(rows_index, (section == 0).astype(jnp.float32))
+    row_ids = shards * (img_rows // GRID_W) + parts * (size // GRID_W)
+    tabs = lane_tables(row_ids, (section == 0).astype(jnp.float32))
     gains = jnp.stack([q_gain, k_gain])
     row_tiles = (shards[:, None] == jnp.arange(seq)[None]).astype(jnp.float32)
-    key_tiles = jnp.arange(HEAD_DIM)[:, None] == jnp.repeat(shards, size)[None]
+    key_tiles = jnp.arange(HEAD_DIM)[:, None] == shards[None]
     key_tiles = key_tiles.astype(jnp.float32)
     place = jnp.stack([shards, parts])
 
     rows3 = w_qkv.transpose(1, 0, 2)
-    half = depth // 2
-
-    def for_heads(rows):
-        rows = rows.reshape(rows.shape[0], -1, seq, HEAD_DIM).transpose(2, 0, 1, 3)
-        return rows.reshape(seq, -1, HEAD_DIM)
-
-    mine = for_heads(lax.dynamic_slice_in_dim(rows3[1:], section * half, half, 1))
-    mine = lax.all_to_all(mine, "seq", 0, 0)
+    mine = lax.all_to_all(kv_weights(section_at, rows3), "seq", 0, 0)
 
     full, part = norm_tokens(tp_at, image[0], modulation.transpose(1, 0, 2))
 
@@ -420,9 +506,8 @@
     def to_core(x):
         return lax.ppermute(x, "seq", [(s, s ^ 1) for s in range(seq)])
 
-    def shared(came):
-        passed = lax.ppermute(came, "tp", both)
-        return [came, passed, to_core(came), to_core(passed)]
+    def to_tp(x):
+        return lax.ppermute(x, "tp", both)
 
     near = along_z(part, [(0, 1), (1, 0), (2, 3), (3, 2)])
     middle = along_z(part, [(1, 2), (2, 1)])
@@ -431,42 +516,46 @@
     far_end = along_z(far, [(1, 0), (2, 3)])
     inner = (chip == 1) | (chip == 2)
     third = jnp.where(inner, middle, middle_end)
-    x_a = pack([full, to_core(full)] + shared(near))
-    third, mine = lax.optimization_barrier((third, mine))
-    peer = lax.ppermute(mine, "section", both)
+    fourth = jnp.where(inner, far, far_end)
 
     text = text_kv[0].reshape(-1, 2, seq, HEAD_DIM).transpose(2, 1, 0, 3).reshape(seq, -1, HEAD_DIM)
     mask = jnp.pad(
         region_mask.astype(jnp.bfloat16), ((0, 15), (0, HEAD_DIM - region_mask.shape[1]))
     )
-    mask = jnp.broadcast_to(mask, (seq,) + mask.shape)
-    direct = jnp.concatenate([for_heads(rows3[:1]), text, mask], axis=1)
+    direct = direct_rows(rows3, text, mask)
+
+    near_tp = to_tp(near)
+    third, near_tp, mine = lax.optimization_barrier((third, near_tp, mine))
+    third_tp = to_tp(third)
+    some = seq // 2
+    peers = [lax.ppermute(mine[:some], "section", both), lax.ppermute(mine[some:], "section", both)]
     direct, mine = lax.optimization_barrier((direct, mine))
     direct = lax.all_to_all(direct, "seq", 0, 0)
-
-    fourth = jnp.where(inner, far, far_end)
-    w_sent, w_kept = load_out(tp_at, w_out)
-    cols = w_sent.shape[1]
+    cols = w_out.shape[1] // 2
     gate = lax.dynamic_slice_in_dim(mods[2:3], tp * cols, cols, 1)
     residual = lax.dynamic_slice_in_dim(image[0], tp * cols, cols, 1)
-    early = (cosine, sine, gains, row_tiles, key_tiles, place, gate, residual, w_sent, w_kept, x_a)
-    fourth, early = lax.optimization_barrier((fourth, early))
-    cosine, sine, gains, row_tiles, key_tiles, place, gate, residual, w_sent, w_kept, x_a = early
-    x_b = pack(shared(third) + shared(fourth))
-
-    kv_a, w_kv = first_kv(section_at, x_a, mine, peer, cosine, sine, gains)
+    early = (tabs, gains, row_tiles, key_tiles, place, gate, residual)
+    fourth, third_tp, peers[0], early = lax.optimization_barrier((fourth, third_tp, peers[0], early))
+    tabs, gains, row_tiles, key_tiles, place, gate, residual = early
+    fourth_tp = to_tp(fourth)
+    fourth, fourth_tp, peers[1] = lax.optimization_barrier((fourth, fourth_tp, peers[1]))
+    a = [full, to_core(full), near, near_tp, to_core(near), to_core(near_tp)]
+    b = [third, third_tp, to_core(third), to_core(third_tp)]
+    b += [fourth, fourth_tp, to_core(fourth), to_core(fourth_tp)]
+
+    kv_a = project_kv(0, section_at, tabs, gains, mine, peers, a)
     cond_a = lax.ppermute(kv_a, "section", [(0, 1)])
-    kv_b = second_kv(x_b, w_kv, cosine, sine, gains)
+    kv_b = project_kv(1, section_at, tabs, gains, mine, peers, b)
     cond_b = lax.ppermute(kv_b, "section", [(0, 1)])
     query, num, den, keep = attend_own(
-        (x_a, x_b), direct, cosine, sine, gains, row_tiles, key_tiles, (kv_a, kv_b)
+        tabs, gains, row_tiles, key_tiles, (kv_a, kv_b), direct, a + b
     )
     num, den = attend_first(section_at, keep, query, cond_a, num, den)
     attn = attend_second(section_at, place, keep, query, cond_b, num, den, seq)
 
     attn = lax.all_to_all(attn, "seq", 0, 0)
-    other = lax.ppermute(project_out(attn, w_sent), "tp", both)
-    kept = project_out(attn, w_kept, residual, gate)
+    other = to_tp(project_out(tp_at, attn, w_out))
+    kept = project_out(tp_at, attn, w_out, residual, gate)
     return (kept + gate * other.astype(jnp.float32)).astype(jnp.bfloat16)[None]
 
 
@@ -563,7 +652,7 @@
         and lax.axis_size("section") == 2
         and lax.axis_size("tp") == 2
         and w_qkv.shape[0] % 128 == 0
-        and image.shape[1] == TILE
+        and image.shape[1] == TILE == 2 * GRID_W
         and region_mask.shape == (1, seq)
         and arrays[1].shape[1] % 16 == 0
         and arrays[4].shape[1] % 1024 == 0

time: 150 us -> 194 us (1.29)
  Pallas kernels: 19.6 us -> 96.9 us
  local copies, waits for them, and re-layouts: 37.5 us -> 10 us
  other arithmetic: 11.6 us -> 7.83 us
  waiting for transfers between devices: 30.7 us -> 28.6 us
    pallas_call x5 -> x4, Pallas kernels: 8.19 us -> 69.9 us  [the longest x1 34.1 us: direct_rows(): call(direct_kernel, 'direct_rows', jax.ShapeDtypeStruct(shape, w.dtype),...]
    unnamed x75 -> x48, local copies, waits for them, and re-layouts: 23.3 us -> 5.25 us
    pallas_call x2, Pallas kernels: 1.91 us -> 8.62 us  [project_out(): call(kept_kernel if kept else sent_kernel, 'out_kept' if kept else 'out_s...]
    ppermute x5, waiting for transfers between devices: 6.19 us -> 0.01 us  [along_z(): return lax.ppermute(x, 'seq', z_pairs(seq, pairs))]
    pallas_call x1, Pallas kernels: 6.54 us -> 10.6 us  [attend_own(): call(own_kernel, 'attend_own', [jax.ShapeDtypeStruct((rows, HEAD_DIM), jn...]
    ppermute x5 -> x6, waiting for transfers between devices: 24.5 us -> 28.6 us  [the longest x4 16.2 us: to_tp(): return lax.ppermute(x, 'tp', both)]
    slice x2 -> x1, local copies, waits for them, and re-layouts: 3.94 us -> 0.05 us  [head_body(): mine[some:]]
    mul x2 -> x0, other arithmetic: 3.78 us -> none  [the longest x1 3.18 us: lane_tables(): jnp.sin(angles) * jnp.where(lane % 2 == 0, -1.0, 1.0)]
  transfers between devices with their start and end apart: 21 -> 22, of which waited for: 5 -> 6; matrix products, arithmetic and copies ran while one was open for 19% -> 6% of each run, Pallas kernels for 11% -> 45%
where the time goes in v8:
time: 194 us; the launch traced here: 193 us
  Pallas kernels  96.9 us (50%)
  starting transfers between devices  35.2 us (18%)
  waiting for transfers between devices  28.6 us (15%)
  blocking collectives  14.2 us (7%)
  local copies, waits for them, and re-layouts  10 us (5%)
  other arithmetic  7.83 us (4%)
    pallas_call x1, Pallas kernels, direct_rows(): call(direct_kernel, 'direct_rows', jax.ShapeDtypeStruct(shape, w.dtype),...  34.1 us
    pallas_call x1, Pallas kernels, kv_weights(): call(kv_weights_kernel, 'kv_weights', jax.ShapeDtypeStruct(shape, w.dtype...  25.1 us
    ppermute x4, waiting for transfers between devices, to_tp(): return lax.ppermute(x, 'tp', both)  16.2 us
    all_to_all x1, blocking collectives, head_body(): attn = lax.all_to_all(attn, 'seq', 0, 0)  14.2 us
    pallas_call x2, Pallas kernels, project_kv(): call(lambda *refs: kv_kernel(chunk, *refs), 'project_kv' + 'ab'[chunk], j...  10.8 us
    pallas_call x1, Pallas kernels, attend_own(): call(own_kernel, 'attend_own', [jax.ShapeDtypeStruct((rows, HEAD_DIM), jn...  10.6 us
    ppermute x5, starting transfers between devices, along_z(): return lax.ppermute(x, 'seq', z_pairs(seq, pairs))  10.6 us
    pallas_call x2, Pallas kernels, project_out(): call(kept_kernel if kept else sent_kernel, 'out_kept' if kept else 'out_s...  8.62 us
  transfers between devices with their start and end apart: 22, of which 6 were waited for; matrix products, arithmetic and copies ran while one was open for 6% of the time, Pallas kernels for 45%

profile of v8, /device:TPU:0, one launch (start us, length us, event | category | flops | bytes accessed | tf_op | source)
XLA Modules:
  0.0 193.1 jit_solution(9049007939315273558)
XLA Ops:
  0.0 2.9 %norm_tokens.1 = (bf16[128,3072]{1,0:T(8,128)(2,1)}, bf16[64,3072]{1,0:T(8,128)(2,1)}) custom-call(s32[1]{0:T(128)} %bitcast.tp_ref.half_ref, bf16[128,3072]{1,0:T(8,128)(2,1)} %bitcast.27, f32[3,1,3072]{2,1,0:T(1,128)} %bitcast.29), custom_call_target="tpu_custom_call" | custom-call | flops 3932160 | bytes 1572864 | tf_op jit(solution)/shard_map/norm_tokens/pallas_call | solution.py:93
  3.6 5.9 %collective-permute-start = (bf16[64,3072]{1,0:T(8,128)(2,1)}, bf16[64,3072]{1,0:T(8,128)(2,1)S(1)}, u32[]{:S(2)}, u32[]{:S(2)}) collective-permute-start(bf16[64,3072]{1,0:T(8,128)(2,1)} %get-tuple-element.31), channel_id=1, source_target_pairs={{0,4},{2,6},{4,0},{6,2},{8,12},{10,14},{12,8},{14,10},{1,5},{3,7},... | collective-permute-start | bytes 1179656 | tf_op jit(solution)/shard_map/ppermute | solution.py:504
  9.5 25.1 %kv_weights.1 = bf16[8,384,128]{2,1,0:T(8,128)(2,1)} custom-call(s32[1]{0:T(128)} %bitcast.1.section_ref.refs_0_, bf16[3,384,1024]{2,1,0:T(8,128)(2,1)} %bitcast.25), custom_call_target="tpu_custom_call" | custom-call | bytes 1572864 | tf_op jit(solution)/shard_map/kv_weights/pallas_call | solution.py:132
  34.6 3.6 %all-to-all-start = ((bf16[8,384,128]{2,1,0:T(8,128)(2,1)}), bf16[8,384,128]{2,1,0:T(8,128)(2,1)S(1)}, u32[]{:S(2)}, u32[]{:S(2)}) async-start(bf16[8,384,128]{2,1,0:T(8,128)(2,1)} %kv_weights.1), calls=%async_computation | async-start | bytes 1572864 | tf_op jit(solution)/shard_map/all_to_all | solution.py:499
  48.4 34.1 %direct_rows.1 = bf16[8,528,128]{2,1,0:T(8,128)(2,1)} custom-call(bf16[3,384,1024]{2,1,0:T(8,128)(2,1)} %bitcast.26, bf16[8,128,128]{2,1,0:T(8,128)(2,1)} %bitcast.28, bf16[16,128]{1,0:T(8,128)(2,1)} %pad.4.mask_ref), custom_call_target="tpu_custom_call" | custom-call | bytes 2162688 | tf_op jit(solution)/shard_map/direct_rows/pallas_call | solution.py:156
  87.8 7.4 %collective-permute-done.5.refs_9_.refs_3_ = bf16[64,3072]{1,0:T(8,128)(2,1)} collective-permute-done((bf16[64,3072]{1,0:T(8,128)(2,1)S(1)}, bf16[64,3072]{1,0:T(8,128)(2,1)}, u32[]{:S(2)}, u32[]{:S(2)}) %collective-permute-start.5) | collective-permute-done | bytes 393248 | tf_op jit(solution)/shard_map/ppermute | solution.py:510
  95.2 7.4 %all-to-all-start.1 = ((bf16[8,528,128]{2,1,0:T(8,128)(2,1)}), bf16[8,528,128]{2,1,0:T(8,128)(2,1)S(1)}, u32[]{:S(2)}, u32[]{:S(2)}) async-start(bf16[8,528,128]{2,1,0:T(8,128)(2,1)} %direct_rows.1), calls=%async_computation.1 | async-start | bytes 2162688 | tf_op jit(solution)/shard_map/all_to_all | solution.py:533
  102.7 1.6 collective-permute-start.7
  104.2 1.5 collective-permute-start.6
  107.4 7.2 %collective-permute-done.7.refs_4_ = bf16[4,384,128]{2,1,0:T(8,128)(2,1)S(1)} collective-permute-done((bf16[4,384,128]{2,1,0:T(8,128)(2,1)S(1)}, bf16[4,384,128]{2,1,0:T(8,128)(2,1)S(1)}, u32[]{:S(2)}, u32[]{:S(2)}) %collective-permute-start.7) | collective-permute-done | bytes 393248 | tf_op jit(solution)/shard_map/ppermute | solution.py:531
  117.5 5.2 %collective-permute-done.9.refs_5_ = bf16[4,384,128]{2,1,0:T(8,128)(2,1)S(1)} collective-permute-done((bf16[4,384,128]{2,1,0:T(8,128)(2,1)S(1)}, bf16[4,384,128]{2,1,0:T(8,128)(2,1)S(1)}, u32[]{:S(2)}, u32[]{:S(2)}) %collective-permute-start.9) | collective-permute-done | bytes 393248 | tf_op jit(solution)/shard_map/ppermute | solution.py:531
  122.7 3.2 %collective-permute-done.8.refs_11_ = bf16[64,3072]{1,0:T(8,128)(2,1)S(1)} collective-permute-done((bf16[64,3072]{1,0:T(8,128)(2,1)S(1)}, bf16[64,3072]{1,0:T(8,128)(2,1)S(1)}, u32[]{:S(2)}, u32[]{:S(2)}) %collective-permute-start.8) | collective-permute-done | bytes 393248 | tf_op jit(solution)/shard_map/ppermute | solution.py:510
  127.5 5.4 %project_kva.1.kva = bf16[2,512,128]{2,1,0:T(8,128)(2,1)} custom-call(s32[1]{0:T(128)} %bitcast.1.section_ref.refs_0_, f32[2,80,128]{2,1,0:T(8,128)} %pad_maximum_fusion.refs_1_.tabs_ref, f32[2,128]{1,0:T(2,128)} %pad_maximum_fusion.1.refs_2_.gain_ref, bf16[8,384,128]{2,1,0:T(8,128)(2,1)} %copy-done, bf16[4,384,128]{2,1,0:T(8,128)(2,1)} %copy-done.15, ...), custom_call_target="tpu_custom_call" | custom-call | flops 805306368 | bytes 4718592 | tf_op jit(solution)/shard_map/project_kva/pallas_call | solution.py:233
  132.9 2.6 %collective-permute-start.18 = (bf16[2,512,128]{2,1,0:T(8,128)(2,1)}, bf16[2,512,128]{2,1,0:T(8,128)(2,1)S(1)}, u32[]{:S(2)}, u32[]{:S(2)}) collective-permute-start(bf16[2,512,128]{2,1,0:T(8,128)(2,1)} %project_kva.1.kva), channel_id=1, source_target_pairs={{0,16},{1,17},{2,18},{3,19},{4,20},{5,21},{6,22},{7,23},{8,24},{9,... | collective-permute-start | bytes 786440 | tf_op jit(solution)/shard_map/ppermute | solution.py:547
  137.4 5.4 %project_kvb.1.kvb = bf16[2,512,128]{2,1,0:T(8,128)(2,1)} custom-call(s32[1]{0:T(128)} %bitcast.1.section_ref.refs_0_, f32[2,80,128]{2,1,0:T(8,128)} %pad_maximum_fusion.refs_1_.tabs_ref, f32[2,128]{1,0:T(2,128)} %pad_maximum_fusion.1.refs_2_.gain_ref, bf16[8,384,128]{2,1,0:T(8,128)(2,1)} %copy-done, bf16[4,384,128]{2,1,0:T(8,128)(2,1)} %copy-done.15, ...), custom_call_target="tpu_custom_call" | custom-call | flops 805306368 | bytes 4718592 | tf_op jit(solution)/shard_map/project_kvb/pallas_call | solution.py:233
  145.1 10.6 %attend_own.1 = (bf16[1024,128]{1,0:T(8,128)(2,1)}, f32[1024,128]{1,0:T(8,128)}, f32[1024,128]{1,0:T(8,128)}, f32[16,1024]{1,0:T(8,128)}) custom-call(f32[2,80,128]{2,1,0:T(8,128)} %pad_maximum_fusion.refs_1_.tabs_ref, f32[2,128]{1,0:T(2,128)} %pad_maximum_fusion.1.refs_2_.gain_ref, f32[16,8]{1,0:T(8,128)} %fusion.3.rows_ref, f32[128,16]{1,0:T(8,128)} %fusion.1.keys_ref, ...), custom_call_target="tpu_custom_call" | custom-call | flops 1610612736 | bytes 6291456 | tf_op jit(solution)/shard_map/attend_own/pallas_call | solution.py:369
  156.5 2.6 %attend_first.1 = (f32[1024,128]{1,0:T(8,128)}, f32[1024,128]{1,0:T(8,128)}) custom-call(s32[1]{0:T(128)} %bitcast.1.section_ref.refs_0_, f32[16,1024]{1,0:T(8,128)} %get-tuple-element.49.keep_ref, bf16[1024,128]{1,0:T(8,128)(2,1)} %get-tuple-element.50.q_ref, bf16[2,512,128]{2,1,0:T(8,128)(2,1)} %copy-done.18, f32[1024,128]{1,0:T(8,128)} %get-tuple-element.51.num_in, ...), custom_call_target="tpu_custom_call" | custom-call | flops 268435456 | bytes 2097152 | tf_op jit(solution)/shard_map/attend_first/pallas_call | solution.py:390
  159.8 2.2 %attend_second.1 = bf16[8,128,128]{2,1,0:T(8,128)(2,1)} custom-call(s32[1]{0:T(128)} %bitcast.1.section_ref.refs_0_, s32[2,16]{1,0:T(2,128)} %pad_add_fusion.place_ref, f32[16,1024]{1,0:T(8,128)} %get-tuple-element.49.keep_ref, bf16[1024,128]{1,0:T(8,128)(2,1)} %get-tuple-element.50.q_ref, bf16[2,512,128]{2,1,0:T(8,128)(2,1)} %copy-done.19, ...), custom_call_target="tpu_custom_call" | custom-call | flops 268435456 | bytes 2097152 | tf_op jit(solution)/shard_map/attend_second/pallas_call | solution.py:400
  162.0 14.2 %all_to_all.15.attn_ref = bf16[8,128,128]{2,1,0:T(8,128)(2,1)} all-to-all(bf16[8,128,128]{2,1,0:T(8,128)(2,1)} %attend_second.1), channel_id=1, replica_groups=mesh['section'=2,'seq'=8,'tp'=2] {'seq'}, dimensions={0} | all-to-all | bytes 524288 | tf_op jit(solution)/shard_map/all_to_all | solution.py:556
  176.2 4.2 %out_sent.1 = bf16[128,1536]{1,0:T(8,128)(2,1)} custom-call(s32[1]{0:T(128)} %bitcast.tp_ref.half_ref, bf16[8,128,128]{2,1,0:T(8,128)(2,1)} %all_to_all.15.attn_ref, bf16[1024,3072]{1,0:T(8,128)(2,1)} %w_hbm.3), custom_call_target="tpu_custom_call" | custom-call | flops 402653184 | bytes 3145728 | tf_op jit(solution)/shard_map/out_sent/pallas_call | solution.py:444
  180.4 1.6 collective-permute-start.19
  181.9 4.4 %out_kept.1 = f32[128,1536]{1,0:T(8,128)} custom-call(s32[1]{0:T(128)} %bitcast.tp_ref.half_ref, bf16[8,128,128]{2,1,0:T(8,128)(2,1)} %all_to_all.15.attn_ref, bf16[1024,3072]{1,0:T(8,128)(2,1)} %w_hbm.3, bf16[128,1536]{1,0:T(8,128)(2,1)} %dynamic-slice_bitcast_fusion.image_ref, f32[1,1536]{1,0:T(1,128)} %copy-done.20), custom_call_target="tpu_custom_call" | custom-call | flops 402653184 | bytes 3145728 | tf_op jit(solution)/shard_map/out_kept/pallas_call | solution.py:444
  186.4 4.7 %collective-permute-done.19 = bf16[128,1536]{1,0:T(8,128)(2,1)S(1)} collective-permute-done((bf16[128,1536]{1,0:T(8,128)(2,1)}, bf16[128,1536]{1,0:T(8,128)(2,1)S(1)}, u32[]{:S(2)}, u32[]{:S(2)}) %collective-permute-start.19) | collective-permute-done | bytes 393248 | tf_op jit(solution)/shard_map/ppermute | solution.py:510
  191.1 2.0 %fusion = bf16[1,128,1536]{2,1,0:T(8,128)(2,1)} fusion(f32[128,1536]{1,0:T(8,128)} %out_kept.1, bf16[128,1536]{1,0:T(8,128)(2,1)S(1)} %collective-permute-done.19, f32[1536]{0:T(1024)S(1)} %reduce), kind=kLoop, calls=%fused_computation.1 | loop fusion | flops 786432 | bytes 1579008 | tf_op jit(solution)/shard_map/broadcast_in_dim | solution.py:559
  (117 shorter events, 27.8 us)
Async XLA Ops:
  2.9 39.6 %collective-permute-start.3 = (bf16[64,3072]{1,0:T(8,128)(2,1)}, bf16[64,3072]{1,0:T(8,128)(2,1)S(1)}, u32[]{:S(2)}, u32[]{:S(2)}) collective-permute-start(bf16[64,3072]{1,0:T(8,128)(2,1)} %get-tuple-element.31), channel_id=1, source_target_pairs={{4,8},{6,10},{8,4},{10,6},{5,9},{7,11},{9,5},{11,7},{20,24},{22,26... | collective-permute-start | bytes 1179656 | tf_op jit(solution)/shard_map/ppermute | solution.py:504
  3.6 40.2 %collective-permute-start = (bf16[64,3072]{1,0:T(8,128)(2,1)}, bf16[64,3072]{1,0:T(8,128)(2,1)S(1)}, u32[]{:S(2)}, u32[]{:S(2)}) collective-permute-start(bf16[64,3072]{1,0:T(8,128)(2,1)} %get-tuple-element.31), channel_id=1, source_target_pairs={{0,4},{2,6},{4,0},{6,2},{8,12},{10,14},{12,8},{14,10},{1,5},{3,7},... | collective-permute-start | bytes 1179656 | tf_op jit(solution)/shard_map/ppermute | solution.py:504
  34.6 60.6 %all-to-all-start = ((bf16[8,384,128]{2,1,0:T(8,128)(2,1)}), bf16[8,384,128]{2,1,0:T(8,128)(2,1)S(1)}, u32[]{:S(2)}, u32[]{:S(2)}) async-start(bf16[8,384,128]{2,1,0:T(8,128)(2,1)} %kv_weights.1), calls=%async_computation | async-start | bytes 1572864 | tf_op jit(solution)/shard_map/all_to_all | solution.py:499
  38.2 88.3 %collective-permute-start.10 = (bf16[128,3072]{1,0:T(8,128)(2,1)S(1)}, bf16[128,3072]{1,0:T(8,128)(2,1)}, u32[]{:S(2)}, u32[]{:S(2)}) collective-permute-start(bf16[128,3072]{1,0:T(8,128)(2,1)S(1)} %copy-done.4), channel_id=1, source_target_pairs={{0,2},{2,0},{4,6},{6,4},{8,10},{10,8},{12,14},{14,12},{1,3},{3,1},... | collective-permute-start | bytes 2359304 | tf_op jit(solution)/shard_map/ppermute | solution.py:507
  42.5 139.4 %copy-start.20 = (f32[1,1536]{1,0:T(1,128)}, f32[1,1536]{1,0:T(1,128)S(1)}, u32[]{:S(2)}) copy-start(f32[1,1536]{1,0:T(1,128)S(1)} %dynamic-slice_bitcast_fusion.1.gate_ref) | copy-start | bytes 18436
  42.5 44.2 %collective-permute-start.4 = (bf16[64,3072]{1,0:T(8,128)(2,1)S(1)}, bf16[64,3072]{1,0:T(8,128)(2,1)}, u32[]{:S(2)}, u32[]{:S(2)}) collective-permute-start(bf16[64,3072]{1,0:T(8,128)(2,1)S(1)} %collective-permute-done.3), channel_id=1, source_target_pairs={{4,0},{6,2},{8,12},{10,14},{5,1},{7,3},{9,13},{11,15},{20,16},{22,... | collective-permute-start | bytes 1179656 | tf_op jit(solution)/shard_map/ppermute | solution.py:504
  43.8 73.2 %copy-start.6 = (bf16[64,3072]{1,0:T(8,128)(2,1)}, bf16[64,3072]{1,0:T(8,128)(2,1)S(1)}, u32[]{:S(2)}) copy-start(bf16[64,3072]{1,0:T(8,128)(2,1)S(1)} %collective-permute-done.refs_8_.refs_2_) | copy-start | bytes 1179652
  43.8 41.6 %collective-permute-start.1 = (bf16[64,3072]{1,0:T(8,128)(2,1)S(1)}, bf16[64,3072]{1,0:T(8,128)(2,1)}, u32[]{:S(2)}, u32[]{:S(2)}) collective-permute-start(bf16[64,3072]{1,0:T(8,128)(2,1)S(1)} %collective-permute-done.refs_8_.refs_2_), channel_id=1, source_target_pairs={{4,8},{6,10},{8,4},{10,6},{5,9},{7,11},{9,5},{11,7},{20,24},{22,26... | collective-permute-start | bytes 1179656 | tf_op jit(solution)/shard_map/ppermute | solution.py:504
  83.9 11.3 %collective-permute-start.5 = (bf16[64,3072]{1,0:T(8,128)(2,1)S(1)}, bf16[64,3072]{1,0:T(8,128)(2,1)}, u32[]{:S(2)}, u32[]{:S(2)}) collective-permute-start(bf16[64,3072]{1,0:T(8,128)(2,1)S(1)} %collective-permute-done.refs_8_.refs_2_), channel_id=1, source_target_pairs={{0,1},{1,0},{2,3},{3,2},{4,5},{5,4},{6,7},{7,6},{8,9},{9,8},{10,11... | collective-permute-start | bytes 1179656 | tf_op jit(solution)/shard_map/ppermute | solution.py:510
  85.4 20.3 %collective-permute-start.2 = (bf16[64,3072]{1,0:T(8,128)(2,1)}, bf16[64,3072]{1,0:T(8,128)(2,1)}, u32[]{:S(2)}, u32[]{:S(2)}) collective-permute-start(bf16[64,3072]{1,0:T(8,128)(2,1)} %collective-permute-done.1), channel_id=1, source_target_pairs={{4,0},{6,2},{8,12},{10,14},{5,1},{7,3},{9,13},{11,15},{20,16},{22,... | collective-permute-start | bytes 1179656 | tf_op jit(solution)/shard_map/ppermute | solution.py:504
  95.2 48.9 %all-to-all-start.1 = ((bf16[8,528,128]{2,1,0:T(8,128)(2,1)}), bf16[8,528,128]{2,1,0:T(8,128)(2,1)S(1)}, u32[]{:S(2)}, u32[]{:S(2)}) async-start(bf16[8,528,128]{2,1,0:T(8,128)(2,1)} %direct_rows.1), calls=%async_computation.1 | async-start | bytes 2162688 | tf_op jit(solution)/shard_map/all_to_all | solution.py:533
  102.7 12.0 %collective-permute-start.7 = (bf16[4,384,128]{2,1,0:T(8,128)(2,1)S(1)}, bf16[4,384,128]{2,1,0:T(8,128)(2,1)S(1)}, u32[]{:S(2)}, u32[]{:S(2)}) collective-permute-start(bf16[4,384,128]{2,1,0:T(8,128)(2,1)S(1)} %get-tuple-element.58), channel_id=1, source_target_pairs={{0,16},{16,0},{1,17},{17,1},{2,18},{18,2},{3,19},{19,3},{4,20},{20... | collective-permute-start | bytes 1179656 | tf_op jit(solution)/shard_map/ppermute | solution.py:531
  104.2 11.2 %collective-permute-start.6 = (bf16[64,3072]{1,0:T(8,128)(2,1)S(1)}, bf16[64,3072]{1,0:T(8,128)(2,1)S(1)}, u32[]{:S(2)}, u32[]{:S(2)}) collective-permute-start(bf16[64,3072]{1,0:T(8,128)(2,1)S(1)} %broadcast_select_fusion.refs_6_), channel_id=1, source_target_pairs={{0,1},{1,0},{2,3},{3,2},{4,5},{5,4},{6,7},{7,6},{8,9},{9,8},{10,11... | collective-permute-start | bytes 1179656 | tf_op jit(solution)/shard_map/ppermute | solution.py:510
  106.8 15.9 %collective-permute-start.9 = (bf16[4,384,128]{2,1,0:T(8,128)(2,1)S(1)}, bf16[4,384,128]{2,1,0:T(8,128)(2,1)S(1)}, u32[]{:S(2)}, u32[]{:S(2)}) collective-permute-start(bf16[4,384,128]{2,1,0:T(8,128)(2,1)S(1)} %get-tuple-element.57), channel_id=1, source_target_pairs={{0,16},{16,0},{1,17},{17,1},{2,18},{18,2},{3,19},{19,3},{4,20},{20... | collective-permute-start | bytes 1179656 | tf_op jit(solution)/shard_map/ppermute | solution.py:531
  115.5 10.4 %collective-permute-start.8 = (bf16[64,3072]{1,0:T(8,128)(2,1)S(1)}, bf16[64,3072]{1,0:T(8,128)(2,1)S(1)}, u32[]{:S(2)}, u32[]{:S(2)}) collective-permute-start(bf16[64,3072]{1,0:T(8,128)(2,1)S(1)} %broadcast_select_fusion.1.refs_10_), channel_id=1, source_target_pairs={{0,1},{1,0},{2,3},{3,2},{4,5},{5,4},{6,7},{7,6},{8,9},{9,8},{10,11... | collective-permute-start | bytes 1179656 | tf_op jit(solution)/shard_map/ppermute | solution.py:510
  117.0 8.9 %collective-permute-start.11 = (bf16[64,3072]{1,0:T(8,128)(2,1)S(1)}, bf16[64,3072]{1,0:T(8,128)(2,1)S(1)}, u32[]{:S(2)}, u32[]{:S(2)}) collective-permute-start(bf16[64,3072]{1,0:T(8,128)(2,1)S(1)} %collective-permute-done.refs_8_.refs_2_), channel_id=1, source_target_pairs={{0,2},{2,0},{4,6},{6,4},{8,10},{10,8},{12,14},{14,12},{1,3},{3,1},... | collective-permute-start | bytes 1179656 | tf_op jit(solution)/shard_map/ppermute | solution.py:507
  117.0 9.5 %collective-permute-start.12 = (bf16[64,3072]{1,0:T(8,128)(2,1)}, bf16[64,3072]{1,0:T(8,128)(2,1)S(1)}, u32[]{:S(2)}, u32[]{:S(2)}) collective-permute-start(bf16[64,3072]{1,0:T(8,128)(2,1)} %collective-permute-done.5.refs_9_.refs_3_), channel_id=1, source_target_pairs={{0,2},{2,0},{4,6},{6,4},{8,10},{10,8},{12,14},{14,12},{1,3},{3,1},... | collective-permute-start | bytes 1179656 | tf_op jit(solution)/shard_map/ppermute | solution.py:507
  122.7 12.8 %collective-permute-start.13 = (bf16[64,3072]{1,0:T(8,128)(2,1)S(1)}, bf16[64,3072]{1,0:T(8,128)(2,1)S(1)}, u32[]{:S(2)}, u32[]{:S(2)}) collective-permute-start(bf16[64,3072]{1,0:T(8,128)(2,1)S(1)} %broadcast_select_fusion.refs_6_), channel_id=1, source_target_pairs={{0,2},{2,0},{4,6},{6,4},{8,10},{10,8},{12,14},{14,12},{1,3},{3,1},... | collective-permute-start | bytes 1179656 | tf_op jit(solution)/shard_map/ppermute | solution.py:507
  125.9 9.6 %collective-permute-start.14 = (bf16[64,3072]{1,0:T(8,128)(2,1)S(1)}, bf16[64,3072]{1,0:T(8,128)(2,1)S(1)}, u32[]{:S(2)}, u32[]{:S(2)}) collective-permute-start(bf16[64,3072]{1,0:T(8,128)(2,1)S(1)} %collective-permute-done.6.refs_7_), channel_id=1, source_target_pairs={{0,2},{2,0},{4,6},{6,4},{8,10},{10,8},{12,14},{14,12},{1,3},{3,1},... | collective-permute-start | bytes 1179656 | tf_op jit(solution)/shard_map/ppermute | solution.py:507
  125.9 9.6 %collective-permute-start.15 = (bf16[64,3072]{1,0:T(8,128)(2,1)S(1)}, bf16[64,3072]{1,0:T(8,128)(2,1)S(1)}, u32[]{:S(2)}, u32[]{:S(2)}) collective-permute-start(bf16[64,3072]{1,0:T(8,128)(2,1)S(1)} %broadcast_select_fusion.1.refs_10_), channel_id=1, source_target_pairs={{0,2},{2,0},{4,6},{6,4},{8,10},{10,8},{12,14},{14,12},{1,3},{3,1},... | collective-permute-start | bytes 1179656 | tf_op jit(solution)/shard_map/ppermute | solution.py:507
  126.4 9.1 %collective-permute-start.16 = (bf16[64,3072]{1,0:T(8,128)(2,1)S(1)}, bf16[64,3072]{1,0:T(8,128)(2,1)S(1)}, u32[]{:S(2)}, u32[]{:S(2)}) collective-permute-start(bf16[64,3072]{1,0:T(8,128)(2,1)S(1)} %collective-permute-done.8.refs_11_), channel_id=1, source_target_pairs={{0,2},{2,0},{4,6},{6,4},{8,10},{10,8},{12,14},{14,12},{1,3},{3,1},... | collective-permute-start | bytes 1179656 | tf_op jit(solution)/shard_map/ppermute | solution.py:507
  132.9 22.9 %collective-permute-start.18 = (bf16[2,512,128]{2,1,0:T(8,128)(2,1)}, bf16[2,512,128]{2,1,0:T(8,128)(2,1)S(1)}, u32[]{:S(2)}, u32[]{:S(2)}) collective-permute-start(bf16[2,512,128]{2,1,0:T(8,128)(2,1)} %project_kva.1.kva), channel_id=1, source_target_pairs={{0,16},{1,17},{2,18},{3,19},{4,20},{5,21},{6,22},{7,23},{8,24},{9,... | collective-permute-start | bytes 786440 | tf_op jit(solution)/shard_map/ppermute | solution.py:547
  142.8 16.3 %collective-permute-start.17 = (bf16[2,512,128]{2,1,0:T(8,128)(2,1)}, bf16[2,512,128]{2,1,0:T(8,128)(2,1)S(1)}, u32[]{:S(2)}, u32[]{:S(2)}) collective-permute-start(bf16[2,512,128]{2,1,0:T(8,128)(2,1)} %project_kvb.1.kvb), channel_id=1, source_target_pairs={{0,16},{1,17},{2,18},{3,19},{4,20},{5,21},{6,22},{7,23},{8,24},{9,... | collective-permute-start | bytes 786440 | tf_op jit(solution)/shard_map/ppermute | solution.py:549
  180.4 10.8 %collective-permute-start.19 = (bf16[128,1536]{1,0:T(8,128)(2,1)}, bf16[128,1536]{1,0:T(8,128)(2,1)S(1)}, u32[]{:S(2)}, u32[]{:S(2)}) collective-permute-start(bf16[128,1536]{1,0:T(8,128)(2,1)} %out_sent.1), channel_id=1, source_target_pairs={{0,1},{1,0},{2,3},{3,2},{4,5},{5,4},{6,7},{7,6},{8,9},{9,8},{10,11... | collective-permute-start | bytes 1179656 | tf_op jit(solution)/shard_map/ppermute | solution.py:510
  (22 other events, 336.0 us)

commit v9 on v8

--- a/solution.py
+++ b/solution.py
@@ -8,7 +8,7 @@
 HEAD_DIM = 128
 GRID_W = 64
 TILE = 128
-VMEM_LIMIT = 56 * 1024 * 1024
+VMEM_LIMIT = 24 * 1024 * 1024
 
 
 def axis_freqs(width):
@@ -42,7 +42,7 @@
 
 VMEM = pl.BlockSpec(memory_space=pltpu.VMEM)
 SMEM = pl.BlockSpec(memory_space=pltpu.SMEM)
-ANY = pl.BlockSpec(memory_space=pl.ANY)
+HBM = pl.BlockSpec(memory_space=pltpu.HBM)
 
 
 def call(kernel, name, out_shape, flops, moved, exps, limit=VMEM_LIMIT, **spec):
@@ -97,7 +97,7 @@
             jax.ShapeDtypeStruct((rows // 2, depth), jnp.bfloat16),
         ],
         10 * rows * depth, 4 * rows * depth, 0,
-        in_specs=[SMEM, ANY, ANY],
+        in_specs=[SMEM, HBM, HBM],
         out_specs=[VMEM, VMEM],
         scratch_shapes=[
             pltpu.VMEM(image.shape, image.dtype),
@@ -107,47 +107,36 @@
     )(tp, image, mods)
 
 
-def kv_weights_kernel(section_ref, w_ref, out_ref, sems):
-    heads, held, _ = out_ref.shape
-    half = held // 2
+def kv_weights_kernel(section_ref, w_hbm, out_ref, w_ref, sems):
+    half = w_ref.shape[1]
     rows = pl.ds(pl.multiple_of(section_ref[0] * half, half), half)
-    finished(
-        started(
-            [
-                (
-                    w_ref.at[1 + kind, rows, pl.ds(s * HEAD_DIM, HEAD_DIM)],
-                    out_ref.at[s, pl.ds(kind * half, half), :],
-                )
-                for s in range(heads)
-                for kind in range(2)
-            ],
-            sems,
-        )
-    )
+    copies = started([(w_hbm.at[1 + k, rows, :], w_ref.at[k]) for k in range(2)], sems)
+    for k in range(2):
+        copies[k].wait()
+        for s in range(out_ref.shape[0]):
+            out_ref[s, k * half : (k + 1) * half, :] = w_ref[k, :, s * HEAD_DIM : (s + 1) * HEAD_DIM]
 
 
 def kv_weights(section, w):
     _, depth, width = w.shape
-    shape = (width // HEAD_DIM, depth, HEAD_DIM)
-    return call(
-        kv_weights_kernel, "kv_weights", jax.ShapeDtypeStruct(shape, w.dtype),
+    return call(
+        kv_weights_kernel, "kv_weights",
+        jax.ShapeDtypeStruct((width // HEAD_DIM, depth, HEAD_DIM), w.dtype),
         0, 4 * depth * width, 0,
-        in_specs=[SMEM, ANY],
-        out_specs=ANY,
-        scratch_shapes=[pltpu.SemaphoreType.DMA((2 * shape[0],))],
+        in_specs=[SMEM, HBM],
+        out_specs=VMEM,
+        scratch_shapes=[pltpu.VMEM((2, depth // 2, width), w.dtype), pltpu.SemaphoreType.DMA((2,))],
     )(section, w)
 
 
-def direct_kernel(w_ref, text_ref, mask_ref, out_ref, sems):
-    heads = out_ref.shape[0]
-    depth, count, last = w_ref.shape[1], text_ref.shape[1], mask_ref.shape[0]
-    pairs = []
-    for s in range(heads):
-        lanes = pl.ds(s * HEAD_DIM, HEAD_DIM)
-        pairs.append((w_ref.at[0, :, lanes], out_ref.at[s, pl.ds(0, depth), :]))
-        pairs.append((text_ref.at[s], out_ref.at[s, pl.ds(depth, count), :]))
-        pairs.append((mask_ref, out_ref.at[s, pl.ds(depth + count, last), :]))
-    finished(started(pairs, sems))
+def direct_kernel(w_hbm, text_hbm, mask_ref, out_ref, w_ref, text_ref, sems):
+    depth, count = w_ref.shape[0], text_ref.shape[1]
+    copies = started([(w_hbm.at[0], w_ref), (text_hbm, text_ref)], sems)
+    finished(copies)
+    for s in range(out_ref.shape[0]):
+        out_ref[s, :depth, :] = w_ref[:, s * HEAD_DIM : (s + 1) * HEAD_DIM]
+        out_ref[s, depth : depth + count, :] = text_ref[s]
+        out_ref[s, depth + count :, :] = mask_ref[...]
 
 
 def direct_rows(w, text, mask):
@@ -156,9 +145,13 @@
     return call(
         direct_kernel, "direct_rows", jax.ShapeDtypeStruct(shape, w.dtype),
         0, 4 * heads * shape[1] * HEAD_DIM, 0,
-        in_specs=[ANY, ANY, ANY],
-        out_specs=ANY,
-        scratch_shapes=[pltpu.SemaphoreType.DMA((3 * heads,))],
+        in_specs=[HBM, HBM, VMEM],
+        out_specs=VMEM,
+        scratch_shapes=[
+            pltpu.VMEM(w.shape[1:], w.dtype),
+            pltpu.VMEM(text.shape, text.dtype),
+            pltpu.SemaphoreType.DMA((2,)),
+        ],
     )(w, text, mask)
 
 
@@ -192,6 +185,18 @@
     return pairs
 
 
+def blocks(rows):
+    return [(b, slice(b * BLOCK, (b + 1) * BLOCK)) for b in range(rows // BLOCK)]
+
+
+def arrived(copies, piece_refs, rows):
+    at = 0
+    for copy, ref in zip(copies, piece_refs):
+        if rows.start <= at < rows.stop:
+            copy.wait()
+        at += ref.shape[0]
+
+
 def kv_kernel(chunk, section_ref, tabs_ref, gain_ref, mine_hbm, peer_a, peer_b, *refs):
     piece_refs, (kv_ref, x_ref, mine, peer, w_ref, sems) = refs[:-6], refs[-6:]
     sources, held, _ = mine.shape
@@ -215,16 +220,17 @@
             a, b = mine[s, at, :], peer[s, at, :]
             w_ref[2 * s * half : (2 * s + 1) * half, lanes] = jnp.where(first, a, b)
             w_ref[(2 * s + 1) * half : (2 * s + 2) * half, lanes] = jnp.where(first, b, a)
-    finished(tokens)
-    both = jnp.dot(x_ref[...], w_ref[...], preferred_element_type=jnp.float32)
-    rows = x_ref.shape[0]
-    kv_ref[0] = normed_rotated(
-        both[:, :HEAD_DIM],
-        gain_ref[1:2, :],
-        table_of(tabs_ref, 0, chunk * rows, rows),
-        table_of(tabs_ref, 1, chunk * rows, rows),
-    )
-    kv_ref[1] = both[:, HEAD_DIM:].astype(jnp.bfloat16)
+    for b, at in blocks(x_ref.shape[0]):
+        arrived(tokens, piece_refs, at)
+        both = jnp.dot(x_ref[at, :], w_ref[...], preferred_element_type=jnp.float32)
+        start = chunk * x_ref.shape[0] + b * BLOCK
+        kv_ref[0, at, :] = normed_rotated(
+            both[:, :HEAD_DIM],
+            gain_ref[1:2, :],
+            table_of(tabs_ref, 0, start, BLOCK),
+            table_of(tabs_ref, 1, start, BLOCK),
+        )
+        kv_ref[1, at, :] = both[:, HEAD_DIM:].astype(jnp.bfloat16)
 
 
 def project_kv(chunk, section, tabs, gains, mine, peers, pieces):
@@ -234,7 +240,7 @@
         lambda *refs: kv_kernel(chunk, *refs), "project_kv" + "ab"[chunk],
         jax.ShapeDtypeStruct((2, rows, HEAD_DIM), jnp.bfloat16),
         4 * rows * depth * HEAD_DIM, 2 * (rows * depth + 2 * mine.size), 0,
-        in_specs=[SMEM, VMEM, VMEM] + [ANY] * (3 + len(pieces)),
+        in_specs=[SMEM, VMEM, VMEM] + [HBM] * (3 + len(pieces)),
         out_specs=VMEM,
         scratch_shapes=[
             pltpu.VMEM((rows, depth), jnp.bfloat16),
@@ -274,11 +280,8 @@
     q_ref, num_ref, den_ref, keep_ref, x_ref, direct, sems = refs[-7:]
     rows, depth = x_ref.shape
     sources, held, _ = direct.shape
-    copies = started(
-        [(direct_hbm.at[s], direct.at[s]) for s in range(sources)]
-        + piece_copies(piece_refs, x_ref),
-        sems,
-    )
+    copies = started([(direct_hbm.at[s], direct.at[s]) for s in range(sources)], sems)
+    tokens = started(piece_copies(piece_refs, x_ref), sems, sources)
     finished(copies)
     wide = depth // sources
     w = direct[:, :wide, :].reshape(depth, HEAD_DIM)
@@ -287,8 +290,8 @@
         direct[:, wide : wide + count, :].reshape(-1, HEAD_DIM),
         direct[:, wide + count : wide + 2 * count, :].reshape(-1, HEAD_DIM),
     )
-    for b in range(rows // BLOCK):
-        at = slice(b * BLOCK, (b + 1) * BLOCK)
+    for b, at in blocks(rows):
+        arrived(tokens, piece_refs, at)
         query = jnp.dot(x_ref[at, :], w, preferred_element_type=jnp.float32)
         query = normed_rotated(
             query,
@@ -375,7 +378,7 @@
             jax.ShapeDtypeStruct((row_tiles.shape[0], rows), jnp.float32),
         ],
         2 * rows * HEAD_DIM * (2 * keys + depth), 2 * rows * depth, rows * keys,
-        in_specs=[VMEM] * 6 + [ANY] * (1 + len(pieces)),
+        in_specs=[VMEM] * 6 + [HBM] * (1 + len(pieces)),
         out_specs=[VMEM] * 4,
         scratch_shapes=[
             pltpu.VMEM((rows, depth), jnp.bfloat16),
@@ -410,45 +413,28 @@
     return jnp.concatenate([attn_ref[h] for h in range(attn_ref.shape[0])], axis=1)
 
 
-def product(half, attn_ref, w_hbm, w_ref, sems):
-    depth, width = w_ref.shape
-    rows = depth // sems.shape[0]
-    columns = pl.ds(pl.multiple_of(half * width, width), width)
-    finished(
-        started(
-            [
-                (w_hbm.at[pl.ds(i * rows, rows), columns], w_ref.at[pl.ds(i * rows, rows), :])
-                for i in range(sems.shape[0])
-            ],
-            sems,
-        )
-    )
-    return jnp.dot(token_rows(attn_ref), w_ref[...], preferred_element_type=jnp.float32)
-
-
-def sent_kernel(half_ref, attn_ref, w_hbm, out_ref, w_ref, sems):
-    branch = product(1 - half_ref[0], attn_ref, w_hbm, w_ref, sems)
+def sent_kernel(attn_ref, w_ref, out_ref):
+    branch = jnp.dot(token_rows(attn_ref), w_ref[...], preferred_element_type=jnp.float32)
     out_ref[...] = branch.astype(jnp.bfloat16)
 
 
-def kept_kernel(half_ref, attn_ref, w_hbm, image_ref, gate_ref, out_ref, w_ref, sems):
-    branch = product(half_ref[0], attn_ref, w_hbm, w_ref, sems)
+def kept_kernel(attn_ref, w_ref, image_ref, gate_ref, out_ref):
+    branch = jnp.dot(token_rows(attn_ref), w_ref[...], preferred_element_type=jnp.float32)
     out_ref[...] = image_ref[...].astype(jnp.float32) + gate_ref[...] * branch
 
 
-def project_out(half, attn, w, image=None, gate=None):
+def project_out(attn, w, image=None, gate=None):
     rows = attn.shape[1]
-    depth, width = w.shape[0], w.shape[1] // 2
+    depth, width = w.shape
     kept = image is not None
-    more = (image, gate) if kept else ()
+    args = (attn, w) + ((image, gate) if kept else ())
     return call(
         kept_kernel if kept else sent_kernel, "out_kept" if kept else "out_sent",
         jax.ShapeDtypeStruct((rows, width), jnp.float32 if kept else jnp.bfloat16),
         2 * rows * depth * width, 2 * depth * width, 0,
-        in_specs=[SMEM, VMEM, ANY] + [VMEM] * len(more),
+        in_specs=[VMEM] * len(args),
         out_specs=VMEM,
-        scratch_shapes=[pltpu.VMEM((depth, width), w.dtype), pltpu.SemaphoreType.DMA((8,))],
-    )(half, attn, w, *more)
+    )(*args)
 
 
 def lane_tables(row_ids, time_index):
@@ -525,7 +511,7 @@
     direct = direct_rows(rows3, text, mask)
 
     near_tp = to_tp(near)
-    third, near_tp, mine = lax.optimization_barrier((third, near_tp, mine))
+    third, near_tp = lax.optimization_barrier((third, near_tp))
     third_tp = to_tp(third)
     some = seq // 2
     peers = [lax.ppermute(mine[:some], "section", both), lax.ppermute(mine[some:], "section", both)]
@@ -534,9 +520,11 @@
     cols = w_out.shape[1] // 2
     gate = lax.dynamic_slice_in_dim(mods[2:3], tp * cols, cols, 1)
     residual = lax.dynamic_slice_in_dim(image[0], tp * cols, cols, 1)
-    early = (tabs, gains, row_tiles, key_tiles, place, gate, residual)
+    w_sent = lax.dynamic_slice_in_dim(w_out, (1 - tp) * cols, cols, 1)
+    w_kept = lax.dynamic_slice_in_dim(w_out, tp * cols, cols, 1)
+    early = (tabs, gains, row_tiles, key_tiles, place, gate, residual, w_sent, w_kept)
     fourth, third_tp, peers[0], early = lax.optimization_barrier((fourth, third_tp, peers[0], early))
-    tabs, gains, row_tiles, key_tiles, place, gate, residual = early
+    tabs, gains, row_tiles, key_tiles, place, gate, residual, w_sent, w_kept = early
     fourth_tp = to_tp(fourth)
     fourth, fourth_tp, peers[1] = lax.optimization_barrier((fourth, fourth_tp, peers[1]))
     a = [full, to_core(full), near, near_tp, to_core(near), to_core(near_tp)]
@@ -554,8 +542,8 @@
     attn = attend_second(section_at, place, keep, query, cond_b, num, den, seq)
 
     attn = lax.all_to_all(attn, "seq", 0, 0)
-    other = to_tp(project_out(tp_at, attn, w_out))
-    kept = project_out(tp_at, attn, w_out, residual, gate)
+    other = to_tp(project_out(attn, w_sent))
+    kept = project_out(attn, w_kept, residual, gate)
     return (kept + gate * other.astype(jnp.float32)).astype(jnp.bfloat16)[None]
 
 

time: 194 us -> 148 us (0.76)
  Pallas kernels: 96.9 us -> 27.2 us
  local copies, waits for them, and re-layouts: 10 us -> 28.3 us
  waiting for transfers between devices: 28.6 us -> 34.7 us
    pallas_call x1, Pallas kernels: 34.1 us -> 0.25 us  [direct_rows(): call(direct_kernel, 'direct_rows', jax.ShapeDtypeStruct(shape, w.dtype),...]
    pallas_call x1, Pallas kernels: 25.1 us -> 1.4 us  [kv_weights(): call(kv_weights_kernel, 'kv_weights', jax.ShapeDtypeStruct((width // HEAD...]
    unnamed x48 -> x68, local copies, waits for them, and re-layouts: 5.25 us -> 18.2 us
    ppermute x5, waiting for transfers between devices: 0.01 us -> 9.55 us  [along_z(): return lax.ppermute(x, 'seq', z_pairs(seq, pairs))]
    pallas_call x2, Pallas kernels: 8.62 us -> 1.9 us  [project_out(): call(kept_kernel if kept else sent_kernel, 'out_kept' if kept else 'out_s...]
    dynamic_slice x0 -> x1, local copies, waits for them, and re-layouts: none -> 4.87 us  [head_body(): w_kept = lax.dynamic_slice_in_dim(w_out, tp * cols, cols, 1)]
    ppermute x4, waiting for transfers between devices: 16.2 us -> 13.3 us  [to_tp(): return lax.ppermute(x, 'tp', both)]
    ppermute x1, waiting for transfers between devices: 7.23 us -> 4.72 us  [head_body(): lax.ppermute(mine[:some], 'section', both)]
  transfers between devices with their start and end apart: 22 -> 22, of which waited for: 6 -> 7; matrix products, arithmetic and copies ran while one was open for 6% -> 10% of each run, Pallas kernels for 45% -> 15%
where the time goes in v9:
time: 148 us; the launch traced here: 147 us
  starting transfers between devices  36.3 us (25%)
  waiting for transfers between devices  34.7 us (23%)
  local copies, waits for them, and re-layouts  28.3 us (19%)
  Pallas kernels  27.2 us (18%)
  blocking collectives  13.9 us (9%)
  other arithmetic  6.07 us (4%)
    unnamed x68, local copies, waits for them, and re-layouts  18.2 us
    all_to_all x1, blocking collectives, head_body(): attn = lax.all_to_all(attn, 'seq', 0, 0)  13.9 us
    ppermute x4, waiting for transfers between devices, to_tp(): return lax.ppermute(x, 'tp', both)  13.3 us
    ppermute x5, starting transfers between devices, along_z(): return lax.ppermute(x, 'seq', z_pairs(seq, pairs))  10.6 us
    pallas_call x2, Pallas kernels, project_kv(): call(lambda *refs: kv_kernel(chunk, *refs), 'project_kv' + 'ab'[chunk], j...  9.86 us
    ppermute x5, waiting for transfers between devices, along_z(): return lax.ppermute(x, 'seq', z_pairs(seq, pairs))  9.55 us
    pallas_call x1, Pallas kernels, attend_own(): call(own_kernel, 'attend_own', [jax.ShapeDtypeStruct((rows, HEAD_DIM), jn...  8.84 us
    ppermute x1, waiting for transfers between devices, head_body(): lax.ppermute(mine[some:], 'section', both)  7.02 us
  transfers between devices with their start and end apart: 22, of which 7 were waited for; matrix products, arithmetic and copies ran while one was open for 10% of the time, Pallas kernels for 15%

profile of v9, /device:TPU:0, one launch (start us, length us, event | category | flops | bytes accessed | tf_op | source)
XLA Modules:
  0.0 146.9 jit_solution(10254632648795518652)
XLA Ops:
  1.9 2.7 %norm_tokens.1 = (bf16[128,3072]{1,0:T(8,128)(2,1)}, bf16[64,3072]{1,0:T(8,128)(2,1)}) custom-call(s32[1]{0:T(128)} %bitcast.1.tp_ref, bf16[128,3072]{1,0:T(8,128)(2,1)S(1)} %bitcast.27, f32[3,1,3072]{2,1,0:T(1,128)S(1)} %bitcast.29), custom_call_target="tpu_custom_call" | custom-call | flops 3932160 | bytes 1572864 | tf_op jit(solution)/shard_map/norm_tokens/pallas_call | solution.py:93
  6.1 5.1 %collective-permute-start = (bf16[64,3072]{1,0:T(8,128)(2,1)}, bf16[64,3072]{1,0:T(8,128)(2,1)}, u32[]{:S(2)}, u32[]{:S(2)}) collective-permute-start(bf16[64,3072]{1,0:T(8,128)(2,1)} %get-tuple-element.32), channel_id=1, source_target_pairs={{0,4},{2,6},{4,0},{6,2},{8,12},{10,14},{12,8},{14,10},{1,5},{3,7},... | collective-permute-start | bytes 1179656 | tf_op jit(solution)/shard_map/ppermute | solution.py:490
  11.3 1.7 %copy-done.1 = bf16[384,3,1024]{2,0,1:T(8,128)(2,1)S(1)} copy-done((bf16[384,3,1024]{2,0,1:T(8,128)(2,1)S(1)}, bf16[384,3,1024]{2,0,1:T(8,128)(2,1)}, u32[]{:S(2)}) %copy-start.1) | copy-done | bytes 2359320
  14.4 4.3 %all-to-all-start = ((bf16[8,384,128]{2,1,0:T(8,128)(2,1)}), bf16[8,384,128]{2,1,0:T(8,128)(2,1)}, u32[]{:S(2)}, u32[]{:S(2)}) async-start(bf16[8,384,128]{2,1,0:T(8,128)(2,1)} %kv_weights.1), calls=%async_computation | async-start | bytes 1572864 | tf_op jit(solution)/shard_map/all_to_all | solution.py:485
  30.4 4.9 %constant_dynamic-slice_fusion = (bf16[1024,1536]{1,0:T(8,128)(2,1)S(1)}, bf16[1024,1536]{1,0:T(8,128)(2,1)}) fusion(bf16[1024,3072]{1,0:T(8,128)(2,1)} %param.12, s32[]{:T(128)S(6)} %select_n.78, s32[]{:T(128)S(6)} %select_n.79), kind=kLoop, calls=%fused_computation.20 | loop fusion | bytes 12582920 | tf_op jit(solution)/shard_map/dynamic_slice | solution.py:524
  35.3 1.5 %collective-permute-start.5 = (bf16[64,3072]{1,0:T(8,128)(2,1)}, bf16[64,3072]{1,0:T(8,128)(2,1)}, u32[]{:S(2)}, u32[]{:S(2)}) collective-permute-start(bf16[64,3072]{1,0:T(8,128)(2,1)} %collective-permute-done.refs_8_.refs_2_), channel_id=1, source_target_pairs={{0,1},{1,0},{2,3},{3,2},{4,5},{5,4},{6,7},{7,6},{8,9},{9,8},{10,11... | collective-permute-start | bytes 1179656 | tf_op jit(solution)/shard_map/ppermute | solution.py:496
  38.1 6.5 %collective-permute-done.4 = bf16[64,3072]{1,0:T(8,128)(2,1)S(1)} collective-permute-done((bf16[64,3072]{1,0:T(8,128)(2,1)}, bf16[64,3072]{1,0:T(8,128)(2,1)S(1)}, u32[]{:S(2)}, u32[]{:S(2)}) %collective-permute-start.4) | collective-permute-done | bytes 393248 | tf_op jit(solution)/shard_map/ppermute | solution.py:490
  44.6 2.2 %collective-permute-done.5.refs_9_.refs_3_ = bf16[64,3072]{1,0:T(8,128)(2,1)} collective-permute-done((bf16[64,3072]{1,0:T(8,128)(2,1)}, bf16[64,3072]{1,0:T(8,128)(2,1)}, u32[]{:S(2)}, u32[]{:S(2)}) %collective-permute-start.5) | collective-permute-done | bytes 393248 | tf_op jit(solution)/shard_map/ppermute | solution.py:496
  46.8 1.5 %collective-permute-start.6 = (bf16[64,3072]{1,0:T(8,128)(2,1)S(1)}, bf16[64,3072]{1,0:T(8,128)(2,1)}, u32[]{:S(2)}, u32[]{:S(2)}) collective-permute-start(bf16[64,3072]{1,0:T(8,128)(2,1)S(1)} %broadcast_select_fusion.refs_6_), channel_id=1, source_target_pairs={{0,1},{1,0},{2,3},{3,2},{4,5},{5,4},{6,7},{7,6},{8,9},{9,8},{10,11... | collective-permute-start | bytes 1179656 | tf_op jit(solution)/shard_map/ppermute | solution.py:496
  48.3 6.7 %all-to-all-start.1 = ((bf16[8,528,128]{2,1,0:T(8,128)(2,1)}), bf16[8,528,128]{2,1,0:T(8,128)(2,1)}, u32[]{:S(2)}, u32[]{:S(2)}) async-start(bf16[8,528,128]{2,1,0:T(8,128)(2,1)} %copy-done.3), calls=%async_computation.1 | async-start | bytes 2162688 | tf_op jit(solution)/shard_map/all_to_all | solution.py:519
  56.2 1.6 %collective-permute-start.7 = (bf16[4,384,128]{2,1,0:T(8,128)(2,1)S(1)}, bf16[4,384,128]{2,1,0:T(8,128)(2,1)S(1)}, u32[]{:S(2)}, u32[]{:S(2)}) collective-permute-start(bf16[4,384,128]{2,1,0:T(8,128)(2,1)S(1)} %get-tuple-element.62), channel_id=1, source_target_pairs={{0,16},{16,0},{1,17},{17,1},{2,18},{18,2},{3,19},{19,3},{4,20},{20... | collective-permute-start | bytes 1179656 | tf_op jit(solution)/shard_map/ppermute | solution.py:517
  57.7 3.1 %collective-permute-done.2 = bf16[64,3072]{1,0:T(8,128)(2,1)} collective-permute-done((bf16[64,3072]{1,0:T(8,128)(2,1)}, bf16[64,3072]{1,0:T(8,128)(2,1)}, u32[]{:S(2)}, u32[]{:S(2)}) %collective-permute-start.2) | collective-permute-done | bytes 393248 | tf_op jit(solution)/shard_map/ppermute | solution.py:490
  61.8 1.6 %collective-permute-start.9 = (bf16[4,384,128]{2,1,0:T(8,128)(2,1)S(1)}, bf16[4,384,128]{2,1,0:T(8,128)(2,1)S(1)}, u32[]{:S(2)}, u32[]{:S(2)}) collective-permute-start(bf16[4,384,128]{2,1,0:T(8,128)(2,1)S(1)} %get-tuple-element.61), channel_id=1, source_target_pairs={{0,16},{16,0},{1,17},{17,1},{2,18},{18,2},{3,19},{19,3},{4,20},{20... | collective-permute-start | bytes 1179656 | tf_op jit(solution)/shard_map/ppermute | solution.py:517
  63.4 4.7 %collective-permute-done.7.refs_4_ = bf16[4,384,128]{2,1,0:T(8,128)(2,1)S(1)} collective-permute-done((bf16[4,384,128]{2,1,0:T(8,128)(2,1)S(1)}, bf16[4,384,128]{2,1,0:T(8,128)(2,1)S(1)}, u32[]{:S(2)}, u32[]{:S(2)}) %collective-permute-start.7) | collective-permute-done | bytes 393248 | tf_op jit(solution)/shard_map/ppermute | solution.py:517
  69.2 7.0 %collective-permute-done.9.refs_5_ = bf16[4,384,128]{2,1,0:T(8,128)(2,1)S(1)} collective-permute-done((bf16[4,384,128]{2,1,0:T(8,128)(2,1)S(1)}, bf16[4,384,128]{2,1,0:T(8,128)(2,1)S(1)}, u32[]{:S(2)}, u32[]{:S(2)}) %collective-permute-start.9) | collective-permute-done | bytes 393248 | tf_op jit(solution)/shard_map/ppermute | solution.py:517
  76.2 2.4 %collective-permute-done.8.refs_11_ = bf16[64,3072]{1,0:T(8,128)(2,1)S(1)} collective-permute-done((bf16[64,3072]{1,0:T(8,128)(2,1)S(1)}, bf16[64,3072]{1,0:T(8,128)(2,1)S(1)}, u32[]{:S(2)}, u32[]{:S(2)}) %collective-permute-start.8) | collective-permute-done | bytes 393248 | tf_op jit(solution)/shard_map/ppermute | solution.py:496
  80.7 4.8 %project_kva.1.kva = bf16[2,512,128]{2,1,0:T(8,128)(2,1)} custom-call(s32[1]{0:T(128)} %bitcast.section_ref.refs_0_, f32[2,80,128]{2,1,0:T(8,128)S(1)} %copy-done.23, f32[2,128]{1,0:T(2,128)S(1)} %copy-done.27, bf16[8,384,128]{2,1,0:T(8,128)(2,1)} %all-to-all-done.refs_3_, bf16[4,384,128]{2,1,0:T(8,128)(2,1)S(1)} %collective-permute-done.7.refs_4_, ...), custom_call_target="tpu_custom_call" | custom-call | flops 805306368 | bytes 4718592 | tf_op jit(solution)/shard_map/project_kva/pallas_call | solution.py:239
  85.5 4.1 %collective-permute-start.18 = (bf16[2,512,128]{2,1,0:T(8,128)(2,1)}, bf16[2,512,128]{2,1,0:T(8,128)(2,1)}, u32[]{:S(2)}, u32[]{:S(2)}) collective-permute-start(bf16[2,512,128]{2,1,0:T(8,128)(2,1)} %project_kva.1.kva), channel_id=1, source_target_pairs={{0,16},{1,17},{2,18},{3,19},{4,20},{5,21},{6,22},{7,23},{8,24},{9,... | collective-permute-start | bytes 786440 | tf_op jit(solution)/shard_map/ppermute | solution.py:535
  89.7 5.0 %project_kvb.1.kvb = bf16[2,512,128]{2,1,0:T(8,128)(2,1)} custom-call(s32[1]{0:T(128)} %bitcast.section_ref.refs_0_, f32[2,80,128]{2,1,0:T(8,128)S(1)} %copy-done.23, f32[2,128]{1,0:T(2,128)S(1)} %copy-done.27, bf16[8,384,128]{2,1,0:T(8,128)(2,1)} %all-to-all-done.refs_3_, bf16[4,384,128]{2,1,0:T(8,128)(2,1)S(1)} %collective-permute-done.7.refs_4_, ...), custom_call_target="tpu_custom_call" | custom-call | flops 805306368 | bytes 4718592 | tf_op jit(solution)/shard_map/project_kvb/pallas_call | solution.py:239
  95.6 2.0 %collective-permute-start.17 = (bf16[2,512,128]{2,1,0:T(8,128)(2,1)}, bf16[2,512,128]{2,1,0:T(8,128)(2,1)}, u32[]{:S(2)}, u32[]{:S(2)}) collective-permute-start(bf16[2,512,128]{2,1,0:T(8,128)(2,1)} %project_kvb.1.kvb), channel_id=1, source_target_pairs={{0,16},{1,17},{2,18},{3,19},{4,20},{5,21},{6,22},{7,23},{8,24},{9,... | collective-permute-start | bytes 786440 | tf_op jit(solution)/shard_map/ppermute | solution.py:537
  107.9 8.8 %attend_own.1 = (bf16[1024,128]{1,0:T(8,128)(2,1)S(1)}, f32[1024,128]{1,0:T(8,128)S(1)}, f32[1024,128]{1,0:T(8,128)S(1)}, f32[16,1024]{1,0:T(8,128)S(1)}) custom-call(f32[2,80,128]{2,1,0:T(8,128)S(1)} %copy-done.24, f32[2,128]{1,0:T(2,128)S(1)} %copy-done.28, f32[16,8]{1,0:T(8,128)S(1)} %fusion.3.rows_ref, f32[128,16]{1,0:T(8,128)S(1)} %copy-done.25, ...), custom_call_target="tpu_custom_call" | custom-call | flops 1610612736 | bytes 6291456 | tf_op jit(solution)/shard_map/attend_own/pallas_call | solution.py:372
  119.0 13.9 %all_to_all.15.attn_ref = bf16[8,128,128]{2,1,0:T(8,128)(2,1)S(1)} all-to-all(bf16[8,128,128]{2,1,0:T(8,128)(2,1)S(1)} %attend_second.1), channel_id=1, replica_groups=mesh['section'=2,'seq'=8,'tp'=2] {'seq'}, dimensions={0} | all-to-all | bytes 524288 | tf_op jit(solution)/shard_map/all_to_all | solution.py:544
  136.4 8.7 %collective-permute-done.19 = bf16[128,1536]{1,0:T(8,128)(2,1)} collective-permute-done((bf16[128,1536]{1,0:T(8,128)(2,1)}, bf16[128,1536]{1,0:T(8,128)(2,1)}, u32[]{:S(2)}, u32[]{:S(2)}) %collective-permute-start.19) | collective-permute-done | bytes 393248 | tf_op jit(solution)/shard_map/ppermute | solution.py:496
  145.1 1.8 %fusion = bf16[1,128,1536]{2,1,0:T(8,128)(2,1)} fusion(f32[128,1536]{1,0:T(8,128)S(1)} %out_kept.1, bf16[128,1536]{1,0:T(8,128)(2,1)} %collective-permute-done.19, f32[1536]{0:T(1024)S(1)} %reduce), kind=kLoop, calls=%fused_computation.1 | loop fusion | flops 786432 | bytes 1579008 | tf_op jit(solution)/shard_map/broadcast_in_dim | solution.py:547
  (138 shorter events, 39.7 us)
Async XLA Ops:
  0.0 22.5 %copy-start.31 = (f32[128]{0:T(128)S(1)}, f32[128]{0:T(128)}, u32[]{:S(2)}) copy-start(f32[128]{0:T(128)} %param.14) | copy-start | bytes 1540
  4.7 23.0 %collective-permute-start.3 = (bf16[64,3072]{1,0:T(8,128)(2,1)}, bf16[64,3072]{1,0:T(8,128)(2,1)}, u32[]{:S(2)}, u32[]{:S(2)}) collective-permute-start(bf16[64,3072]{1,0:T(8,128)(2,1)} %get-tuple-element.32), channel_id=1, source_target_pairs={{4,8},{6,10},{8,4},{10,6},{5,9},{7,11},{9,5},{11,7},{20,24},{22,26... | collective-permute-start | bytes 1179656 | tf_op jit(solution)/shard_map/ppermute | solution.py:490
  6.1 22.9 %collective-permute-start = (bf16[64,3072]{1,0:T(8,128)(2,1)}, bf16[64,3072]{1,0:T(8,128)(2,1)}, u32[]{:S(2)}, u32[]{:S(2)}) collective-permute-start(bf16[64,3072]{1,0:T(8,128)(2,1)} %get-tuple-element.32), channel_id=1, source_target_pairs={{0,4},{2,6},{4,0},{6,2},{8,12},{10,14},{12,8},{14,10},{1,5},{3,7},... | collective-permute-start | bytes 1179656 | tf_op jit(solution)/shard_map/ppermute | solution.py:490
  14.4 34.0 %all-to-all-start = ((bf16[8,384,128]{2,1,0:T(8,128)(2,1)}), bf16[8,384,128]{2,1,0:T(8,128)(2,1)}, u32[]{:S(2)}, u32[]{:S(2)}) async-start(bf16[8,384,128]{2,1,0:T(8,128)(2,1)} %kv_weights.1), calls=%async_computation | async-start | bytes 1572864 | tf_op jit(solution)/shard_map/all_to_all | solution.py:485
  18.7 60.4 %collective-permute-start.10 = (bf16[128,3072]{1,0:T(8,128)(2,1)}, bf16[128,3072]{1,0:T(8,128)(2,1)}, u32[]{:S(2)}, u32[]{:S(2)}) collective-permute-start(bf16[128,3072]{1,0:T(8,128)(2,1)} %get-tuple-element.43.refs_6_.refs_0_), channel_id=1, source_target_pairs={{0,2},{2,0},{4,6},{6,4},{8,10},{10,8},{12,14},{14,12},{1,3},{3,1},... | collective-permute-start | bytes 2359304 | tf_op jit(solution)/shard_map/ppermute | solution.py:493
  27.7 16.9 %collective-permute-start.4 = (bf16[64,3072]{1,0:T(8,128)(2,1)}, bf16[64,3072]{1,0:T(8,128)(2,1)S(1)}, u32[]{:S(2)}, u32[]{:S(2)}) collective-permute-start(bf16[64,3072]{1,0:T(8,128)(2,1)} %collective-permute-done.3), channel_id=1, source_target_pairs={{4,0},{6,2},{8,12},{10,14},{5,1},{7,3},{9,13},{11,15},{20,16},{22,... | collective-permute-start | bytes 1179656 | tf_op jit(solution)/shard_map/ppermute | solution.py:490
  29.0 7.8 %collective-permute-start.1 = (bf16[64,3072]{1,0:T(8,128)(2,1)}, bf16[64,3072]{1,0:T(8,128)(2,1)}, u32[]{:S(2)}, u32[]{:S(2)}) collective-permute-start(bf16[64,3072]{1,0:T(8,128)(2,1)} %collective-permute-done.refs_8_.refs_2_), channel_id=1, source_target_pairs={{4,8},{6,10},{8,4},{10,6},{5,9},{7,11},{9,5},{11,7},{20,24},{22,26... | collective-permute-start | bytes 1179656 | tf_op jit(solution)/shard_map/ppermute | solution.py:490
  35.3 11.5 %collective-permute-start.5 = (bf16[64,3072]{1,0:T(8,128)(2,1)}, bf16[64,3072]{1,0:T(8,128)(2,1)}, u32[]{:S(2)}, u32[]{:S(2)}) collective-permute-start(bf16[64,3072]{1,0:T(8,128)(2,1)} %collective-permute-done.refs_8_.refs_2_), channel_id=1, source_target_pairs={{0,1},{1,0},{2,3},{3,2},{4,5},{5,4},{6,7},{7,6},{8,9},{9,8},{10,11... | collective-permute-start | bytes 1179656 | tf_op jit(solution)/shard_map/ppermute | solution.py:496
  36.8 24.0 %collective-permute-start.2 = (bf16[64,3072]{1,0:T(8,128)(2,1)}, bf16[64,3072]{1,0:T(8,128)(2,1)}, u32[]{:S(2)}, u32[]{:S(2)}) collective-permute-start(bf16[64,3072]{1,0:T(8,128)(2,1)} %collective-permute-done.1), channel_id=1, source_target_pairs={{4,0},{6,2},{8,12},{10,14},{5,1},{7,3},{9,13},{11,15},{20,16},{22,... | collective-permute-start | bytes 1179656 | tf_op jit(solution)/shard_map/ppermute | solution.py:490
  46.8 16.6 %collective-permute-start.6 = (bf16[64,3072]{1,0:T(8,128)(2,1)S(1)}, bf16[64,3072]{1,0:T(8,128)(2,1)}, u32[]{:S(2)}, u32[]{:S(2)}) collective-permute-start(bf16[64,3072]{1,0:T(8,128)(2,1)S(1)} %broadcast_select_fusion.refs_6_), channel_id=1, source_target_pairs={{0,1},{1,0},{2,3},{3,2},{4,5},{5,4},{6,7},{7,6},{8,9},{9,8},{10,11... | collective-permute-start | bytes 1179656 | tf_op jit(solution)/shard_map/ppermute | solution.py:496
  48.3 49.3 %all-to-all-start.1 = ((bf16[8,528,128]{2,1,0:T(8,128)(2,1)}), bf16[8,528,128]{2,1,0:T(8,128)(2,1)}, u32[]{:S(2)}, u32[]{:S(2)}) async-start(bf16[8,528,128]{2,1,0:T(8,128)(2,1)} %copy-done.3), calls=%async_computation.1 | async-start | bytes 2162688 | tf_op jit(solution)/shard_map/all_to_all | solution.py:519
  56.2 12.0 %collective-permute-start.7 = (bf16[4,384,128]{2,1,0:T(8,128)(2,1)S(1)}, bf16[4,384,128]{2,1,0:T(8,128)(2,1)S(1)}, u32[]{:S(2)}, u32[]{:S(2)}) collective-permute-start(bf16[4,384,128]{2,1,0:T(8,128)(2,1)S(1)} %get-tuple-element.62), channel_id=1, source_target_pairs={{0,16},{16,0},{1,17},{17,1},{2,18},{18,2},{3,19},{19,3},{4,20},{20... | collective-permute-start | bytes 1179656 | tf_op jit(solution)/shard_map/ppermute | solution.py:517
  61.8 32.9 %copy-start.4 = (bf16[64,3072]{1,0:T(8,128)(2,1)}, bf16[64,3072]{1,0:T(8,128)(2,1)S(1)}, u32[]{:S(2)}) copy-start(bf16[64,3072]{1,0:T(8,128)(2,1)S(1)} %broadcast_select_fusion.1.refs_10_) | copy-start | bytes 1179652
  61.8 14.3 %collective-permute-start.9 = (bf16[4,384,128]{2,1,0:T(8,128)(2,1)S(1)}, bf16[4,384,128]{2,1,0:T(8,128)(2,1)S(1)}, u32[]{:S(2)}, u32[]{:S(2)}) collective-permute-start(bf16[4,384,128]{2,1,0:T(8,128)(2,1)S(1)} %get-tuple-element.61), channel_id=1, source_target_pairs={{0,16},{16,0},{1,17},{17,1},{2,18},{18,2},{3,19},{19,3},{4,20},{20... | collective-permute-start | bytes 1179656 | tf_op jit(solution)/shard_map/ppermute | solution.py:517
  68.1 10.5 %collective-permute-start.8 = (bf16[64,3072]{1,0:T(8,128)(2,1)S(1)}, bf16[64,3072]{1,0:T(8,128)(2,1)S(1)}, u32[]{:S(2)}, u32[]{:S(2)}) collective-permute-start(bf16[64,3072]{1,0:T(8,128)(2,1)S(1)} %broadcast_select_fusion.1.refs_10_), channel_id=1, source_target_pairs={{0,1},{1,0},{2,3},{3,2},{4,5},{5,4},{6,7},{7,6},{8,9},{9,8},{10,11... | collective-permute-start | bytes 1179656 | tf_op jit(solution)/shard_map/ppermute | solution.py:496
  68.6 10.0 %collective-permute-start.11 = (bf16[64,3072]{1,0:T(8,128)(2,1)}, bf16[64,3072]{1,0:T(8,128)(2,1)S(1)}, u32[]{:S(2)}, u32[]{:S(2)}) collective-permute-start(bf16[64,3072]{1,0:T(8,128)(2,1)} %collective-permute-done.refs_8_.refs_2_), channel_id=1, source_target_pairs={{0,2},{2,0},{4,6},{6,4},{8,10},{10,8},{12,14},{14,12},{1,3},{3,1},... | collective-permute-start | bytes 1179656 | tf_op jit(solution)/shard_map/ppermute | solution.py:493
  68.6 10.6 %collective-permute-start.12 = (bf16[64,3072]{1,0:T(8,128)(2,1)}, bf16[64,3072]{1,0:T(8,128)(2,1)S(1)}, u32[]{:S(2)}, u32[]{:S(2)}) collective-permute-start(bf16[64,3072]{1,0:T(8,128)(2,1)} %collective-permute-done.5.refs_9_.refs_3_), channel_id=1, source_target_pairs={{0,2},{2,0},{4,6},{6,4},{8,10},{10,8},{12,14},{14,12},{1,3},{3,1},... | collective-permute-start | bytes 1179656 | tf_op jit(solution)/shard_map/ppermute | solution.py:493
  76.2 13.5 %collective-permute-start.13 = (bf16[64,3072]{1,0:T(8,128)(2,1)S(1)}, bf16[64,3072]{1,0:T(8,128)(2,1)S(1)}, u32[]{:S(2)}, u32[]{:S(2)}) collective-permute-start(bf16[64,3072]{1,0:T(8,128)(2,1)S(1)} %broadcast_select_fusion.refs_6_), channel_id=1, source_target_pairs={{0,2},{2,0},{4,6},{6,4},{8,10},{10,8},{12,14},{14,12},{1,3},{3,1},... | collective-permute-start | bytes 1179656 | tf_op jit(solution)/shard_map/ppermute | solution.py:493
  78.6 11.1 %collective-permute-start.14 = (bf16[64,3072]{1,0:T(8,128)(2,1)}, bf16[64,3072]{1,0:T(8,128)(2,1)S(1)}, u32[]{:S(2)}, u32[]{:S(2)}) collective-permute-start(bf16[64,3072]{1,0:T(8,128)(2,1)} %collective-permute-done.6.refs_7_), channel_id=1, source_target_pairs={{0,2},{2,0},{4,6},{6,4},{8,10},{10,8},{12,14},{14,12},{1,3},{3,1},... | collective-permute-start | bytes 1179656 | tf_op jit(solution)/shard_map/ppermute | solution.py:493
  78.6 11.1 %collective-permute-start.15 = (bf16[64,3072]{1,0:T(8,128)(2,1)S(1)}, bf16[64,3072]{1,0:T(8,128)(2,1)S(1)}, u32[]{:S(2)}, u32[]{:S(2)}) collective-permute-start(bf16[64,3072]{1,0:T(8,128)(2,1)S(1)} %broadcast_select_fusion.1.refs_10_), channel_id=1, source_target_pairs={{0,2},{2,0},{4,6},{6,4},{8,10},{10,8},{12,14},{14,12},{1,3},{3,1},... | collective-permute-start | bytes 1179656 | tf_op jit(solution)/shard_map/ppermute | solution.py:493
  79.1 10.6 %collective-permute-start.16 = (bf16[64,3072]{1,0:T(8,128)(2,1)S(1)}, bf16[64,3072]{1,0:T(8,128)(2,1)S(1)}, u32[]{:S(2)}, u32[]{:S(2)}) collective-permute-start(bf16[64,3072]{1,0:T(8,128)(2,1)S(1)} %collective-permute-done.8.refs_11_), channel_id=1, source_target_pairs={{0,2},{2,0},{4,6},{6,4},{8,10},{10,8},{12,14},{14,12},{1,3},{3,1},... | collective-permute-start | bytes 1179656 | tf_op jit(solution)/shard_map/ppermute | solution.py:493
  85.5 31.2 %collective-permute-start.18 = (bf16[2,512,128]{2,1,0:T(8,128)(2,1)}, bf16[2,512,128]{2,1,0:T(8,128)(2,1)}, u32[]{:S(2)}, u32[]{:S(2)}) collective-permute-start(bf16[2,512,128]{2,1,0:T(8,128)(2,1)} %project_kva.1.kva), channel_id=1, source_target_pairs={{0,16},{1,17},{2,18},{3,19},{4,20},{5,21},{6,22},{7,23},{8,24},{9,... | collective-permute-start | bytes 786440 | tf_op jit(solution)/shard_map/ppermute | solution.py:535
  95.6 22.4 %collective-permute-start.17 = (bf16[2,512,128]{2,1,0:T(8,128)(2,1)}, bf16[2,512,128]{2,1,0:T(8,128)(2,1)}, u32[]{:S(2)}, u32[]{:S(2)}) collective-permute-start(bf16[2,512,128]{2,1,0:T(8,128)(2,1)} %project_kvb.1.kvb), channel_id=1, source_target_pairs={{0,16},{1,17},{2,18},{3,19},{4,20},{5,21},{6,22},{7,23},{8,24},{9,... | collective-permute-start | bytes 786440 | tf_op jit(solution)/shard_map/ppermute | solution.py:537
  134.3 10.8 %collective-permute-start.19 = (bf16[128,1536]{1,0:T(8,128)(2,1)}, bf16[128,1536]{1,0:T(8,128)(2,1)}, u32[]{:S(2)}, u32[]{:S(2)}) collective-permute-start(bf16[128,1536]{1,0:T(8,128)(2,1)} %out_sent.1), channel_id=1, source_target_pairs={{0,1},{1,0},{2,3},{3,2},{4,5},{5,4},{6,7},{7,6},{8,9},{9,8},{10,11... | collective-permute-start | bytes 1179656 | tf_op jit(solution)/shard_map/ppermute | solution.py:496
  (32 other events, 189.4 us)

commit v10 on v9

--- a/solution.py
+++ b/solution.py
@@ -9,6 +9,7 @@
 GRID_W = 64
 TILE = 128
 VMEM_LIMIT = 24 * 1024 * 1024
+VMEM_WHOLE = 56 * 1024 * 1024
 
 
 def axis_freqs(width):
@@ -96,7 +97,7 @@
             jax.ShapeDtypeStruct((rows, depth), jnp.bfloat16),
             jax.ShapeDtypeStruct((rows // 2, depth), jnp.bfloat16),
         ],
-        10 * rows * depth, 4 * rows * depth, 0,
+        10 * rows * depth, 4 * rows * depth, 0, VMEM_WHOLE,
         in_specs=[SMEM, HBM, HBM],
         out_specs=[VMEM, VMEM],
         scratch_shapes=[
@@ -122,7 +123,7 @@
     return call(
         kv_weights_kernel, "kv_weights",
         jax.ShapeDtypeStruct((width // HEAD_DIM, depth, HEAD_DIM), w.dtype),
-        0, 4 * depth * width, 0,
+        0, 4 * depth * width, 0, VMEM_WHOLE,
         in_specs=[SMEM, HBM],
         out_specs=VMEM,
         scratch_shapes=[pltpu.VMEM((2, depth // 2, width), w.dtype), pltpu.SemaphoreType.DMA((2,))],
@@ -144,7 +145,7 @@
     shape = (heads, w.shape[1] + count + mask.shape[0], HEAD_DIM)
     return call(
         direct_kernel, "direct_rows", jax.ShapeDtypeStruct(shape, w.dtype),
-        0, 4 * heads * shape[1] * HEAD_DIM, 0,
+        0, 4 * heads * shape[1] * HEAD_DIM, 0, VMEM_WHOLE,
         in_specs=[HBM, HBM, VMEM],
         out_specs=VMEM,
         scratch_shapes=[
@@ -239,7 +240,7 @@
     return call(
         lambda *refs: kv_kernel(chunk, *refs), "project_kv" + "ab"[chunk],
         jax.ShapeDtypeStruct((2, rows, HEAD_DIM), jnp.bfloat16),
-        4 * rows * depth * HEAD_DIM, 2 * (rows * depth + 2 * mine.size), 0,
+        4 * rows * depth * HEAD_DIM, 2 * (rows * depth + 2 * mine.size), 0, VMEM_WHOLE,
         in_specs=[SMEM, VMEM, VMEM] + [HBM] * (3 + len(pieces)),
         out_specs=VMEM,
         scratch_shapes=[
@@ -377,7 +378,7 @@
             jax.ShapeDtypeStruct((rows, HEAD_DIM), jnp.float32),
             jax.ShapeDtypeStruct((row_tiles.shape[0], rows), jnp.float32),
         ],
-        2 * rows * HEAD_DIM * (2 * keys + depth), 2 * rows * depth, rows * keys,
+        2 * rows * HEAD_DIM * (2 * keys + depth), 2 * rows * depth, rows * keys, VMEM_WHOLE,
         in_specs=[VMEM] * 6 + [HBM] * (1 + len(pieces)),
         out_specs=[VMEM] * 4,
         scratch_shapes=[
@@ -511,10 +512,10 @@
     direct = direct_rows(rows3, text, mask)
 
     near_tp = to_tp(near)
-    third, near_tp = lax.optimization_barrier((third, near_tp))
-    third_tp = to_tp(third)
     some = seq // 2
     peers = [lax.ppermute(mine[:some], "section", both), lax.ppermute(mine[some:], "section", both)]
+    third, near_tp, peers[0] = lax.optimization_barrier((third, near_tp, peers[0]))
+    third_tp = to_tp(third)
     direct, mine = lax.optimization_barrier((direct, mine))
     direct = lax.all_to_all(direct, "seq", 0, 0)
     cols = w_out.shape[1] // 2
@@ -523,10 +524,9 @@
     w_sent = lax.dynamic_slice_in_dim(w_out, (1 - tp) * cols, cols, 1)
     w_kept = lax.dynamic_slice_in_dim(w_out, tp * cols, cols, 1)
     early = (tabs, gains, row_tiles, key_tiles, place, gate, residual, w_sent, w_kept)
-    fourth, third_tp, peers[0], early = lax.optimization_barrier((fourth, third_tp, peers[0], early))
+    fourth, third_tp, peers[1], early = lax.optimization_barrier((fourth, third_tp, peers[1], early))
     tabs, gains, row_tiles, key_tiles, place, gate, residual, w_sent, w_kept = early
     fourth_tp = to_tp(fourth)
-    fourth, fourth_tp, peers[1] = lax.optimization_barrier((fourth, fourth_tp, peers[1]))
     a = [full, to_core(full), near, near_tp, to_core(near), to_core(near_tp)]
     b = [third, third_tp, to_core(third), to_core(third_tp)]
     b += [fourth, fourth_tp, to_core(fourth), to_core(fourth_tp)]

time: 148 us -> 147 us (level)
  local copies, waits for them, and re-layouts: 28.3 us -> 21.2 us
  Pallas kernels: 27.2 us -> 32.3 us
  other arithmetic: 6.07 us -> 9.71 us
  starting transfers between devices: 36.3 us -> 34.4 us
    unnamed x68 -> x42, local copies, waits for them, and re-layouts: 18.2 us -> 7.62 us
    ppermute x5, waiting for transfers between devices: 9.55 us -> 0.01 us  [along_z(): return lax.ppermute(x, 'seq', z_pairs(seq, pairs))]
    ppermute x4, waiting for transfers between devices: 13.3 us -> 18.9 us  [to_tp(): return lax.ppermute(x, 'tp', both)]
    ppermute x1, waiting for transfers between devices: 4.72 us -> 8.75 us  [head_body(): lax.ppermute(mine[:some], 'section', both)]
    pallas_call x1, Pallas kernels: 0.25 us -> 3.06 us  [direct_rows(): call(direct_kernel, 'direct_rows', jax.ShapeDtypeStruct(shape, w.dtype),...]
    another operation x2, local copies, waits for them, and re-layouts: 1.91 us -> 3.54 us  [head_body(): text_kv[0].reshape(-1, 2, seq, HEAD_DIM).transpose(2, 1, 0, 3)]
    pallas_call x2, Pallas kernels: 9.86 us -> 11.5 us  [project_kv(): call(lambda *refs: kv_kernel(chunk, *refs), 'project_kv' + 'ab'[chunk], j...]
  transfers between devices with their start and end apart: 22 -> 22, of which waited for: 7 -> 5; matrix products, arithmetic and copies ran while one was open for 10% -> 15% of each run, Pallas kernels for 15% -> 18%
where the time goes in v10:
time: 147 us; the launch traced here: 146 us
  starting transfers between devices  34.4 us (23%)
  waiting for transfers between devices  34.2 us (23%)
  Pallas kernels  32.3 us (22%)
  local copies, waits for them, and re-layouts  21.2 us (14%)
  blocking collectives  13.7 us (9%)
  other arithmetic  9.71 us (7%)
    ppermute x4, waiting for transfers between devices, to_tp(): return lax.ppermute(x, 'tp', both)  18.9 us
    all_to_all x1, blocking collectives, head_body(): attn = lax.all_to_all(attn, 'seq', 0, 0)  13.7 us
    pallas_call x2, Pallas kernels, project_kv(): call(lambda *refs: kv_kernel(chunk, *refs), 'project_kv' + 'ab'[chunk], j...  11.5 us
    ppermute x5, starting transfers between devices, along_z(): return lax.ppermute(x, 'seq', z_pairs(seq, pairs))  10.6 us
    pallas_call x1, Pallas kernels, attend_own(): call(own_kernel, 'attend_own', [jax.ShapeDtypeStruct((rows, HEAD_DIM), jn...  9.68 us
    ppermute x1, waiting for transfers between devices, head_body(): lax.ppermute(mine[:some], 'section', both)  8.75 us
    unnamed x42, local copies, waits for them, and re-layouts  7.62 us
    all_to_all x1, starting transfers between devices, head_body(): direct = lax.all_to_all(direct, 'seq', 0, 0)  7.56 us
  transfers between devices with their start and end apart: 22, of which 5 were waited for; matrix products, arithmetic and copies ran while one was open for 15% of the time, Pallas kernels for 18%

profile of v10, /device:TPU:0, one launch (start us, length us, event | category | flops | bytes accessed | tf_op | source)
XLA Modules:
  0.0 145.9 jit_solution(4082296661826118118)
XLA Ops:
  0.0 3.0 %norm_tokens.1 = (bf16[128,3072]{1,0:T(8,128)(2,1)}, bf16[64,3072]{1,0:T(8,128)(2,1)}) custom-call(s32[1]{0:T(128)} %bitcast.1.tp_ref, bf16[128,3072]{1,0:T(8,128)(2,1)} %bitcast.27, f32[3,1,3072]{2,1,0:T(1,128)} %bitcast.29), custom_call_target="tpu_custom_call" | custom-call | flops 3932160 | bytes 1572864 | tf_op jit(solution)/shard_map/norm_tokens/pallas_call | solution.py:94
  3.0 1.5 collective-permute-start.3
  4.4 5.1 %collective-permute-start = (bf16[64,3072]{1,0:T(8,128)(2,1)}, bf16[64,3072]{1,0:T(8,128)(2,1)S(1)}, u32[]{:S(2)}, u32[]{:S(2)}) collective-permute-start(bf16[64,3072]{1,0:T(8,128)(2,1)} %get-tuple-element.30), channel_id=1, source_target_pairs={{0,4},{2,6},{4,0},{6,2},{8,12},{10,14},{12,8},{14,10},{1,5},{3,7},... | collective-permute-start | bytes 1179656 | tf_op jit(solution)/shard_map/ppermute | solution.py:491
  9.6 2.1 %kv_weights.1 = bf16[8,384,128]{2,1,0:T(8,128)(2,1)} custom-call(s32[1]{0:T(128)} %bitcast.section_ref.refs_0_, bf16[3,384,1024]{2,1,0:T(8,128)(2,1)} %bitcast.25), custom_call_target="tpu_custom_call" | custom-call | bytes 1572864 | tf_op jit(solution)/shard_map/kv_weights/pallas_call | solution.py:123
  11.6 4.2 %all-to-all-start = ((bf16[8,384,128]{2,1,0:T(8,128)(2,1)}), bf16[8,384,128]{2,1,0:T(8,128)(2,1)}, u32[]{:S(2)}, u32[]{:S(2)}) async-start(bf16[8,384,128]{2,1,0:T(8,128)(2,1)} %kv_weights.1), calls=%async_computation | async-start | bytes 1572864 | tf_op jit(solution)/shard_map/all_to_all | solution.py:486
  18.9 4.9 %constant_dynamic-slice_fusion = (bf16[1024,1536]{1,0:T(8,128)(2,1)S(1)}, bf16[1024,1536]{1,0:T(8,128)(2,1)}) fusion(bf16[1024,3072]{1,0:T(8,128)(2,1)} %param.12, s32[]{:T(128)S(6)} %select_n.78, s32[]{:T(128)S(6)} %select_n.79), kind=kLoop, calls=%fused_computation.20 | loop fusion | bytes 12582920 | tf_op jit(solution)/shard_map/dynamic_slice | solution.py:525
  31.8 1.8 %reshape_squeeze.3 = bf16[64,2,8,128]{3,2,1,0:T(8,128)(2,1)} reshape(bf16[1,64,2,1024]{3,2,1,0:T(2,128)(2,1)} %param.9) | data formatting | bytes 524288 | tf_op jit(solution)/shard_map/reshape;squeeze | solution.py:508
  33.6 1.7 %copy.10 = bf16[64,2,8,128]{3,0,1,2:T(8,128)(2,1)} copy(bf16[64,2,8,128]{3,2,1,0:T(8,128)(2,1)} %reshape_squeeze.3) | data formatting | bytes 524288 | tf_op jit(solution)/shard_map/reshape;squeeze | solution.py:508
  36.6 3.1 %direct_rows.1 = bf16[8,528,128]{2,1,0:T(8,128)(2,1)} custom-call(bf16[3,384,1024]{2,1,0:T(8,128)(2,1)} %bitcast.26, bf16[8,128,128]{2,1,0:T(8,128)(2,1)} %bitcast.28, bf16[16,128]{1,0:T(8,128)(2,1)} %pad.4.mask_ref), custom_call_target="tpu_custom_call" | custom-call | bytes 2162688 | tf_op jit(solution)/shard_map/direct_rows/pallas_call | solution.py:146
  40.3 1.5 %collective-permute-start.5 = (bf16[64,3072]{1,0:T(8,128)(2,1)S(1)}, bf16[64,3072]{1,0:T(8,128)(2,1)}, u32[]{:S(2)}, u32[]{:S(2)}) collective-permute-start(bf16[64,3072]{1,0:T(8,128)(2,1)S(1)} %collective-permute-done.refs_8_.refs_2_), channel_id=1, source_target_pairs={{0,1},{1,0},{2,3},{3,2},{4,5},{5,4},{6,7},{7,6},{8,9},{9,8},{10,11... | collective-permute-start | bytes 1179656 | tf_op jit(solution)/shard_map/ppermute | solution.py:497
  43.1 7.6 %all-to-all-start.1 = ((bf16[8,528,128]{2,1,0:T(8,128)(2,1)}), bf16[8,528,128]{2,1,0:T(8,128)(2,1)}, u32[]{:S(2)}, u32[]{:S(2)}) async-start(bf16[8,528,128]{2,1,0:T(8,128)(2,1)} %direct_rows.1), calls=%async_computation.1 | async-start | bytes 2162688 | tf_op jit(solution)/shard_map/all_to_all | solution.py:520
  51.9 1.6 %collective-permute-start.6 = (bf16[4,384,128]{2,1,0:T(8,128)(2,1)S(1)}, bf16[4,384,128]{2,1,0:T(8,128)(2,1)S(1)}, u32[]{:S(2)}, u32[]{:S(2)}) collective-permute-start(bf16[4,384,128]{2,1,0:T(8,128)(2,1)S(1)} %get-tuple-element.58), channel_id=1, source_target_pairs={{0,16},{16,0},{1,17},{17,1},{2,18},{18,2},{3,19},{19,3},{4,20},{20... | collective-permute-start | bytes 1179656 | tf_op jit(solution)/shard_map/ppermute | solution.py:516
  55.1 8.8 %collective-permute-done.6.refs_4_ = bf16[4,384,128]{2,1,0:T(8,128)(2,1)S(1)} collective-permute-done((bf16[4,384,128]{2,1,0:T(8,128)(2,1)S(1)}, bf16[4,384,128]{2,1,0:T(8,128)(2,1)S(1)}, u32[]{:S(2)}, u32[]{:S(2)}) %collective-permute-start.6) | collective-permute-done | bytes 393248 | tf_op jit(solution)/shard_map/ppermute | solution.py:516
  65.4 6.5 %collective-permute-done.8.refs_5_ = bf16[4,384,128]{2,1,0:T(8,128)(2,1)S(1)} collective-permute-done((bf16[4,384,128]{2,1,0:T(8,128)(2,1)S(1)}, bf16[4,384,128]{2,1,0:T(8,128)(2,1)S(1)}, u32[]{:S(2)}, u32[]{:S(2)}) %collective-permute-start.8) | collective-permute-done | bytes 393248 | tf_op jit(solution)/shard_map/ppermute | solution.py:516
  71.9 2.3 %collective-permute-done.7.refs_7_ = bf16[64,3072]{1,0:T(8,128)(2,1)S(1)} collective-permute-done((bf16[64,3072]{1,0:T(8,128)(2,1)S(1)}, bf16[64,3072]{1,0:T(8,128)(2,1)S(1)}, u32[]{:S(2)}, u32[]{:S(2)}) %collective-permute-start.7) | collective-permute-done | bytes 393248 | tf_op jit(solution)/shard_map/ppermute | solution.py:497
  75.8 7.9 %collective-permute-done.14.refs_11_ = bf16[64,3072]{1,0:T(8,128)(2,1)S(1)} collective-permute-done((bf16[64,3072]{1,0:T(8,128)(2,1)S(1)}, bf16[64,3072]{1,0:T(8,128)(2,1)S(1)}, u32[]{:S(2)}, u32[]{:S(2)}) %collective-permute-start.14) | collective-permute-done | bytes 393248 | tf_op jit(solution)/shard_map/ppermute | solution.py:497
  84.5 5.7 %project_kva.1.kva = bf16[2,512,128]{2,1,0:T(8,128)(2,1)} custom-call(s32[1]{0:T(128)} %bitcast.section_ref.refs_0_, f32[2,80,128]{2,1,0:T(8,128)} %pad_maximum_fusion.refs_1_.tabs_ref, f32[2,128]{1,0:T(2,128)} %pad_maximum_fusion.1.refs_2_.gain_ref, bf16[8,384,128]{2,1,0:T(8,128)(2,1)} %all-to-all-done.refs_3_, bf16[4,384,128]{2,1,0:T(8,128)(2,1)} %copy-done.17, ...), custom_call_target="tpu_custom_call" | custom-call | flops 805306368 | bytes 4718592 | tf_op jit(solution)/shard_map/project_kva/pallas_call | solution.py:240
  90.3 3.4 %collective-permute-start.18 = (bf16[2,512,128]{2,1,0:T(8,128)(2,1)}, bf16[2,512,128]{2,1,0:T(8,128)(2,1)S(1)}, u32[]{:S(2)}, u32[]{:S(2)}) collective-permute-start(bf16[2,512,128]{2,1,0:T(8,128)(2,1)} %project_kva.1.kva), channel_id=1, source_target_pairs={{0,16},{1,17},{2,18},{3,19},{4,20},{5,21},{6,22},{7,23},{8,24},{9,... | collective-permute-start | bytes 786440 | tf_op jit(solution)/shard_map/ppermute | solution.py:535
  95.6 5.7 %project_kvb.1.kvb = bf16[2,512,128]{2,1,0:T(8,128)(2,1)} custom-call(s32[1]{0:T(128)} %bitcast.section_ref.refs_0_, f32[2,80,128]{2,1,0:T(8,128)} %pad_maximum_fusion.refs_1_.tabs_ref, f32[2,128]{1,0:T(2,128)} %pad_maximum_fusion.1.refs_2_.gain_ref, bf16[8,384,128]{2,1,0:T(8,128)(2,1)} %all-to-all-done.refs_3_, bf16[4,384,128]{2,1,0:T(8,128)(2,1)} %copy-done.17, ...), custom_call_target="tpu_custom_call" | custom-call | flops 805306368 | bytes 4718592 | tf_op jit(solution)/shard_map/project_kvb/pallas_call | solution.py:240
  101.3 2.0 %collective-permute-start.17 = (bf16[2,512,128]{2,1,0:T(8,128)(2,1)}, bf16[2,512,128]{2,1,0:T(8,128)(2,1)}, u32[]{:S(2)}, u32[]{:S(2)}) collective-permute-start(bf16[2,512,128]{2,1,0:T(8,128)(2,1)} %project_kvb.1.kvb), channel_id=1, source_target_pairs={{0,16},{1,17},{2,18},{3,19},{4,20},{5,21},{6,22},{7,23},{8,24},{9,... | collective-permute-start | bytes 786440 | tf_op jit(solution)/shard_map/ppermute | solution.py:537
  103.3 9.7 %attend_own.1 = (bf16[1024,128]{1,0:T(8,128)(2,1)}, f32[1024,128]{1,0:T(8,128)}, f32[1024,128]{1,0:T(8,128)}, f32[16,1024]{1,0:T(8,128)}) custom-call(f32[2,80,128]{2,1,0:T(8,128)} %pad_maximum_fusion.refs_1_.tabs_ref, f32[2,128]{1,0:T(2,128)} %pad_maximum_fusion.1.refs_2_.gain_ref, f32[16,8]{1,0:T(8,128)} %fusion.3.rows_ref, f32[128,16]{1,0:T(8,128)} %fusion.1.keys_ref, ...), custom_call_target="tpu_custom_call" | custom-call | flops 1610612736 | bytes 6291456 | tf_op jit(solution)/shard_map/attend_own/pallas_call | solution.py:373
  118.2 13.7 %all_to_all.15.attn_ref = bf16[8,128,128]{2,1,0:T(8,128)(2,1)S(1)} all-to-all(bf16[8,128,128]{2,1,0:T(8,128)(2,1)S(1)} %attend_second.1), channel_id=1, replica_groups=mesh['section'=2,'seq'=8,'tp'=2] {'seq'}, dimensions={0} | all-to-all | bytes 524288 | tf_op jit(solution)/shard_map/all_to_all | solution.py:544
  135.4 8.7 %collective-permute-done.19 = bf16[128,1536]{1,0:T(8,128)(2,1)} collective-permute-done((bf16[128,1536]{1,0:T(8,128)(2,1)}, bf16[128,1536]{1,0:T(8,128)(2,1)}, u32[]{:S(2)}, u32[]{:S(2)}) %collective-permute-start.19) | collective-permute-done | bytes 393248 | tf_op jit(solution)/shard_map/ppermute | solution.py:497
  144.0 1.8 %fusion = bf16[1,128,1536]{2,1,0:T(8,128)(2,1)} fusion(f32[128,1536]{1,0:T(8,128)S(1)} %out_kept.1, bf16[128,1536]{1,0:T(8,128)(2,1)} %collective-permute-done.19, f32[1536]{0:T(1024)S(1)} %reduce), kind=kLoop, calls=%fused_computation.1 | loop fusion | flops 786432 | bytes 1579008 | tf_op jit(solution)/shard_map/broadcast_in_dim | solution.py:547
  (112 shorter events, 31.2 us)
Async XLA Ops:
  3.0 26.3 %collective-permute-start.3 = (bf16[64,3072]{1,0:T(8,128)(2,1)}, bf16[64,3072]{1,0:T(8,128)(2,1)}, u32[]{:S(2)}, u32[]{:S(2)}) collective-permute-start(bf16[64,3072]{1,0:T(8,128)(2,1)} %get-tuple-element.30), channel_id=1, source_target_pairs={{4,8},{6,10},{8,4},{10,6},{5,9},{7,11},{9,5},{11,7},{20,24},{22,26... | collective-permute-start | bytes 1179656 | tf_op jit(solution)/shard_map/ppermute | solution.py:491
  4.4 21.4 %collective-permute-start = (bf16[64,3072]{1,0:T(8,128)(2,1)}, bf16[64,3072]{1,0:T(8,128)(2,1)S(1)}, u32[]{:S(2)}, u32[]{:S(2)}) collective-permute-start(bf16[64,3072]{1,0:T(8,128)(2,1)} %get-tuple-element.30), channel_id=1, source_target_pairs={{0,4},{2,6},{4,0},{6,2},{8,12},{10,14},{12,8},{14,10},{1,5},{3,7},... | collective-permute-start | bytes 1179656 | tf_op jit(solution)/shard_map/ppermute | solution.py:491
  11.6 31.5 %all-to-all-start = ((bf16[8,384,128]{2,1,0:T(8,128)(2,1)}), bf16[8,384,128]{2,1,0:T(8,128)(2,1)}, u32[]{:S(2)}, u32[]{:S(2)}) async-start(bf16[8,384,128]{2,1,0:T(8,128)(2,1)} %kv_weights.1), calls=%async_computation | async-start | bytes 1572864 | tf_op jit(solution)/shard_map/all_to_all | solution.py:486
  15.9 59.4 %collective-permute-start.9 = (bf16[128,3072]{1,0:T(8,128)(2,1)}, bf16[128,3072]{1,0:T(8,128)(2,1)}, u32[]{:S(2)}, u32[]{:S(2)}) collective-permute-start(bf16[128,3072]{1,0:T(8,128)(2,1)} %get-tuple-element.40.refs_6_.refs_0_), channel_id=1, source_target_pairs={{0,2},{2,0},{4,6},{6,4},{8,10},{10,8},{12,14},{14,12},{1,3},{3,1},... | collective-permute-start | bytes 2359304 | tf_op jit(solution)/shard_map/ppermute | solution.py:494
  25.8 16.0 %collective-permute-start.1 = (bf16[64,3072]{1,0:T(8,128)(2,1)S(1)}, bf16[64,3072]{1,0:T(8,128)(2,1)}, u32[]{:S(2)}, u32[]{:S(2)}) collective-permute-start(bf16[64,3072]{1,0:T(8,128)(2,1)S(1)} %collective-permute-done.refs_8_.refs_2_), channel_id=1, source_target_pairs={{4,8},{6,10},{8,4},{10,6},{5,9},{7,11},{9,5},{11,7},{20,24},{22,26... | collective-permute-start | bytes 1179656 | tf_op jit(solution)/shard_map/ppermute | solution.py:491
  29.3 22.6 %collective-permute-start.4 = (bf16[64,3072]{1,0:T(8,128)(2,1)}, bf16[64,3072]{1,0:T(8,128)(2,1)}, u32[]{:S(2)}, u32[]{:S(2)}) collective-permute-start(bf16[64,3072]{1,0:T(8,128)(2,1)} %collective-permute-done.3), channel_id=1, source_target_pairs={{4,0},{6,2},{8,12},{10,14},{5,1},{7,3},{9,13},{11,15},{20,16},{22,... | collective-permute-start | bytes 1179656 | tf_op jit(solution)/shard_map/ppermute | solution.py:491
  40.3 14.2 %collective-permute-start.5 = (bf16[64,3072]{1,0:T(8,128)(2,1)S(1)}, bf16[64,3072]{1,0:T(8,128)(2,1)}, u32[]{:S(2)}, u32[]{:S(2)}) collective-permute-start(bf16[64,3072]{1,0:T(8,128)(2,1)S(1)} %collective-permute-done.refs_8_.refs_2_), channel_id=1, source_target_pairs={{0,1},{1,0},{2,3},{3,2},{4,5},{5,4},{6,7},{7,6},{8,9},{9,8},{10,11... | collective-permute-start | bytes 1179656 | tf_op jit(solution)/shard_map/ppermute | solution.py:497
  41.8 33.4 %collective-permute-start.10 = (bf16[64,3072]{1,0:T(8,128)(2,1)S(1)}, bf16[64,3072]{1,0:T(8,128)(2,1)}, u32[]{:S(2)}, u32[]{:S(2)}) collective-permute-start(bf16[64,3072]{1,0:T(8,128)(2,1)S(1)} %collective-permute-done.refs_8_.refs_2_), channel_id=1, source_target_pairs={{0,2},{2,0},{4,6},{6,4},{8,10},{10,8},{12,14},{14,12},{1,3},{3,1},... | collective-permute-start | bytes 1179656 | tf_op jit(solution)/shard_map/ppermute | solution.py:494
  41.8 22.5 %collective-permute-start.2 = (bf16[64,3072]{1,0:T(8,128)(2,1)}, bf16[64,3072]{1,0:T(8,128)(2,1)}, u32[]{:S(2)}, u32[]{:S(2)}) collective-permute-start(bf16[64,3072]{1,0:T(8,128)(2,1)} %collective-permute-done.1), channel_id=1, source_target_pairs={{4,0},{6,2},{8,12},{10,14},{5,1},{7,3},{9,13},{11,15},{20,16},{22,... | collective-permute-start | bytes 1179656 | tf_op jit(solution)/shard_map/ppermute | solution.py:491
  43.1 60.2 %all-to-all-start.1 = ((bf16[8,528,128]{2,1,0:T(8,128)(2,1)}), bf16[8,528,128]{2,1,0:T(8,128)(2,1)}, u32[]{:S(2)}, u32[]{:S(2)}) async-start(bf16[8,528,128]{2,1,0:T(8,128)(2,1)} %direct_rows.1), calls=%async_computation.1 | async-start | bytes 2162688 | tf_op jit(solution)/shard_map/all_to_all | solution.py:520
  51.9 12.0 %collective-permute-start.6 = (bf16[4,384,128]{2,1,0:T(8,128)(2,1)S(1)}, bf16[4,384,128]{2,1,0:T(8,128)(2,1)S(1)}, u32[]{:S(2)}, u32[]{:S(2)}) collective-permute-start(bf16[4,384,128]{2,1,0:T(8,128)(2,1)S(1)} %get-tuple-element.58), channel_id=1, source_target_pairs={{0,16},{16,0},{1,17},{17,1},{2,18},{18,2},{3,19},{19,3},{4,20},{20... | collective-permute-start | bytes 1179656 | tf_op jit(solution)/shard_map/ppermute | solution.py:516
  54.5 39.3 %copy-start.6 = (bf16[64,3072]{1,0:T(8,128)(2,1)}, bf16[64,3072]{1,0:T(8,128)(2,1)S(1)}, u32[]{:S(2)}) copy-start(bf16[64,3072]{1,0:T(8,128)(2,1)S(1)} %broadcast_select_fusion.refs_6_) | copy-start | bytes 1179652
  54.5 17.4 %collective-permute-start.8 = (bf16[4,384,128]{2,1,0:T(8,128)(2,1)S(1)}, bf16[4,384,128]{2,1,0:T(8,128)(2,1)S(1)}, u32[]{:S(2)}, u32[]{:S(2)}) collective-permute-start(bf16[4,384,128]{2,1,0:T(8,128)(2,1)S(1)} %get-tuple-element.57), channel_id=1, source_target_pairs={{0,16},{16,0},{1,17},{17,1},{2,18},{18,2},{3,19},{19,3},{4,20},{20... | collective-permute-start | bytes 1179656 | tf_op jit(solution)/shard_map/ppermute | solution.py:516
  63.9 10.4 %collective-permute-start.7 = (bf16[64,3072]{1,0:T(8,128)(2,1)S(1)}, bf16[64,3072]{1,0:T(8,128)(2,1)S(1)}, u32[]{:S(2)}, u32[]{:S(2)}) collective-permute-start(bf16[64,3072]{1,0:T(8,128)(2,1)S(1)} %broadcast_select_fusion.refs_6_), channel_id=1, source_target_pairs={{0,1},{1,0},{2,3},{3,2},{4,5},{5,4},{6,7},{7,6},{8,9},{9,8},{10,11... | collective-permute-start | bytes 1179656 | tf_op jit(solution)/shard_map/ppermute | solution.py:497
  65.4 28.4 %copy-start.7 = (bf16[64,3072]{1,0:T(8,128)(2,1)}, bf16[64,3072]{1,0:T(8,128)(2,1)S(1)}, u32[]{:S(2)}) copy-start(bf16[64,3072]{1,0:T(8,128)(2,1)S(1)} %broadcast_select_fusion.1.refs_10_) | copy-start | bytes 1179652
  74.2 9.4 %collective-permute-start.14 = (bf16[64,3072]{1,0:T(8,128)(2,1)S(1)}, bf16[64,3072]{1,0:T(8,128)(2,1)S(1)}, u32[]{:S(2)}, u32[]{:S(2)}) collective-permute-start(bf16[64,3072]{1,0:T(8,128)(2,1)S(1)} %broadcast_select_fusion.1.refs_10_), channel_id=1, source_target_pairs={{0,1},{1,0},{2,3},{3,2},{4,5},{5,4},{6,7},{7,6},{8,9},{9,8},{10,11... | collective-permute-start | bytes 1179656 | tf_op jit(solution)/shard_map/ppermute | solution.py:497
  74.7 8.9 %collective-permute-start.11 = (bf16[64,3072]{1,0:T(8,128)(2,1)}, bf16[64,3072]{1,0:T(8,128)(2,1)S(1)}, u32[]{:S(2)}, u32[]{:S(2)}) collective-permute-start(bf16[64,3072]{1,0:T(8,128)(2,1)} %collective-permute-done.5.refs_9_.refs_3_), channel_id=1, source_target_pairs={{0,2},{2,0},{4,6},{6,4},{8,10},{10,8},{12,14},{14,12},{1,3},{3,1},... | collective-permute-start | bytes 1179656 | tf_op jit(solution)/shard_map/ppermute | solution.py:494
  74.7 19.0 %collective-permute-start.12 = (bf16[64,3072]{1,0:T(8,128)(2,1)S(1)}, bf16[64,3072]{1,0:T(8,128)(2,1)S(1)}, u32[]{:S(2)}, u32[]{:S(2)}) collective-permute-start(bf16[64,3072]{1,0:T(8,128)(2,1)S(1)} %broadcast_select_fusion.refs_6_), channel_id=1, source_target_pairs={{0,2},{2,0},{4,6},{6,4},{8,10},{10,8},{12,14},{14,12},{1,3},{3,1},... | collective-permute-start | bytes 1179656 | tf_op jit(solution)/shard_map/ppermute | solution.py:494
  75.2 18.5 %collective-permute-start.15 = (bf16[64,3072]{1,0:T(8,128)(2,1)S(1)}, bf16[64,3072]{1,0:T(8,128)(2,1)S(1)}, u32[]{:S(2)}, u32[]{:S(2)}) collective-permute-start(bf16[64,3072]{1,0:T(8,128)(2,1)S(1)} %broadcast_select_fusion.1.refs_10_), channel_id=1, source_target_pairs={{0,2},{2,0},{4,6},{6,4},{8,10},{10,8},{12,14},{14,12},{1,3},{3,1},... | collective-permute-start | bytes 1179656 | tf_op jit(solution)/shard_map/ppermute | solution.py:494
  75.3 18.5 %collective-permute-start.13 = (bf16[64,3072]{1,0:T(8,128)(2,1)S(1)}, bf16[64,3072]{1,0:T(8,128)(2,1)S(1)}, u32[]{:S(2)}, u32[]{:S(2)}) collective-permute-start(bf16[64,3072]{1,0:T(8,128)(2,1)S(1)} %collective-permute-done.7.refs_7_), channel_id=1, source_target_pairs={{0,2},{2,0},{4,6},{6,4},{8,10},{10,8},{12,14},{14,12},{1,3},{3,1},... | collective-permute-start | bytes 1179656 | tf_op jit(solution)/shard_map/ppermute | solution.py:494
  83.7 10.1 %collective-permute-start.16 = (bf16[64,3072]{1,0:T(8,128)(2,1)S(1)}, bf16[64,3072]{1,0:T(8,128)(2,1)S(1)}, u32[]{:S(2)}, u32[]{:S(2)}) collective-permute-start(bf16[64,3072]{1,0:T(8,128)(2,1)S(1)} %collective-permute-done.14.refs_11_), channel_id=1, source_target_pairs={{0,2},{2,0},{4,6},{6,4},{8,10},{10,8},{12,14},{14,12},{1,3},{3,1},... | collective-permute-start | bytes 1179656 | tf_op jit(solution)/shard_map/ppermute | solution.py:494
  90.3 22.7 %collective-permute-start.18 = (bf16[2,512,128]{2,1,0:T(8,128)(2,1)}, bf16[2,512,128]{2,1,0:T(8,128)(2,1)S(1)}, u32[]{:S(2)}, u32[]{:S(2)}) collective-permute-start(bf16[2,512,128]{2,1,0:T(8,128)(2,1)} %project_kva.1.kva), channel_id=1, source_target_pairs={{0,16},{1,17},{2,18},{3,19},{4,20},{5,21},{6,22},{7,23},{8,24},{9,... | collective-permute-start | bytes 786440 | tf_op jit(solution)/shard_map/ppermute | solution.py:535
  101.3 15.8 %collective-permute-start.17 = (bf16[2,512,128]{2,1,0:T(8,128)(2,1)}, bf16[2,512,128]{2,1,0:T(8,128)(2,1)}, u32[]{:S(2)}, u32[]{:S(2)}) collective-permute-start(bf16[2,512,128]{2,1,0:T(8,128)(2,1)} %project_kvb.1.kvb), channel_id=1, source_target_pairs={{0,16},{1,17},{2,18},{3,19},{4,20},{5,21},{6,22},{7,23},{8,24},{9,... | collective-permute-start | bytes 786440 | tf_op jit(solution)/shard_map/ppermute | solution.py:537
  133.2 10.8 %collective-permute-start.19 = (bf16[128,1536]{1,0:T(8,128)(2,1)}, bf16[128,1536]{1,0:T(8,128)(2,1)}, u32[]{:S(2)}, u32[]{:S(2)}) collective-permute-start(bf16[128,1536]{1,0:T(8,128)(2,1)} %out_sent.1), channel_id=1, source_target_pairs={{0,1},{1,0},{2,3},{3,2},{4,5},{5,4},{6,7},{7,6},{8,9},{9,8},{10,11... | collective-permute-start | bytes 1179656 | tf_op jit(solution)/shard_map/ppermute | solution.py:497
  (19 other events, 131.3 us)

commit v11 on v10

--- a/solution.py
+++ b/solution.py
@@ -198,8 +198,9 @@
         at += ref.shape[0]
 
 
-def kv_kernel(chunk, section_ref, tabs_ref, gain_ref, mine_hbm, peer_a, peer_b, *refs):
-    piece_refs, (kv_ref, x_ref, mine, peer, w_ref, sems) = refs[:-6], refs[-6:]
+def kv_kernel(chunk, section_ref, tabs_hbm, gain_hbm, mine_hbm, peer_a, peer_b, *refs):
+    piece_refs = refs[:-8]
+    kv_ref, x_ref, mine, peer, w_ref, tabs_ref, gain_ref, sems = refs[-8:]
     sources, held, _ = mine.shape
     half = held // 2
     some = sources // 2
@@ -208,10 +209,12 @@
             (mine_hbm, mine),
             (peer_a, peer.at[pl.ds(0, some)]),
             (peer_b, peer.at[pl.ds(some, some)]),
+            (tabs_hbm, tabs_ref),
+            (gain_hbm, gain_ref),
         ],
         sems,
     )
-    tokens = started(piece_copies(piece_refs, x_ref), sems, 3)
+    tokens = started(piece_copies(piece_refs, x_ref), sems, 5)
     finished(weights)
     first = section_ref[0] == 0
     for s in range(sources):
@@ -241,14 +244,16 @@
         lambda *refs: kv_kernel(chunk, *refs), "project_kv" + "ab"[chunk],
         jax.ShapeDtypeStruct((2, rows, HEAD_DIM), jnp.bfloat16),
         4 * rows * depth * HEAD_DIM, 2 * (rows * depth + 2 * mine.size), 0, VMEM_WHOLE,
-        in_specs=[SMEM, VMEM, VMEM] + [HBM] * (3 + len(pieces)),
+        in_specs=[SMEM] + [HBM] * (5 + len(pieces)),
         out_specs=VMEM,
         scratch_shapes=[
             pltpu.VMEM((rows, depth), jnp.bfloat16),
             pltpu.VMEM(mine.shape, jnp.bfloat16),
             pltpu.VMEM(mine.shape, jnp.bfloat16),
             pltpu.VMEM((depth, 2 * HEAD_DIM), jnp.bfloat16),
-            pltpu.SemaphoreType.DMA((3 + len(pieces),)),
+            pltpu.VMEM(tabs.shape, tabs.dtype),
+            pltpu.VMEM(gains.shape, gains.dtype),
+            pltpu.SemaphoreType.DMA((5 + len(pieces),)),
         ],
     )(section, tabs, gains, mine, *peers, *pieces)
 
@@ -276,13 +281,16 @@
 BLOCK = 256
 
 
-def own_kernel(tabs_ref, gain_ref, rows_ref, keys_ref, kva, kvb, direct_hbm, *refs):
-    piece_refs = refs[:-7]
-    q_ref, num_ref, den_ref, keep_ref, x_ref, direct, sems = refs[-7:]
+def own_kernel(
+    section_ref, rows_ref, keys_ref, kva, kvb, cond, tabs_hbm, gain_hbm, direct_hbm, *refs
+):
+    piece_refs = refs[:-9]
+    q_ref, num_ref, den_ref, keep_ref, x_ref, direct, tabs_ref, gain_ref, sems = refs[-9:]
     rows, depth = x_ref.shape
     sources, held, _ = direct.shape
     copies = started([(direct_hbm.at[s], direct.at[s]) for s in range(sources)], sems)
-    tokens = started(piece_copies(piece_refs, x_ref), sems, sources)
+    copies += started([(tabs_hbm, tabs_ref), (gain_hbm, gain_ref)], sems, sources)
+    tokens = started(piece_copies(piece_refs, x_ref), sems, sources + 2)
     finished(copies)
     wide = depth // sources
     w = direct[:, :wide, :].reshape(depth, HEAD_DIM)
@@ -318,6 +326,13 @@
             mask[:, g : g + 1], (keep_ref.shape[0], size)
         )
 
+    @pl.when(section_ref[0] != 0)
+    def _():
+        for b, at in blocks(rows):
+            num, den = cond_sum(keep_ref, q_ref, cond, 0, b)
+            num_ref[at, :] += num
+            den_ref[at, :] += jnp.broadcast_to(den, num.shape)
+
 
 def cond_sum(keep_ref, q_ref, cond, chunk, b):
     groups = keep_ref.shape[0] * BLOCK // q_ref.shape[0]
@@ -326,24 +341,17 @@
     return summed(kept_weights(q_ref[b * BLOCK : (b + 1) * BLOCK, :], cond, keep), cond[1])
 
 
-def first_cond_kernel(section_ref, keep_ref, q_ref, cond, num_in, den_in, num_ref, den_ref):
-    @pl.when(section_ref[0] == 0)
-    def _():
-        num_ref[...] = num_in[...]
-        den_ref[...] = den_in[...]
-
-    @pl.when(section_ref[0] != 0)
-    def _():
-        for b in range(num_ref.shape[0] // BLOCK):
-            at = slice(b * BLOCK, (b + 1) * BLOCK)
-            num, den = cond_sum(keep_ref, q_ref, cond, 0, b)
-            num_ref[at, :] = num_in[at, :] + num
-            den_ref[at, :] = den_in[at, :] + den
-
-
-def second_cond_kernel(section_ref, place_ref, keep_ref, q_ref, cond, num_ref, den_ref, out_ref):
+def second_cond_kernel(
+    section_ref, place_ref, keep_hbm, q_hbm, num_hbm, den_hbm, cond, out_ref,
+    keep_ref, q_ref, num_ref, den_ref, sems,
+):
     groups = keep_ref.shape[0] * BLOCK // num_ref.shape[0]
     size = BLOCK // groups
+    finished(
+        started(
+            [(num_hbm, num_ref), (den_hbm, den_ref), (q_hbm, q_ref), (keep_hbm, keep_ref)], sems
+        )
+    )
 
     def store(b, num, den):
         value = (num / den).astype(jnp.bfloat16)
@@ -354,22 +362,20 @@
 
     @pl.when(section_ref[0] == 0)
     def _():
-        for b in range(num_ref.shape[0] // BLOCK):
-            at = slice(b * BLOCK, (b + 1) * BLOCK)
+        for b, at in blocks(num_ref.shape[0]):
             store(b, num_ref[at, :], den_ref[at, :])
 
     @pl.when(section_ref[0] != 0)
     def _():
-        for b in range(num_ref.shape[0] // BLOCK):
-            at = slice(b * BLOCK, (b + 1) * BLOCK)
+        for b, at in blocks(num_ref.shape[0]):
             num, den = cond_sum(keep_ref, q_ref, cond, 1, b)
             store(b, num_ref[at, :] + num, den_ref[at, :] + den)
 
 
-def attend_own(tabs, gains, row_tiles, key_tiles, kvs, direct, pieces):
+def attend_own(section, tabs, gains, row_tiles, key_tiles, kvs, cond, direct, pieces):
     depth = pieces[0].shape[1]
     rows = sum(p.shape[0] for p in pieces)
-    keys = rows + rows // 2
+    keys = 2 * rows
     return call(
         own_kernel, "attend_own",
         [
@@ -379,24 +385,16 @@
             jax.ShapeDtypeStruct((row_tiles.shape[0], rows), jnp.float32),
         ],
         2 * rows * HEAD_DIM * (2 * keys + depth), 2 * rows * depth, rows * keys, VMEM_WHOLE,
-        in_specs=[VMEM] * 6 + [HBM] * (1 + len(pieces)),
+        in_specs=[SMEM] + [VMEM] * 5 + [HBM] * (3 + len(pieces)),
         out_specs=[VMEM] * 4,
         scratch_shapes=[
             pltpu.VMEM((rows, depth), jnp.bfloat16),
             pltpu.VMEM(direct.shape, jnp.bfloat16),
-            pltpu.SemaphoreType.DMA((direct.shape[0] + len(pieces),)),
-        ],
-    )(tabs, gains, row_tiles, key_tiles, *kvs, direct, *pieces)
-
-
-def attend_first(section, keep, query, cond, num, den):
-    rows, keys = num.shape[0], cond.shape[1]
-    return call(
-        first_cond_kernel, "attend_first", [jax.ShapeDtypeStruct(num.shape, jnp.float32)] * 2,
-        4 * rows * keys * HEAD_DIM, 2 * rows * HEAD_DIM * 8, rows * keys,
-        in_specs=[SMEM] + [VMEM] * 5,
-        out_specs=[VMEM] * 2,
-    )(section, keep, query, cond, num, den)
+            pltpu.VMEM(tabs.shape, tabs.dtype),
+            pltpu.VMEM(gains.shape, gains.dtype),
+            pltpu.SemaphoreType.DMA((direct.shape[0] + 2 + len(pieces),)),
+        ],
+    )(section, row_tiles, key_tiles, *kvs, cond, tabs, gains, direct, *pieces)
 
 
 def attend_second(section, place, keep, query, cond, num, den, seq):
@@ -404,10 +402,12 @@
     return call(
         second_cond_kernel, "attend_second",
         jax.ShapeDtypeStruct((seq, rows // seq, HEAD_DIM), jnp.bfloat16),
-        4 * rows * keys * HEAD_DIM, 2 * rows * HEAD_DIM * 8, rows * keys,
-        in_specs=[SMEM, SMEM] + [VMEM] * 5,
+        4 * rows * keys * HEAD_DIM, 2 * rows * HEAD_DIM * 8, rows * keys, VMEM_WHOLE,
+        in_specs=[SMEM, SMEM] + [HBM] * 4 + [VMEM],
         out_specs=VMEM,
-    )(section, place, keep, query, cond, num, den)
+        scratch_shapes=[pltpu.VMEM(x.shape, x.dtype) for x in (keep, query, num, den)]
+        + [pltpu.SemaphoreType.DMA((4,))],
+    )(section, place, keep, query, num, den, cond)
 
 
 def token_rows(attn_ref):
@@ -466,8 +466,48 @@
     tp_at = tp.astype(jnp.int32).reshape(1)
     both = [(0, 1), (1, 0)]
 
-    upper = chip >= 2
-    chips = jnp.stack([chip, chip ^ 1, jnp.where(upper, 1, 2), jnp.where(upper, 0, 3)])
+    rows3 = w_qkv.transpose(1, 0, 2)
+    mine = lax.all_to_all(kv_weights(section_at, rows3), "seq", 0, 0)
+
+    full, part = norm_tokens(tp_at, image[0], modulation.transpose(1, 0, 2))
+
+    def along_z(x, pairs):
+        return lax.ppermute(x, "seq", z_pairs(seq, pairs))
+
+    def to_core(x):
+        return lax.ppermute(x, "seq", [(s, s ^ 1) for s in range(seq)])
+
+    def to_tp(x):
+        return lax.ppermute(x, "tp", both)
+
+    near = along_z(part, [(0, 1), (1, 0), (2, 3), (3, 2)])
+    middle = along_z(part, [(1, 2), (2, 1)])
+    far = along_z(near, [(1, 2), (2, 1)])
+    middle_end = along_z(middle, [(1, 0), (2, 3)])
+    far_end = along_z(far, [(1, 0), (2, 3)])
+    inner = (chip == 1) | (chip == 2)
+    third = jnp.where(inner, middle, middle_end)
+    fourth = jnp.where(inner, far, far_end)
+
+    text = text_kv[0].reshape(-1, 2, seq, HEAD_DIM).transpose(2, 1, 0, 3).reshape(seq, -1, HEAD_DIM)
+    mask = jnp.pad(
+        region_mask.astype(jnp.bfloat16), ((0, 15), (0, HEAD_DIM - region_mask.shape[1]))
+    )
+    direct = direct_rows(rows3, text, mask)
+
+    near_tp = to_tp(near)
+    direct, mine, w_late, at_chip = lax.optimization_barrier(
+        (direct, mine, w_out, chip.astype(jnp.int32))
+    )
+    direct = lax.all_to_all(direct, "seq", 0, 0)
+    some = seq // 2
+    peers = [lax.ppermute(mine[:some], "section", both), lax.ppermute(mine[some:], "section", both)]
+    cols = w_out.shape[1] // 2
+    w_sent = lax.dynamic_slice_in_dim(w_late, (1 - tp) * cols, cols, 1)
+    w_kept = lax.dynamic_slice_in_dim(w_late, tp * cols, cols, 1)
+
+    upper = at_chip >= 2
+    chips = jnp.stack([at_chip, at_chip ^ 1, jnp.where(upper, 1, 2), jnp.where(upper, 0, 3)])
     cores = jnp.stack([core, 1 - core])
     parts = jnp.stack([tp, 1 - tp])
     shards = chips[:, None, None] * 2 + cores[None, :, None] + 0 * parts[None, None, :]
@@ -482,66 +522,29 @@
     key_tiles = key_tiles.astype(jnp.float32)
     place = jnp.stack([shards, parts])
 
-    rows3 = w_qkv.transpose(1, 0, 2)
-    mine = lax.all_to_all(kv_weights(section_at, rows3), "seq", 0, 0)
-
-    full, part = norm_tokens(tp_at, image[0], modulation.transpose(1, 0, 2))
-
-    def along_z(x, pairs):
-        return lax.ppermute(x, "seq", z_pairs(seq, pairs))
-
-    def to_core(x):
-        return lax.ppermute(x, "seq", [(s, s ^ 1) for s in range(seq)])
-
-    def to_tp(x):
-        return lax.ppermute(x, "tp", both)
-
-    near = along_z(part, [(0, 1), (1, 0), (2, 3), (3, 2)])
-    middle = along_z(part, [(1, 2), (2, 1)])
-    far = along_z(near, [(1, 2), (2, 1)])
-    middle_end = along_z(middle, [(1, 0), (2, 3)])
-    far_end = along_z(far, [(1, 0), (2, 3)])
-    inner = (chip == 1) | (chip == 2)
-    third = jnp.where(inner, middle, middle_end)
-    fourth = jnp.where(inner, far, far_end)
-
-    text = text_kv[0].reshape(-1, 2, seq, HEAD_DIM).transpose(2, 1, 0, 3).reshape(seq, -1, HEAD_DIM)
-    mask = jnp.pad(
-        region_mask.astype(jnp.bfloat16), ((0, 15), (0, HEAD_DIM - region_mask.shape[1]))
-    )
-    direct = direct_rows(rows3, text, mask)
-
-    near_tp = to_tp(near)
-    some = seq // 2
-    peers = [lax.ppermute(mine[:some], "section", both), lax.ppermute(mine[some:], "section", both)]
-    third, near_tp, peers[0] = lax.optimization_barrier((third, near_tp, peers[0]))
+    early = (tabs, gains, row_tiles, key_tiles, place, w_sent, w_kept)
+    third, near_tp, peers[0], early = lax.optimization_barrier((third, near_tp, peers[0], early))
+    tabs, gains, row_tiles, key_tiles, place, w_sent, w_kept = early
     third_tp = to_tp(third)
-    direct, mine = lax.optimization_barrier((direct, mine))
-    direct = lax.all_to_all(direct, "seq", 0, 0)
-    cols = w_out.shape[1] // 2
-    gate = lax.dynamic_slice_in_dim(mods[2:3], tp * cols, cols, 1)
-    residual = lax.dynamic_slice_in_dim(image[0], tp * cols, cols, 1)
-    w_sent = lax.dynamic_slice_in_dim(w_out, (1 - tp) * cols, cols, 1)
-    w_kept = lax.dynamic_slice_in_dim(w_out, tp * cols, cols, 1)
-    early = (tabs, gains, row_tiles, key_tiles, place, gate, residual, w_sent, w_kept)
-    fourth, third_tp, peers[1], early = lax.optimization_barrier((fourth, third_tp, peers[1], early))
-    tabs, gains, row_tiles, key_tiles, place, gate, residual, w_sent, w_kept = early
+    fourth, third_tp, peers[1] = lax.optimization_barrier((fourth, third_tp, peers[1]))
     fourth_tp = to_tp(fourth)
     a = [full, to_core(full), near, near_tp, to_core(near), to_core(near_tp)]
-    b = [third, third_tp, to_core(third), to_core(third_tp)]
-    b += [fourth, fourth_tp, to_core(fourth), to_core(fourth_tp)]
-
     kv_a = project_kv(0, section_at, tabs, gains, mine, peers, a)
     cond_a = lax.ppermute(kv_a, "section", [(0, 1)])
+    b = [third, third_tp, to_core(third), to_core(third_tp), fourth, fourth_tp, to_core(fourth)]
+    fourth_tp, kv_a = lax.optimization_barrier((fourth_tp, kv_a))
+    b[5] = fourth_tp
+    b.append(to_core(fourth_tp))
     kv_b = project_kv(1, section_at, tabs, gains, mine, peers, b)
     cond_b = lax.ppermute(kv_b, "section", [(0, 1)])
     query, num, den, keep = attend_own(
-        tabs, gains, row_tiles, key_tiles, (kv_a, kv_b), direct, a + b
-    )
-    num, den = attend_first(section_at, keep, query, cond_a, num, den)
+        section_at, tabs, gains, row_tiles, key_tiles, (kv_a, kv_b), cond_a, direct, a + b
+    )
     attn = attend_second(section_at, place, keep, query, cond_b, num, den, seq)
 
     attn = lax.all_to_all(attn, "seq", 0, 0)
+    gate = lax.dynamic_slice_in_dim(mods[2:3], tp * cols, cols, 1)
+    residual = lax.dynamic_slice_in_dim(image[0], tp * cols, cols, 1)
     other = to_tp(project_out(attn, w_sent))
     kept = project_out(attn, w_kept, residual, gate)
     return (kept + gate * other.astype(jnp.float32)).astype(jnp.bfloat16)[None]

time: 147 us -> 135 us (0.918)
  local copies, waits for them, and re-layouts: 21.2 us -> 12.1 us
  other arithmetic: 9.71 us -> 6.33 us
  starting transfers between devices: 34.4 us -> 37.6 us
  waiting for transfers between devices: 34.2 us -> 31.3 us
    ppermute x5, waiting for transfers between devices: 0.01 us -> 12 us  [along_z(): return lax.ppermute(x, 'seq', z_pairs(seq, pairs))]
    ppermute x1, waiting for transfers between devices: 8.75 us -> 0.01 us  [head_body(): lax.ppermute(mine[:some], 'section', both)]
    ppermute x4, waiting for transfers between devices: 18.9 us -> 10.7 us  [to_tp(): return lax.ppermute(x, 'tp', both)]
    unnamed x42 -> x38, local copies, waits for them, and re-layouts: 7.62 us -> 3.23 us
    ppermute x4, starting transfers between devices: 3.05 us -> 6.15 us  [to_tp(): return lax.ppermute(x, 'tp', both)]
    another operation x2, local copies, waits for them, and re-layouts: 3.54 us -> 0.97 us  [head_body(): text_kv[0].reshape(-1, 2, seq, HEAD_DIM).transpose(2, 1, 0, 3)]
    ppermute x1, waiting for transfers between devices: 6.47 us -> 8.61 us  [head_body(): lax.ppermute(mine[some:], 'section', both)]
    pallas_call x1, Pallas kernels: 1.05 us -> 3.05 us  [attend_second(): call(second_cond_kernel, 'attend_second', jax.ShapeDtypeStruct((seq, rows...]
  transfers between devices with their start and end apart: 22 -> 22, of which waited for: 5 -> 4; matrix products, arithmetic and copies ran while one was open for 15% -> 11% of each run, Pallas kernels for 18% -> 19%
where the time goes in v11:
time: 135 us; the launch traced here: 134 us
  starting transfers between devices  37.6 us (28%)
  Pallas kernels  32.3 us (24%)
  waiting for transfers between devices  31.3 us (23%)
  blocking collectives  14 us (10%)
  local copies, waits for them, and re-layouts  12.1 us (9%)
  other arithmetic  6.33 us (5%)
    all_to_all x1, blocking collectives, head_body(): attn = lax.all_to_all(attn, 'seq', 0, 0)  14 us
    ppermute x5, waiting for transfers between devices, along_z(): return lax.ppermute(x, 'seq', z_pairs(seq, pairs))  12 us
    ppermute x4, waiting for transfers between devices, to_tp(): return lax.ppermute(x, 'tp', both)  10.7 us
    ppermute x5, starting transfers between devices, along_z(): return lax.ppermute(x, 'seq', z_pairs(seq, pairs))  10.6 us
    pallas_call x1, Pallas kernels, attend_own(): call(own_kernel, 'attend_own', [jax.ShapeDtypeStruct((rows, HEAD_DIM), jn...  10.2 us
    pallas_call x2, Pallas kernels, project_kv(): call(lambda *refs: kv_kernel(chunk, *refs), 'project_kv' + 'ab'[chunk], j...  9.82 us
    all_to_all x1, starting transfers between devices, head_body(): direct = lax.all_to_all(direct, 'seq', 0, 0)  9.08 us
    ppermute x1, waiting for transfers between devices, head_body(): lax.ppermute(mine[some:], 'section', both)  8.61 us
  transfers between devices with their start and end apart: 22, of which 4 were waited for; matrix products, arithmetic and copies ran while one was open for 11% of the time, Pallas kernels for 19%

profile of v11, /device:TPU:0, one launch (start us, length us, event | category | flops | bytes accessed | tf_op | source)
XLA Modules:
  0.0 134.0 jit_solution(14682401889090179280)
XLA Ops:
  0.0 2.9 %norm_tokens.1 = (bf16[128,3072]{1,0:T(8,128)(2,1)}, bf16[64,3072]{1,0:T(8,128)(2,1)}) custom-call(s32[1]{0:T(128)} %bitcast.1.tp_ref, bf16[128,3072]{1,0:T(8,128)(2,1)} %bitcast.27, f32[3,1,3072]{2,1,0:T(1,128)} %bitcast.29), custom_call_target="tpu_custom_call" | custom-call | flops 3932160 | bytes 1572864 | tf_op jit(solution)/shard_map/norm_tokens/pallas_call | solution.py:94
  3.6 5.9 %collective-permute-start.2 = (bf16[64,3072]{1,0:T(8,128)(2,1)}, bf16[64,3072]{1,0:T(8,128)(2,1)}, u32[]{:S(2)}, u32[]{:S(2)}) collective-permute-start(bf16[64,3072]{1,0:T(8,128)(2,1)} %get-tuple-element.30), channel_id=1, source_target_pairs={{0,4},{2,6},{4,0},{6,2},{8,12},{10,14},{12,8},{14,10},{1,5},{3,7},... | collective-permute-start | bytes 1179656 | tf_op jit(solution)/shard_map/ppermute | solution.py:475
  9.5 2.1 %kv_weights.1 = bf16[8,384,128]{2,1,0:T(8,128)(2,1)} custom-call(s32[1]{0:T(128)} %bitcast.section_ref.refs_0_, bf16[3,384,1024]{2,1,0:T(8,128)(2,1)} %bitcast.25), custom_call_target="tpu_custom_call" | custom-call | bytes 1572864 | tf_op jit(solution)/shard_map/kv_weights/pallas_call | solution.py:123
  11.7 3.6 %all-to-all-start = ((bf16[8,384,128]{2,1,0:T(8,128)(2,1)}), bf16[8,384,128]{2,1,0:T(8,128)(2,1)S(1)}, u32[]{:S(2)}, u32[]{:S(2)}) async-start(bf16[8,384,128]{2,1,0:T(8,128)(2,1)} %kv_weights.1), calls=%async_computation | async-start | bytes 1572864 | tf_op jit(solution)/shard_map/all_to_all | solution.py:470
  17.8 3.0 %direct_rows.1 = bf16[8,528,128]{2,1,0:T(8,128)(2,1)} custom-call(bf16[3,384,1024]{2,1,0:T(8,128)(2,1)} %bitcast.26, bf16[8,128,128]{2,1,0:T(8,128)(2,1)} %bitcast.28, bf16[16,128]{1,0:T(8,128)(2,1)} %pad.4.mask_ref), custom_call_target="tpu_custom_call" | custom-call | bytes 2162688 | tf_op jit(solution)/shard_map/direct_rows/pallas_call | solution.py:146
  22.2 1.4 %collective-permute-start.5 = (bf16[64,3072]{1,0:T(8,128)(2,1)}, bf16[64,3072]{1,0:T(8,128)(2,1)}, u32[]{:S(2)}, u32[]{:S(2)}) collective-permute-start(bf16[64,3072]{1,0:T(8,128)(2,1)} %collective-permute-done.2.refs_8_.refs_2_), channel_id=1, source_target_pairs={{4,8},{6,10},{8,4},{10,6},{5,9},{7,11},{9,5},{11,7},{20,24},{22,26... | collective-permute-start | bytes 1179656 | tf_op jit(solution)/shard_map/ppermute | solution.py:475
  24.9 1.5 %collective-permute-start.3 = (bf16[64,3072]{1,0:T(8,128)(2,1)}, bf16[64,3072]{1,0:T(8,128)(2,1)}, u32[]{:S(2)}, u32[]{:S(2)}) collective-permute-start(bf16[64,3072]{1,0:T(8,128)(2,1)} %collective-permute-done.2.refs_8_.refs_2_), channel_id=1, source_target_pairs={{0,1},{1,0},{2,3},{3,2},{4,5},{5,4},{6,7},{7,6},{8,9},{9,8},{10,11... | collective-permute-start | bytes 1179656 | tf_op jit(solution)/shard_map/ppermute | solution.py:481
  27.7 12.0 %collective-permute-done.1 = bf16[64,3072]{1,0:T(8,128)(2,1)S(1)} collective-permute-done((bf16[64,3072]{1,0:T(8,128)(2,1)S(1)}, bf16[64,3072]{1,0:T(8,128)(2,1)S(1)}, u32[]{:S(2)}, u32[]{:S(2)}) %collective-permute-start.1) | collective-permute-done | bytes 393248 | tf_op jit(solution)/shard_map/ppermute | solution.py:475
  41.7 1.5 %collective-permute-start.4 = (bf16[4,384,128]{2,1,0:T(8,128)(2,1)}, bf16[4,384,128]{2,1,0:T(8,128)(2,1)}, u32[]{:S(2)}, u32[]{:S(2)}) collective-permute-start(bf16[4,384,128]{2,1,0:T(8,128)(2,1)} %get-tuple-element.58), channel_id=1, source_target_pairs={{0,16},{16,0},{1,17},{17,1},{2,18},{18,2},{3,19},{19,3},{4,20},{20... | collective-permute-start | bytes 1179656 | tf_op jit(solution)/shard_map/ppermute | solution.py:504
  43.2 9.1 %all-to-all-start.1 = ((bf16[8,528,128]{2,1,0:T(8,128)(2,1)}), bf16[8,528,128]{2,1,0:T(8,128)(2,1)}, u32[]{:S(2)}, u32[]{:S(2)}) async-start(bf16[8,528,128]{2,1,0:T(8,128)(2,1)} %direct_rows.1), calls=%async_computation.1 | async-start | bytes 2162688 | tf_op jit(solution)/shard_map/all_to_all | solution.py:502
  52.3 4.9 %constant_dynamic-slice_fusion = (bf16[1024,1536]{1,0:T(8,128)(2,1)S(1)}, bf16[1024,1536]{1,0:T(8,128)(2,1)}) fusion(bf16[1024,3072]{1,0:T(8,128)(2,1)} %param.12, s32[]{:T(128)S(6)} %select_n.78, s32[]{:T(128)S(6)} %select_n.77), kind=kLoop, calls=%fused_computation.21 | loop fusion | bytes 12582920 | tf_op jit(solution)/shard_map/dynamic_slice | solution.py:507
  59.9 1.5 %collective-permute-start.7 = (bf16[64,3072]{1,0:T(8,128)(2,1)S(1)}, bf16[64,3072]{1,0:T(8,128)(2,1)S(1)}, u32[]{:S(2)}, u32[]{:S(2)}) collective-permute-start(bf16[64,3072]{1,0:T(8,128)(2,1)S(1)} %broadcast_select_fusion.1.refs_6_), channel_id=1, source_target_pairs={{0,1},{1,0},{2,3},{3,2},{4,5},{5,4},{6,7},{7,6},{8,9},{9,8},{10,11... | collective-permute-start | bytes 1179656 | tf_op jit(solution)/shard_map/ppermute | solution.py:481
  62.5 8.6 %collective-permute-done.8.refs_5_ = bf16[4,384,128]{2,1,0:T(8,128)(2,1)S(1)} collective-permute-done((bf16[4,384,128]{2,1,0:T(8,128)(2,1)}, bf16[4,384,128]{2,1,0:T(8,128)(2,1)S(1)}, u32[]{:S(2)}, u32[]{:S(2)}) %collective-permute-start.8) | collective-permute-done | bytes 393248 | tf_op jit(solution)/shard_map/ppermute | solution.py:504
  71.2 1.5 %collective-permute-start.9 = (bf16[64,3072]{1,0:T(8,128)(2,1)S(1)}, bf16[64,3072]{1,0:T(8,128)(2,1)S(1)}, u32[]{:S(2)}, u32[]{:S(2)}) collective-permute-start(bf16[64,3072]{1,0:T(8,128)(2,1)S(1)} %broadcast_select_fusion.refs_10_), channel_id=1, source_target_pairs={{0,1},{1,0},{2,3},{3,2},{4,5},{5,4},{6,7},{7,6},{8,9},{9,8},{10,11... | collective-permute-start | bytes 1179656 | tf_op jit(solution)/shard_map/ppermute | solution.py:481
  74.0 4.9 %project_kva.1.kva = bf16[2,512,128]{2,1,0:T(8,128)(2,1)} custom-call(s32[1]{0:T(128)} %bitcast.section_ref.refs_0_, f32[2,80,128]{2,1,0:T(8,128)} %pad_maximum_fusion.refs_1_.tabs_hbm, f32[2,128]{1,0:T(2,128)} %pad_maximum_fusion.1.refs_2_.gain_hbm, bf16[8,384,128]{2,1,0:T(8,128)(2,1)} %copy-done.1, bf16[4,384,128]{2,1,0:T(8,128)(2,1)} %collective-permute-done.4.refs_4_, ...), custom_call_target="tpu_custom_call" | custom-call | flops 805306368 | bytes 4718592 | tf_op jit(solution)/shard_map/project_kva/pallas_call | solution.py:243
  79.0 3.1 %collective-permute-done.9.refs_11_ = bf16[64,3072]{1,0:T(8,128)(2,1)S(1)} collective-permute-done((bf16[64,3072]{1,0:T(8,128)(2,1)S(1)}, bf16[64,3072]{1,0:T(8,128)(2,1)S(1)}, u32[]{:S(2)}, u32[]{:S(2)}) %collective-permute-start.9) | collective-permute-done | bytes 393248 | tf_op jit(solution)/shard_map/ppermute | solution.py:481
  82.0 3.7 %collective-permute-start.17 = (bf16[2,512,128]{2,1,0:T(8,128)(2,1)}, bf16[2,512,128]{2,1,0:T(8,128)(2,1)}, u32[]{:S(2)}, u32[]{:S(2)}) collective-permute-start(bf16[2,512,128]{2,1,0:T(8,128)(2,1)} %project_kva.1.kva), channel_id=1, source_target_pairs={{0,16},{1,17},{2,18},{3,19},{4,20},{5,21},{6,22},{7,23},{8,24},{9,... | collective-permute-start | bytes 786440 | tf_op jit(solution)/shard_map/ppermute | solution.py:533
  87.6 4.9 %project_kvb.1.kvb = bf16[2,512,128]{2,1,0:T(8,128)(2,1)} custom-call(s32[1]{0:T(128)} %bitcast.section_ref.refs_0_, f32[2,80,128]{2,1,0:T(8,128)} %pad_maximum_fusion.refs_1_.tabs_hbm, f32[2,128]{1,0:T(2,128)} %pad_maximum_fusion.1.refs_2_.gain_hbm, bf16[8,384,128]{2,1,0:T(8,128)(2,1)} %copy-done.1, bf16[4,384,128]{2,1,0:T(8,128)(2,1)} %collective-permute-done.4.refs_4_, ...), custom_call_target="tpu_custom_call" | custom-call | flops 805306368 | bytes 4718592 | tf_op jit(solution)/shard_map/project_kvb/pallas_call | solution.py:243
  92.5 1.5 %collective-permute-start.18 = (bf16[2,512,128]{2,1,0:T(8,128)(2,1)}, bf16[2,512,128]{2,1,0:T(8,128)(2,1)S(1)}, u32[]{:S(2)}, u32[]{:S(2)}) collective-permute-start(bf16[2,512,128]{2,1,0:T(8,128)(2,1)} %project_kvb.1.kvb), channel_id=1, source_target_pairs={{0,16},{1,17},{2,18},{3,19},{4,20},{5,21},{6,22},{7,23},{8,24},{9,... | collective-permute-start | bytes 786440 | tf_op jit(solution)/shard_map/ppermute | solution.py:539
  94.0 10.2 %attend_own.1 = (bf16[1024,128]{1,0:T(8,128)(2,1)}, f32[1024,128]{1,0:T(8,128)}, f32[1024,128]{1,0:T(8,128)}, f32[16,1024]{1,0:T(8,128)}) custom-call(s32[1]{0:T(128)} %bitcast.section_ref.refs_0_, f32[16,8]{1,0:T(8,128)} %fusion.3.rows_ref, f32[128,16]{1,0:T(8,128)} %fusion.1.keys_ref, bf16[2,512,128]{2,1,0:T(8,128)(2,1)} %project_kva.1.kva, ...), custom_call_target="tpu_custom_call" | custom-call | flops 1879048192 | bytes 6291456 | tf_op jit(solution)/shard_map/attend_own/pallas_call | solution.py:379
  105.0 3.0 %attend_second.1 = bf16[8,128,128]{2,1,0:T(8,128)(2,1)} custom-call(s32[1]{0:T(128)} %bitcast.section_ref.refs_0_, s32[2,16]{1,0:T(2,128)} %pad_add_fusion.place_ref, f32[16,1024]{1,0:T(8,128)} %get-tuple-element.49.keep_hbm, bf16[1024,128]{1,0:T(8,128)(2,1)} %get-tuple-element.50.q_hbm, f32[1024,128]{1,0:T(8,128)} %get-tuple-element.51.num_hbm, ...), custom_call_target="tpu_custom_call" | custom-call | flops 268435456 | bytes 2097152 | tf_op jit(solution)/shard_map/attend_second/pallas_call | solution.py:402
  108.0 14.0 %all_to_all.15.attn_ref = bf16[8,128,128]{2,1,0:T(8,128)(2,1)S(1)} all-to-all(bf16[8,128,128]{2,1,0:T(8,128)(2,1)} %attend_second.1), channel_id=1, replica_groups=mesh['section'=2,'seq'=8,'tp'=2] {'seq'}, dimensions={0} | all-to-all | bytes 524288 | tf_op jit(solution)/shard_map/all_to_all | solution.py:545
  122.6 1.6 %collective-permute-start.19 = (bf16[128,1536]{1,0:T(8,128)(2,1)S(1)}, bf16[128,1536]{1,0:T(8,128)(2,1)S(1)}, u32[]{:S(2)}, u32[]{:S(2)}) collective-permute-start(bf16[128,1536]{1,0:T(8,128)(2,1)S(1)} %out_sent.1), channel_id=1, source_target_pairs={{0,1},{1,0},{2,3},{3,2},{4,5},{5,4},{6,7},{7,6},{8,9},{9,8},{10,11... | collective-permute-start | bytes 1179656 | tf_op jit(solution)/shard_map/ppermute | solution.py:481
  125.6 7.6 %collective-permute-done.19 = bf16[128,1536]{1,0:T(8,128)(2,1)S(1)} collective-permute-done((bf16[128,1536]{1,0:T(8,128)(2,1)S(1)}, bf16[128,1536]{1,0:T(8,128)(2,1)S(1)}, u32[]{:S(2)}, u32[]{:S(2)}) %collective-permute-start.19) | collective-permute-done | bytes 393248 | tf_op jit(solution)/shard_map/ppermute | solution.py:481
  (106 shorter events, 19.5 us)
Async XLA Ops:
  2.9 17.9 %collective-permute-start = (bf16[64,3072]{1,0:T(8,128)(2,1)}, bf16[64,3072]{1,0:T(8,128)(2,1)S(1)}, u32[]{:S(2)}, u32[]{:S(2)}) collective-permute-start(bf16[64,3072]{1,0:T(8,128)(2,1)} %get-tuple-element.30), channel_id=1, source_target_pairs={{4,8},{6,10},{8,4},{10,6},{5,9},{7,11},{9,5},{11,7},{20,24},{22,26... | collective-permute-start | bytes 1179656 | tf_op jit(solution)/shard_map/ppermute | solution.py:475
  3.6 18.5 %collective-permute-start.2 = (bf16[64,3072]{1,0:T(8,128)(2,1)}, bf16[64,3072]{1,0:T(8,128)(2,1)}, u32[]{:S(2)}, u32[]{:S(2)}) collective-permute-start(bf16[64,3072]{1,0:T(8,128)(2,1)} %get-tuple-element.30), channel_id=1, source_target_pairs={{0,4},{2,6},{4,0},{6,2},{8,12},{10,14},{12,8},{14,10},{1,5},{3,7},... | collective-permute-start | bytes 1179656 | tf_op jit(solution)/shard_map/ppermute | solution.py:475
  11.7 28.0 %all-to-all-start = ((bf16[8,384,128]{2,1,0:T(8,128)(2,1)}), bf16[8,384,128]{2,1,0:T(8,128)(2,1)S(1)}, u32[]{:S(2)}, u32[]{:S(2)}) async-start(bf16[8,384,128]{2,1,0:T(8,128)(2,1)} %kv_weights.1), calls=%async_computation | async-start | bytes 1572864 | tf_op jit(solution)/shard_map/all_to_all | solution.py:470
  15.2 58.0 %collective-permute-start.10 = (bf16[128,3072]{1,0:T(8,128)(2,1)}, bf16[128,3072]{1,0:T(8,128)(2,1)}, u32[]{:S(2)}, u32[]{:S(2)}) collective-permute-start(bf16[128,3072]{1,0:T(8,128)(2,1)} %get-tuple-element.43.refs_6_.refs_0_), channel_id=1, source_target_pairs={{0,2},{2,0},{4,6},{6,4},{8,10},{10,8},{12,14},{14,12},{1,3},{3,1},... | collective-permute-start | bytes 2359304 | tf_op jit(solution)/shard_map/ppermute | solution.py:478
  20.9 18.8 %collective-permute-start.1 = (bf16[64,3072]{1,0:T(8,128)(2,1)S(1)}, bf16[64,3072]{1,0:T(8,128)(2,1)S(1)}, u32[]{:S(2)}, u32[]{:S(2)}) collective-permute-start(bf16[64,3072]{1,0:T(8,128)(2,1)S(1)} %collective-permute-done), channel_id=1, source_target_pairs={{4,0},{6,2},{8,12},{10,14},{5,1},{7,3},{9,13},{11,15},{20,16},{22,... | collective-permute-start | bytes 1179656 | tf_op jit(solution)/shard_map/ppermute | solution.py:475
  22.2 4.2 %collective-permute-start.5 = (bf16[64,3072]{1,0:T(8,128)(2,1)}, bf16[64,3072]{1,0:T(8,128)(2,1)}, u32[]{:S(2)}, u32[]{:S(2)}) collective-permute-start(bf16[64,3072]{1,0:T(8,128)(2,1)} %collective-permute-done.2.refs_8_.refs_2_), channel_id=1, source_target_pairs={{4,8},{6,10},{8,4},{10,6},{5,9},{7,11},{9,5},{11,7},{20,24},{22,26... | collective-permute-start | bytes 1179656 | tf_op jit(solution)/shard_map/ppermute | solution.py:475
  24.9 34.5 %collective-permute-start.3 = (bf16[64,3072]{1,0:T(8,128)(2,1)}, bf16[64,3072]{1,0:T(8,128)(2,1)}, u32[]{:S(2)}, u32[]{:S(2)}) collective-permute-start(bf16[64,3072]{1,0:T(8,128)(2,1)} %collective-permute-done.2.refs_8_.refs_2_), channel_id=1, source_target_pairs={{0,1},{1,0},{2,3},{3,2},{4,5},{5,4},{6,7},{7,6},{8,9},{9,8},{10,11... | collective-permute-start | bytes 1179656 | tf_op jit(solution)/shard_map/ppermute | solution.py:481
  26.4 46.3 %collective-permute-start.11 = (bf16[64,3072]{1,0:T(8,128)(2,1)}, bf16[64,3072]{1,0:T(8,128)(2,1)}, u32[]{:S(2)}, u32[]{:S(2)}) collective-permute-start(bf16[64,3072]{1,0:T(8,128)(2,1)} %collective-permute-done.2.refs_8_.refs_2_), channel_id=1, source_target_pairs={{0,2},{2,0},{4,6},{6,4},{8,10},{10,8},{12,14},{14,12},{1,3},{3,1},... | collective-permute-start | bytes 1179656 | tf_op jit(solution)/shard_map/ppermute | solution.py:478
  26.4 35.0 %collective-permute-start.6 = (bf16[64,3072]{1,0:T(8,128)(2,1)}, bf16[64,3072]{1,0:T(8,128)(2,1)}, u32[]{:S(2)}, u32[]{:S(2)}) collective-permute-start(bf16[64,3072]{1,0:T(8,128)(2,1)} %collective-permute-done.5), channel_id=1, source_target_pairs={{4,0},{6,2},{8,12},{10,14},{5,1},{7,3},{9,13},{11,15},{20,16},{22,... | collective-permute-start | bytes 1179656 | tf_op jit(solution)/shard_map/ppermute | solution.py:475
  39.7 33.0 %copy-start.2 = (bf16[64,3072]{1,0:T(8,128)(2,1)}, bf16[64,3072]{1,0:T(8,128)(2,1)S(1)}, u32[]{:S(2)}) copy-start(bf16[64,3072]{1,0:T(8,128)(2,1)S(1)} %broadcast_select_fusion.1.refs_6_) | copy-start | bytes 1179652
  41.7 18.2 %collective-permute-start.4 = (bf16[4,384,128]{2,1,0:T(8,128)(2,1)}, bf16[4,384,128]{2,1,0:T(8,128)(2,1)}, u32[]{:S(2)}, u32[]{:S(2)}) collective-permute-start(bf16[4,384,128]{2,1,0:T(8,128)(2,1)} %get-tuple-element.58), channel_id=1, source_target_pairs={{0,16},{16,0},{1,17},{17,1},{2,18},{18,2},{3,19},{19,3},{4,20},{20... | collective-permute-start | bytes 1179656 | tf_op jit(solution)/shard_map/ppermute | solution.py:504
  43.2 50.8 %all-to-all-start.1 = ((bf16[8,528,128]{2,1,0:T(8,128)(2,1)}), bf16[8,528,128]{2,1,0:T(8,128)(2,1)}, u32[]{:S(2)}, u32[]{:S(2)}) async-start(bf16[8,528,128]{2,1,0:T(8,128)(2,1)} %direct_rows.1), calls=%async_computation.1 | async-start | bytes 2162688 | tf_op jit(solution)/shard_map/all_to_all | solution.py:502
  59.4 11.7 %collective-permute-start.8 = (bf16[4,384,128]{2,1,0:T(8,128)(2,1)}, bf16[4,384,128]{2,1,0:T(8,128)(2,1)S(1)}, u32[]{:S(2)}, u32[]{:S(2)}) collective-permute-start(bf16[4,384,128]{2,1,0:T(8,128)(2,1)} %get-tuple-element.57), channel_id=1, source_target_pairs={{0,16},{16,0},{1,17},{17,1},{2,18},{18,2},{3,19},{19,3},{4,20},{20... | collective-permute-start | bytes 1179656 | tf_op jit(solution)/shard_map/ppermute | solution.py:504
  59.9 11.2 %collective-permute-start.7 = (bf16[64,3072]{1,0:T(8,128)(2,1)S(1)}, bf16[64,3072]{1,0:T(8,128)(2,1)S(1)}, u32[]{:S(2)}, u32[]{:S(2)}) collective-permute-start(bf16[64,3072]{1,0:T(8,128)(2,1)S(1)} %broadcast_select_fusion.1.refs_6_), channel_id=1, source_target_pairs={{0,1},{1,0},{2,3},{3,2},{4,5},{5,4},{6,7},{7,6},{8,9},{9,8},{10,11... | collective-permute-start | bytes 1179656 | tf_op jit(solution)/shard_map/ppermute | solution.py:481
  61.4 11.9 %collective-permute-start.12 = (bf16[64,3072]{1,0:T(8,128)(2,1)}, bf16[64,3072]{1,0:T(8,128)(2,1)S(1)}, u32[]{:S(2)}, u32[]{:S(2)}) collective-permute-start(bf16[64,3072]{1,0:T(8,128)(2,1)} %collective-permute-done.3.refs_9_.refs_3_), channel_id=1, source_target_pairs={{0,2},{2,0},{4,6},{6,4},{8,10},{10,8},{12,14},{14,12},{1,3},{3,1},... | collective-permute-start | bytes 1179656 | tf_op jit(solution)/shard_map/ppermute | solution.py:478
  71.2 10.9 %collective-permute-start.9 = (bf16[64,3072]{1,0:T(8,128)(2,1)S(1)}, bf16[64,3072]{1,0:T(8,128)(2,1)S(1)}, u32[]{:S(2)}, u32[]{:S(2)}) collective-permute-start(bf16[64,3072]{1,0:T(8,128)(2,1)S(1)} %broadcast_select_fusion.refs_10_), channel_id=1, source_target_pairs={{0,1},{1,0},{2,3},{3,2},{4,5},{5,4},{6,7},{7,6},{8,9},{9,8},{10,11... | collective-permute-start | bytes 1179656 | tf_op jit(solution)/shard_map/ppermute | solution.py:481
  72.7 13.1 %collective-permute-start.13 = (bf16[64,3072]{1,0:T(8,128)(2,1)S(1)}, bf16[64,3072]{1,0:T(8,128)(2,1)S(1)}, u32[]{:S(2)}, u32[]{:S(2)}) collective-permute-start(bf16[64,3072]{1,0:T(8,128)(2,1)S(1)} %broadcast_select_fusion.1.refs_6_), channel_id=1, source_target_pairs={{0,2},{2,0},{4,6},{6,4},{8,10},{10,8},{12,14},{14,12},{1,3},{3,1},... | collective-permute-start | bytes 1179656 | tf_op jit(solution)/shard_map/ppermute | solution.py:478
  72.7 13.1 %collective-permute-start.15 = (bf16[64,3072]{1,0:T(8,128)(2,1)S(1)}, bf16[64,3072]{1,0:T(8,128)(2,1)S(1)}, u32[]{:S(2)}, u32[]{:S(2)}) collective-permute-start(bf16[64,3072]{1,0:T(8,128)(2,1)S(1)} %broadcast_select_fusion.refs_10_), channel_id=1, source_target_pairs={{0,2},{2,0},{4,6},{6,4},{8,10},{10,8},{12,14},{14,12},{1,3},{3,1},... | collective-permute-start | bytes 1179656 | tf_op jit(solution)/shard_map/ppermute | solution.py:478
  73.2 12.6 %collective-permute-start.14 = (bf16[64,3072]{1,0:T(8,128)(2,1)S(1)}, bf16[64,3072]{1,0:T(8,128)(2,1)S(1)}, u32[]{:S(2)}, u32[]{:S(2)}) collective-permute-start(bf16[64,3072]{1,0:T(8,128)(2,1)S(1)} %collective-permute-done.7.refs_7_), channel_id=1, source_target_pairs={{0,2},{2,0},{4,6},{6,4},{8,10},{10,8},{12,14},{14,12},{1,3},{3,1},... | collective-permute-start | bytes 1179656 | tf_op jit(solution)/shard_map/ppermute | solution.py:478
  82.0 3.8 %collective-permute-start.16 = (bf16[64,3072]{1,0:T(8,128)(2,1)S(1)}, bf16[64,3072]{1,0:T(8,128)(2,1)S(1)}, u32[]{:S(2)}, u32[]{:S(2)}) collective-permute-start(bf16[64,3072]{1,0:T(8,128)(2,1)S(1)} %collective-permute-done.9.refs_11_), channel_id=1, source_target_pairs={{0,2},{2,0},{4,6},{6,4},{8,10},{10,8},{12,14},{14,12},{1,3},{3,1},... | collective-permute-start | bytes 1179656 | tf_op jit(solution)/shard_map/ppermute | solution.py:478
  82.0 11.9 %collective-permute-start.17 = (bf16[2,512,128]{2,1,0:T(8,128)(2,1)}, bf16[2,512,128]{2,1,0:T(8,128)(2,1)}, u32[]{:S(2)}, u32[]{:S(2)}) collective-permute-start(bf16[2,512,128]{2,1,0:T(8,128)(2,1)} %project_kva.1.kva), channel_id=1, source_target_pairs={{0,16},{1,17},{2,18},{3,19},{4,20},{5,21},{6,22},{7,23},{8,24},{9,... | collective-permute-start | bytes 786440 | tf_op jit(solution)/shard_map/ppermute | solution.py:533
  92.5 11.8 %collective-permute-start.18 = (bf16[2,512,128]{2,1,0:T(8,128)(2,1)}, bf16[2,512,128]{2,1,0:T(8,128)(2,1)S(1)}, u32[]{:S(2)}, u32[]{:S(2)}) collective-permute-start(bf16[2,512,128]{2,1,0:T(8,128)(2,1)} %project_kvb.1.kvb), channel_id=1, source_target_pairs={{0,16},{1,17},{2,18},{3,19},{4,20},{5,21},{6,22},{7,23},{8,24},{9,... | collective-permute-start | bytes 786440 | tf_op jit(solution)/shard_map/ppermute | solution.py:539
  94.0 28.1 %copy-start = (bf16[1024,1536]{1,0:T(8,128)(2,1)S(1)}, bf16[1024,1536]{1,0:T(8,128)(2,1)}, u32[]{:S(2)}) copy-start(bf16[1024,1536]{1,0:T(8,128)(2,1)} %get-tuple-element.54.w_ref) | copy-start | bytes 9437188
  122.6 10.5 %collective-permute-start.19 = (bf16[128,1536]{1,0:T(8,128)(2,1)S(1)}, bf16[128,1536]{1,0:T(8,128)(2,1)S(1)}, u32[]{:S(2)}, u32[]{:S(2)}) collective-permute-start(bf16[128,1536]{1,0:T(8,128)(2,1)S(1)} %out_sent.1), channel_id=1, source_target_pairs={{0,1},{1,0},{2,3},{3,2},{4,5},{5,4},{6,7},{7,6},{8,9},{9,8},{10,11... | collective-permute-start | bytes 1179656 | tf_op jit(solution)/shard_map/ppermute | solution.py:481
  (17 other events, 145.1 us)

commit v12 on v11

--- a/solution.py
+++ b/solution.py
@@ -198,23 +198,15 @@
         at += ref.shape[0]
 
 
-def kv_kernel(chunk, section_ref, tabs_hbm, gain_hbm, mine_hbm, peer_a, peer_b, *refs):
+def kv_kernel(chunk, section_ref, tabs_hbm, gain_hbm, mine_hbm, peer_hbm, *refs):
     piece_refs = refs[:-8]
     kv_ref, x_ref, mine, peer, w_ref, tabs_ref, gain_ref, sems = refs[-8:]
     sources, held, _ = mine.shape
     half = held // 2
-    some = sources // 2
     weights = started(
-        [
-            (mine_hbm, mine),
-            (peer_a, peer.at[pl.ds(0, some)]),
-            (peer_b, peer.at[pl.ds(some, some)]),
-            (tabs_hbm, tabs_ref),
-            (gain_hbm, gain_ref),
-        ],
-        sems,
-    )
-    tokens = started(piece_copies(piece_refs, x_ref), sems, 5)
+        [(mine_hbm, mine), (peer_hbm, peer), (tabs_hbm, tabs_ref), (gain_hbm, gain_ref)], sems
+    )
+    tokens = started(piece_copies(piece_refs, x_ref), sems, 4)
     finished(weights)
     first = section_ref[0] == 0
     for s in range(sources):
@@ -237,14 +229,14 @@
         kv_ref[1, at, :] = both[:, HEAD_DIM:].astype(jnp.bfloat16)
 
 
-def project_kv(chunk, section, tabs, gains, mine, peers, pieces):
+def project_kv(chunk, section, tabs, gains, mine, peer, pieces):
     depth = pieces[0].shape[1]
     rows = sum(p.shape[0] for p in pieces)
     return call(
         lambda *refs: kv_kernel(chunk, *refs), "project_kv" + "ab"[chunk],
         jax.ShapeDtypeStruct((2, rows, HEAD_DIM), jnp.bfloat16),
         4 * rows * depth * HEAD_DIM, 2 * (rows * depth + 2 * mine.size), 0, VMEM_WHOLE,
-        in_specs=[SMEM] + [HBM] * (5 + len(pieces)),
+        in_specs=[SMEM] + [HBM] * (4 + len(pieces)),
         out_specs=VMEM,
         scratch_shapes=[
             pltpu.VMEM((rows, depth), jnp.bfloat16),
@@ -253,9 +245,9 @@
             pltpu.VMEM((depth, 2 * HEAD_DIM), jnp.bfloat16),
             pltpu.VMEM(tabs.shape, tabs.dtype),
             pltpu.VMEM(gains.shape, gains.dtype),
-            pltpu.SemaphoreType.DMA((5 + len(pieces),)),
-        ],
-    )(section, tabs, gains, mine, *peers, *pieces)
+            pltpu.SemaphoreType.DMA((4 + len(pieces),)),
+        ],
+    )(section, tabs, gains, mine, peer, *pieces)
 
 
 def weights_of(query, keys):
@@ -481,6 +473,7 @@
         return lax.ppermute(x, "tp", both)
 
     near = along_z(part, [(0, 1), (1, 0), (2, 3), (3, 2)])
+    near, w_late, at_chip = lax.optimization_barrier((near, w_out, chip.astype(jnp.int32)))
     middle = along_z(part, [(1, 2), (2, 1)])
     far = along_z(near, [(1, 2), (2, 1)])
     middle_end = along_z(middle, [(1, 0), (2, 3)])
@@ -488,20 +481,8 @@
     inner = (chip == 1) | (chip == 2)
     third = jnp.where(inner, middle, middle_end)
     fourth = jnp.where(inner, far, far_end)
-
-    text = text_kv[0].reshape(-1, 2, seq, HEAD_DIM).transpose(2, 1, 0, 3).reshape(seq, -1, HEAD_DIM)
-    mask = jnp.pad(
-        region_mask.astype(jnp.bfloat16), ((0, 15), (0, HEAD_DIM - region_mask.shape[1]))
-    )
-    direct = direct_rows(rows3, text, mask)
-
     near_tp = to_tp(near)
-    direct, mine, w_late, at_chip = lax.optimization_barrier(
-        (direct, mine, w_out, chip.astype(jnp.int32))
-    )
-    direct = lax.all_to_all(direct, "seq", 0, 0)
-    some = seq // 2
-    peers = [lax.ppermute(mine[:some], "section", both), lax.ppermute(mine[some:], "section", both)]
+    peer = lax.ppermute(mine, "section", both)
     cols = w_out.shape[1] // 2
     w_sent = lax.dynamic_slice_in_dim(w_late, (1 - tp) * cols, cols, 1)
     w_kept = lax.dynamic_slice_in_dim(w_late, tp * cols, cols, 1)
@@ -523,19 +504,28 @@
     place = jnp.stack([shards, parts])
 
     early = (tabs, gains, row_tiles, key_tiles, place, w_sent, w_kept)
-    third, near_tp, peers[0], early = lax.optimization_barrier((third, near_tp, peers[0], early))
+    third, near_tp, text_late, early = lax.optimization_barrier((third, near_tp, text_kv, early))
     tabs, gains, row_tiles, key_tiles, place, w_sent, w_kept = early
     third_tp = to_tp(third)
-    fourth, third_tp, peers[1] = lax.optimization_barrier((fourth, third_tp, peers[1]))
+
+    text = text_late[0].reshape(-1, 2, seq, HEAD_DIM).transpose(2, 1, 0, 3).reshape(seq, -1, HEAD_DIM)
+    mask = jnp.pad(
+        region_mask.astype(jnp.bfloat16), ((0, 15), (0, HEAD_DIM - region_mask.shape[1]))
+    )
+    direct = direct_rows(rows3, text, mask)
+
+    direct, third_tp = lax.optimization_barrier((direct, third_tp))
+    direct = lax.all_to_all(direct, "seq", 0, 0)
+    fourth, third_tp, peer = lax.optimization_barrier((fourth, third_tp, peer))
     fourth_tp = to_tp(fourth)
     a = [full, to_core(full), near, near_tp, to_core(near), to_core(near_tp)]
-    kv_a = project_kv(0, section_at, tabs, gains, mine, peers, a)
+    kv_a = project_kv(0, section_at, tabs, gains, mine, peer, a)
     cond_a = lax.ppermute(kv_a, "section", [(0, 1)])
     b = [third, third_tp, to_core(third), to_core(third_tp), fourth, fourth_tp, to_core(fourth)]
     fourth_tp, kv_a = lax.optimization_barrier((fourth_tp, kv_a))
     b[5] = fourth_tp
     b.append(to_core(fourth_tp))
-    kv_b = project_kv(1, section_at, tabs, gains, mine, peers, b)
+    kv_b = project_kv(1, section_at, tabs, gains, mine, peer, b)
     cond_b = lax.ppermute(kv_b, "section", [(0, 1)])
     query, num, den, keep = attend_own(
         section_at, tabs, gains, row_tiles, key_tiles, (kv_a, kv_b), cond_a, direct, a + b

time: 135 us -> 143 us (1.059)
  waiting for transfers between devices: 31.3 us -> 41.1 us
  starting transfers between devices: 37.6 us -> 32.3 us
  local copies, waits for them, and re-layouts: 12.1 us -> 14.6 us
    ppermute x2 -> x1, waiting for transfers between devices: 8.61 us -> 16.9 us  [head_body(): peer = lax.ppermute(mine, 'section', both)]
    all_to_all x1, starting transfers between devices: 9.08 us -> 5.27 us  [head_body(): direct = lax.all_to_all(direct, 'seq', 0, 0)]
    ppermute x5, starting transfers between devices: 10.6 us -> 7.72 us  [along_z(): return lax.ppermute(x, 'seq', z_pairs(seq, pairs))]
    another operation x2, local copies, waits for them, and re-layouts: 0.97 us -> 3.55 us  [head_body(): text_late[0].reshape(-1, 2, seq, HEAD_DIM).transpose(2, 1, 0, 3)]
    ppermute x5, waiting for transfers between devices: 12 us -> 14.2 us  [along_z(): return lax.ppermute(x, 'seq', z_pairs(seq, pairs))]
    all_to_all x1, starting transfers between devices: 3.56 us -> 5.66 us  [head_body(): mine = lax.all_to_all(kv_weights(section_at, rows3), 'seq', 0, 0)]
    unnamed x38 -> x34, local copies, waits for them, and re-layouts: 3.23 us -> 4.09 us
  transfers between devices with their start and end apart: 22 -> 21, of which waited for: 4 -> 5; matrix products, arithmetic and copies ran while one was open for 11% -> 12% of each run, Pallas kernels for 19% -> 18%
where the time goes in v12:
time: 143 us; the launch traced here: 142 us
  waiting for transfers between devices  41.1 us (29%)
  Pallas kernels  32.4 us (23%)
  starting transfers between devices  32.3 us (23%)
  local copies, waits for them, and re-layouts  14.6 us (10%)
  blocking collectives  14.1 us (10%)
  other arithmetic  7.35 us (5%)
    ppermute x1, waiting for transfers between devices, head_body(): peer = lax.ppermute(mine, 'section', both)  16.9 us
    ppermute x5, waiting for transfers between devices, along_z(): return lax.ppermute(x, 'seq', z_pairs(seq, pairs))  14.2 us
    all_to_all x1, blocking collectives, head_body(): attn = lax.all_to_all(attn, 'seq', 0, 0)  14.1 us
    pallas_call x1, Pallas kernels, attend_own(): call(own_kernel, 'attend_own', [jax.ShapeDtypeStruct((rows, HEAD_DIM), jn...  10.3 us
    ppermute x4, waiting for transfers between devices, to_tp(): return lax.ppermute(x, 'tp', both)  10.1 us
    pallas_call x2, Pallas kernels, project_kv(): call(lambda *refs: kv_kernel(chunk, *refs), 'project_kv' + 'ab'[chunk], j...  9.81 us
    ppermute x5, starting transfers between devices, along_z(): return lax.ppermute(x, 'seq', z_pairs(seq, pairs))  7.72 us
    all_to_all x1, starting transfers between devices, head_body(): mine = lax.all_to_all(kv_weights(section_at, rows3), 'seq', 0, 0)  5.66 us
  transfers between devices with their start and end apart: 21, of which 5 were waited for; matrix products, arithmetic and copies ran while one was open for 12% of the time, Pallas kernels for 18%

profile of v12, /device:TPU:0, one launch (start us, length us, event | category | flops | bytes accessed | tf_op | source)
XLA Modules:
  0.0 142.2 jit_solution(12116295174195463728)
XLA Ops:
  0.0 2.9 %norm_tokens.1 = (bf16[128,3072]{1,0:T(8,128)(2,1)}, bf16[64,3072]{1,0:T(8,128)(2,1)}) custom-call(s32[1]{0:T(128)} %bitcast.1.tp_ref, bf16[128,3072]{1,0:T(8,128)(2,1)} %bitcast.27, f32[3,1,3072]{2,1,0:T(1,128)} %bitcast.29), custom_call_target="tpu_custom_call" | custom-call | flops 3932160 | bytes 1572864 | tf_op jit(solution)/shard_map/norm_tokens/pallas_call | solution.py:94
  2.9 3.1 %collective-permute-start.2 = (bf16[64,3072]{1,0:T(8,128)(2,1)}, bf16[64,3072]{1,0:T(8,128)(2,1)}, u32[]{:S(2)}, u32[]{:S(2)}) collective-permute-start(bf16[64,3072]{1,0:T(8,128)(2,1)} %get-tuple-element.31), channel_id=1, source_target_pairs={{0,4},{2,6},{4,0},{6,2},{8,12},{10,14},{12,8},{14,10},{1,5},{3,7},... | collective-permute-start | bytes 1179656 | tf_op jit(solution)/shard_map/ppermute | solution.py:467
  6.7 2.1 %kv_weights.1 = bf16[8,384,128]{2,1,0:T(8,128)(2,1)} custom-call(s32[1]{0:T(128)} %bitcast.section_ref.refs_0_, bf16[3,384,1024]{2,1,0:T(8,128)(2,1)} %bitcast.25), custom_call_target="tpu_custom_call" | custom-call | bytes 1572864 | tf_op jit(solution)/shard_map/kv_weights/pallas_call | solution.py:123
  8.8 5.7 %all-to-all-start = ((bf16[8,384,128]{2,1,0:T(8,128)(2,1)}), bf16[8,384,128]{2,1,0:T(8,128)(2,1)}, u32[]{:S(2)}, u32[]{:S(2)}) async-start(bf16[8,384,128]{2,1,0:T(8,128)(2,1)} %kv_weights.1), calls=%async_computation | async-start | bytes 1572864 | tf_op jit(solution)/shard_map/all_to_all | solution.py:462
  15.7 1.5 %collective-permute-start.3 = (bf16[64,3072]{1,0:T(8,128)(2,1)}, bf16[64,3072]{1,0:T(8,128)(2,1)}, u32[]{:S(2)}, u32[]{:S(2)}) collective-permute-start(bf16[64,3072]{1,0:T(8,128)(2,1)} %collective-permute-done.2.refs_7_.refs_2_), channel_id=1, source_target_pairs={{0,1},{1,0},{2,3},{3,2},{4,5},{5,4},{6,7},{7,6},{8,9},{9,8},{10,11... | collective-permute-start | bytes 1179656 | tf_op jit(solution)/shard_map/ppermute | solution.py:473
  19.9 4.9 %constant_dynamic-slice_fusion = (bf16[1024,1536]{1,0:T(8,128)(2,1)S(1)}, bf16[1024,1536]{1,0:T(8,128)(2,1)}) fusion(bf16[1024,3072]{1,0:T(8,128)(2,1)} %param.12, s32[]{:T(128)S(6)} %select_n.78, s32[]{:T(128)S(6)} %select_n.77), kind=kLoop, calls=%fused_computation.21 | loop fusion | bytes 12582920 | tf_op jit(solution)/shard_map/dynamic_slice | solution.py:488
  28.1 14.2 %collective-permute-done.1 = bf16[64,3072]{1,0:T(8,128)(2,1)} collective-permute-done((bf16[64,3072]{1,0:T(8,128)(2,1)S(1)}, bf16[64,3072]{1,0:T(8,128)(2,1)}, u32[]{:S(2)}, u32[]{:S(2)}) %collective-permute-start.1) | collective-permute-done | bytes 393248 | tf_op jit(solution)/shard_map/ppermute | solution.py:467
  46.5 1.8 %reshape_squeeze.3 = bf16[64,2,8,128]{3,2,1,0:T(8,128)(2,1)} reshape(bf16[1,64,2,1024]{3,2,1,0:T(2,128)(2,1)} %param.9) | data formatting | bytes 524288 | tf_op jit(solution)/shard_map/reshape;squeeze | solution.py:511
  48.3 1.7 %copy.10 = bf16[64,2,8,128]{3,0,1,2:T(8,128)(2,1)} copy(bf16[64,2,8,128]{3,2,1,0:T(8,128)(2,1)} %reshape_squeeze.3) | data formatting | bytes 524288 | tf_op jit(solution)/shard_map/reshape;squeeze | solution.py:511
  50.0 3.1 %direct_rows.1 = bf16[8,528,128]{2,1,0:T(8,128)(2,1)} custom-call(bf16[3,384,1024]{2,1,0:T(8,128)(2,1)} %bitcast.26, bf16[8,128,128]{2,1,0:T(8,128)(2,1)} %bitcast.28, bf16[16,128]{1,0:T(8,128)(2,1)} %pad.4.mask_ref), custom_call_target="tpu_custom_call" | custom-call | bytes 2162688 | tf_op jit(solution)/shard_map/direct_rows/pallas_call | solution.py:146
  53.5 5.3 %all-to-all-start.1 = ((bf16[8,528,128]{2,1,0:T(8,128)(2,1)}), bf16[8,528,128]{2,1,0:T(8,128)(2,1)}, u32[]{:S(2)}, u32[]{:S(2)}) async-start(bf16[8,528,128]{2,1,0:T(8,128)(2,1)} %direct_rows.1), calls=%async_computation.1 | async-start | bytes 2162688 | tf_op jit(solution)/shard_map/all_to_all | solution.py:518
  58.7 1.5 %collective-permute-start.7 = (bf16[8,384,128]{2,1,0:T(8,128)(2,1)}, bf16[8,384,128]{2,1,0:T(8,128)(2,1)S(1)}, u32[]{:S(2)}, u32[]{:S(2)}) collective-permute-start(bf16[8,384,128]{2,1,0:T(8,128)(2,1)} %all-to-all-done.refs_3_), channel_id=1, source_target_pairs={{0,16},{16,0},{1,17},{17,1},{2,18},{18,2},{3,19},{19,3},{4,20},{20... | collective-permute-start | bytes 2359304 | tf_op jit(solution)/shard_map/ppermute | solution.py:485
  62.0 16.9 %collective-permute-done.7.refs_4_ = bf16[8,384,128]{2,1,0:T(8,128)(2,1)S(1)} collective-permute-done((bf16[8,384,128]{2,1,0:T(8,128)(2,1)}, bf16[8,384,128]{2,1,0:T(8,128)(2,1)S(1)}, u32[]{:S(2)}, u32[]{:S(2)}) %collective-permute-start.7) | collective-permute-done | bytes 786464 | tf_op jit(solution)/shard_map/ppermute | solution.py:485
  78.9 1.5 %collective-permute-start.8 = (bf16[64,3072]{1,0:T(8,128)(2,1)S(1)}, bf16[64,3072]{1,0:T(8,128)(2,1)S(1)}, u32[]{:S(2)}, u32[]{:S(2)}) collective-permute-start(bf16[64,3072]{1,0:T(8,128)(2,1)S(1)} %broadcast_select_fusion.refs_9_.refs_10_), channel_id=1, source_target_pairs={{0,1},{1,0},{2,3},{3,2},{4,5},{5,4},{6,7},{7,6},{8,9},{9,8},{10,11... | collective-permute-start | bytes 1179656 | tf_op jit(solution)/shard_map/ppermute | solution.py:473
  82.6 4.9 %project_kva.1.kva = bf16[2,512,128]{2,1,0:T(8,128)(2,1)} custom-call(s32[1]{0:T(128)} %bitcast.section_ref.refs_0_, f32[2,80,128]{2,1,0:T(8,128)} %pad_maximum_fusion.refs_1_.tabs_hbm, f32[2,128]{1,0:T(2,128)} %pad_maximum_fusion.1.refs_2_.gain_hbm, bf16[8,384,128]{2,1,0:T(8,128)(2,1)} %all-to-all-done.refs_3_, bf16[8,384,128]{2,1,0:T(8,128)(2,1)} %copy-done.3, ...), custom_call_target="tpu_custom_call" | custom-call | flops 805306368 | bytes 4718592 | tf_op jit(solution)/shard_map/project_kva/pallas_call | solution.py:235
  87.5 2.1 %collective-permute-done.8.refs_10_.refs_11_ = bf16[64,3072]{1,0:T(8,128)(2,1)S(1)} collective-permute-done((bf16[64,3072]{1,0:T(8,128)(2,1)S(1)}, bf16[64,3072]{1,0:T(8,128)(2,1)S(1)}, u32[]{:S(2)}, u32[]{:S(2)}) %collective-permute-start.8) | collective-permute-done | bytes 393248 | tf_op jit(solution)/shard_map/ppermute | solution.py:473
  89.6 4.1 %collective-permute-start.16 = (bf16[2,512,128]{2,1,0:T(8,128)(2,1)}, bf16[2,512,128]{2,1,0:T(8,128)(2,1)}, u32[]{:S(2)}, u32[]{:S(2)}) collective-permute-start(bf16[2,512,128]{2,1,0:T(8,128)(2,1)} %project_kva.1.kva), channel_id=1, source_target_pairs={{0,16},{1,17},{2,18},{3,19},{4,20},{5,21},{6,22},{7,23},{8,24},{9,... | collective-permute-start | bytes 786440 | tf_op jit(solution)/shard_map/ppermute | solution.py:523
  95.6 4.9 %project_kvb.1.kvb = bf16[2,512,128]{2,1,0:T(8,128)(2,1)} custom-call(s32[1]{0:T(128)} %bitcast.section_ref.refs_0_, f32[2,80,128]{2,1,0:T(8,128)} %pad_maximum_fusion.refs_1_.tabs_hbm, f32[2,128]{1,0:T(2,128)} %pad_maximum_fusion.1.refs_2_.gain_hbm, bf16[8,384,128]{2,1,0:T(8,128)(2,1)} %all-to-all-done.refs_3_, bf16[8,384,128]{2,1,0:T(8,128)(2,1)} %copy-done.3, ...), custom_call_target="tpu_custom_call" | custom-call | flops 805306368 | bytes 4718592 | tf_op jit(solution)/shard_map/project_kvb/pallas_call | solution.py:235
  100.5 1.5 %collective-permute-start.17 = (bf16[2,512,128]{2,1,0:T(8,128)(2,1)}, bf16[2,512,128]{2,1,0:T(8,128)(2,1)S(1)}, u32[]{:S(2)}, u32[]{:S(2)}) collective-permute-start(bf16[2,512,128]{2,1,0:T(8,128)(2,1)} %project_kvb.1.kvb), channel_id=1, source_target_pairs={{0,16},{1,17},{2,18},{3,19},{4,20},{5,21},{6,22},{7,23},{8,24},{9,... | collective-permute-start | bytes 786440 | tf_op jit(solution)/shard_map/ppermute | solution.py:529
  102.0 10.3 %attend_own.1 = (bf16[1024,128]{1,0:T(8,128)(2,1)}, f32[1024,128]{1,0:T(8,128)}, f32[1024,128]{1,0:T(8,128)}, f32[16,1024]{1,0:T(8,128)}) custom-call(s32[1]{0:T(128)} %bitcast.section_ref.refs_0_, f32[16,8]{1,0:T(8,128)} %fusion.3.rows_ref, f32[128,16]{1,0:T(8,128)} %fusion.1.keys_ref, bf16[2,512,128]{2,1,0:T(8,128)(2,1)} %project_kva.1.kva, ...), custom_call_target="tpu_custom_call" | custom-call | flops 1879048192 | bytes 6291456 | tf_op jit(solution)/shard_map/attend_own/pallas_call | solution.py:371
  113.0 3.1 %attend_second.1 = bf16[8,128,128]{2,1,0:T(8,128)(2,1)} custom-call(s32[1]{0:T(128)} %bitcast.section_ref.refs_0_, s32[2,16]{1,0:T(2,128)} %pad_add_fusion.place_ref, f32[16,1024]{1,0:T(8,128)} %get-tuple-element.51.keep_hbm, bf16[1024,128]{1,0:T(8,128)(2,1)} %get-tuple-element.52.q_hbm, f32[1024,128]{1,0:T(8,128)} %get-tuple-element.53.num_hbm, ...), custom_call_target="tpu_custom_call" | custom-call | flops 268435456 | bytes 2097152 | tf_op jit(solution)/shard_map/attend_second/pallas_call | solution.py:394
  116.1 14.1 %all_to_all.15.attn_ref = bf16[8,128,128]{2,1,0:T(8,128)(2,1)S(1)} all-to-all(bf16[8,128,128]{2,1,0:T(8,128)(2,1)} %attend_second.1), channel_id=1, replica_groups=mesh['section'=2,'seq'=8,'tp'=2] {'seq'}, dimensions={0} | all-to-all | bytes 524288 | tf_op jit(solution)/shard_map/all_to_all | solution.py:535
  130.8 1.6 %collective-permute-start.18 = (bf16[128,1536]{1,0:T(8,128)(2,1)S(1)}, bf16[128,1536]{1,0:T(8,128)(2,1)S(1)}, u32[]{:S(2)}, u32[]{:S(2)}) collective-permute-start(bf16[128,1536]{1,0:T(8,128)(2,1)S(1)} %out_sent.1), channel_id=1, source_target_pairs={{0,1},{1,0},{2,3},{3,2},{4,5},{5,4},{6,7},{7,6},{8,9},{9,8},{10,11... | collective-permute-start | bytes 1179656 | tf_op jit(solution)/shard_map/ppermute | solution.py:473
  133.7 7.6 %collective-permute-done.18 = bf16[128,1536]{1,0:T(8,128)(2,1)S(1)} collective-permute-done((bf16[128,1536]{1,0:T(8,128)(2,1)S(1)}, bf16[128,1536]{1,0:T(8,128)(2,1)S(1)}, u32[]{:S(2)}, u32[]{:S(2)}) %collective-permute-start.18) | collective-permute-done | bytes 393248 | tf_op jit(solution)/shard_map/ppermute | solution.py:473
  (99 shorter events, 21.7 us)
Async XLA Ops:
  2.9 12.8 %collective-permute-start.2 = (bf16[64,3072]{1,0:T(8,128)(2,1)}, bf16[64,3072]{1,0:T(8,128)(2,1)}, u32[]{:S(2)}, u32[]{:S(2)}) collective-permute-start(bf16[64,3072]{1,0:T(8,128)(2,1)} %get-tuple-element.31), channel_id=1, source_target_pairs={{0,4},{2,6},{4,0},{6,2},{8,12},{10,14},{12,8},{14,10},{1,5},{3,7},... | collective-permute-start | bytes 1179656 | tf_op jit(solution)/shard_map/ppermute | solution.py:467
  6.0 18.8 %collective-permute-start = (bf16[64,3072]{1,0:T(8,128)(2,1)}, bf16[64,3072]{1,0:T(8,128)(2,1)S(1)}, u32[]{:S(2)}, u32[]{:S(2)}) collective-permute-start(bf16[64,3072]{1,0:T(8,128)(2,1)} %get-tuple-element.31), channel_id=1, source_target_pairs={{4,8},{6,10},{8,4},{10,6},{5,9},{7,11},{9,5},{11,7},{20,24},{22,26... | collective-permute-start | bytes 1179656 | tf_op jit(solution)/shard_map/ppermute | solution.py:467
  8.8 44.7 %all-to-all-start = ((bf16[8,384,128]{2,1,0:T(8,128)(2,1)}), bf16[8,384,128]{2,1,0:T(8,128)(2,1)}, u32[]{:S(2)}, u32[]{:S(2)}) async-start(bf16[8,384,128]{2,1,0:T(8,128)(2,1)} %kv_weights.1), calls=%async_computation | async-start | bytes 1572864 | tf_op jit(solution)/shard_map/all_to_all | solution.py:462
  15.7 27.5 %collective-permute-start.3 = (bf16[64,3072]{1,0:T(8,128)(2,1)}, bf16[64,3072]{1,0:T(8,128)(2,1)}, u32[]{:S(2)}, u32[]{:S(2)}) collective-permute-start(bf16[64,3072]{1,0:T(8,128)(2,1)} %collective-permute-done.2.refs_7_.refs_2_), channel_id=1, source_target_pairs={{0,1},{1,0},{2,3},{3,2},{4,5},{5,4},{6,7},{7,6},{8,9},{9,8},{10,11... | collective-permute-start | bytes 1179656 | tf_op jit(solution)/shard_map/ppermute | solution.py:473
  17.2 26.7 %collective-permute-start.4 = (bf16[64,3072]{1,0:T(8,128)(2,1)}, bf16[64,3072]{1,0:T(8,128)(2,1)}, u32[]{:S(2)}, u32[]{:S(2)}) collective-permute-start(bf16[64,3072]{1,0:T(8,128)(2,1)} %collective-permute-done.2.refs_7_.refs_2_), channel_id=1, source_target_pairs={{4,8},{6,10},{8,4},{10,6},{5,9},{7,11},{9,5},{11,7},{20,24},{22,26... | collective-permute-start | bytes 1179656 | tf_op jit(solution)/shard_map/ppermute | solution.py:467
  24.8 17.4 %collective-permute-start.1 = (bf16[64,3072]{1,0:T(8,128)(2,1)S(1)}, bf16[64,3072]{1,0:T(8,128)(2,1)}, u32[]{:S(2)}, u32[]{:S(2)}) collective-permute-start(bf16[64,3072]{1,0:T(8,128)(2,1)S(1)} %collective-permute-done), channel_id=1, source_target_pairs={{4,0},{6,2},{8,12},{10,14},{5,1},{7,3},{9,13},{11,15},{20,16},{22,... | collective-permute-start | bytes 1179656 | tf_op jit(solution)/shard_map/ppermute | solution.py:467
  43.2 37.2 %copy-start.1 = (bf16[64,3072]{1,0:T(8,128)(2,1)}, bf16[64,3072]{1,0:T(8,128)(2,1)S(1)}, u32[]{:S(2)}) copy-start(bf16[64,3072]{1,0:T(8,128)(2,1)S(1)} %broadcast_select_fusion.1.refs_5_.refs_6_) | copy-start | bytes 1179652
  43.3 10.2 %collective-permute-start.6 = (bf16[64,3072]{1,0:T(8,128)(2,1)S(1)}, bf16[64,3072]{1,0:T(8,128)(2,1)}, u32[]{:S(2)}, u32[]{:S(2)}) collective-permute-start(bf16[64,3072]{1,0:T(8,128)(2,1)S(1)} %broadcast_select_fusion.1.refs_5_.refs_6_), channel_id=1, source_target_pairs={{0,1},{1,0},{2,3},{3,2},{4,5},{5,4},{6,7},{7,6},{8,9},{9,8},{10,11... | collective-permute-start | bytes 1179656 | tf_op jit(solution)/shard_map/ppermute | solution.py:473
  43.9 17.0 %collective-permute-start.5 = (bf16[64,3072]{1,0:T(8,128)(2,1)}, bf16[64,3072]{1,0:T(8,128)(2,1)}, u32[]{:S(2)}, u32[]{:S(2)}) collective-permute-start(bf16[64,3072]{1,0:T(8,128)(2,1)} %collective-permute-done.4), channel_id=1, source_target_pairs={{4,0},{6,2},{8,12},{10,14},{5,1},{7,3},{9,13},{11,15},{20,16},{22,... | collective-permute-start | bytes 1179656 | tf_op jit(solution)/shard_map/ppermute | solution.py:467
  53.5 48.5 %all-to-all-start.1 = ((bf16[8,528,128]{2,1,0:T(8,128)(2,1)}), bf16[8,528,128]{2,1,0:T(8,128)(2,1)}, u32[]{:S(2)}, u32[]{:S(2)}) async-start(bf16[8,528,128]{2,1,0:T(8,128)(2,1)} %direct_rows.1), calls=%async_computation.1 | async-start | bytes 2162688 | tf_op jit(solution)/shard_map/all_to_all | solution.py:518
  58.7 20.2 %collective-permute-start.7 = (bf16[8,384,128]{2,1,0:T(8,128)(2,1)}, bf16[8,384,128]{2,1,0:T(8,128)(2,1)S(1)}, u32[]{:S(2)}, u32[]{:S(2)}) collective-permute-start(bf16[8,384,128]{2,1,0:T(8,128)(2,1)} %all-to-all-done.refs_3_), channel_id=1, source_target_pairs={{0,16},{16,0},{1,17},{17,1},{2,18},{18,2},{3,19},{19,3},{4,20},{20... | collective-permute-start | bytes 2359304 | tf_op jit(solution)/shard_map/ppermute | solution.py:485
  60.2 20.7 %collective-permute-start.9 = (bf16[128,3072]{1,0:T(8,128)(2,1)}, bf16[128,3072]{1,0:T(8,128)(2,1)S(1)}, u32[]{:S(2)}, u32[]{:S(2)}) collective-permute-start(bf16[128,3072]{1,0:T(8,128)(2,1)} %get-tuple-element.45.refs_5_.refs_0_), channel_id=1, source_target_pairs={{0,2},{2,0},{4,6},{6,4},{8,10},{10,8},{12,14},{14,12},{1,3},{3,1},... | collective-permute-start | bytes 2359304 | tf_op jit(solution)/shard_map/ppermute | solution.py:470
  60.4 20.0 %collective-permute-start.10 = (bf16[64,3072]{1,0:T(8,128)(2,1)}, bf16[64,3072]{1,0:T(8,128)(2,1)S(1)}, u32[]{:S(2)}, u32[]{:S(2)}) collective-permute-start(bf16[64,3072]{1,0:T(8,128)(2,1)} %collective-permute-done.2.refs_7_.refs_2_), channel_id=1, source_target_pairs={{0,2},{2,0},{4,6},{6,4},{8,10},{10,8},{12,14},{14,12},{1,3},{3,1},... | collective-permute-start | bytes 1179656 | tf_op jit(solution)/shard_map/ppermute | solution.py:470
  60.7 20.3 %collective-permute-start.11 = (bf16[64,3072]{1,0:T(8,128)(2,1)}, bf16[64,3072]{1,0:T(8,128)(2,1)S(1)}, u32[]{:S(2)}, u32[]{:S(2)}) collective-permute-start(bf16[64,3072]{1,0:T(8,128)(2,1)} %collective-permute-done.3.refs_8_.refs_3_), channel_id=1, source_target_pairs={{0,2},{2,0},{4,6},{6,4},{8,10},{10,8},{12,14},{14,12},{1,3},{3,1},... | collective-permute-start | bytes 1179656 | tf_op jit(solution)/shard_map/ppermute | solution.py:470
  62.0 31.8 %copy-start.2 = (bf16[64,3072]{1,0:T(8,128)(2,1)}, bf16[64,3072]{1,0:T(8,128)(2,1)S(1)}, u32[]{:S(2)}) copy-start(bf16[64,3072]{1,0:T(8,128)(2,1)S(1)} %broadcast_select_fusion.refs_9_.refs_10_) | copy-start | bytes 1179652
  78.9 10.7 %collective-permute-start.8 = (bf16[64,3072]{1,0:T(8,128)(2,1)S(1)}, bf16[64,3072]{1,0:T(8,128)(2,1)S(1)}, u32[]{:S(2)}, u32[]{:S(2)}) collective-permute-start(bf16[64,3072]{1,0:T(8,128)(2,1)S(1)} %broadcast_select_fusion.refs_9_.refs_10_), channel_id=1, source_target_pairs={{0,1},{1,0},{2,3},{3,2},{4,5},{5,4},{6,7},{7,6},{8,9},{9,8},{10,11... | collective-permute-start | bytes 1179656 | tf_op jit(solution)/shard_map/ppermute | solution.py:473
  80.4 13.3 %collective-permute-start.12 = (bf16[64,3072]{1,0:T(8,128)(2,1)S(1)}, bf16[64,3072]{1,0:T(8,128)(2,1)S(1)}, u32[]{:S(2)}, u32[]{:S(2)}) collective-permute-start(bf16[64,3072]{1,0:T(8,128)(2,1)S(1)} %broadcast_select_fusion.1.refs_5_.refs_6_), channel_id=1, source_target_pairs={{0,2},{2,0},{4,6},{6,4},{8,10},{10,8},{12,14},{14,12},{1,3},{3,1},... | collective-permute-start | bytes 1179656 | tf_op jit(solution)/shard_map/ppermute | solution.py:470
  80.4 13.3 %collective-permute-start.14 = (bf16[64,3072]{1,0:T(8,128)(2,1)S(1)}, bf16[64,3072]{1,0:T(8,128)(2,1)S(1)}, u32[]{:S(2)}, u32[]{:S(2)}) collective-permute-start(bf16[64,3072]{1,0:T(8,128)(2,1)S(1)} %broadcast_select_fusion.refs_9_.refs_10_), channel_id=1, source_target_pairs={{0,2},{2,0},{4,6},{6,4},{8,10},{10,8},{12,14},{14,12},{1,3},{3,1},... | collective-permute-start | bytes 1179656 | tf_op jit(solution)/shard_map/ppermute | solution.py:470
  80.9 12.8 %collective-permute-start.13 = (bf16[64,3072]{1,0:T(8,128)(2,1)}, bf16[64,3072]{1,0:T(8,128)(2,1)S(1)}, u32[]{:S(2)}, u32[]{:S(2)}) collective-permute-start(bf16[64,3072]{1,0:T(8,128)(2,1)} %collective-permute-done.6.refs_6_.refs_7_), channel_id=1, source_target_pairs={{0,2},{2,0},{4,6},{6,4},{8,10},{10,8},{12,14},{14,12},{1,3},{3,1},... | collective-permute-start | bytes 1179656 | tf_op jit(solution)/shard_map/ppermute | solution.py:470
  89.6 4.1 %collective-permute-start.15 = (bf16[64,3072]{1,0:T(8,128)(2,1)S(1)}, bf16[64,3072]{1,0:T(8,128)(2,1)S(1)}, u32[]{:S(2)}, u32[]{:S(2)}) collective-permute-start(bf16[64,3072]{1,0:T(8,128)(2,1)S(1)} %collective-permute-done.8.refs_10_.refs_11_), channel_id=1, source_target_pairs={{0,2},{2,0},{4,6},{6,4},{8,10},{10,8},{12,14},{14,12},{1,3},{3,1},... | collective-permute-start | bytes 1179656 | tf_op jit(solution)/shard_map/ppermute | solution.py:470
  89.6 12.3 %collective-permute-start.16 = (bf16[2,512,128]{2,1,0:T(8,128)(2,1)}, bf16[2,512,128]{2,1,0:T(8,128)(2,1)}, u32[]{:S(2)}, u32[]{:S(2)}) collective-permute-start(bf16[2,512,128]{2,1,0:T(8,128)(2,1)} %project_kva.1.kva), channel_id=1, source_target_pairs={{0,16},{1,17},{2,18},{3,19},{4,20},{5,21},{6,22},{7,23},{8,24},{9,... | collective-permute-start | bytes 786440 | tf_op jit(solution)/shard_map/ppermute | solution.py:523
  100.5 11.8 %collective-permute-start.17 = (bf16[2,512,128]{2,1,0:T(8,128)(2,1)}, bf16[2,512,128]{2,1,0:T(8,128)(2,1)S(1)}, u32[]{:S(2)}, u32[]{:S(2)}) collective-permute-start(bf16[2,512,128]{2,1,0:T(8,128)(2,1)} %project_kvb.1.kvb), channel_id=1, source_target_pairs={{0,16},{1,17},{2,18},{3,19},{4,20},{5,21},{6,22},{7,23},{8,24},{9,... | collective-permute-start | bytes 786440 | tf_op jit(solution)/shard_map/ppermute | solution.py:529
  102.0 28.2 %copy-start = (bf16[1024,1536]{1,0:T(8,128)(2,1)S(1)}, bf16[1024,1536]{1,0:T(8,128)(2,1)}, u32[]{:S(2)}) copy-start(bf16[1024,1536]{1,0:T(8,128)(2,1)} %get-tuple-element.56.w_ref) | copy-start | bytes 9437188
  130.8 10.5 %collective-permute-start.18 = (bf16[128,1536]{1,0:T(8,128)(2,1)S(1)}, bf16[128,1536]{1,0:T(8,128)(2,1)S(1)}, u32[]{:S(2)}, u32[]{:S(2)}) collective-permute-start(bf16[128,1536]{1,0:T(8,128)(2,1)S(1)} %out_sent.1), channel_id=1, source_target_pairs={{0,1},{1,0},{2,3},{3,2},{4,5},{5,4},{6,7},{7,6},{8,9},{9,8},{10,11... | collective-permute-start | bytes 1179656 | tf_op jit(solution)/shard_map/ppermute | solution.py:473
  (14 other events, 67.2 us)

commit v13 on v11

--- a/solution.py
+++ b/solution.py
@@ -481,6 +481,7 @@
         return lax.ppermute(x, "tp", both)
 
     near = along_z(part, [(0, 1), (1, 0), (2, 3), (3, 2)])
+    near, w_late, at_chip = lax.optimization_barrier((near, w_out, chip.astype(jnp.int32)))
     middle = along_z(part, [(1, 2), (2, 1)])
     far = along_z(near, [(1, 2), (2, 1)])
     middle_end = along_z(middle, [(1, 0), (2, 3)])
@@ -496,9 +497,7 @@
     direct = direct_rows(rows3, text, mask)
 
     near_tp = to_tp(near)
-    direct, mine, w_late, at_chip = lax.optimization_barrier(
-        (direct, mine, w_out, chip.astype(jnp.int32))
-    )
+    direct, mine = lax.optimization_barrier((direct, mine))
     direct = lax.all_to_all(direct, "seq", 0, 0)
     some = seq // 2
     peers = [lax.ppermute(mine[:some], "section", both), lax.ppermute(mine[some:], "section", both)]

time: 135 us -> 136 us (level)
  starting transfers between devices: 37.6 us -> 41 us
  waiting for transfers between devices: 31.3 us -> 28.8 us
    ppermute x5, waiting for transfers between devices: 12 us -> 0.01 us  [along_z(): return lax.ppermute(x, 'seq', z_pairs(seq, pairs))]
    ppermute x1, waiting for transfers between devices: 0.01 us -> 8.75 us  [head_body(): lax.ppermute(mine[:some], 'section', both)]
    all_to_all x1, starting transfers between devices: 9.08 us -> 12.6 us  [head_body(): direct = lax.all_to_all(direct, 'seq', 0, 0)]
    ppermute x1, waiting for transfers between devices: 8.61 us -> 5.46 us  [head_body(): lax.ppermute(mine[some:], 'section', both)]
    all_to_all x1, waiting for transfers between devices: 0.01 us -> 2.83 us  [head_body(): mine = lax.all_to_all(kv_weights(section_at, rows3), 'seq', 0, 0)]
    ppermute x5, starting transfers between devices: 10.6 us -> 8.49 us  [along_z(): return lax.ppermute(x, 'seq', z_pairs(seq, pairs))]
    all_to_all x1, starting transfers between devices: 3.56 us -> 4.92 us  [head_body(): mine = lax.all_to_all(kv_weights(section_at, rows3), 'seq', 0, 0)]
  transfers between devices with their start and end apart: 22 -> 22, of which waited for: 4 -> 6; matrix products, arithmetic and copies ran while one was open for 11% -> 11% of each run, Pallas kernels for 19% -> 19%
where the time goes in v13:
time: 136 us; the launch traced here: 135 us
  starting transfers between devices  41 us (30%)
  Pallas kernels  32.3 us (24%)
  waiting for transfers between devices  28.8 us (21%)
  blocking collectives  13.3 us (10%)
  local copies, waits for them, and re-layouts  12.3 us (9%)
  other arithmetic  6.72 us (5%)
    all_to_all x1, blocking collectives, head_body(): attn = lax.all_to_all(attn, 'seq', 0, 0)  13.3 us
    all_to_all x1, starting transfers between devices, head_body(): direct = lax.all_to_all(direct, 'seq', 0, 0)  12.6 us
    ppermute x4, waiting for transfers between devices, to_tp(): return lax.ppermute(x, 'tp', both)  11.7 us
    pallas_call x1, Pallas kernels, attend_own(): call(own_kernel, 'attend_own', [jax.ShapeDtypeStruct((rows, HEAD_DIM), jn...  10.2 us
    pallas_call x2, Pallas kernels, project_kv(): call(lambda *refs: kv_kernel(chunk, *refs), 'project_kv' + 'ab'[chunk], j...  9.82 us
    ppermute x1, waiting for transfers between devices, head_body(): lax.ppermute(mine[:some], 'section', both)  8.75 us
    ppermute x5, starting transfers between devices, along_z(): return lax.ppermute(x, 'seq', z_pairs(seq, pairs))  8.49 us
    ppermute x4, starting transfers between devices, to_tp(): return lax.ppermute(x, 'tp', both)  6.14 us
  transfers between devices with their start and end apart: 22, of which 6 were waited for; matrix products, arithmetic and copies ran while one was open for 11% of the time, Pallas kernels for 19%

profile of v13, /device:TPU:0, one launch (start us, length us, event | category | flops | bytes accessed | tf_op | source)
XLA Modules:
  0.0 134.9 jit_solution(11868943339696773680)
XLA Ops:
  0.0 2.9 %norm_tokens.1 = (bf16[128,3072]{1,0:T(8,128)(2,1)}, bf16[64,3072]{1,0:T(8,128)(2,1)}) custom-call(s32[1]{0:T(128)} %bitcast.1.tp_ref, bf16[128,3072]{1,0:T(8,128)(2,1)} %bitcast.27, f32[3,1,3072]{2,1,0:T(1,128)} %bitcast.29), custom_call_target="tpu_custom_call" | custom-call | flops 3932160 | bytes 1572864 | tf_op jit(solution)/shard_map/norm_tokens/pallas_call | solution.py:94
  3.0 3.1 %collective-permute-start.2 = (bf16[64,3072]{1,0:T(8,128)(2,1)}, bf16[64,3072]{1,0:T(8,128)(2,1)S(1)}, u32[]{:S(2)}, u32[]{:S(2)}) collective-permute-start(bf16[64,3072]{1,0:T(8,128)(2,1)} %get-tuple-element.31), channel_id=1, source_target_pairs={{0,4},{2,6},{4,0},{6,2},{8,12},{10,14},{12,8},{14,10},{1,5},{3,7},... | collective-permute-start | bytes 1179656 | tf_op jit(solution)/shard_map/ppermute | solution.py:475
  7.5 2.1 %kv_weights.1 = bf16[8,384,128]{2,1,0:T(8,128)(2,1)} custom-call(s32[1]{0:T(128)} %bitcast.section_ref.refs_0_, bf16[3,384,1024]{2,1,0:T(8,128)(2,1)} %bitcast.25), custom_call_target="tpu_custom_call" | custom-call | bytes 1572864 | tf_op jit(solution)/shard_map/kv_weights/pallas_call | solution.py:123
  9.6 4.9 %all-to-all-start = ((bf16[8,384,128]{2,1,0:T(8,128)(2,1)}), bf16[8,384,128]{2,1,0:T(8,128)(2,1)}, u32[]{:S(2)}, u32[]{:S(2)}) async-start(bf16[8,384,128]{2,1,0:T(8,128)(2,1)} %kv_weights.1), calls=%async_computation | async-start | bytes 1572864 | tf_op jit(solution)/shard_map/all_to_all | solution.py:470
  17.2 3.0 %direct_rows.1 = bf16[8,528,128]{2,1,0:T(8,128)(2,1)} custom-call(bf16[3,384,1024]{2,1,0:T(8,128)(2,1)} %bitcast.26, bf16[8,128,128]{2,1,0:T(8,128)(2,1)} %bitcast.28, bf16[16,128]{1,0:T(8,128)(2,1)} %pad.4.mask_ref), custom_call_target="tpu_custom_call" | custom-call | bytes 2162688 | tf_op jit(solution)/shard_map/direct_rows/pallas_call | solution.py:146
  21.4 1.5 %collective-permute-start.3 = (bf16[64,3072]{1,0:T(8,128)(2,1)S(1)}, bf16[64,3072]{1,0:T(8,128)(2,1)}, u32[]{:S(2)}, u32[]{:S(2)}) collective-permute-start(bf16[64,3072]{1,0:T(8,128)(2,1)S(1)} %collective-permute-done.2.refs_8_.refs_2_), channel_id=1, source_target_pairs={{0,1},{1,0},{2,3},{3,2},{4,5},{5,4},{6,7},{7,6},{8,9},{9,8},{10,11... | collective-permute-start | bytes 1179656 | tf_op jit(solution)/shard_map/ppermute | solution.py:481
  26.5 4.9 %constant_dynamic-slice_fusion = (bf16[1024,1536]{1,0:T(8,128)(2,1)S(1)}, bf16[1024,1536]{1,0:T(8,128)(2,1)}) fusion(bf16[1024,3072]{1,0:T(8,128)(2,1)} %param.12, s32[]{:T(128)S(6)} %select_n.78, s32[]{:T(128)S(6)} %select_n.77), kind=kLoop, calls=%fused_computation.21 | loop fusion | bytes 12582920 | tf_op jit(solution)/shard_map/dynamic_slice | solution.py:506
  34.6 2.8 %all-to-all-done.refs_3_ = bf16[8,384,128]{2,1,0:T(8,128)(2,1)} async-done(((bf16[8,384,128]{2,1,0:T(8,128)(2,1)}), bf16[8,384,128]{2,1,0:T(8,128)(2,1)}, u32[]{:S(2)}, u32[]{:S(2)}) %all-to-all-start) | async-done | bytes 786464 | tf_op jit(solution)/shard_map/all_to_all | solution.py:470
  37.4 12.6 %all-to-all-start.1 = ((bf16[8,528,128]{2,1,0:T(8,128)(2,1)}), bf16[8,528,128]{2,1,0:T(8,128)(2,1)}, u32[]{:S(2)}, u32[]{:S(2)}) async-start(bf16[8,528,128]{2,1,0:T(8,128)(2,1)} %direct_rows.1), calls=%async_computation.1 | async-start | bytes 2162688 | tf_op jit(solution)/shard_map/all_to_all | solution.py:501
  51.2 1.6 %collective-permute-start.4 = (bf16[4,384,128]{2,1,0:T(8,128)(2,1)S(1)}, bf16[4,384,128]{2,1,0:T(8,128)(2,1)S(1)}, u32[]{:S(2)}, u32[]{:S(2)}) collective-permute-start(bf16[4,384,128]{2,1,0:T(8,128)(2,1)S(1)} %get-tuple-element.60), channel_id=1, source_target_pairs={{0,16},{16,0},{1,17},{17,1},{2,18},{18,2},{3,19},{19,3},{4,20},{20... | collective-permute-start | bytes 1179656 | tf_op jit(solution)/shard_map/ppermute | solution.py:503
  54.5 8.8 %collective-permute-done.4.refs_4_ = bf16[4,384,128]{2,1,0:T(8,128)(2,1)S(1)} collective-permute-done((bf16[4,384,128]{2,1,0:T(8,128)(2,1)S(1)}, bf16[4,384,128]{2,1,0:T(8,128)(2,1)S(1)}, u32[]{:S(2)}, u32[]{:S(2)}) %collective-permute-start.4) | collective-permute-done | bytes 393248 | tf_op jit(solution)/shard_map/ppermute | solution.py:503
  63.2 1.5 %collective-permute-start.7 = (bf16[64,3072]{1,0:T(8,128)(2,1)S(1)}, bf16[64,3072]{1,0:T(8,128)(2,1)S(1)}, u32[]{:S(2)}, u32[]{:S(2)}) collective-permute-start(bf16[64,3072]{1,0:T(8,128)(2,1)S(1)} %broadcast_select_fusion.1.refs_6_), channel_id=1, source_target_pairs={{0,1},{1,0},{2,3},{3,2},{4,5},{5,4},{6,7},{7,6},{8,9},{9,8},{10,11... | collective-permute-start | bytes 1179656 | tf_op jit(solution)/shard_map/ppermute | solution.py:481
  65.8 5.5 %collective-permute-done.8.refs_5_ = bf16[4,384,128]{2,1,0:T(8,128)(2,1)S(1)} collective-permute-done((bf16[4,384,128]{2,1,0:T(8,128)(2,1)S(1)}, bf16[4,384,128]{2,1,0:T(8,128)(2,1)S(1)}, u32[]{:S(2)}, u32[]{:S(2)}) %collective-permute-start.8) | collective-permute-done | bytes 393248 | tf_op jit(solution)/shard_map/ppermute | solution.py:503
  71.3 2.4 %collective-permute-done.7.refs_7_ = bf16[64,3072]{1,0:T(8,128)(2,1)S(1)} collective-permute-done((bf16[64,3072]{1,0:T(8,128)(2,1)S(1)}, bf16[64,3072]{1,0:T(8,128)(2,1)S(1)}, u32[]{:S(2)}, u32[]{:S(2)}) %collective-permute-start.7) | collective-permute-done | bytes 393248 | tf_op jit(solution)/shard_map/ppermute | solution.py:481
  73.7 1.5 %collective-permute-start.9 = (bf16[64,3072]{1,0:T(8,128)(2,1)S(1)}, bf16[64,3072]{1,0:T(8,128)(2,1)S(1)}, u32[]{:S(2)}, u32[]{:S(2)}) collective-permute-start(bf16[64,3072]{1,0:T(8,128)(2,1)S(1)} %broadcast_select_fusion.refs_10_), channel_id=1, source_target_pairs={{0,1},{1,0},{2,3},{3,2},{4,5},{5,4},{6,7},{7,6},{8,9},{9,8},{10,11... | collective-permute-start | bytes 1179656 | tf_op jit(solution)/shard_map/ppermute | solution.py:481
  76.6 4.9 %project_kva.1.kva = bf16[2,512,128]{2,1,0:T(8,128)(2,1)} custom-call(s32[1]{0:T(128)} %bitcast.section_ref.refs_0_, f32[2,80,128]{2,1,0:T(8,128)} %pad_maximum_fusion.refs_1_.tabs_hbm, f32[2,128]{1,0:T(2,128)} %pad_maximum_fusion.1.refs_2_.gain_hbm, bf16[8,384,128]{2,1,0:T(8,128)(2,1)} %all-to-all-done.refs_3_, bf16[4,384,128]{2,1,0:T(8,128)(2,1)} %copy-done.4, ...), custom_call_target="tpu_custom_call" | custom-call | flops 805306368 | bytes 4718592 | tf_op jit(solution)/shard_map/project_kva/pallas_call | solution.py:243
  81.5 1.7 %collective-permute-done.9.refs_11_ = bf16[64,3072]{1,0:T(8,128)(2,1)S(1)} collective-permute-done((bf16[64,3072]{1,0:T(8,128)(2,1)S(1)}, bf16[64,3072]{1,0:T(8,128)(2,1)S(1)}, u32[]{:S(2)}, u32[]{:S(2)}) %collective-permute-start.9) | collective-permute-done | bytes 393248 | tf_op jit(solution)/shard_map/ppermute | solution.py:481
  83.2 4.1 %collective-permute-start.17 = (bf16[2,512,128]{2,1,0:T(8,128)(2,1)}, bf16[2,512,128]{2,1,0:T(8,128)(2,1)}, u32[]{:S(2)}, u32[]{:S(2)}) collective-permute-start(bf16[2,512,128]{2,1,0:T(8,128)(2,1)} %project_kva.1.kva), channel_id=1, source_target_pairs={{0,16},{1,17},{2,18},{3,19},{4,20},{5,21},{6,22},{7,23},{8,24},{9,... | collective-permute-start | bytes 786440 | tf_op jit(solution)/shard_map/ppermute | solution.py:532
  89.1 4.9 %project_kvb.1.kvb = bf16[2,512,128]{2,1,0:T(8,128)(2,1)} custom-call(s32[1]{0:T(128)} %bitcast.section_ref.refs_0_, f32[2,80,128]{2,1,0:T(8,128)} %pad_maximum_fusion.refs_1_.tabs_hbm, f32[2,128]{1,0:T(2,128)} %pad_maximum_fusion.1.refs_2_.gain_hbm, bf16[8,384,128]{2,1,0:T(8,128)(2,1)} %all-to-all-done.refs_3_, bf16[4,384,128]{2,1,0:T(8,128)(2,1)} %copy-done.4, ...), custom_call_target="tpu_custom_call" | custom-call | flops 805306368 | bytes 4718592 | tf_op jit(solution)/shard_map/project_kvb/pallas_call | solution.py:243
  95.6 10.2 %attend_own.1 = (bf16[1024,128]{1,0:T(8,128)(2,1)}, f32[1024,128]{1,0:T(8,128)}, f32[1024,128]{1,0:T(8,128)}, f32[16,1024]{1,0:T(8,128)}) custom-call(s32[1]{0:T(128)} %bitcast.section_ref.refs_0_, f32[16,8]{1,0:T(8,128)} %fusion.3.rows_ref, f32[128,16]{1,0:T(8,128)} %fusion.1.keys_ref, bf16[2,512,128]{2,1,0:T(8,128)(2,1)} %project_kva.1.kva, ...), custom_call_target="tpu_custom_call" | custom-call | flops 1879048192 | bytes 6291456 | tf_op jit(solution)/shard_map/attend_own/pallas_call | solution.py:379
  106.6 3.0 %attend_second.1 = bf16[8,128,128]{2,1,0:T(8,128)(2,1)} custom-call(s32[1]{0:T(128)} %bitcast.section_ref.refs_0_, s32[2,16]{1,0:T(2,128)} %pad_add_fusion.place_ref, f32[16,1024]{1,0:T(8,128)} %get-tuple-element.51.keep_hbm, bf16[1024,128]{1,0:T(8,128)(2,1)} %get-tuple-element.52.q_hbm, f32[1024,128]{1,0:T(8,128)} %get-tuple-element.53.num_hbm, ...), custom_call_target="tpu_custom_call" | custom-call | flops 268435456 | bytes 2097152 | tf_op jit(solution)/shard_map/attend_second/pallas_call | solution.py:402
  109.6 13.3 %all_to_all.15.attn_ref = bf16[8,128,128]{2,1,0:T(8,128)(2,1)S(1)} all-to-all(bf16[8,128,128]{2,1,0:T(8,128)(2,1)} %attend_second.1), channel_id=1, replica_groups=mesh['section'=2,'seq'=8,'tp'=2] {'seq'}, dimensions={0} | all-to-all | bytes 524288 | tf_op jit(solution)/shard_map/all_to_all | solution.py:544
  123.5 1.6 %collective-permute-start.19 = (bf16[128,1536]{1,0:T(8,128)(2,1)S(1)}, bf16[128,1536]{1,0:T(8,128)(2,1)S(1)}, u32[]{:S(2)}, u32[]{:S(2)}) collective-permute-start(bf16[128,1536]{1,0:T(8,128)(2,1)S(1)} %out_sent.1), channel_id=1, source_target_pairs={{0,1},{1,0},{2,3},{3,2},{4,5},{5,4},{6,7},{7,6},{8,9},{9,8},{10,11... | collective-permute-start | bytes 1179656 | tf_op jit(solution)/shard_map/ppermute | solution.py:481
  126.4 7.6 %collective-permute-done.19 = bf16[128,1536]{1,0:T(8,128)(2,1)S(1)} collective-permute-done((bf16[128,1536]{1,0:T(8,128)(2,1)S(1)}, bf16[128,1536]{1,0:T(8,128)(2,1)S(1)}, u32[]{:S(2)}, u32[]{:S(2)}) %collective-permute-start.19) | collective-permute-done | bytes 393248 | tf_op jit(solution)/shard_map/ppermute | solution.py:481
  (106 shorter events, 23.9 us)
Async XLA Ops:
  3.0 18.0 %collective-permute-start.2 = (bf16[64,3072]{1,0:T(8,128)(2,1)}, bf16[64,3072]{1,0:T(8,128)(2,1)S(1)}, u32[]{:S(2)}, u32[]{:S(2)}) collective-permute-start(bf16[64,3072]{1,0:T(8,128)(2,1)} %get-tuple-element.31), channel_id=1, source_target_pairs={{0,4},{2,6},{4,0},{6,2},{8,12},{10,14},{12,8},{14,10},{1,5},{3,7},... | collective-permute-start | bytes 1179656 | tf_op jit(solution)/shard_map/ppermute | solution.py:475
  6.0 18.3 %collective-permute-start = (bf16[64,3072]{1,0:T(8,128)(2,1)}, bf16[64,3072]{1,0:T(8,128)(2,1)}, u32[]{:S(2)}, u32[]{:S(2)}) collective-permute-start(bf16[64,3072]{1,0:T(8,128)(2,1)} %get-tuple-element.31), channel_id=1, source_target_pairs={{4,8},{6,10},{8,4},{10,6},{5,9},{7,11},{9,5},{11,7},{20,24},{22,26... | collective-permute-start | bytes 1179656 | tf_op jit(solution)/shard_map/ppermute | solution.py:475
  9.6 27.8 %all-to-all-start = ((bf16[8,384,128]{2,1,0:T(8,128)(2,1)}), bf16[8,384,128]{2,1,0:T(8,128)(2,1)}, u32[]{:S(2)}, u32[]{:S(2)}) async-start(bf16[8,384,128]{2,1,0:T(8,128)(2,1)} %kv_weights.1), calls=%async_computation | async-start | bytes 1572864 | tf_op jit(solution)/shard_map/all_to_all | solution.py:470
  14.5 61.2 %collective-permute-start.10 = (bf16[128,3072]{1,0:T(8,128)(2,1)}, bf16[128,3072]{1,0:T(8,128)(2,1)}, u32[]{:S(2)}, u32[]{:S(2)}) collective-permute-start(bf16[128,3072]{1,0:T(8,128)(2,1)} %get-tuple-element.45.refs_6_.refs_0_), channel_id=1, source_target_pairs={{0,2},{2,0},{4,6},{6,4},{8,10},{10,8},{12,14},{14,12},{1,3},{3,1},... | collective-permute-start | bytes 2359304 | tf_op jit(solution)/shard_map/ppermute | solution.py:478
  21.4 32.5 %collective-permute-start.3 = (bf16[64,3072]{1,0:T(8,128)(2,1)S(1)}, bf16[64,3072]{1,0:T(8,128)(2,1)}, u32[]{:S(2)}, u32[]{:S(2)}) collective-permute-start(bf16[64,3072]{1,0:T(8,128)(2,1)S(1)} %collective-permute-done.2.refs_8_.refs_2_), channel_id=1, source_target_pairs={{0,1},{1,0},{2,3},{3,2},{4,5},{5,4},{6,7},{7,6},{8,9},{9,8},{10,11... | collective-permute-start | bytes 1179656 | tf_op jit(solution)/shard_map/ppermute | solution.py:481
  22.9 10.4 %collective-permute-start.5 = (bf16[64,3072]{1,0:T(8,128)(2,1)S(1)}, bf16[64,3072]{1,0:T(8,128)(2,1)}, u32[]{:S(2)}, u32[]{:S(2)}) collective-permute-start(bf16[64,3072]{1,0:T(8,128)(2,1)S(1)} %collective-permute-done.2.refs_8_.refs_2_), channel_id=1, source_target_pairs={{4,8},{6,10},{8,4},{10,6},{5,9},{7,11},{9,5},{11,7},{20,24},{22,26... | collective-permute-start | bytes 1179656 | tf_op jit(solution)/shard_map/ppermute | solution.py:475
  24.3 50.9 %collective-permute-start.11 = (bf16[64,3072]{1,0:T(8,128)(2,1)S(1)}, bf16[64,3072]{1,0:T(8,128)(2,1)}, u32[]{:S(2)}, u32[]{:S(2)}) collective-permute-start(bf16[64,3072]{1,0:T(8,128)(2,1)S(1)} %collective-permute-done.2.refs_8_.refs_2_), channel_id=1, source_target_pairs={{0,2},{2,0},{4,6},{6,4},{8,10},{10,8},{12,14},{14,12},{1,3},{3,1},... | collective-permute-start | bytes 1179656 | tf_op jit(solution)/shard_map/ppermute | solution.py:478
  24.4 26.8 %collective-permute-start.1 = (bf16[64,3072]{1,0:T(8,128)(2,1)}, bf16[64,3072]{1,0:T(8,128)(2,1)}, u32[]{:S(2)}, u32[]{:S(2)}) collective-permute-start(bf16[64,3072]{1,0:T(8,128)(2,1)} %collective-permute-done), channel_id=1, source_target_pairs={{4,0},{6,2},{8,12},{10,14},{5,1},{7,3},{9,13},{11,15},{20,16},{22,... | collective-permute-start | bytes 1179656 | tf_op jit(solution)/shard_map/ppermute | solution.py:475
  33.3 31.4 %collective-permute-start.6 = (bf16[64,3072]{1,0:T(8,128)(2,1)}, bf16[64,3072]{1,0:T(8,128)(2,1)}, u32[]{:S(2)}, u32[]{:S(2)}) collective-permute-start(bf16[64,3072]{1,0:T(8,128)(2,1)} %collective-permute-done.5), channel_id=1, source_target_pairs={{4,0},{6,2},{8,12},{10,14},{5,1},{7,3},{9,13},{11,15},{20,16},{22,... | collective-permute-start | bytes 1179656 | tf_op jit(solution)/shard_map/ppermute | solution.py:475
  37.4 58.1 %all-to-all-start.1 = ((bf16[8,528,128]{2,1,0:T(8,128)(2,1)}), bf16[8,528,128]{2,1,0:T(8,128)(2,1)}, u32[]{:S(2)}, u32[]{:S(2)}) async-start(bf16[8,528,128]{2,1,0:T(8,128)(2,1)} %direct_rows.1), calls=%async_computation.1 | async-start | bytes 2162688 | tf_op jit(solution)/shard_map/all_to_all | solution.py:501
  51.2 12.0 %collective-permute-start.4 = (bf16[4,384,128]{2,1,0:T(8,128)(2,1)S(1)}, bf16[4,384,128]{2,1,0:T(8,128)(2,1)S(1)}, u32[]{:S(2)}, u32[]{:S(2)}) collective-permute-start(bf16[4,384,128]{2,1,0:T(8,128)(2,1)S(1)} %get-tuple-element.60), channel_id=1, source_target_pairs={{0,16},{16,0},{1,17},{17,1},{2,18},{18,2},{3,19},{19,3},{4,20},{20... | collective-permute-start | bytes 1179656 | tf_op jit(solution)/shard_map/ppermute | solution.py:503
  53.8 33.6 %copy-start.1 = (bf16[64,3072]{1,0:T(8,128)(2,1)}, bf16[64,3072]{1,0:T(8,128)(2,1)S(1)}, u32[]{:S(2)}) copy-start(bf16[64,3072]{1,0:T(8,128)(2,1)S(1)} %broadcast_select_fusion.1.refs_6_) | copy-start | bytes 1179652
  53.9 17.4 %collective-permute-start.8 = (bf16[4,384,128]{2,1,0:T(8,128)(2,1)S(1)}, bf16[4,384,128]{2,1,0:T(8,128)(2,1)S(1)}, u32[]{:S(2)}, u32[]{:S(2)}) collective-permute-start(bf16[4,384,128]{2,1,0:T(8,128)(2,1)S(1)} %get-tuple-element.59), channel_id=1, source_target_pairs={{0,16},{16,0},{1,17},{17,1},{2,18},{18,2},{3,19},{19,3},{4,20},{20... | collective-permute-start | bytes 1179656 | tf_op jit(solution)/shard_map/ppermute | solution.py:503
  63.2 10.5 %collective-permute-start.7 = (bf16[64,3072]{1,0:T(8,128)(2,1)S(1)}, bf16[64,3072]{1,0:T(8,128)(2,1)S(1)}, u32[]{:S(2)}, u32[]{:S(2)}) collective-permute-start(bf16[64,3072]{1,0:T(8,128)(2,1)S(1)} %broadcast_select_fusion.1.refs_6_), channel_id=1, source_target_pairs={{0,1},{1,0},{2,3},{3,2},{4,5},{5,4},{6,7},{7,6},{8,9},{9,8},{10,11... | collective-permute-start | bytes 1179656 | tf_op jit(solution)/shard_map/ppermute | solution.py:481
  64.7 11.1 %collective-permute-start.12 = (bf16[64,3072]{1,0:T(8,128)(2,1)}, bf16[64,3072]{1,0:T(8,128)(2,1)S(1)}, u32[]{:S(2)}, u32[]{:S(2)}) collective-permute-start(bf16[64,3072]{1,0:T(8,128)(2,1)} %collective-permute-done.3.refs_9_.refs_3_), channel_id=1, source_target_pairs={{0,2},{2,0},{4,6},{6,4},{8,10},{10,8},{12,14},{14,12},{1,3},{3,1},... | collective-permute-start | bytes 1179656 | tf_op jit(solution)/shard_map/ppermute | solution.py:478
  73.7 9.5 %collective-permute-start.9 = (bf16[64,3072]{1,0:T(8,128)(2,1)S(1)}, bf16[64,3072]{1,0:T(8,128)(2,1)S(1)}, u32[]{:S(2)}, u32[]{:S(2)}) collective-permute-start(bf16[64,3072]{1,0:T(8,128)(2,1)S(1)} %broadcast_select_fusion.refs_10_), channel_id=1, source_target_pairs={{0,1},{1,0},{2,3},{3,2},{4,5},{5,4},{6,7},{7,6},{8,9},{9,8},{10,11... | collective-permute-start | bytes 1179656 | tf_op jit(solution)/shard_map/ppermute | solution.py:481
  75.2 12.2 %collective-permute-start.13 = (bf16[64,3072]{1,0:T(8,128)(2,1)S(1)}, bf16[64,3072]{1,0:T(8,128)(2,1)S(1)}, u32[]{:S(2)}, u32[]{:S(2)}) collective-permute-start(bf16[64,3072]{1,0:T(8,128)(2,1)S(1)} %broadcast_select_fusion.1.refs_6_), channel_id=1, source_target_pairs={{0,2},{2,0},{4,6},{6,4},{8,10},{10,8},{12,14},{14,12},{1,3},{3,1},... | collective-permute-start | bytes 1179656 | tf_op jit(solution)/shard_map/ppermute | solution.py:478
  75.2 12.2 %collective-permute-start.15 = (bf16[64,3072]{1,0:T(8,128)(2,1)S(1)}, bf16[64,3072]{1,0:T(8,128)(2,1)S(1)}, u32[]{:S(2)}, u32[]{:S(2)}) collective-permute-start(bf16[64,3072]{1,0:T(8,128)(2,1)S(1)} %broadcast_select_fusion.refs_10_), channel_id=1, source_target_pairs={{0,2},{2,0},{4,6},{6,4},{8,10},{10,8},{12,14},{14,12},{1,3},{3,1},... | collective-permute-start | bytes 1179656 | tf_op jit(solution)/shard_map/ppermute | solution.py:478
  75.7 11.6 %collective-permute-start.14 = (bf16[64,3072]{1,0:T(8,128)(2,1)S(1)}, bf16[64,3072]{1,0:T(8,128)(2,1)S(1)}, u32[]{:S(2)}, u32[]{:S(2)}) collective-permute-start(bf16[64,3072]{1,0:T(8,128)(2,1)S(1)} %collective-permute-done.7.refs_7_), channel_id=1, source_target_pairs={{0,2},{2,0},{4,6},{6,4},{8,10},{10,8},{12,14},{14,12},{1,3},{3,1},... | collective-permute-start | bytes 1179656 | tf_op jit(solution)/shard_map/ppermute | solution.py:478
  83.2 4.2 %collective-permute-start.16 = (bf16[64,3072]{1,0:T(8,128)(2,1)S(1)}, bf16[64,3072]{1,0:T(8,128)(2,1)S(1)}, u32[]{:S(2)}, u32[]{:S(2)}) collective-permute-start(bf16[64,3072]{1,0:T(8,128)(2,1)S(1)} %collective-permute-done.9.refs_11_), channel_id=1, source_target_pairs={{0,2},{2,0},{4,6},{6,4},{8,10},{10,8},{12,14},{14,12},{1,3},{3,1},... | collective-permute-start | bytes 1179656 | tf_op jit(solution)/shard_map/ppermute | solution.py:478
  83.2 12.3 %collective-permute-start.17 = (bf16[2,512,128]{2,1,0:T(8,128)(2,1)}, bf16[2,512,128]{2,1,0:T(8,128)(2,1)}, u32[]{:S(2)}, u32[]{:S(2)}) collective-permute-start(bf16[2,512,128]{2,1,0:T(8,128)(2,1)} %project_kva.1.kva), channel_id=1, source_target_pairs={{0,16},{1,17},{2,18},{3,19},{4,20},{5,21},{6,22},{7,23},{8,24},{9,... | collective-permute-start | bytes 786440 | tf_op jit(solution)/shard_map/ppermute | solution.py:532
  94.1 11.8 %collective-permute-start.18 = (bf16[2,512,128]{2,1,0:T(8,128)(2,1)}, bf16[2,512,128]{2,1,0:T(8,128)(2,1)S(1)}, u32[]{:S(2)}, u32[]{:S(2)}) collective-permute-start(bf16[2,512,128]{2,1,0:T(8,128)(2,1)} %project_kvb.1.kvb), channel_id=1, source_target_pairs={{0,16},{1,17},{2,18},{3,19},{4,20},{5,21},{6,22},{7,23},{8,24},{9,... | collective-permute-start | bytes 786440 | tf_op jit(solution)/shard_map/ppermute | solution.py:538
  95.6 27.3 %copy-start = (bf16[1024,1536]{1,0:T(8,128)(2,1)S(1)}, bf16[1024,1536]{1,0:T(8,128)(2,1)}, u32[]{:S(2)}) copy-start(bf16[1024,1536]{1,0:T(8,128)(2,1)} %get-tuple-element.56.w_ref) | copy-start | bytes 9437188
  123.5 10.5 %collective-permute-start.19 = (bf16[128,1536]{1,0:T(8,128)(2,1)S(1)}, bf16[128,1536]{1,0:T(8,128)(2,1)S(1)}, u32[]{:S(2)}, u32[]{:S(2)}) collective-permute-start(bf16[128,1536]{1,0:T(8,128)(2,1)S(1)} %out_sent.1), channel_id=1, source_target_pairs={{0,1},{1,0},{2,3},{3,2},{4,5},{5,4},{6,7},{7,6},{8,9},{9,8},{10,11... | collective-permute-start | bytes 1179656 | tf_op jit(solution)/shard_map/ppermute | solution.py:481
  (17 other events, 142.8 us)

commit v14 on v13

--- a/solution.py
+++ b/solution.py
@@ -497,10 +497,10 @@
     direct = direct_rows(rows3, text, mask)
 
     near_tp = to_tp(near)
-    direct, mine = lax.optimization_barrier((direct, mine))
-    direct = lax.all_to_all(direct, "seq", 0, 0)
     some = seq // 2
     peers = [lax.ppermute(mine[:some], "section", both), lax.ppermute(mine[some:], "section", both)]
+    direct, peers[0] = lax.optimization_barrier((direct, peers[0]))
+    direct = lax.all_to_all(direct, "seq", 0, 0)
     cols = w_out.shape[1] // 2
     w_sent = lax.dynamic_slice_in_dim(w_late, (1 - tp) * cols, cols, 1)
     w_kept = lax.dynamic_slice_in_dim(w_late, tp * cols, cols, 1)
@@ -522,10 +522,10 @@
     place = jnp.stack([shards, parts])
 
     early = (tabs, gains, row_tiles, key_tiles, place, w_sent, w_kept)
-    third, near_tp, peers[0], early = lax.optimization_barrier((third, near_tp, peers[0], early))
+    third, near_tp, early = lax.optimization_barrier((third, near_tp, early))
     tabs, gains, row_tiles, key_tiles, place, w_sent, w_kept = early
     third_tp = to_tp(third)
-    fourth, third_tp, peers[1] = lax.optimization_barrier((fourth, third_tp, peers[1]))
+    fourth, third_tp, peers[0] = lax.optimization_barrier((fourth, third_tp, peers[0]))
     fourth_tp = to_tp(fourth)
     a = [full, to_core(full), near, near_tp, to_core(near), to_core(near_tp)]
     kv_a = project_kv(0, section_at, tabs, gains, mine, peers, a)

time: 136 us -> 132 us (0.971)
  starting transfers between devices: 41 us -> 35.2 us
    all_to_all x1, starting transfers between devices: 12.6 us -> 5.76 us  [head_body(): direct = lax.all_to_all(direct, 'seq', 0, 0)]
    all_to_all x1, waiting for transfers between devices: 2.83 us -> 8.98 us  [head_body(): mine = lax.all_to_all(kv_weights(section_at, rows3), 'seq', 0, 0)]
    ppermute x1, waiting for transfers between devices: 8.75 us -> 3 us  [head_body(): lax.ppermute(mine[:some], 'section', both)]
    ppermute x1, waiting for transfers between devices: 5.46 us -> 0.01 us  [head_body(): lax.ppermute(mine[some:], 'section', both)]
    ppermute x4, waiting for transfers between devices: 11.7 us -> 16.2 us  [to_tp(): return lax.ppermute(x, 'tp', both)]
  transfers between devices with their start and end apart: 22 -> 22, of which waited for: 6 -> 6; matrix products, arithmetic and copies ran while one was open for 11% -> 11% of each run, Pallas kernels for 19% -> 20%
where the time goes in v14:
time: 132 us; the launch traced here: 131 us
  starting transfers between devices  35.2 us (27%)
  Pallas kernels  32.3 us (24%)
  waiting for transfers between devices  29.3 us (22%)
  blocking collectives  14.1 us (11%)
  local copies, waits for them, and re-layouts  12.8 us (10%)
  other arithmetic  6.72 us (5%)
    ppermute x4, waiting for transfers between devices, to_tp(): return lax.ppermute(x, 'tp', both)  16.2 us
    all_to_all x1, blocking collectives, head_body(): attn = lax.all_to_all(attn, 'seq', 0, 0)  14.1 us
    pallas_call x1, Pallas kernels, attend_own(): call(own_kernel, 'attend_own', [jax.ShapeDtypeStruct((rows, HEAD_DIM), jn...  10.2 us
    pallas_call x2, Pallas kernels, project_kv(): call(lambda *refs: kv_kernel(chunk, *refs), 'project_kv' + 'ab'[chunk], j...  9.82 us
    all_to_all x1, waiting for transfers between devices, head_body(): mine = lax.all_to_all(kv_weights(section_at, rows3), 'seq', 0, 0)  8.98 us
    ppermute x5, starting transfers between devices, along_z(): return lax.ppermute(x, 'seq', z_pairs(seq, pairs))  8.51 us
    ppermute x4, starting transfers between devices, to_tp(): return lax.ppermute(x, 'tp', both)  6.22 us
    all_to_all x1, starting transfers between devices, head_body(): direct = lax.all_to_all(direct, 'seq', 0, 0)  5.76 us
  transfers between devices with their start and end apart: 22, of which 6 were waited for; matrix products, arithmetic and copies ran while one was open for 11% of the time, Pallas kernels for 20%

profile of v14, /device:TPU:0, one launch (start us, length us, event | category | flops | bytes accessed | tf_op | source)
XLA Modules:
  0.0 130.9 jit_solution(14687565448111453120)
XLA Ops:
  0.0 2.9 %norm_tokens.1 = (bf16[128,3072]{1,0:T(8,128)(2,1)}, bf16[64,3072]{1,0:T(8,128)(2,1)}) custom-call(s32[1]{0:T(128)} %bitcast.1.tp_ref, bf16[128,3072]{1,0:T(8,128)(2,1)} %bitcast.27, f32[3,1,3072]{2,1,0:T(1,128)} %bitcast.29), custom_call_target="tpu_custom_call" | custom-call | flops 3932160 | bytes 1572864 | tf_op jit(solution)/shard_map/norm_tokens/pallas_call | solution.py:94
  3.0 3.1 %collective-permute-start.2 = (bf16[64,3072]{1,0:T(8,128)(2,1)}, bf16[64,3072]{1,0:T(8,128)(2,1)}, u32[]{:S(2)}, u32[]{:S(2)}) collective-permute-start(bf16[64,3072]{1,0:T(8,128)(2,1)} %get-tuple-element.30), channel_id=1, source_target_pairs={{0,4},{2,6},{4,0},{6,2},{8,12},{10,14},{12,8},{14,10},{1,5},{3,7},... | collective-permute-start | bytes 1179656 | tf_op jit(solution)/shard_map/ppermute | solution.py:475
  7.5 2.1 %kv_weights.1 = bf16[8,384,128]{2,1,0:T(8,128)(2,1)} custom-call(s32[1]{0:T(128)} %bitcast.section_ref.refs_0_, bf16[3,384,1024]{2,1,0:T(8,128)(2,1)} %bitcast.25), custom_call_target="tpu_custom_call" | custom-call | bytes 1572864 | tf_op jit(solution)/shard_map/kv_weights/pallas_call | solution.py:123
  9.6 4.9 %all-to-all-start = ((bf16[8,384,128]{2,1,0:T(8,128)(2,1)}), bf16[8,384,128]{2,1,0:T(8,128)(2,1)S(1)}, u32[]{:S(2)}, u32[]{:S(2)}) async-start(bf16[8,384,128]{2,1,0:T(8,128)(2,1)} %kv_weights.1), calls=%async_computation | async-start | bytes 1572864 | tf_op jit(solution)/shard_map/all_to_all | solution.py:470
  17.9 3.0 %direct_rows.1 = bf16[8,528,128]{2,1,0:T(8,128)(2,1)} custom-call(bf16[3,384,1024]{2,1,0:T(8,128)(2,1)} %bitcast.26, bf16[8,128,128]{2,1,0:T(8,128)(2,1)} %bitcast.28, bf16[16,128]{1,0:T(8,128)(2,1)} %pad.4.mask_ref), custom_call_target="tpu_custom_call" | custom-call | bytes 2162688 | tf_op jit(solution)/shard_map/direct_rows/pallas_call | solution.py:146
  21.4 1.5 %collective-permute-start.3 = (bf16[64,3072]{1,0:T(8,128)(2,1)}, bf16[64,3072]{1,0:T(8,128)(2,1)}, u32[]{:S(2)}, u32[]{:S(2)}) collective-permute-start(bf16[64,3072]{1,0:T(8,128)(2,1)} %collective-permute-done.2.refs_8_.refs_2_), channel_id=1, source_target_pairs={{0,1},{1,0},{2,3},{3,2},{4,5},{5,4},{6,7},{7,6},{8,9},{9,8},{10,11... | collective-permute-start | bytes 1179656 | tf_op jit(solution)/shard_map/ppermute | solution.py:481
  28.4 9.0 %all-to-all-done.refs_3_ = bf16[8,384,128]{2,1,0:T(8,128)(2,1)S(1)} async-done(((bf16[8,384,128]{2,1,0:T(8,128)(2,1)}), bf16[8,384,128]{2,1,0:T(8,128)(2,1)S(1)}, u32[]{:S(2)}, u32[]{:S(2)}) %all-to-all-start) | async-done | bytes 786464 | tf_op jit(solution)/shard_map/all_to_all | solution.py:470
  38.4 1.5 %collective-permute-start.7 = (bf16[4,384,128]{2,1,0:T(8,128)(2,1)S(1)}, bf16[4,384,128]{2,1,0:T(8,128)(2,1)S(1)}, u32[]{:S(2)}, u32[]{:S(2)}) collective-permute-start(bf16[4,384,128]{2,1,0:T(8,128)(2,1)S(1)} %get-tuple-element.58), channel_id=1, source_target_pairs={{0,16},{16,0},{1,17},{17,1},{2,18},{18,2},{3,19},{19,3},{4,20},{20... | collective-permute-start | bytes 1179656 | tf_op jit(solution)/shard_map/ppermute | solution.py:501
  39.9 4.9 %constant_dynamic-slice_fusion = (bf16[1024,1536]{1,0:T(8,128)(2,1)S(1)}, bf16[1024,1536]{1,0:T(8,128)(2,1)}) fusion(bf16[1024,3072]{1,0:T(8,128)(2,1)} %param.12, s32[]{:T(128)S(6)} %select_n.78, s32[]{:T(128)S(6)} %select_n.77), kind=kLoop, calls=%fused_computation.21 | loop fusion | bytes 12582920 | tf_op jit(solution)/shard_map/dynamic_slice | solution.py:506
  44.8 3.0 %collective-permute-done.7.refs_4_ = bf16[4,384,128]{2,1,0:T(8,128)(2,1)S(1)} collective-permute-done((bf16[4,384,128]{2,1,0:T(8,128)(2,1)S(1)}, bf16[4,384,128]{2,1,0:T(8,128)(2,1)S(1)}, u32[]{:S(2)}, u32[]{:S(2)}) %collective-permute-start.7) | collective-permute-done | bytes 393248 | tf_op jit(solution)/shard_map/ppermute | solution.py:501
  49.1 5.8 %all-to-all-start.1 = ((bf16[8,528,128]{2,1,0:T(8,128)(2,1)}), bf16[8,528,128]{2,1,0:T(8,128)(2,1)}, u32[]{:S(2)}, u32[]{:S(2)}) async-start(bf16[8,528,128]{2,1,0:T(8,128)(2,1)} %direct_rows.1), calls=%async_computation.1 | async-start | bytes 2162688 | tf_op jit(solution)/shard_map/all_to_all | solution.py:503
  56.0 1.6 %collective-permute-start.6 = (bf16[64,3072]{1,0:T(8,128)(2,1)S(1)}, bf16[64,3072]{1,0:T(8,128)(2,1)S(1)}, u32[]{:S(2)}, u32[]{:S(2)}) collective-permute-start(bf16[64,3072]{1,0:T(8,128)(2,1)S(1)} %broadcast_select_fusion.1.refs_6_), channel_id=1, source_target_pairs={{0,1},{1,0},{2,3},{3,2},{4,5},{5,4},{6,7},{7,6},{8,9},{9,8},{10,11... | collective-permute-start | bytes 1179656 | tf_op jit(solution)/shard_map/ppermute | solution.py:481
  61.3 6.3 %collective-permute-done.6.refs_7_ = bf16[64,3072]{1,0:T(8,128)(2,1)S(1)} collective-permute-done((bf16[64,3072]{1,0:T(8,128)(2,1)S(1)}, bf16[64,3072]{1,0:T(8,128)(2,1)S(1)}, u32[]{:S(2)}, u32[]{:S(2)}) %collective-permute-start.6) | collective-permute-done | bytes 393248 | tf_op jit(solution)/shard_map/ppermute | solution.py:481
  67.6 1.5 %collective-permute-start.8 = (bf16[64,3072]{1,0:T(8,128)(2,1)S(1)}, bf16[64,3072]{1,0:T(8,128)(2,1)S(1)}, u32[]{:S(2)}, u32[]{:S(2)}) collective-permute-start(bf16[64,3072]{1,0:T(8,128)(2,1)S(1)} %broadcast_select_fusion.refs_10_), channel_id=1, source_target_pairs={{0,1},{1,0},{2,3},{3,2},{4,5},{5,4},{6,7},{7,6},{8,9},{9,8},{10,11... | collective-permute-start | bytes 1179656 | tf_op jit(solution)/shard_map/ppermute | solution.py:481
  71.1 4.9 %project_kva.1.kva = bf16[2,512,128]{2,1,0:T(8,128)(2,1)} custom-call(s32[1]{0:T(128)} %bitcast.section_ref.refs_0_, f32[2,80,128]{2,1,0:T(8,128)} %pad_maximum_fusion.refs_1_.tabs_hbm, f32[2,128]{1,0:T(2,128)} %pad_maximum_fusion.1.refs_2_.gain_hbm, bf16[8,384,128]{2,1,0:T(8,128)(2,1)} %copy-done.1, bf16[4,384,128]{2,1,0:T(8,128)(2,1)} %copy-done.5, ...), custom_call_target="tpu_custom_call" | custom-call | flops 805306368 | bytes 4718592 | tf_op jit(solution)/shard_map/project_kva/pallas_call | solution.py:243
  76.0 2.4 %collective-permute-done.8.refs_11_ = bf16[64,3072]{1,0:T(8,128)(2,1)S(1)} collective-permute-done((bf16[64,3072]{1,0:T(8,128)(2,1)S(1)}, bf16[64,3072]{1,0:T(8,128)(2,1)S(1)}, u32[]{:S(2)}, u32[]{:S(2)}) %collective-permute-start.8) | collective-permute-done | bytes 393248 | tf_op jit(solution)/shard_map/ppermute | solution.py:481
  78.4 4.1 %collective-permute-start.17 = (bf16[2,512,128]{2,1,0:T(8,128)(2,1)}, bf16[2,512,128]{2,1,0:T(8,128)(2,1)}, u32[]{:S(2)}, u32[]{:S(2)}) collective-permute-start(bf16[2,512,128]{2,1,0:T(8,128)(2,1)} %project_kva.1.kva), channel_id=1, source_target_pairs={{0,16},{1,17},{2,18},{3,19},{4,20},{5,21},{6,22},{7,23},{8,24},{9,... | collective-permute-start | bytes 786440 | tf_op jit(solution)/shard_map/ppermute | solution.py:532
  84.3 4.9 %project_kvb.1.kvb = bf16[2,512,128]{2,1,0:T(8,128)(2,1)} custom-call(s32[1]{0:T(128)} %bitcast.section_ref.refs_0_, f32[2,80,128]{2,1,0:T(8,128)} %pad_maximum_fusion.refs_1_.tabs_hbm, f32[2,128]{1,0:T(2,128)} %pad_maximum_fusion.1.refs_2_.gain_hbm, bf16[8,384,128]{2,1,0:T(8,128)(2,1)} %copy-done.1, bf16[4,384,128]{2,1,0:T(8,128)(2,1)} %copy-done.5, ...), custom_call_target="tpu_custom_call" | custom-call | flops 805306368 | bytes 4718592 | tf_op jit(solution)/shard_map/project_kvb/pallas_call | solution.py:243
  89.2 1.5 %collective-permute-start.18 = (bf16[2,512,128]{2,1,0:T(8,128)(2,1)}, bf16[2,512,128]{2,1,0:T(8,128)(2,1)S(1)}, u32[]{:S(2)}, u32[]{:S(2)}) collective-permute-start(bf16[2,512,128]{2,1,0:T(8,128)(2,1)} %project_kvb.1.kvb), channel_id=1, source_target_pairs={{0,16},{1,17},{2,18},{3,19},{4,20},{5,21},{6,22},{7,23},{8,24},{9,... | collective-permute-start | bytes 786440 | tf_op jit(solution)/shard_map/ppermute | solution.py:538
  90.7 10.2 %attend_own.1 = (bf16[1024,128]{1,0:T(8,128)(2,1)}, f32[1024,128]{1,0:T(8,128)}, f32[1024,128]{1,0:T(8,128)}, f32[16,1024]{1,0:T(8,128)}) custom-call(s32[1]{0:T(128)} %bitcast.section_ref.refs_0_, f32[16,8]{1,0:T(8,128)} %fusion.3.rows_ref, f32[128,16]{1,0:T(8,128)} %fusion.1.keys_ref, bf16[2,512,128]{2,1,0:T(8,128)(2,1)} %project_kva.1.kva, ...), custom_call_target="tpu_custom_call" | custom-call | flops 1879048192 | bytes 6291456 | tf_op jit(solution)/shard_map/attend_own/pallas_call | solution.py:379
  101.7 3.0 %attend_second.1 = bf16[8,128,128]{2,1,0:T(8,128)(2,1)} custom-call(s32[1]{0:T(128)} %bitcast.section_ref.refs_0_, s32[2,16]{1,0:T(2,128)} %pad_add_fusion.place_ref, f32[16,1024]{1,0:T(8,128)} %get-tuple-element.49.keep_hbm, bf16[1024,128]{1,0:T(8,128)(2,1)} %get-tuple-element.50.q_hbm, f32[1024,128]{1,0:T(8,128)} %get-tuple-element.51.num_hbm, ...), custom_call_target="tpu_custom_call" | custom-call | flops 268435456 | bytes 2097152 | tf_op jit(solution)/shard_map/attend_second/pallas_call | solution.py:402
  104.8 14.1 %all_to_all.15.attn_ref = bf16[8,128,128]{2,1,0:T(8,128)(2,1)S(1)} all-to-all(bf16[8,128,128]{2,1,0:T(8,128)(2,1)} %attend_second.1), channel_id=1, replica_groups=mesh['section'=2,'seq'=8,'tp'=2] {'seq'}, dimensions={0} | all-to-all | bytes 524288 | tf_op jit(solution)/shard_map/all_to_all | solution.py:544
  119.5 1.6 %collective-permute-start.19 = (bf16[128,1536]{1,0:T(8,128)(2,1)S(1)}, bf16[128,1536]{1,0:T(8,128)(2,1)S(1)}, u32[]{:S(2)}, u32[]{:S(2)}) collective-permute-start(bf16[128,1536]{1,0:T(8,128)(2,1)S(1)} %out_sent.1), channel_id=1, source_target_pairs={{0,1},{1,0},{2,3},{3,2},{4,5},{5,4},{6,7},{7,6},{8,9},{9,8},{10,11... | collective-permute-start | bytes 1179656 | tf_op jit(solution)/shard_map/ppermute | solution.py:481
  122.4 7.6 %collective-permute-done.19 = bf16[128,1536]{1,0:T(8,128)(2,1)S(1)} collective-permute-done((bf16[128,1536]{1,0:T(8,128)(2,1)S(1)}, bf16[128,1536]{1,0:T(8,128)(2,1)S(1)}, u32[]{:S(2)}, u32[]{:S(2)}) %collective-permute-start.19) | collective-permute-done | bytes 393248 | tf_op jit(solution)/shard_map/ppermute | solution.py:481
  (106 shorter events, 25.0 us)
Async XLA Ops:
  3.0 18.0 %collective-permute-start.2 = (bf16[64,3072]{1,0:T(8,128)(2,1)}, bf16[64,3072]{1,0:T(8,128)(2,1)}, u32[]{:S(2)}, u32[]{:S(2)}) collective-permute-start(bf16[64,3072]{1,0:T(8,128)(2,1)} %get-tuple-element.30), channel_id=1, source_target_pairs={{0,4},{2,6},{4,0},{6,2},{8,12},{10,14},{12,8},{14,10},{1,5},{3,7},... | collective-permute-start | bytes 1179656 | tf_op jit(solution)/shard_map/ppermute | solution.py:475
  6.1 18.2 %collective-permute-start = (bf16[64,3072]{1,0:T(8,128)(2,1)}, bf16[64,3072]{1,0:T(8,128)(2,1)}, u32[]{:S(2)}, u32[]{:S(2)}) collective-permute-start(bf16[64,3072]{1,0:T(8,128)(2,1)} %get-tuple-element.30), channel_id=1, source_target_pairs={{4,8},{6,10},{8,4},{10,6},{5,9},{7,11},{9,5},{11,7},{20,24},{22,26... | collective-permute-start | bytes 1179656 | tf_op jit(solution)/shard_map/ppermute | solution.py:475
  9.6 27.7 %all-to-all-start = ((bf16[8,384,128]{2,1,0:T(8,128)(2,1)}), bf16[8,384,128]{2,1,0:T(8,128)(2,1)S(1)}, u32[]{:S(2)}, u32[]{:S(2)}) async-start(bf16[8,384,128]{2,1,0:T(8,128)(2,1)} %kv_weights.1), calls=%async_computation | async-start | bytes 1572864 | tf_op jit(solution)/shard_map/all_to_all | solution.py:470
  14.5 54.6 %collective-permute-start.10 = (bf16[128,3072]{1,0:T(8,128)(2,1)}, bf16[128,3072]{1,0:T(8,128)(2,1)}, u32[]{:S(2)}, u32[]{:S(2)}) collective-permute-start(bf16[128,3072]{1,0:T(8,128)(2,1)} %get-tuple-element.43.refs_6_.refs_0_), channel_id=1, source_target_pairs={{0,2},{2,0},{4,6},{6,4},{8,10},{10,8},{12,14},{14,12},{1,3},{3,1},... | collective-permute-start | bytes 2359304 | tf_op jit(solution)/shard_map/ppermute | solution.py:478
  21.4 34.6 %collective-permute-start.3 = (bf16[64,3072]{1,0:T(8,128)(2,1)}, bf16[64,3072]{1,0:T(8,128)(2,1)}, u32[]{:S(2)}, u32[]{:S(2)}) collective-permute-start(bf16[64,3072]{1,0:T(8,128)(2,1)} %collective-permute-done.2.refs_8_.refs_2_), channel_id=1, source_target_pairs={{0,1},{1,0},{2,3},{3,2},{4,5},{5,4},{6,7},{7,6},{8,9},{9,8},{10,11... | collective-permute-start | bytes 1179656 | tf_op jit(solution)/shard_map/ppermute | solution.py:481
  22.9 21.9 %collective-permute-start.4 = (bf16[64,3072]{1,0:T(8,128)(2,1)}, bf16[64,3072]{1,0:T(8,128)(2,1)}, u32[]{:S(2)}, u32[]{:S(2)}) collective-permute-start(bf16[64,3072]{1,0:T(8,128)(2,1)} %collective-permute-done.2.refs_8_.refs_2_), channel_id=1, source_target_pairs={{4,8},{6,10},{8,4},{10,6},{5,9},{7,11},{9,5},{11,7},{20,24},{22,26... | collective-permute-start | bytes 1179656 | tf_op jit(solution)/shard_map/ppermute | solution.py:475
  24.3 30.6 %collective-permute-start.1 = (bf16[64,3072]{1,0:T(8,128)(2,1)}, bf16[64,3072]{1,0:T(8,128)(2,1)}, u32[]{:S(2)}, u32[]{:S(2)}) collective-permute-start(bf16[64,3072]{1,0:T(8,128)(2,1)} %collective-permute-done), channel_id=1, source_target_pairs={{4,0},{6,2},{8,12},{10,14},{5,1},{7,3},{9,13},{11,15},{20,16},{22,... | collective-permute-start | bytes 1179656 | tf_op jit(solution)/shard_map/ppermute | solution.py:475
  38.4 9.4 %collective-permute-start.7 = (bf16[4,384,128]{2,1,0:T(8,128)(2,1)S(1)}, bf16[4,384,128]{2,1,0:T(8,128)(2,1)S(1)}, u32[]{:S(2)}, u32[]{:S(2)}) collective-permute-start(bf16[4,384,128]{2,1,0:T(8,128)(2,1)S(1)} %get-tuple-element.58), channel_id=1, source_target_pairs={{0,16},{16,0},{1,17},{17,1},{2,18},{18,2},{3,19},{19,3},{4,20},{20... | collective-permute-start | bytes 1179656 | tf_op jit(solution)/shard_map/ppermute | solution.py:501
  44.8 24.2 %collective-permute-start.11 = (bf16[64,3072]{1,0:T(8,128)(2,1)}, bf16[64,3072]{1,0:T(8,128)(2,1)}, u32[]{:S(2)}, u32[]{:S(2)}) collective-permute-start(bf16[64,3072]{1,0:T(8,128)(2,1)} %collective-permute-done.2.refs_8_.refs_2_), channel_id=1, source_target_pairs={{0,2},{2,0},{4,6},{6,4},{8,10},{10,8},{12,14},{14,12},{1,3},{3,1},... | collective-permute-start | bytes 1179656 | tf_op jit(solution)/shard_map/ppermute | solution.py:478
  47.8 11.0 %collective-permute-start.5 = (bf16[64,3072]{1,0:T(8,128)(2,1)}, bf16[64,3072]{1,0:T(8,128)(2,1)}, u32[]{:S(2)}, u32[]{:S(2)}) collective-permute-start(bf16[64,3072]{1,0:T(8,128)(2,1)} %collective-permute-done.4), channel_id=1, source_target_pairs={{4,0},{6,2},{8,12},{10,14},{5,1},{7,3},{9,13},{11,15},{20,16},{22,... | collective-permute-start | bytes 1179656 | tf_op jit(solution)/shard_map/ppermute | solution.py:475
  49.1 41.6 %all-to-all-start.1 = ((bf16[8,528,128]{2,1,0:T(8,128)(2,1)}), bf16[8,528,128]{2,1,0:T(8,128)(2,1)}, u32[]{:S(2)}, u32[]{:S(2)}) async-start(bf16[8,528,128]{2,1,0:T(8,128)(2,1)} %direct_rows.1), calls=%async_computation.1 | async-start | bytes 2162688 | tf_op jit(solution)/shard_map/all_to_all | solution.py:503
  56.0 26.6 %copy-start.2 = (bf16[64,3072]{1,0:T(8,128)(2,1)}, bf16[64,3072]{1,0:T(8,128)(2,1)S(1)}, u32[]{:S(2)}) copy-start(bf16[64,3072]{1,0:T(8,128)(2,1)S(1)} %broadcast_select_fusion.1.refs_6_) | copy-start | bytes 1179652
  56.0 11.6 %collective-permute-start.6 = (bf16[64,3072]{1,0:T(8,128)(2,1)S(1)}, bf16[64,3072]{1,0:T(8,128)(2,1)S(1)}, u32[]{:S(2)}, u32[]{:S(2)}) collective-permute-start(bf16[64,3072]{1,0:T(8,128)(2,1)S(1)} %broadcast_select_fusion.1.refs_6_), channel_id=1, source_target_pairs={{0,1},{1,0},{2,3},{3,2},{4,5},{5,4},{6,7},{7,6},{8,9},{9,8},{10,11... | collective-permute-start | bytes 1179656 | tf_op jit(solution)/shard_map/ppermute | solution.py:481
  57.6 12.0 %collective-permute-start.12 = (bf16[64,3072]{1,0:T(8,128)(2,1)}, bf16[64,3072]{1,0:T(8,128)(2,1)S(1)}, u32[]{:S(2)}, u32[]{:S(2)}) collective-permute-start(bf16[64,3072]{1,0:T(8,128)(2,1)} %collective-permute-done.3.refs_9_.refs_3_), channel_id=1, source_target_pairs={{0,2},{2,0},{4,6},{6,4},{8,10},{10,8},{12,14},{14,12},{1,3},{3,1},... | collective-permute-start | bytes 1179656 | tf_op jit(solution)/shard_map/ppermute | solution.py:478
  58.8 10.8 %collective-permute-start.9 = (bf16[4,384,128]{2,1,0:T(8,128)(2,1)}, bf16[4,384,128]{2,1,0:T(8,128)(2,1)S(1)}, u32[]{:S(2)}, u32[]{:S(2)}) collective-permute-start(bf16[4,384,128]{2,1,0:T(8,128)(2,1)} %get-tuple-element.57), channel_id=1, source_target_pairs={{0,16},{16,0},{1,17},{17,1},{2,18},{18,2},{3,19},{19,3},{4,20},{20... | collective-permute-start | bytes 1179656 | tf_op jit(solution)/shard_map/ppermute | solution.py:501
  67.6 10.8 %collective-permute-start.8 = (bf16[64,3072]{1,0:T(8,128)(2,1)S(1)}, bf16[64,3072]{1,0:T(8,128)(2,1)S(1)}, u32[]{:S(2)}, u32[]{:S(2)}) collective-permute-start(bf16[64,3072]{1,0:T(8,128)(2,1)S(1)} %broadcast_select_fusion.refs_10_), channel_id=1, source_target_pairs={{0,1},{1,0},{2,3},{3,2},{4,5},{5,4},{6,7},{7,6},{8,9},{9,8},{10,11... | collective-permute-start | bytes 1179656 | tf_op jit(solution)/shard_map/ppermute | solution.py:481
  69.1 13.4 %collective-permute-start.13 = (bf16[64,3072]{1,0:T(8,128)(2,1)S(1)}, bf16[64,3072]{1,0:T(8,128)(2,1)S(1)}, u32[]{:S(2)}, u32[]{:S(2)}) collective-permute-start(bf16[64,3072]{1,0:T(8,128)(2,1)S(1)} %broadcast_select_fusion.1.refs_6_), channel_id=1, source_target_pairs={{0,2},{2,0},{4,6},{6,4},{8,10},{10,8},{12,14},{14,12},{1,3},{3,1},... | collective-permute-start | bytes 1179656 | tf_op jit(solution)/shard_map/ppermute | solution.py:478
  69.1 13.4 %collective-permute-start.15 = (bf16[64,3072]{1,0:T(8,128)(2,1)S(1)}, bf16[64,3072]{1,0:T(8,128)(2,1)S(1)}, u32[]{:S(2)}, u32[]{:S(2)}) collective-permute-start(bf16[64,3072]{1,0:T(8,128)(2,1)S(1)} %broadcast_select_fusion.refs_10_), channel_id=1, source_target_pairs={{0,2},{2,0},{4,6},{6,4},{8,10},{10,8},{12,14},{14,12},{1,3},{3,1},... | collective-permute-start | bytes 1179656 | tf_op jit(solution)/shard_map/ppermute | solution.py:478
  69.6 12.9 %collective-permute-start.14 = (bf16[64,3072]{1,0:T(8,128)(2,1)S(1)}, bf16[64,3072]{1,0:T(8,128)(2,1)S(1)}, u32[]{:S(2)}, u32[]{:S(2)}) collective-permute-start(bf16[64,3072]{1,0:T(8,128)(2,1)S(1)} %collective-permute-done.6.refs_7_), channel_id=1, source_target_pairs={{0,2},{2,0},{4,6},{6,4},{8,10},{10,8},{12,14},{14,12},{1,3},{3,1},... | collective-permute-start | bytes 1179656 | tf_op jit(solution)/shard_map/ppermute | solution.py:478
  78.4 4.2 %collective-permute-start.16 = (bf16[64,3072]{1,0:T(8,128)(2,1)S(1)}, bf16[64,3072]{1,0:T(8,128)(2,1)S(1)}, u32[]{:S(2)}, u32[]{:S(2)}) collective-permute-start(bf16[64,3072]{1,0:T(8,128)(2,1)S(1)} %collective-permute-done.8.refs_11_), channel_id=1, source_target_pairs={{0,2},{2,0},{4,6},{6,4},{8,10},{10,8},{12,14},{14,12},{1,3},{3,1},... | collective-permute-start | bytes 1179656 | tf_op jit(solution)/shard_map/ppermute | solution.py:478
  78.4 12.3 %collective-permute-start.17 = (bf16[2,512,128]{2,1,0:T(8,128)(2,1)}, bf16[2,512,128]{2,1,0:T(8,128)(2,1)}, u32[]{:S(2)}, u32[]{:S(2)}) collective-permute-start(bf16[2,512,128]{2,1,0:T(8,128)(2,1)} %project_kva.1.kva), channel_id=1, source_target_pairs={{0,16},{1,17},{2,18},{3,19},{4,20},{5,21},{6,22},{7,23},{8,24},{9,... | collective-permute-start | bytes 786440 | tf_op jit(solution)/shard_map/ppermute | solution.py:532
  89.2 11.8 %collective-permute-start.18 = (bf16[2,512,128]{2,1,0:T(8,128)(2,1)}, bf16[2,512,128]{2,1,0:T(8,128)(2,1)S(1)}, u32[]{:S(2)}, u32[]{:S(2)}) collective-permute-start(bf16[2,512,128]{2,1,0:T(8,128)(2,1)} %project_kvb.1.kvb), channel_id=1, source_target_pairs={{0,16},{1,17},{2,18},{3,19},{4,20},{5,21},{6,22},{7,23},{8,24},{9,... | collective-permute-start | bytes 786440 | tf_op jit(solution)/shard_map/ppermute | solution.py:538
  90.7 28.1 %copy-start = (bf16[1024,1536]{1,0:T(8,128)(2,1)S(1)}, bf16[1024,1536]{1,0:T(8,128)(2,1)}, u32[]{:S(2)}) copy-start(bf16[1024,1536]{1,0:T(8,128)(2,1)} %get-tuple-element.54.w_ref) | copy-start | bytes 9437188
  119.5 10.5 %collective-permute-start.19 = (bf16[128,1536]{1,0:T(8,128)(2,1)S(1)}, bf16[128,1536]{1,0:T(8,128)(2,1)S(1)}, u32[]{:S(2)}, u32[]{:S(2)}) collective-permute-start(bf16[128,1536]{1,0:T(8,128)(2,1)S(1)} %out_sent.1), channel_id=1, source_target_pairs={{0,1},{1,0},{2,3},{3,2},{4,5},{5,4},{6,7},{7,6},{8,9},{9,8},{10,11... | collective-permute-start | bytes 1179656 | tf_op jit(solution)/shard_map/ppermute | solution.py:481
  (17 other events, 151.0 us)

commit v15 on v14

--- a/solution.py
+++ b/solution.py
@@ -278,7 +278,7 @@
     return (weights.reshape(groups, rows // groups, keys) * keep[:, None, :]).reshape(rows, keys)
 
 
-BLOCK = 256
+BLOCK = 512
 
 
 def own_kernel(

time: 132 us -> 134 us (1.015)
  Pallas kernels: 32.3 us -> 34.1 us
    pallas_call x1, Pallas kernels: 10.2 us -> 12.7 us  [attend_own(): call(own_kernel, 'attend_own', [jax.ShapeDtypeStruct((rows, HEAD_DIM), jn...]
  transfers between devices with their start and end apart: 22 -> 22, of which waited for: 6 -> 6; matrix products, arithmetic and copies ran while one was open for 11% -> 11% of each run, Pallas kernels for 20% -> 21%
where the time goes in v15:
time: 134 us; the launch traced here: 133 us
  starting transfers between devices  35.2 us (26%)
  Pallas kernels  34.1 us (25%)
  waiting for transfers between devices  29.7 us (22%)
  blocking collectives  14.1 us (11%)
  local copies, waits for them, and re-layouts  12.8 us (10%)
  other arithmetic  6.72 us (5%)
    ppermute x4, waiting for transfers between devices, to_tp(): return lax.ppermute(x, 'tp', both)  16.6 us
    all_to_all x1, blocking collectives, head_body(): attn = lax.all_to_all(attn, 'seq', 0, 0)  14.1 us
    pallas_call x1, Pallas kernels, attend_own(): call(own_kernel, 'attend_own', [jax.ShapeDtypeStruct((rows, HEAD_DIM), jn...  12.7 us
    pallas_call x2, Pallas kernels, project_kv(): call(lambda *refs: kv_kernel(chunk, *refs), 'project_kv' + 'ab'[chunk], j...  9.12 us
    all_to_all x1, waiting for transfers between devices, head_body(): mine = lax.all_to_all(kv_weights(section_at, rows3), 'seq', 0, 0)  8.98 us
    ppermute x5, starting transfers between devices, along_z(): return lax.ppermute(x, 'seq', z_pairs(seq, pairs))  8.51 us
    ppermute x4, starting transfers between devices, to_tp(): return lax.ppermute(x, 'tp', both)  6.22 us
    all_to_all x1, starting transfers between devices, head_body(): direct = lax.all_to_all(direct, 'seq', 0, 0)  5.76 us
  transfers between devices with their start and end apart: 22, of which 6 were waited for; matrix products, arithmetic and copies ran while one was open for 11% of the time, Pallas kernels for 21%

profile of v15, /device:TPU:0, one launch (start us, length us, event | category | flops | bytes accessed | tf_op | source)
XLA Modules:
  0.0 133.0 jit_solution(4229035071396021241)
XLA Ops:
  0.0 2.9 %norm_tokens.1 = (bf16[128,3072]{1,0:T(8,128)(2,1)}, bf16[64,3072]{1,0:T(8,128)(2,1)}) custom-call(s32[1]{0:T(128)} %bitcast.1.tp_ref, bf16[128,3072]{1,0:T(8,128)(2,1)} %bitcast.27, f32[3,1,3072]{2,1,0:T(1,128)} %bitcast.29), custom_call_target="tpu_custom_call" | custom-call | flops 3932160 | bytes 1572864 | tf_op jit(solution)/shard_map/norm_tokens/pallas_call | solution.py:94
  3.0 3.1 %collective-permute-start.2 = (bf16[64,3072]{1,0:T(8,128)(2,1)}, bf16[64,3072]{1,0:T(8,128)(2,1)}, u32[]{:S(2)}, u32[]{:S(2)}) collective-permute-start(bf16[64,3072]{1,0:T(8,128)(2,1)} %get-tuple-element.30), channel_id=1, source_target_pairs={{0,4},{2,6},{4,0},{6,2},{8,12},{10,14},{12,8},{14,10},{1,5},{3,7},... | collective-permute-start | bytes 1179656 | tf_op jit(solution)/shard_map/ppermute | solution.py:475
  7.5 2.1 %kv_weights.1 = bf16[8,384,128]{2,1,0:T(8,128)(2,1)} custom-call(s32[1]{0:T(128)} %bitcast.section_ref.refs_0_, bf16[3,384,1024]{2,1,0:T(8,128)(2,1)} %bitcast.25), custom_call_target="tpu_custom_call" | custom-call | bytes 1572864 | tf_op jit(solution)/shard_map/kv_weights/pallas_call | solution.py:123
  9.6 4.9 %all-to-all-start = ((bf16[8,384,128]{2,1,0:T(8,128)(2,1)}), bf16[8,384,128]{2,1,0:T(8,128)(2,1)S(1)}, u32[]{:S(2)}, u32[]{:S(2)}) async-start(bf16[8,384,128]{2,1,0:T(8,128)(2,1)} %kv_weights.1), calls=%async_computation | async-start | bytes 1572864 | tf_op jit(solution)/shard_map/all_to_all | solution.py:470
  17.9 3.0 %direct_rows.1 = bf16[8,528,128]{2,1,0:T(8,128)(2,1)} custom-call(bf16[3,384,1024]{2,1,0:T(8,128)(2,1)} %bitcast.26, bf16[8,128,128]{2,1,0:T(8,128)(2,1)} %bitcast.28, bf16[16,128]{1,0:T(8,128)(2,1)} %pad.4.mask_ref), custom_call_target="tpu_custom_call" | custom-call | bytes 2162688 | tf_op jit(solution)/shard_map/direct_rows/pallas_call | solution.py:146
  21.4 1.5 %collective-permute-start.3 = (bf16[64,3072]{1,0:T(8,128)(2,1)}, bf16[64,3072]{1,0:T(8,128)(2,1)}, u32[]{:S(2)}, u32[]{:S(2)}) collective-permute-start(bf16[64,3072]{1,0:T(8,128)(2,1)} %collective-permute-done.2.refs_8_.refs_2_), channel_id=1, source_target_pairs={{0,1},{1,0},{2,3},{3,2},{4,5},{5,4},{6,7},{7,6},{8,9},{9,8},{10,11... | collective-permute-start | bytes 1179656 | tf_op jit(solution)/shard_map/ppermute | solution.py:481
  28.4 9.0 %all-to-all-done.refs_3_ = bf16[8,384,128]{2,1,0:T(8,128)(2,1)S(1)} async-done(((bf16[8,384,128]{2,1,0:T(8,128)(2,1)}), bf16[8,384,128]{2,1,0:T(8,128)(2,1)S(1)}, u32[]{:S(2)}, u32[]{:S(2)}) %all-to-all-start) | async-done | bytes 786464 | tf_op jit(solution)/shard_map/all_to_all | solution.py:470
  38.4 1.5 %collective-permute-start.7 = (bf16[4,384,128]{2,1,0:T(8,128)(2,1)S(1)}, bf16[4,384,128]{2,1,0:T(8,128)(2,1)S(1)}, u32[]{:S(2)}, u32[]{:S(2)}) collective-permute-start(bf16[4,384,128]{2,1,0:T(8,128)(2,1)S(1)} %get-tuple-element.58), channel_id=1, source_target_pairs={{0,16},{16,0},{1,17},{17,1},{2,18},{18,2},{3,19},{19,3},{4,20},{20... | collective-permute-start | bytes 1179656 | tf_op jit(solution)/shard_map/ppermute | solution.py:501
  39.9 4.9 %constant_dynamic-slice_fusion = (bf16[1024,1536]{1,0:T(8,128)(2,1)S(1)}, bf16[1024,1536]{1,0:T(8,128)(2,1)}) fusion(bf16[1024,3072]{1,0:T(8,128)(2,1)} %param.12, s32[]{:T(128)S(6)} %select_n.78, s32[]{:T(128)S(6)} %select_n.77), kind=kLoop, calls=%fused_computation.21 | loop fusion | bytes 12582920 | tf_op jit(solution)/shard_map/dynamic_slice | solution.py:506
  44.8 3.0 %collective-permute-done.7.refs_4_ = bf16[4,384,128]{2,1,0:T(8,128)(2,1)S(1)} collective-permute-done((bf16[4,384,128]{2,1,0:T(8,128)(2,1)S(1)}, bf16[4,384,128]{2,1,0:T(8,128)(2,1)S(1)}, u32[]{:S(2)}, u32[]{:S(2)}) %collective-permute-start.7) | collective-permute-done | bytes 393248 | tf_op jit(solution)/shard_map/ppermute | solution.py:501
  49.1 5.8 %all-to-all-start.1 = ((bf16[8,528,128]{2,1,0:T(8,128)(2,1)}), bf16[8,528,128]{2,1,0:T(8,128)(2,1)}, u32[]{:S(2)}, u32[]{:S(2)}) async-start(bf16[8,528,128]{2,1,0:T(8,128)(2,1)} %direct_rows.1), calls=%async_computation.1 | async-start | bytes 2162688 | tf_op jit(solution)/shard_map/all_to_all | solution.py:503
  56.0 1.6 %collective-permute-start.6 = (bf16[64,3072]{1,0:T(8,128)(2,1)S(1)}, bf16[64,3072]{1,0:T(8,128)(2,1)S(1)}, u32[]{:S(2)}, u32[]{:S(2)}) collective-permute-start(bf16[64,3072]{1,0:T(8,128)(2,1)S(1)} %broadcast_select_fusion.1.refs_6_), channel_id=1, source_target_pairs={{0,1},{1,0},{2,3},{3,2},{4,5},{5,4},{6,7},{7,6},{8,9},{9,8},{10,11... | collective-permute-start | bytes 1179656 | tf_op jit(solution)/shard_map/ppermute | solution.py:481
  61.3 6.3 %collective-permute-done.6.refs_7_ = bf16[64,3072]{1,0:T(8,128)(2,1)S(1)} collective-permute-done((bf16[64,3072]{1,0:T(8,128)(2,1)S(1)}, bf16[64,3072]{1,0:T(8,128)(2,1)S(1)}, u32[]{:S(2)}, u32[]{:S(2)}) %collective-permute-start.6) | collective-permute-done | bytes 393248 | tf_op jit(solution)/shard_map/ppermute | solution.py:481
  67.6 1.5 %collective-permute-start.8 = (bf16[64,3072]{1,0:T(8,128)(2,1)S(1)}, bf16[64,3072]{1,0:T(8,128)(2,1)S(1)}, u32[]{:S(2)}, u32[]{:S(2)}) collective-permute-start(bf16[64,3072]{1,0:T(8,128)(2,1)S(1)} %broadcast_select_fusion.refs_10_), channel_id=1, source_target_pairs={{0,1},{1,0},{2,3},{3,2},{4,5},{5,4},{6,7},{7,6},{8,9},{9,8},{10,11... | collective-permute-start | bytes 1179656 | tf_op jit(solution)/shard_map/ppermute | solution.py:481
  71.1 4.5 %project_kva.1.kva = bf16[2,512,128]{2,1,0:T(8,128)(2,1)} custom-call(s32[1]{0:T(128)} %bitcast.section_ref.refs_0_, f32[2,80,128]{2,1,0:T(8,128)} %pad_maximum_fusion.refs_1_.tabs_hbm, f32[2,128]{1,0:T(2,128)} %pad_maximum_fusion.1.refs_2_.gain_hbm, bf16[8,384,128]{2,1,0:T(8,128)(2,1)} %copy-done.1, bf16[4,384,128]{2,1,0:T(8,128)(2,1)} %copy-done.5, ...), custom_call_target="tpu_custom_call" | custom-call | flops 805306368 | bytes 4718592 | tf_op jit(solution)/shard_map/project_kva/pallas_call | solution.py:243
  75.6 2.7 %collective-permute-done.8.refs_11_ = bf16[64,3072]{1,0:T(8,128)(2,1)S(1)} collective-permute-done((bf16[64,3072]{1,0:T(8,128)(2,1)S(1)}, bf16[64,3072]{1,0:T(8,128)(2,1)S(1)}, u32[]{:S(2)}, u32[]{:S(2)}) %collective-permute-start.8) | collective-permute-done | bytes 393248 | tf_op jit(solution)/shard_map/ppermute | solution.py:481
  78.4 4.1 %collective-permute-start.17 = (bf16[2,512,128]{2,1,0:T(8,128)(2,1)}, bf16[2,512,128]{2,1,0:T(8,128)(2,1)}, u32[]{:S(2)}, u32[]{:S(2)}) collective-permute-start(bf16[2,512,128]{2,1,0:T(8,128)(2,1)} %project_kva.1.kva), channel_id=1, source_target_pairs={{0,16},{1,17},{2,18},{3,19},{4,20},{5,21},{6,22},{7,23},{8,24},{9,... | collective-permute-start | bytes 786440 | tf_op jit(solution)/shard_map/ppermute | solution.py:532
  84.3 4.6 %project_kvb.1.kvb = bf16[2,512,128]{2,1,0:T(8,128)(2,1)} custom-call(s32[1]{0:T(128)} %bitcast.section_ref.refs_0_, f32[2,80,128]{2,1,0:T(8,128)} %pad_maximum_fusion.refs_1_.tabs_hbm, f32[2,128]{1,0:T(2,128)} %pad_maximum_fusion.1.refs_2_.gain_hbm, bf16[8,384,128]{2,1,0:T(8,128)(2,1)} %copy-done.1, bf16[4,384,128]{2,1,0:T(8,128)(2,1)} %copy-done.5, ...), custom_call_target="tpu_custom_call" | custom-call | flops 805306368 | bytes 4718592 | tf_op jit(solution)/shard_map/project_kvb/pallas_call | solution.py:243
  88.9 1.5 %collective-permute-start.18 = (bf16[2,512,128]{2,1,0:T(8,128)(2,1)}, bf16[2,512,128]{2,1,0:T(8,128)(2,1)S(1)}, u32[]{:S(2)}, u32[]{:S(2)}) collective-permute-start(bf16[2,512,128]{2,1,0:T(8,128)(2,1)} %project_kvb.1.kvb), channel_id=1, source_target_pairs={{0,16},{1,17},{2,18},{3,19},{4,20},{5,21},{6,22},{7,23},{8,24},{9,... | collective-permute-start | bytes 786440 | tf_op jit(solution)/shard_map/ppermute | solution.py:538
  90.4 12.7 %attend_own.1 = (bf16[1024,128]{1,0:T(8,128)(2,1)}, f32[1024,128]{1,0:T(8,128)}, f32[1024,128]{1,0:T(8,128)}, f32[16,1024]{1,0:T(8,128)}) custom-call(s32[1]{0:T(128)} %bitcast.section_ref.refs_0_, f32[16,8]{1,0:T(8,128)} %fusion.3.rows_ref, f32[128,16]{1,0:T(8,128)} %fusion.1.keys_ref, bf16[2,512,128]{2,1,0:T(8,128)(2,1)} %project_kva.1.kva, ...), custom_call_target="tpu_custom_call" | custom-call | flops 1879048192 | bytes 6291456 | tf_op jit(solution)/shard_map/attend_own/pallas_call | solution.py:379
  103.9 3.0 %attend_second.1 = bf16[8,128,128]{2,1,0:T(8,128)(2,1)} custom-call(s32[1]{0:T(128)} %bitcast.section_ref.refs_0_, s32[2,16]{1,0:T(2,128)} %pad_add_fusion.place_ref, f32[16,1024]{1,0:T(8,128)} %get-tuple-element.49.keep_hbm, bf16[1024,128]{1,0:T(8,128)(2,1)} %get-tuple-element.50.q_hbm, f32[1024,128]{1,0:T(8,128)} %get-tuple-element.51.num_hbm, ...), custom_call_target="tpu_custom_call" | custom-call | flops 268435456 | bytes 2097152 | tf_op jit(solution)/shard_map/attend_second/pallas_call | solution.py:402
  107.0 14.1 %all_to_all.15.attn_ref = bf16[8,128,128]{2,1,0:T(8,128)(2,1)S(1)} all-to-all(bf16[8,128,128]{2,1,0:T(8,128)(2,1)} %attend_second.1), channel_id=1, replica_groups=mesh['section'=2,'seq'=8,'tp'=2] {'seq'}, dimensions={0} | all-to-all | bytes 524288 | tf_op jit(solution)/shard_map/all_to_all | solution.py:544
  121.6 1.6 %collective-permute-start.19 = (bf16[128,1536]{1,0:T(8,128)(2,1)S(1)}, bf16[128,1536]{1,0:T(8,128)(2,1)S(1)}, u32[]{:S(2)}, u32[]{:S(2)}) collective-permute-start(bf16[128,1536]{1,0:T(8,128)(2,1)S(1)} %out_sent.1), channel_id=1, source_target_pairs={{0,1},{1,0},{2,3},{3,2},{4,5},{5,4},{6,7},{7,6},{8,9},{9,8},{10,11... | collective-permute-start | bytes 1179656 | tf_op jit(solution)/shard_map/ppermute | solution.py:481
  124.6 7.6 %collective-permute-done.19 = bf16[128,1536]{1,0:T(8,128)(2,1)S(1)} collective-permute-done((bf16[128,1536]{1,0:T(8,128)(2,1)S(1)}, bf16[128,1536]{1,0:T(8,128)(2,1)S(1)}, u32[]{:S(2)}, u32[]{:S(2)}) %collective-permute-start.19) | collective-permute-done | bytes 393248 | tf_op jit(solution)/shard_map/ppermute | solution.py:481
  (106 shorter events, 25.0 us)
Async XLA Ops:
  3.0 18.0 %collective-permute-start.2 = (bf16[64,3072]{1,0:T(8,128)(2,1)}, bf16[64,3072]{1,0:T(8,128)(2,1)}, u32[]{:S(2)}, u32[]{:S(2)}) collective-permute-start(bf16[64,3072]{1,0:T(8,128)(2,1)} %get-tuple-element.30), channel_id=1, source_target_pairs={{0,4},{2,6},{4,0},{6,2},{8,12},{10,14},{12,8},{14,10},{1,5},{3,7},... | collective-permute-start | bytes 1179656 | tf_op jit(solution)/shard_map/ppermute | solution.py:475
  6.1 18.2 %collective-permute-start = (bf16[64,3072]{1,0:T(8,128)(2,1)}, bf16[64,3072]{1,0:T(8,128)(2,1)}, u32[]{:S(2)}, u32[]{:S(2)}) collective-permute-start(bf16[64,3072]{1,0:T(8,128)(2,1)} %get-tuple-element.30), channel_id=1, source_target_pairs={{4,8},{6,10},{8,4},{10,6},{5,9},{7,11},{9,5},{11,7},{20,24},{22,26... | collective-permute-start | bytes 1179656 | tf_op jit(solution)/shard_map/ppermute | solution.py:475
  9.6 27.7 %all-to-all-start = ((bf16[8,384,128]{2,1,0:T(8,128)(2,1)}), bf16[8,384,128]{2,1,0:T(8,128)(2,1)S(1)}, u32[]{:S(2)}, u32[]{:S(2)}) async-start(bf16[8,384,128]{2,1,0:T(8,128)(2,1)} %kv_weights.1), calls=%async_computation | async-start | bytes 1572864 | tf_op jit(solution)/shard_map/all_to_all | solution.py:470
  14.5 54.6 %collective-permute-start.10 = (bf16[128,3072]{1,0:T(8,128)(2,1)}, bf16[128,3072]{1,0:T(8,128)(2,1)}, u32[]{:S(2)}, u32[]{:S(2)}) collective-permute-start(bf16[128,3072]{1,0:T(8,128)(2,1)} %get-tuple-element.43.refs_6_.refs_0_), channel_id=1, source_target_pairs={{0,2},{2,0},{4,6},{6,4},{8,10},{10,8},{12,14},{14,12},{1,3},{3,1},... | collective-permute-start | bytes 2359304 | tf_op jit(solution)/shard_map/ppermute | solution.py:478
  21.4 34.6 %collective-permute-start.3 = (bf16[64,3072]{1,0:T(8,128)(2,1)}, bf16[64,3072]{1,0:T(8,128)(2,1)}, u32[]{:S(2)}, u32[]{:S(2)}) collective-permute-start(bf16[64,3072]{1,0:T(8,128)(2,1)} %collective-permute-done.2.refs_8_.refs_2_), channel_id=1, source_target_pairs={{0,1},{1,0},{2,3},{3,2},{4,5},{5,4},{6,7},{7,6},{8,9},{9,8},{10,11... | collective-permute-start | bytes 1179656 | tf_op jit(solution)/shard_map/ppermute | solution.py:481
  22.9 21.9 %collective-permute-start.4 = (bf16[64,3072]{1,0:T(8,128)(2,1)}, bf16[64,3072]{1,0:T(8,128)(2,1)}, u32[]{:S(2)}, u32[]{:S(2)}) collective-permute-start(bf16[64,3072]{1,0:T(8,128)(2,1)} %collective-permute-done.2.refs_8_.refs_2_), channel_id=1, source_target_pairs={{4,8},{6,10},{8,4},{10,6},{5,9},{7,11},{9,5},{11,7},{20,24},{22,26... | collective-permute-start | bytes 1179656 | tf_op jit(solution)/shard_map/ppermute | solution.py:475
  24.3 30.6 %collective-permute-start.1 = (bf16[64,3072]{1,0:T(8,128)(2,1)}, bf16[64,3072]{1,0:T(8,128)(2,1)}, u32[]{:S(2)}, u32[]{:S(2)}) collective-permute-start(bf16[64,3072]{1,0:T(8,128)(2,1)} %collective-permute-done), channel_id=1, source_target_pairs={{4,0},{6,2},{8,12},{10,14},{5,1},{7,3},{9,13},{11,15},{20,16},{22,... | collective-permute-start | bytes 1179656 | tf_op jit(solution)/shard_map/ppermute | solution.py:475
  38.4 9.4 %collective-permute-start.7 = (bf16[4,384,128]{2,1,0:T(8,128)(2,1)S(1)}, bf16[4,384,128]{2,1,0:T(8,128)(2,1)S(1)}, u32[]{:S(2)}, u32[]{:S(2)}) collective-permute-start(bf16[4,384,128]{2,1,0:T(8,128)(2,1)S(1)} %get-tuple-element.58), channel_id=1, source_target_pairs={{0,16},{16,0},{1,17},{17,1},{2,18},{18,2},{3,19},{19,3},{4,20},{20... | collective-permute-start | bytes 1179656 | tf_op jit(solution)/shard_map/ppermute | solution.py:501
  44.8 24.2 %collective-permute-start.11 = (bf16[64,3072]{1,0:T(8,128)(2,1)}, bf16[64,3072]{1,0:T(8,128)(2,1)}, u32[]{:S(2)}, u32[]{:S(2)}) collective-permute-start(bf16[64,3072]{1,0:T(8,128)(2,1)} %collective-permute-done.2.refs_8_.refs_2_), channel_id=1, source_target_pairs={{0,2},{2,0},{4,6},{6,4},{8,10},{10,8},{12,14},{14,12},{1,3},{3,1},... | collective-permute-start | bytes 1179656 | tf_op jit(solution)/shard_map/ppermute | solution.py:478
  47.8 11.0 %collective-permute-start.5 = (bf16[64,3072]{1,0:T(8,128)(2,1)}, bf16[64,3072]{1,0:T(8,128)(2,1)}, u32[]{:S(2)}, u32[]{:S(2)}) collective-permute-start(bf16[64,3072]{1,0:T(8,128)(2,1)} %collective-permute-done.4), channel_id=1, source_target_pairs={{4,0},{6,2},{8,12},{10,14},{5,1},{7,3},{9,13},{11,15},{20,16},{22,... | collective-permute-start | bytes 1179656 | tf_op jit(solution)/shard_map/ppermute | solution.py:475
  49.1 41.3 %all-to-all-start.1 = ((bf16[8,528,128]{2,1,0:T(8,128)(2,1)}), bf16[8,528,128]{2,1,0:T(8,128)(2,1)}, u32[]{:S(2)}, u32[]{:S(2)}) async-start(bf16[8,528,128]{2,1,0:T(8,128)(2,1)} %direct_rows.1), calls=%async_computation.1 | async-start | bytes 2162688 | tf_op jit(solution)/shard_map/all_to_all | solution.py:503
  56.0 26.6 %copy-start.2 = (bf16[64,3072]{1,0:T(8,128)(2,1)}, bf16[64,3072]{1,0:T(8,128)(2,1)S(1)}, u32[]{:S(2)}) copy-start(bf16[64,3072]{1,0:T(8,128)(2,1)S(1)} %broadcast_select_fusion.1.refs_6_) | copy-start | bytes 1179652
  56.0 11.6 %collective-permute-start.6 = (bf16[64,3072]{1,0:T(8,128)(2,1)S(1)}, bf16[64,3072]{1,0:T(8,128)(2,1)S(1)}, u32[]{:S(2)}, u32[]{:S(2)}) collective-permute-start(bf16[64,3072]{1,0:T(8,128)(2,1)S(1)} %broadcast_select_fusion.1.refs_6_), channel_id=1, source_target_pairs={{0,1},{1,0},{2,3},{3,2},{4,5},{5,4},{6,7},{7,6},{8,9},{9,8},{10,11... | collective-permute-start | bytes 1179656 | tf_op jit(solution)/shard_map/ppermute | solution.py:481
  57.6 12.0 %collective-permute-start.12 = (bf16[64,3072]{1,0:T(8,128)(2,1)}, bf16[64,3072]{1,0:T(8,128)(2,1)S(1)}, u32[]{:S(2)}, u32[]{:S(2)}) collective-permute-start(bf16[64,3072]{1,0:T(8,128)(2,1)} %collective-permute-done.3.refs_9_.refs_3_), channel_id=1, source_target_pairs={{0,2},{2,0},{4,6},{6,4},{8,10},{10,8},{12,14},{14,12},{1,3},{3,1},... | collective-permute-start | bytes 1179656 | tf_op jit(solution)/shard_map/ppermute | solution.py:478
  58.8 10.8 %collective-permute-start.9 = (bf16[4,384,128]{2,1,0:T(8,128)(2,1)}, bf16[4,384,128]{2,1,0:T(8,128)(2,1)S(1)}, u32[]{:S(2)}, u32[]{:S(2)}) collective-permute-start(bf16[4,384,128]{2,1,0:T(8,128)(2,1)} %get-tuple-element.57), channel_id=1, source_target_pairs={{0,16},{16,0},{1,17},{17,1},{2,18},{18,2},{3,19},{19,3},{4,20},{20... | collective-permute-start | bytes 1179656 | tf_op jit(solution)/shard_map/ppermute | solution.py:501
  67.6 10.8 %collective-permute-start.8 = (bf16[64,3072]{1,0:T(8,128)(2,1)S(1)}, bf16[64,3072]{1,0:T(8,128)(2,1)S(1)}, u32[]{:S(2)}, u32[]{:S(2)}) collective-permute-start(bf16[64,3072]{1,0:T(8,128)(2,1)S(1)} %broadcast_select_fusion.refs_10_), channel_id=1, source_target_pairs={{0,1},{1,0},{2,3},{3,2},{4,5},{5,4},{6,7},{7,6},{8,9},{9,8},{10,11... | collective-permute-start | bytes 1179656 | tf_op jit(solution)/shard_map/ppermute | solution.py:481
  69.1 13.4 %collective-permute-start.13 = (bf16[64,3072]{1,0:T(8,128)(2,1)S(1)}, bf16[64,3072]{1,0:T(8,128)(2,1)S(1)}, u32[]{:S(2)}, u32[]{:S(2)}) collective-permute-start(bf16[64,3072]{1,0:T(8,128)(2,1)S(1)} %broadcast_select_fusion.1.refs_6_), channel_id=1, source_target_pairs={{0,2},{2,0},{4,6},{6,4},{8,10},{10,8},{12,14},{14,12},{1,3},{3,1},... | collective-permute-start | bytes 1179656 | tf_op jit(solution)/shard_map/ppermute | solution.py:478
  69.1 13.4 %collective-permute-start.15 = (bf16[64,3072]{1,0:T(8,128)(2,1)S(1)}, bf16[64,3072]{1,0:T(8,128)(2,1)S(1)}, u32[]{:S(2)}, u32[]{:S(2)}) collective-permute-start(bf16[64,3072]{1,0:T(8,128)(2,1)S(1)} %broadcast_select_fusion.refs_10_), channel_id=1, source_target_pairs={{0,2},{2,0},{4,6},{6,4},{8,10},{10,8},{12,14},{14,12},{1,3},{3,1},... | collective-permute-start | bytes 1179656 | tf_op jit(solution)/shard_map/ppermute | solution.py:478
  69.6 12.9 %collective-permute-start.14 = (bf16[64,3072]{1,0:T(8,128)(2,1)S(1)}, bf16[64,3072]{1,0:T(8,128)(2,1)S(1)}, u32[]{:S(2)}, u32[]{:S(2)}) collective-permute-start(bf16[64,3072]{1,0:T(8,128)(2,1)S(1)} %collective-permute-done.6.refs_7_), channel_id=1, source_target_pairs={{0,2},{2,0},{4,6},{6,4},{8,10},{10,8},{12,14},{14,12},{1,3},{3,1},... | collective-permute-start | bytes 1179656 | tf_op jit(solution)/shard_map/ppermute | solution.py:478
  78.4 4.2 %collective-permute-start.16 = (bf16[64,3072]{1,0:T(8,128)(2,1)S(1)}, bf16[64,3072]{1,0:T(8,128)(2,1)S(1)}, u32[]{:S(2)}, u32[]{:S(2)}) collective-permute-start(bf16[64,3072]{1,0:T(8,128)(2,1)S(1)} %collective-permute-done.8.refs_11_), channel_id=1, source_target_pairs={{0,2},{2,0},{4,6},{6,4},{8,10},{10,8},{12,14},{14,12},{1,3},{3,1},... | collective-permute-start | bytes 1179656 | tf_op jit(solution)/shard_map/ppermute | solution.py:478
  78.4 12.0 %collective-permute-start.17 = (bf16[2,512,128]{2,1,0:T(8,128)(2,1)}, bf16[2,512,128]{2,1,0:T(8,128)(2,1)}, u32[]{:S(2)}, u32[]{:S(2)}) collective-permute-start(bf16[2,512,128]{2,1,0:T(8,128)(2,1)} %project_kva.1.kva), channel_id=1, source_target_pairs={{0,16},{1,17},{2,18},{3,19},{4,20},{5,21},{6,22},{7,23},{8,24},{9,... | collective-permute-start | bytes 786440 | tf_op jit(solution)/shard_map/ppermute | solution.py:532
  88.9 14.3 %collective-permute-start.18 = (bf16[2,512,128]{2,1,0:T(8,128)(2,1)}, bf16[2,512,128]{2,1,0:T(8,128)(2,1)S(1)}, u32[]{:S(2)}, u32[]{:S(2)}) collective-permute-start(bf16[2,512,128]{2,1,0:T(8,128)(2,1)} %project_kvb.1.kvb), channel_id=1, source_target_pairs={{0,16},{1,17},{2,18},{3,19},{4,20},{5,21},{6,22},{7,23},{8,24},{9,... | collective-permute-start | bytes 786440 | tf_op jit(solution)/shard_map/ppermute | solution.py:538
  90.4 30.7 %copy-start = (bf16[1024,1536]{1,0:T(8,128)(2,1)S(1)}, bf16[1024,1536]{1,0:T(8,128)(2,1)}, u32[]{:S(2)}) copy-start(bf16[1024,1536]{1,0:T(8,128)(2,1)} %get-tuple-element.54.w_ref) | copy-start | bytes 9437188
  121.6 10.6 %collective-permute-start.19 = (bf16[128,1536]{1,0:T(8,128)(2,1)S(1)}, bf16[128,1536]{1,0:T(8,128)(2,1)S(1)}, u32[]{:S(2)}, u32[]{:S(2)}) collective-permute-start(bf16[128,1536]{1,0:T(8,128)(2,1)S(1)} %out_sent.1), channel_id=1, source_target_pairs={{0,1},{1,0},{2,3},{3,2},{4,5},{5,4},{6,7},{7,6},{8,9},{9,8},{10,11... | collective-permute-start | bytes 1179656 | tf_op jit(solution)/shard_map/ppermute | solution.py:481
  (17 other events, 151.0 us)

commit v16 on v15

--- a/solution.py
+++ b/solution.py
@@ -8,6 +8,8 @@
 HEAD_DIM = 128
 GRID_W = 64
 TILE = 128
+BLOCK = 512
+OWN_BLOCK = 256
 VMEM_LIMIT = 24 * 1024 * 1024
 VMEM_WHOLE = 56 * 1024 * 1024
 
@@ -186,8 +188,8 @@
     return pairs
 
 
-def blocks(rows):
-    return [(b, slice(b * BLOCK, (b + 1) * BLOCK)) for b in range(rows // BLOCK)]
+def blocks(rows, block=BLOCK):
+    return [(b, slice(b * block, (b + 1) * block)) for b in range(rows // block)]
 
 
 def arrived(copies, piece_refs, rows):
@@ -278,9 +280,6 @@
     return (weights.reshape(groups, rows // groups, keys) * keep[:, None, :]).reshape(rows, keys)
 
 
-BLOCK = 512
-
-
 def own_kernel(
     section_ref, rows_ref, keys_ref, kva, kvb, cond, tabs_hbm, gain_hbm, direct_hbm, *refs
 ):
@@ -299,14 +298,14 @@
         direct[:, wide : wide + count, :].reshape(-1, HEAD_DIM),
         direct[:, wide + count : wide + 2 * count, :].reshape(-1, HEAD_DIM),
     )
-    for b, at in blocks(rows):
+    for b, at in blocks(rows, OWN_BLOCK):
         arrived(tokens, piece_refs, at)
         query = jnp.dot(x_ref[at, :], w, preferred_element_type=jnp.float32)
         query = normed_rotated(
             query,
             gain_ref[0:1, :],
-            table_of(tabs_ref, 0, b * BLOCK, BLOCK),
-            table_of(tabs_ref, 1, b * BLOCK, BLOCK),
+            table_of(tabs_ref, 0, b * OWN_BLOCK, OWN_BLOCK),
+            table_of(tabs_ref, 1, b * OWN_BLOCK, OWN_BLOCK),
         )
         q_ref[at, :] = query
         num, den = 0.0, 0.0
@@ -328,17 +327,17 @@
 
     @pl.when(section_ref[0] != 0)
     def _():
-        for b, at in blocks(rows):
-            num, den = cond_sum(keep_ref, q_ref, cond, 0, b)
+        for b, at in blocks(rows, OWN_BLOCK):
+            num, den = cond_sum(keep_ref, q_ref, cond, 0, b, OWN_BLOCK)
             num_ref[at, :] += num
             den_ref[at, :] += jnp.broadcast_to(den, num.shape)
 
 
-def cond_sum(keep_ref, q_ref, cond, chunk, b):
-    groups = keep_ref.shape[0] * BLOCK // q_ref.shape[0]
+def cond_sum(keep_ref, q_ref, cond, chunk, b, block=BLOCK):
+    groups = keep_ref.shape[0] * block // q_ref.shape[0]
     keys = cond.shape[1]
     keep = keep_ref[b * groups : (b + 1) * groups, chunk * keys : (chunk + 1) * keys]
-    return summed(kept_weights(q_ref[b * BLOCK : (b + 1) * BLOCK, :], cond, keep), cond[1])
+    return summed(kept_weights(q_ref[b * block : (b + 1) * block, :], cond, keep), cond[1])
 
 
 def second_cond_kernel(
@@ -499,8 +498,6 @@
     near_tp = to_tp(near)
     some = seq // 2
     peers = [lax.ppermute(mine[:some], "section", both), lax.ppermute(mine[some:], "section", both)]
-    direct, peers[0] = lax.optimization_barrier((direct, peers[0]))
-    direct = lax.all_to_all(direct, "seq", 0, 0)
     cols = w_out.shape[1] // 2
     w_sent = lax.dynamic_slice_in_dim(w_late, (1 - tp) * cols, cols, 1)
     w_kept = lax.dynamic_slice_in_dim(w_late, tp * cols, cols, 1)
@@ -525,6 +522,8 @@
     third, near_tp, early = lax.optimization_barrier((third, near_tp, early))
     tabs, gains, row_tiles, key_tiles, place, w_sent, w_kept = early
     third_tp = to_tp(third)
+    direct, third_tp, peers = lax.optimization_barrier((direct, third_tp, peers))
+    direct = lax.all_to_all(direct, "seq", 0, 0)
     fourth, third_tp, peers[0] = lax.optimization_barrier((fourth, third_tp, peers[0]))
     fourth_tp = to_tp(fourth)
     a = [full, to_core(full), near, near_tp, to_core(near), to_core(near_tp)]

time: 134 us -> 134 us (level)
  local copies, waits for them, and re-layouts: 12.8 us -> 16.5 us
  waiting for transfers between devices: 29.7 us -> 32.6 us
  starting transfers between devices: 35.2 us -> 32.6 us
  Pallas kernels: 34.1 us -> 31.6 us
    ppermute x5, waiting for transfers between devices: 1.08 us -> 12.3 us  [along_z(): return lax.ppermute(x, 'seq', z_pairs(seq, pairs))]
    all_to_all x1, waiting for transfers between devices: 8.98 us -> 0.01 us  [head_body(): mine = lax.all_to_all(kv_weights(section_at, rows3), 'seq', 0, 0)]
    ppermute x4, waiting for transfers between devices: 16.6 us -> 10.2 us  [to_tp(): return lax.ppermute(x, 'tp', both)]
    ppermute x1, waiting for transfers between devices: 0.01 us -> 6.11 us  [head_body(): lax.ppermute(mine[some:], 'section', both)]
    another operation x2, local copies, waits for them, and re-layouts: 0.97 us -> 3.55 us  [head_body(): text_kv[0].reshape(-1, 2, seq, HEAD_DIM).transpose(2, 1, 0, 3)]
    pallas_call x1, Pallas kernels: 12.7 us -> 10.2 us  [attend_own(): call(own_kernel, 'attend_own', [jax.ShapeDtypeStruct((rows, HEAD_DIM), jn...]
    all_to_all x1, waiting for transfers between devices: 0.01 us -> 2.09 us  [head_body(): direct = lax.all_to_all(direct, 'seq', 0, 0)]
    all_to_all x1, starting transfers between devices: 5.76 us -> 4.24 us  [head_body(): direct = lax.all_to_all(direct, 'seq', 0, 0)]
  transfers between devices with their start and end apart: 22 -> 22, of which waited for: 6 -> 6; matrix products, arithmetic and copies ran while one was open for 11% -> 13% of each run, Pallas kernels for 21% -> 19%
where the time goes in v16:
time: 134 us; the launch traced here: 132 us
  starting transfers between devices  32.6 us (24%)
  waiting for transfers between devices  32.6 us (24%)
  Pallas kernels  31.6 us (24%)
  local copies, waits for them, and re-layouts  16.5 us (12%)
  blocking collectives  13.1 us (10%)
  other arithmetic  5.71 us (4%)
    all_to_all x1, blocking collectives, head_body(): attn = lax.all_to_all(attn, 'seq', 0, 0)  13.1 us
    ppermute x5, waiting for transfers between devices, along_z(): return lax.ppermute(x, 'seq', z_pairs(seq, pairs))  12.3 us
    pallas_call x1, Pallas kernels, attend_own(): call(own_kernel, 'attend_own', [jax.ShapeDtypeStruct((rows, HEAD_DIM), jn...  10.2 us
    ppermute x4, waiting for transfers between devices, to_tp(): return lax.ppermute(x, 'tp', both)  10.2 us
    pallas_call x2, Pallas kernels, project_kv(): call(lambda *refs: kv_kernel(chunk, *refs), 'project_kv' + 'ab'[chunk], j...  9.12 us
    ppermute x5, starting transfers between devices, along_z(): return lax.ppermute(x, 'seq', z_pairs(seq, pairs))  7.73 us
    ppermute x1, waiting for transfers between devices, head_body(): lax.ppermute(mine[some:], 'section', both)  6.11 us
    ppermute x4, starting transfers between devices, to_tp(): return lax.ppermute(x, 'tp', both)  5.9 us
  transfers between devices with their start and end apart: 22, of which 6 were waited for; matrix products, arithmetic and copies ran while one was open for 13% of the time, Pallas kernels for 19%

profile of v16, /device:TPU:0, one launch (start us, length us, event | category | flops | bytes accessed | tf_op | source)
XLA Modules:
  0.0 132.5 jit_solution(16467410877911005983)
XLA Ops:
  0.0 2.9 %norm_tokens.1 = (bf16[128,3072]{1,0:T(8,128)(2,1)}, bf16[64,3072]{1,0:T(8,128)(2,1)}) custom-call(s32[1]{0:T(128)} %bitcast.1.tp_ref, bf16[128,3072]{1,0:T(8,128)(2,1)} %bitcast.27, f32[3,1,3072]{2,1,0:T(1,128)} %bitcast.29), custom_call_target="tpu_custom_call" | custom-call | flops 3932160 | bytes 1572864 | tf_op jit(solution)/shard_map/norm_tokens/pallas_call | solution.py:96
  2.9 3.1 %collective-permute-start.2 = (bf16[64,3072]{1,0:T(8,128)(2,1)}, bf16[64,3072]{1,0:T(8,128)(2,1)}, u32[]{:S(2)}, u32[]{:S(2)}) collective-permute-start(bf16[64,3072]{1,0:T(8,128)(2,1)} %get-tuple-element.32), channel_id=1, source_target_pairs={{0,4},{2,6},{4,0},{6,2},{8,12},{10,14},{12,8},{14,10},{1,5},{3,7},... | collective-permute-start | bytes 1179656 | tf_op jit(solution)/shard_map/ppermute | solution.py:474
  6.7 2.1 %kv_weights.1 = bf16[8,384,128]{2,1,0:T(8,128)(2,1)} custom-call(s32[1]{0:T(128)} %bitcast.section_ref.refs_0_, bf16[3,384,1024]{2,1,0:T(8,128)(2,1)} %bitcast.25), custom_call_target="tpu_custom_call" | custom-call | bytes 1572864 | tf_op jit(solution)/shard_map/kv_weights/pallas_call | solution.py:125
  8.8 5.7 %all-to-all-start = ((bf16[8,384,128]{2,1,0:T(8,128)(2,1)}), bf16[8,384,128]{2,1,0:T(8,128)(2,1)}, u32[]{:S(2)}, u32[]{:S(2)}) async-start(bf16[8,384,128]{2,1,0:T(8,128)(2,1)} %kv_weights.1), calls=%async_computation | async-start | bytes 1572864 | tf_op jit(solution)/shard_map/all_to_all | solution.py:469
  23.2 4.9 %constant_dynamic-slice_fusion = (bf16[1024,1536]{1,0:T(8,128)(2,1)S(1)}, bf16[1024,1536]{1,0:T(8,128)(2,1)}) fusion(bf16[1024,3072]{1,0:T(8,128)(2,1)} %param.12, s32[]{:T(128)S(6)} %select_n.78, s32[]{:T(128)S(6)} %select_n.77), kind=kLoop, calls=%fused_computation.21 | loop fusion | bytes 12582920 | tf_op jit(solution)/shard_map/dynamic_slice | solution.py:503
  28.1 12.3 %collective-permute-done.1 = bf16[64,3072]{1,0:T(8,128)(2,1)S(1)} collective-permute-done((bf16[64,3072]{1,0:T(8,128)(2,1)S(1)}, bf16[64,3072]{1,0:T(8,128)(2,1)S(1)}, u32[]{:S(2)}, u32[]{:S(2)}) %collective-permute-start.1) | collective-permute-done | bytes 393248 | tf_op jit(solution)/shard_map/ppermute | solution.py:474
  41.3 2.1 %fusion.4 = (bf16[4,384,128]{2,1,0:T(8,128)(2,1)}, bf16[4,384,128]{2,1,0:T(8,128)(2,1)}) fusion(bf16[8,384,128]{2,1,0:T(8,128)(2,1)} %all-to-all-done.refs_3_), kind=kLoop, calls=%fused_computation.31 | loop fusion | bytes 1572864 | tf_op jit(solution)/shard_map/slice | solution.py:500
  46.7 1.8 %reshape_squeeze.3 = bf16[64,2,8,128]{3,2,1,0:T(8,128)(2,1)} reshape(bf16[1,64,2,1024]{3,2,1,0:T(2,128)(2,1)} %param.9) | data formatting | bytes 524288 | tf_op jit(solution)/shard_map/reshape;squeeze | solution.py:492
  48.5 1.7 %copy.10 = bf16[64,2,8,128]{3,0,1,2:T(8,128)(2,1)} copy(bf16[64,2,8,128]{3,2,1,0:T(8,128)(2,1)} %reshape_squeeze.3) | data formatting | bytes 524288 | tf_op jit(solution)/shard_map/reshape;squeeze | solution.py:492
  50.8 3.0 %direct_rows.1 = bf16[8,528,128]{2,1,0:T(8,128)(2,1)} custom-call(bf16[3,384,1024]{2,1,0:T(8,128)(2,1)} %bitcast.26, bf16[8,128,128]{2,1,0:T(8,128)(2,1)} %bitcast.28, bf16[16,128]{1,0:T(8,128)(2,1)} %pad.4.mask_ref), custom_call_target="tpu_custom_call" | custom-call | bytes 2162688 | tf_op jit(solution)/shard_map/direct_rows/pallas_call | solution.py:148
  53.9 1.9 %collective-permute-done.7.refs_4_ = bf16[4,384,128]{2,1,0:T(8,128)(2,1)} collective-permute-done((bf16[4,384,128]{2,1,0:T(8,128)(2,1)}, bf16[4,384,128]{2,1,0:T(8,128)(2,1)}, u32[]{:S(2)}, u32[]{:S(2)}) %collective-permute-start.7) | collective-permute-done | bytes 393248 | tf_op jit(solution)/shard_map/ppermute | solution.py:500
  55.7 6.1 %collective-permute-done.8.refs_5_ = bf16[4,384,128]{2,1,0:T(8,128)(2,1)} collective-permute-done((bf16[4,384,128]{2,1,0:T(8,128)(2,1)}, bf16[4,384,128]{2,1,0:T(8,128)(2,1)}, u32[]{:S(2)}, u32[]{:S(2)}) %collective-permute-start.8) | collective-permute-done | bytes 393248 | tf_op jit(solution)/shard_map/ppermute | solution.py:500
  61.8 4.2 %all-to-all-start.1 = ((bf16[8,528,128]{2,1,0:T(8,128)(2,1)}), bf16[8,528,128]{2,1,0:T(8,128)(2,1)}, u32[]{:S(2)}, u32[]{:S(2)}) async-start(bf16[8,528,128]{2,1,0:T(8,128)(2,1)} %direct_rows.1), calls=%async_computation.1 | async-start | bytes 2162688 | tf_op jit(solution)/shard_map/all_to_all | solution.py:526
  68.0 1.7 %collective-permute-start.9 = (bf16[64,3072]{1,0:T(8,128)(2,1)S(1)}, bf16[64,3072]{1,0:T(8,128)(2,1)S(1)}, u32[]{:S(2)}, u32[]{:S(2)}) collective-permute-start(bf16[64,3072]{1,0:T(8,128)(2,1)S(1)} %broadcast_select_fusion.refs_10_), channel_id=1, source_target_pairs={{0,1},{1,0},{2,3},{3,2},{4,5},{5,4},{6,7},{7,6},{8,9},{9,8},{10,11... | collective-permute-start | bytes 1179656 | tf_op jit(solution)/shard_map/ppermute | solution.py:480
  71.9 4.6 %project_kva.1.kva = bf16[2,512,128]{2,1,0:T(8,128)(2,1)} custom-call(s32[1]{0:T(128)} %bitcast.section_ref.refs_0_, f32[2,80,128]{2,1,0:T(8,128)} %pad_maximum_fusion.refs_1_.tabs_hbm, f32[2,128]{1,0:T(2,128)} %pad_maximum_fusion.1.refs_2_.gain_hbm, bf16[8,384,128]{2,1,0:T(8,128)(2,1)} %all-to-all-done.refs_3_, ...), custom_call_target="tpu_custom_call" | custom-call | flops 805306368 | bytes 4718592 | tf_op jit(solution)/shard_map/project_kva/pallas_call | solution.py:245
  76.5 2.8 %collective-permute-done.9.refs_11_ = bf16[64,3072]{1,0:T(8,128)(2,1)S(1)} collective-permute-done((bf16[64,3072]{1,0:T(8,128)(2,1)S(1)}, bf16[64,3072]{1,0:T(8,128)(2,1)S(1)}, u32[]{:S(2)}, u32[]{:S(2)}) %collective-permute-start.9) | collective-permute-done | bytes 393248 | tf_op jit(solution)/shard_map/ppermute | solution.py:480
  79.3 4.1 %collective-permute-start.17 = (bf16[2,512,128]{2,1,0:T(8,128)(2,1)}, bf16[2,512,128]{2,1,0:T(8,128)(2,1)}, u32[]{:S(2)}, u32[]{:S(2)}) collective-permute-start(bf16[2,512,128]{2,1,0:T(8,128)(2,1)} %project_kva.1.kva), channel_id=1, source_target_pairs={{0,16},{1,17},{2,18},{3,19},{4,20},{5,21},{6,22},{7,23},{8,24},{9,... | collective-permute-start | bytes 786440 | tf_op jit(solution)/shard_map/ppermute | solution.py:531
  85.2 4.6 %project_kvb.1.kvb = bf16[2,512,128]{2,1,0:T(8,128)(2,1)} custom-call(s32[1]{0:T(128)} %bitcast.section_ref.refs_0_, f32[2,80,128]{2,1,0:T(8,128)} %pad_maximum_fusion.refs_1_.tabs_hbm, f32[2,128]{1,0:T(2,128)} %pad_maximum_fusion.1.refs_2_.gain_hbm, bf16[8,384,128]{2,1,0:T(8,128)(2,1)} %all-to-all-done.refs_3_, ...), custom_call_target="tpu_custom_call" | custom-call | flops 805306368 | bytes 4718592 | tf_op jit(solution)/shard_map/project_kvb/pallas_call | solution.py:245
  91.3 2.1 %all-to-all-done.1.direct_hbm = bf16[8,528,128]{2,1,0:T(8,128)(2,1)} async-done(((bf16[8,528,128]{2,1,0:T(8,128)(2,1)}), bf16[8,528,128]{2,1,0:T(8,128)(2,1)}, u32[]{:S(2)}, u32[]{:S(2)}) %all-to-all-start.1) | async-done | bytes 1081376 | tf_op jit(solution)/shard_map/all_to_all | solution.py:526
  93.4 10.2 %attend_own.1 = (bf16[1024,128]{1,0:T(8,128)(2,1)}, f32[1024,128]{1,0:T(8,128)}, f32[1024,128]{1,0:T(8,128)}, f32[16,1024]{1,0:T(8,128)}) custom-call(s32[1]{0:T(128)} %bitcast.section_ref.refs_0_, f32[16,8]{1,0:T(8,128)} %fusion.3.rows_ref, f32[128,16]{1,0:T(8,128)} %fusion.1.keys_ref, bf16[2,512,128]{2,1,0:T(8,128)(2,1)} %project_kva.1.kva, ...), custom_call_target="tpu_custom_call" | custom-call | flops 1879048192 | bytes 6291456 | tf_op jit(solution)/shard_map/attend_own/pallas_call | solution.py:378
  104.3 3.1 %attend_second.1 = bf16[8,128,128]{2,1,0:T(8,128)(2,1)} custom-call(s32[1]{0:T(128)} %bitcast.section_ref.refs_0_, s32[2,16]{1,0:T(2,128)} %pad_add_fusion.place_ref, f32[16,1024]{1,0:T(8,128)} %get-tuple-element.53.keep_hbm, bf16[1024,128]{1,0:T(8,128)(2,1)} %get-tuple-element.54.q_hbm, f32[1024,128]{1,0:T(8,128)} %get-tuple-element.55.num_hbm, ...), custom_call_target="tpu_custom_call" | custom-call | flops 268435456 | bytes 2097152 | tf_op jit(solution)/shard_map/attend_second/pallas_call | solution.py:401
  107.4 13.1 %all_to_all.15.attn_ref = bf16[8,128,128]{2,1,0:T(8,128)(2,1)S(1)} all-to-all(bf16[8,128,128]{2,1,0:T(8,128)(2,1)} %attend_second.1), channel_id=1, replica_groups=mesh['section'=2,'seq'=8,'tp'=2] {'seq'}, dimensions={0} | all-to-all | bytes 524288 | tf_op jit(solution)/shard_map/all_to_all | solution.py:543
  121.1 1.8 %collective-permute-start.19 = (bf16[128,1536]{1,0:T(8,128)(2,1)S(1)}, bf16[128,1536]{1,0:T(8,128)(2,1)S(1)}, u32[]{:S(2)}, u32[]{:S(2)}) collective-permute-start(bf16[128,1536]{1,0:T(8,128)(2,1)S(1)} %out_sent.1), channel_id=1, source_target_pairs={{0,1},{1,0},{2,3},{3,2},{4,5},{5,4},{6,7},{7,6},{8,9},{9,8},{10,11... | collective-permute-start | bytes 1179656 | tf_op jit(solution)/shard_map/ppermute | solution.py:480
  124.2 7.4 %collective-permute-done.19 = bf16[128,1536]{1,0:T(8,128)(2,1)S(1)} collective-permute-done((bf16[128,1536]{1,0:T(8,128)(2,1)S(1)}, bf16[128,1536]{1,0:T(8,128)(2,1)S(1)}, u32[]{:S(2)}, u32[]{:S(2)}) %collective-permute-start.19) | collective-permute-done | bytes 393248 | tf_op jit(solution)/shard_map/ppermute | solution.py:480
  (102 shorter events, 25.0 us)
Async XLA Ops:
  2.9 12.8 %collective-permute-start.2 = (bf16[64,3072]{1,0:T(8,128)(2,1)}, bf16[64,3072]{1,0:T(8,128)(2,1)}, u32[]{:S(2)}, u32[]{:S(2)}) collective-permute-start(bf16[64,3072]{1,0:T(8,128)(2,1)} %get-tuple-element.32), channel_id=1, source_target_pairs={{0,4},{2,6},{4,0},{6,2},{8,12},{10,14},{12,8},{14,10},{1,5},{3,7},... | collective-permute-start | bytes 1179656 | tf_op jit(solution)/shard_map/ppermute | solution.py:474
  6.0 15.2 %collective-permute-start = (bf16[64,3072]{1,0:T(8,128)(2,1)}, bf16[64,3072]{1,0:T(8,128)(2,1)S(1)}, u32[]{:S(2)}, u32[]{:S(2)}) collective-permute-start(bf16[64,3072]{1,0:T(8,128)(2,1)} %get-tuple-element.32), channel_id=1, source_target_pairs={{4,8},{6,10},{8,4},{10,6},{5,9},{7,11},{9,5},{11,7},{20,24},{22,26... | collective-permute-start | bytes 1179656 | tf_op jit(solution)/shard_map/ppermute | solution.py:474
  8.8 32.5 %all-to-all-start = ((bf16[8,384,128]{2,1,0:T(8,128)(2,1)}), bf16[8,384,128]{2,1,0:T(8,128)(2,1)}, u32[]{:S(2)}, u32[]{:S(2)}) async-start(bf16[8,384,128]{2,1,0:T(8,128)(2,1)} %kv_weights.1), calls=%async_computation | async-start | bytes 1572864 | tf_op jit(solution)/shard_map/all_to_all | solution.py:469
  15.7 24.6 %collective-permute-start.3 = (bf16[64,3072]{1,0:T(8,128)(2,1)}, bf16[64,3072]{1,0:T(8,128)(2,1)}, u32[]{:S(2)}, u32[]{:S(2)}) collective-permute-start(bf16[64,3072]{1,0:T(8,128)(2,1)} %collective-permute-done.2.refs_8_.refs_2_), channel_id=1, source_target_pairs={{0,1},{1,0},{2,3},{3,2},{4,5},{5,4},{6,7},{7,6},{8,9},{9,8},{10,11... | collective-permute-start | bytes 1179656 | tf_op jit(solution)/shard_map/ppermute | solution.py:480
  17.2 28.1 %collective-permute-start.4 = (bf16[64,3072]{1,0:T(8,128)(2,1)}, bf16[64,3072]{1,0:T(8,128)(2,1)}, u32[]{:S(2)}, u32[]{:S(2)}) collective-permute-start(bf16[64,3072]{1,0:T(8,128)(2,1)} %collective-permute-done.2.refs_8_.refs_2_), channel_id=1, source_target_pairs={{4,8},{6,10},{8,4},{10,6},{5,9},{7,11},{9,5},{11,7},{20,24},{22,26... | collective-permute-start | bytes 1179656 | tf_op jit(solution)/shard_map/ppermute | solution.py:474
  21.2 19.1 %collective-permute-start.1 = (bf16[64,3072]{1,0:T(8,128)(2,1)S(1)}, bf16[64,3072]{1,0:T(8,128)(2,1)S(1)}, u32[]{:S(2)}, u32[]{:S(2)}) collective-permute-start(bf16[64,3072]{1,0:T(8,128)(2,1)S(1)} %collective-permute-done), channel_id=1, source_target_pairs={{4,0},{6,2},{8,12},{10,14},{5,1},{7,3},{9,13},{11,15},{20,16},{22,... | collective-permute-start | bytes 1179656 | tf_op jit(solution)/shard_map/ppermute | solution.py:474
  40.4 29.4 %copy-start.1 = (bf16[64,3072]{1,0:T(8,128)(2,1)}, bf16[64,3072]{1,0:T(8,128)(2,1)S(1)}, u32[]{:S(2)}) copy-start(bf16[64,3072]{1,0:T(8,128)(2,1)S(1)} %broadcast_select_fusion.1.refs_6_) | copy-start | bytes 1179652
  40.4 13.5 %collective-permute-start.6 = (bf16[64,3072]{1,0:T(8,128)(2,1)S(1)}, bf16[64,3072]{1,0:T(8,128)(2,1)}, u32[]{:S(2)}, u32[]{:S(2)}) collective-permute-start(bf16[64,3072]{1,0:T(8,128)(2,1)S(1)} %broadcast_select_fusion.1.refs_6_), channel_id=1, source_target_pairs={{0,1},{1,0},{2,3},{3,2},{4,5},{5,4},{6,7},{7,6},{8,9},{9,8},{10,11... | collective-permute-start | bytes 1179656 | tf_op jit(solution)/shard_map/ppermute | solution.py:480
  43.3 12.4 %collective-permute-start.7 = (bf16[4,384,128]{2,1,0:T(8,128)(2,1)}, bf16[4,384,128]{2,1,0:T(8,128)(2,1)}, u32[]{:S(2)}, u32[]{:S(2)}) collective-permute-start(bf16[4,384,128]{2,1,0:T(8,128)(2,1)} %get-tuple-element.62), channel_id=1, source_target_pairs={{0,16},{16,0},{1,17},{17,1},{2,18},{18,2},{3,19},{19,3},{4,20},{20... | collective-permute-start | bytes 1179656 | tf_op jit(solution)/shard_map/ppermute | solution.py:500
  44.8 17.0 %collective-permute-start.8 = (bf16[4,384,128]{2,1,0:T(8,128)(2,1)}, bf16[4,384,128]{2,1,0:T(8,128)(2,1)}, u32[]{:S(2)}, u32[]{:S(2)}) collective-permute-start(bf16[4,384,128]{2,1,0:T(8,128)(2,1)} %get-tuple-element.61), channel_id=1, source_target_pairs={{0,16},{16,0},{1,17},{17,1},{2,18},{18,2},{3,19},{19,3},{4,20},{20... | collective-permute-start | bytes 1179656 | tf_op jit(solution)/shard_map/ppermute | solution.py:500
  45.4 21.6 %collective-permute-start.5 = (bf16[64,3072]{1,0:T(8,128)(2,1)}, bf16[64,3072]{1,0:T(8,128)(2,1)}, u32[]{:S(2)}, u32[]{:S(2)}) collective-permute-start(bf16[64,3072]{1,0:T(8,128)(2,1)} %collective-permute-done.4), channel_id=1, source_target_pairs={{4,0},{6,2},{8,12},{10,14},{5,1},{7,3},{9,13},{11,15},{20,16},{22,... | collective-permute-start | bytes 1179656 | tf_op jit(solution)/shard_map/ppermute | solution.py:474
  61.8 31.5 %all-to-all-start.1 = ((bf16[8,528,128]{2,1,0:T(8,128)(2,1)}), bf16[8,528,128]{2,1,0:T(8,128)(2,1)}, u32[]{:S(2)}, u32[]{:S(2)}) async-start(bf16[8,528,128]{2,1,0:T(8,128)(2,1)} %direct_rows.1), calls=%async_computation.1 | async-start | bytes 2162688 | tf_op jit(solution)/shard_map/all_to_all | solution.py:526
  66.1 4.2 %collective-permute-start.10 = (bf16[128,3072]{1,0:T(8,128)(2,1)}, bf16[128,3072]{1,0:T(8,128)(2,1)S(1)}, u32[]{:S(2)}, u32[]{:S(2)}) collective-permute-start(bf16[128,3072]{1,0:T(8,128)(2,1)} %get-tuple-element.47.refs_6_.refs_0_), channel_id=1, source_target_pairs={{0,2},{2,0},{4,6},{6,4},{8,10},{10,8},{12,14},{14,12},{1,3},{3,1},... | collective-permute-start | bytes 2359304 | tf_op jit(solution)/shard_map/ppermute | solution.py:477
  66.5 3.3 %collective-permute-start.11 = (bf16[64,3072]{1,0:T(8,128)(2,1)}, bf16[64,3072]{1,0:T(8,128)(2,1)S(1)}, u32[]{:S(2)}, u32[]{:S(2)}) collective-permute-start(bf16[64,3072]{1,0:T(8,128)(2,1)} %collective-permute-done.2.refs_8_.refs_2_), channel_id=1, source_target_pairs={{0,2},{2,0},{4,6},{6,4},{8,10},{10,8},{12,14},{14,12},{1,3},{3,1},... | collective-permute-start | bytes 1179656 | tf_op jit(solution)/shard_map/ppermute | solution.py:477
  66.6 3.7 %collective-permute-start.12 = (bf16[64,3072]{1,0:T(8,128)(2,1)}, bf16[64,3072]{1,0:T(8,128)(2,1)S(1)}, u32[]{:S(2)}, u32[]{:S(2)}) collective-permute-start(bf16[64,3072]{1,0:T(8,128)(2,1)} %collective-permute-done.3.refs_9_.refs_3_), channel_id=1, source_target_pairs={{0,2},{2,0},{4,6},{6,4},{8,10},{10,8},{12,14},{14,12},{1,3},{3,1},... | collective-permute-start | bytes 1179656 | tf_op jit(solution)/shard_map/ppermute | solution.py:477
  68.0 11.3 %collective-permute-start.9 = (bf16[64,3072]{1,0:T(8,128)(2,1)S(1)}, bf16[64,3072]{1,0:T(8,128)(2,1)S(1)}, u32[]{:S(2)}, u32[]{:S(2)}) collective-permute-start(bf16[64,3072]{1,0:T(8,128)(2,1)S(1)} %broadcast_select_fusion.refs_10_), channel_id=1, source_target_pairs={{0,1},{1,0},{2,3},{3,2},{4,5},{5,4},{6,7},{7,6},{8,9},{9,8},{10,11... | collective-permute-start | bytes 1179656 | tf_op jit(solution)/shard_map/ppermute | solution.py:480
  69.8 13.7 %collective-permute-start.13 = (bf16[64,3072]{1,0:T(8,128)(2,1)S(1)}, bf16[64,3072]{1,0:T(8,128)(2,1)S(1)}, u32[]{:S(2)}, u32[]{:S(2)}) collective-permute-start(bf16[64,3072]{1,0:T(8,128)(2,1)S(1)} %broadcast_select_fusion.1.refs_6_), channel_id=1, source_target_pairs={{0,2},{2,0},{4,6},{6,4},{8,10},{10,8},{12,14},{14,12},{1,3},{3,1},... | collective-permute-start | bytes 1179656 | tf_op jit(solution)/shard_map/ppermute | solution.py:477
  69.8 13.6 %collective-permute-start.15 = (bf16[64,3072]{1,0:T(8,128)(2,1)S(1)}, bf16[64,3072]{1,0:T(8,128)(2,1)S(1)}, u32[]{:S(2)}, u32[]{:S(2)}) collective-permute-start(bf16[64,3072]{1,0:T(8,128)(2,1)S(1)} %broadcast_select_fusion.refs_10_), channel_id=1, source_target_pairs={{0,2},{2,0},{4,6},{6,4},{8,10},{10,8},{12,14},{14,12},{1,3},{3,1},... | collective-permute-start | bytes 1179656 | tf_op jit(solution)/shard_map/ppermute | solution.py:477
  70.3 13.1 %collective-permute-start.14 = (bf16[64,3072]{1,0:T(8,128)(2,1)}, bf16[64,3072]{1,0:T(8,128)(2,1)S(1)}, u32[]{:S(2)}, u32[]{:S(2)}) collective-permute-start(bf16[64,3072]{1,0:T(8,128)(2,1)} %collective-permute-done.6.refs_7_), channel_id=1, source_target_pairs={{0,2},{2,0},{4,6},{6,4},{8,10},{10,8},{12,14},{14,12},{1,3},{3,1},... | collective-permute-start | bytes 1179656 | tf_op jit(solution)/shard_map/ppermute | solution.py:477
  79.3 4.2 %collective-permute-start.16 = (bf16[64,3072]{1,0:T(8,128)(2,1)S(1)}, bf16[64,3072]{1,0:T(8,128)(2,1)S(1)}, u32[]{:S(2)}, u32[]{:S(2)}) collective-permute-start(bf16[64,3072]{1,0:T(8,128)(2,1)S(1)} %collective-permute-done.9.refs_11_), channel_id=1, source_target_pairs={{0,2},{2,0},{4,6},{6,4},{8,10},{10,8},{12,14},{14,12},{1,3},{3,1},... | collective-permute-start | bytes 1179656 | tf_op jit(solution)/shard_map/ppermute | solution.py:477
  79.3 12.0 %collective-permute-start.17 = (bf16[2,512,128]{2,1,0:T(8,128)(2,1)}, bf16[2,512,128]{2,1,0:T(8,128)(2,1)}, u32[]{:S(2)}, u32[]{:S(2)}) collective-permute-start(bf16[2,512,128]{2,1,0:T(8,128)(2,1)} %project_kva.1.kva), channel_id=1, source_target_pairs={{0,16},{1,17},{2,18},{3,19},{4,20},{5,21},{6,22},{7,23},{8,24},{9,... | collective-permute-start | bytes 786440 | tf_op jit(solution)/shard_map/ppermute | solution.py:531
  89.8 13.9 %collective-permute-start.18 = (bf16[2,512,128]{2,1,0:T(8,128)(2,1)}, bf16[2,512,128]{2,1,0:T(8,128)(2,1)S(1)}, u32[]{:S(2)}, u32[]{:S(2)}) collective-permute-start(bf16[2,512,128]{2,1,0:T(8,128)(2,1)} %project_kvb.1.kvb), channel_id=1, source_target_pairs={{0,16},{1,17},{2,18},{3,19},{4,20},{5,21},{6,22},{7,23},{8,24},{9,... | collective-permute-start | bytes 786440 | tf_op jit(solution)/shard_map/ppermute | solution.py:537
  93.4 27.1 %copy-start = (bf16[1024,1536]{1,0:T(8,128)(2,1)S(1)}, bf16[1024,1536]{1,0:T(8,128)(2,1)}, u32[]{:S(2)}) copy-start(bf16[1024,1536]{1,0:T(8,128)(2,1)} %get-tuple-element.58.w_ref) | copy-start | bytes 9437188
  121.1 10.6 %collective-permute-start.19 = (bf16[128,1536]{1,0:T(8,128)(2,1)S(1)}, bf16[128,1536]{1,0:T(8,128)(2,1)S(1)}, u32[]{:S(2)}, u32[]{:S(2)}) collective-permute-start(bf16[128,1536]{1,0:T(8,128)(2,1)S(1)} %out_sent.1), channel_id=1, source_target_pairs={{0,1},{1,0},{2,3},{3,2},{4,5},{5,4},{6,7},{7,6},{8,9},{9,8},{10,11... | collective-permute-start | bytes 1179656 | tf_op jit(solution)/shard_map/ppermute | solution.py:480
  (15 other events, 105.4 us)

commit v17 on v16

--- a/solution.py
+++ b/solution.py
@@ -498,6 +498,8 @@
     near_tp = to_tp(near)
     some = seq // 2
     peers = [lax.ppermute(mine[:some], "section", both), lax.ppermute(mine[some:], "section", both)]
+    direct, peers[0] = lax.optimization_barrier((direct, peers[0]))
+    direct = lax.all_to_all(direct, "seq", 0, 0)
     cols = w_out.shape[1] // 2
     w_sent = lax.dynamic_slice_in_dim(w_late, (1 - tp) * cols, cols, 1)
     w_kept = lax.dynamic_slice_in_dim(w_late, tp * cols, cols, 1)
@@ -522,8 +524,6 @@
     third, near_tp, early = lax.optimization_barrier((third, near_tp, early))
     tabs, gains, row_tiles, key_tiles, place, w_sent, w_kept = early
     third_tp = to_tp(third)
-    direct, third_tp, peers = lax.optimization_barrier((direct, third_tp, peers))
-    direct = lax.all_to_all(direct, "seq", 0, 0)
     fourth, third_tp, peers[0] = lax.optimization_barrier((fourth, third_tp, peers[0]))
     fourth_tp = to_tp(fourth)
     a = [full, to_core(full), near, near_tp, to_core(near), to_core(near_tp)]

time: 134 us -> 131 us (0.978)
  local copies, waits for them, and re-layouts: 16.5 us -> 12.8 us
  waiting for transfers between devices: 32.6 us -> 29.7 us
  starting transfers between devices: 32.6 us -> 35.2 us
    ppermute x5, waiting for transfers between devices: 12.3 us -> 1.08 us  [along_z(): return lax.ppermute(x, 'seq', z_pairs(seq, pairs))]
    all_to_all x1, waiting for transfers between devices: 0.01 us -> 8.98 us  [head_body(): mine = lax.all_to_all(kv_weights(section_at, rows3), 'seq', 0, 0)]
    ppermute x4, waiting for transfers between devices: 10.2 us -> 16.6 us  [to_tp(): return lax.ppermute(x, 'tp', both)]
    ppermute x1, waiting for transfers between devices: 6.11 us -> 0.01 us  [head_body(): lax.ppermute(mine[some:], 'section', both)]
    another operation x2, local copies, waits for them, and re-layouts: 3.55 us -> 0.97 us  [head_body(): text_kv[0].reshape(-1, 2, seq, HEAD_DIM).transpose(2, 1, 0, 3)]
    all_to_all x1, waiting for transfers between devices: 2.09 us -> 0.01 us  [head_body(): direct = lax.all_to_all(direct, 'seq', 0, 0)]
    all_to_all x1, starting transfers between devices: 4.24 us -> 5.76 us  [head_body(): direct = lax.all_to_all(direct, 'seq', 0, 0)]
    unnamed x34 -> x38, local copies, waits for them, and re-layouts: 4.01 us -> 4.1 us
  transfers between devices with their start and end apart: 22 -> 22, of which waited for: 6 -> 6; matrix products, arithmetic and copies ran while one was open for 13% -> 11% of each run, Pallas kernels for 19% -> 19%
where the time goes in v17:
time: 131 us
  starting transfers between devices  35.2 us (27%)
  Pallas kernels  31.6 us (24%)
  waiting for transfers between devices  29.7 us (23%)
  blocking collectives  14.1 us (11%)
  local copies, waits for them, and re-layouts  12.8 us (10%)
  other arithmetic  6.72 us (5%)
    ppermute x4, waiting for transfers between devices, to_tp(): return lax.ppermute(x, 'tp', both)  16.6 us
    all_to_all x1, blocking collectives, head_body(): attn = lax.all_to_all(attn, 'seq', 0, 0)  14.1 us
    pallas_call x1, Pallas kernels, attend_own(): call(own_kernel, 'attend_own', [jax.ShapeDtypeStruct((rows, HEAD_DIM), jn...  10.2 us
    pallas_call x2, Pallas kernels, project_kv(): call(lambda *refs: kv_kernel(chunk, *refs), 'project_kv' + 'ab'[chunk], j...  9.12 us
    all_to_all x1, waiting for transfers between devices, head_body(): mine = lax.all_to_all(kv_weights(section_at, rows3), 'seq', 0, 0)  8.98 us
    ppermute x5, starting transfers between devices, along_z(): return lax.ppermute(x, 'seq', z_pairs(seq, pairs))  8.51 us
    ppermute x4, starting transfers between devices, to_tp(): return lax.ppermute(x, 'tp', both)  6.22 us
    all_to_all x1, starting transfers between devices, head_body(): direct = lax.all_to_all(direct, 'seq', 0, 0)  5.76 us
  transfers between devices with their start and end apart: 22, of which 6 were waited for; matrix products, arithmetic and copies ran while one was open for 11% of the time, Pallas kernels for 19%

profile of v17, /device:TPU:0, one launch (start us, length us, event | category | flops | bytes accessed | tf_op | source)
XLA Modules:
  0.0 130.5 jit_solution(2165515196613076124)
XLA Ops:
  0.0 2.9 %norm_tokens.1 = (bf16[128,3072]{1,0:T(8,128)(2,1)}, bf16[64,3072]{1,0:T(8,128)(2,1)}) custom-call(s32[1]{0:T(128)} %bitcast.1.tp_ref, bf16[128,3072]{1,0:T(8,128)(2,1)} %bitcast.27, f32[3,1,3072]{2,1,0:T(1,128)} %bitcast.29), custom_call_target="tpu_custom_call" | custom-call | flops 3932160 | bytes 1572864 | tf_op jit(solution)/shard_map/norm_tokens/pallas_call | solution.py:96
  3.0 3.1 %collective-permute-start.2 = (bf16[64,3072]{1,0:T(8,128)(2,1)}, bf16[64,3072]{1,0:T(8,128)(2,1)}, u32[]{:S(2)}, u32[]{:S(2)}) collective-permute-start(bf16[64,3072]{1,0:T(8,128)(2,1)} %get-tuple-element.30), channel_id=1, source_target_pairs={{0,4},{2,6},{4,0},{6,2},{8,12},{10,14},{12,8},{14,10},{1,5},{3,7},... | collective-permute-start | bytes 1179656 | tf_op jit(solution)/shard_map/ppermute | solution.py:474
  7.5 2.1 %kv_weights.1 = bf16[8,384,128]{2,1,0:T(8,128)(2,1)} custom-call(s32[1]{0:T(128)} %bitcast.section_ref.refs_0_, bf16[3,384,1024]{2,1,0:T(8,128)(2,1)} %bitcast.25), custom_call_target="tpu_custom_call" | custom-call | bytes 1572864 | tf_op jit(solution)/shard_map/kv_weights/pallas_call | solution.py:125
  9.6 4.9 %all-to-all-start = ((bf16[8,384,128]{2,1,0:T(8,128)(2,1)}), bf16[8,384,128]{2,1,0:T(8,128)(2,1)S(1)}, u32[]{:S(2)}, u32[]{:S(2)}) async-start(bf16[8,384,128]{2,1,0:T(8,128)(2,1)} %kv_weights.1), calls=%async_computation | async-start | bytes 1572864 | tf_op jit(solution)/shard_map/all_to_all | solution.py:469
  17.9 3.0 %direct_rows.1 = bf16[8,528,128]{2,1,0:T(8,128)(2,1)} custom-call(bf16[3,384,1024]{2,1,0:T(8,128)(2,1)} %bitcast.26, bf16[8,128,128]{2,1,0:T(8,128)(2,1)} %bitcast.28, bf16[16,128]{1,0:T(8,128)(2,1)} %pad.4.mask_ref), custom_call_target="tpu_custom_call" | custom-call | bytes 2162688 | tf_op jit(solution)/shard_map/direct_rows/pallas_call | solution.py:148
  21.4 1.5 %collective-permute-start.3 = (bf16[64,3072]{1,0:T(8,128)(2,1)}, bf16[64,3072]{1,0:T(8,128)(2,1)}, u32[]{:S(2)}, u32[]{:S(2)}) collective-permute-start(bf16[64,3072]{1,0:T(8,128)(2,1)} %collective-permute-done.2.refs_8_.refs_2_), channel_id=1, source_target_pairs={{0,1},{1,0},{2,3},{3,2},{4,5},{5,4},{6,7},{7,6},{8,9},{9,8},{10,11... | collective-permute-start | bytes 1179656 | tf_op jit(solution)/shard_map/ppermute | solution.py:480
  28.4 9.0 %all-to-all-done.refs_3_ = bf16[8,384,128]{2,1,0:T(8,128)(2,1)S(1)} async-done(((bf16[8,384,128]{2,1,0:T(8,128)(2,1)}), bf16[8,384,128]{2,1,0:T(8,128)(2,1)S(1)}, u32[]{:S(2)}, u32[]{:S(2)}) %all-to-all-start) | async-done | bytes 786464 | tf_op jit(solution)/shard_map/all_to_all | solution.py:469
  38.4 1.5 %collective-permute-start.7 = (bf16[4,384,128]{2,1,0:T(8,128)(2,1)S(1)}, bf16[4,384,128]{2,1,0:T(8,128)(2,1)S(1)}, u32[]{:S(2)}, u32[]{:S(2)}) collective-permute-start(bf16[4,384,128]{2,1,0:T(8,128)(2,1)S(1)} %get-tuple-element.58), channel_id=1, source_target_pairs={{0,16},{16,0},{1,17},{17,1},{2,18},{18,2},{3,19},{19,3},{4,20},{20... | collective-permute-start | bytes 1179656 | tf_op jit(solution)/shard_map/ppermute | solution.py:500
  39.9 4.9 %constant_dynamic-slice_fusion = (bf16[1024,1536]{1,0:T(8,128)(2,1)S(1)}, bf16[1024,1536]{1,0:T(8,128)(2,1)}) fusion(bf16[1024,3072]{1,0:T(8,128)(2,1)} %param.12, s32[]{:T(128)S(6)} %select_n.78, s32[]{:T(128)S(6)} %select_n.77), kind=kLoop, calls=%fused_computation.21 | loop fusion | bytes 12582920 | tf_op jit(solution)/shard_map/dynamic_slice | solution.py:505
  44.8 3.0 %collective-permute-done.7.refs_4_ = bf16[4,384,128]{2,1,0:T(8,128)(2,1)S(1)} collective-permute-done((bf16[4,384,128]{2,1,0:T(8,128)(2,1)S(1)}, bf16[4,384,128]{2,1,0:T(8,128)(2,1)S(1)}, u32[]{:S(2)}, u32[]{:S(2)}) %collective-permute-start.7) | collective-permute-done | bytes 393248 | tf_op jit(solution)/shard_map/ppermute | solution.py:500
  49.1 5.8 %all-to-all-start.1 = ((bf16[8,528,128]{2,1,0:T(8,128)(2,1)}), bf16[8,528,128]{2,1,0:T(8,128)(2,1)}, u32[]{:S(2)}, u32[]{:S(2)}) async-start(bf16[8,528,128]{2,1,0:T(8,128)(2,1)} %direct_rows.1), calls=%async_computation.1 | async-start | bytes 2162688 | tf_op jit(solution)/shard_map/all_to_all | solution.py:502
  56.0 1.6 %collective-permute-start.6 = (bf16[64,3072]{1,0:T(8,128)(2,1)S(1)}, bf16[64,3072]{1,0:T(8,128)(2,1)S(1)}, u32[]{:S(2)}, u32[]{:S(2)}) collective-permute-start(bf16[64,3072]{1,0:T(8,128)(2,1)S(1)} %broadcast_select_fusion.1.refs_6_), channel_id=1, source_target_pairs={{0,1},{1,0},{2,3},{3,2},{4,5},{5,4},{6,7},{7,6},{8,9},{9,8},{10,11... | collective-permute-start | bytes 1179656 | tf_op jit(solution)/shard_map/ppermute | solution.py:480
  61.3 6.3 %collective-permute-done.6.refs_7_ = bf16[64,3072]{1,0:T(8,128)(2,1)S(1)} collective-permute-done((bf16[64,3072]{1,0:T(8,128)(2,1)S(1)}, bf16[64,3072]{1,0:T(8,128)(2,1)S(1)}, u32[]{:S(2)}, u32[]{:S(2)}) %collective-permute-start.6) | collective-permute-done | bytes 393248 | tf_op jit(solution)/shard_map/ppermute | solution.py:480
  67.6 1.5 %collective-permute-start.8 = (bf16[64,3072]{1,0:T(8,128)(2,1)S(1)}, bf16[64,3072]{1,0:T(8,128)(2,1)S(1)}, u32[]{:S(2)}, u32[]{:S(2)}) collective-permute-start(bf16[64,3072]{1,0:T(8,128)(2,1)S(1)} %broadcast_select_fusion.refs_10_), channel_id=1, source_target_pairs={{0,1},{1,0},{2,3},{3,2},{4,5},{5,4},{6,7},{7,6},{8,9},{9,8},{10,11... | collective-permute-start | bytes 1179656 | tf_op jit(solution)/shard_map/ppermute | solution.py:480
  71.1 4.5 %project_kva.1.kva = bf16[2,512,128]{2,1,0:T(8,128)(2,1)} custom-call(s32[1]{0:T(128)} %bitcast.section_ref.refs_0_, f32[2,80,128]{2,1,0:T(8,128)} %pad_maximum_fusion.refs_1_.tabs_hbm, f32[2,128]{1,0:T(2,128)} %pad_maximum_fusion.1.refs_2_.gain_hbm, bf16[8,384,128]{2,1,0:T(8,128)(2,1)} %copy-done.1, bf16[4,384,128]{2,1,0:T(8,128)(2,1)} %copy-done.5, ...), custom_call_target="tpu_custom_call" | custom-call | flops 805306368 | bytes 4718592 | tf_op jit(solution)/shard_map/project_kva/pallas_call | solution.py:245
  75.6 2.7 %collective-permute-done.8.refs_11_ = bf16[64,3072]{1,0:T(8,128)(2,1)S(1)} collective-permute-done((bf16[64,3072]{1,0:T(8,128)(2,1)S(1)}, bf16[64,3072]{1,0:T(8,128)(2,1)S(1)}, u32[]{:S(2)}, u32[]{:S(2)}) %collective-permute-start.8) | collective-permute-done | bytes 393248 | tf_op jit(solution)/shard_map/ppermute | solution.py:480
  78.4 4.1 %collective-permute-start.17 = (bf16[2,512,128]{2,1,0:T(8,128)(2,1)}, bf16[2,512,128]{2,1,0:T(8,128)(2,1)}, u32[]{:S(2)}, u32[]{:S(2)}) collective-permute-start(bf16[2,512,128]{2,1,0:T(8,128)(2,1)} %project_kva.1.kva), channel_id=1, source_target_pairs={{0,16},{1,17},{2,18},{3,19},{4,20},{5,21},{6,22},{7,23},{8,24},{9,... | collective-permute-start | bytes 786440 | tf_op jit(solution)/shard_map/ppermute | solution.py:531
  84.3 4.6 %project_kvb.1.kvb = bf16[2,512,128]{2,1,0:T(8,128)(2,1)} custom-call(s32[1]{0:T(128)} %bitcast.section_ref.refs_0_, f32[2,80,128]{2,1,0:T(8,128)} %pad_maximum_fusion.refs_1_.tabs_hbm, f32[2,128]{1,0:T(2,128)} %pad_maximum_fusion.1.refs_2_.gain_hbm, bf16[8,384,128]{2,1,0:T(8,128)(2,1)} %copy-done.1, bf16[4,384,128]{2,1,0:T(8,128)(2,1)} %copy-done.5, ...), custom_call_target="tpu_custom_call" | custom-call | flops 805306368 | bytes 4718592 | tf_op jit(solution)/shard_map/project_kvb/pallas_call | solution.py:245
  88.9 1.5 %collective-permute-start.18 = (bf16[2,512,128]{2,1,0:T(8,128)(2,1)}, bf16[2,512,128]{2,1,0:T(8,128)(2,1)S(1)}, u32[]{:S(2)}, u32[]{:S(2)}) collective-permute-start(bf16[2,512,128]{2,1,0:T(8,128)(2,1)} %project_kvb.1.kvb), channel_id=1, source_target_pairs={{0,16},{1,17},{2,18},{3,19},{4,20},{5,21},{6,22},{7,23},{8,24},{9,... | collective-permute-start | bytes 786440 | tf_op jit(solution)/shard_map/ppermute | solution.py:537
  90.4 10.2 %attend_own.1 = (bf16[1024,128]{1,0:T(8,128)(2,1)}, f32[1024,128]{1,0:T(8,128)}, f32[1024,128]{1,0:T(8,128)}, f32[16,1024]{1,0:T(8,128)}) custom-call(s32[1]{0:T(128)} %bitcast.section_ref.refs_0_, f32[16,8]{1,0:T(8,128)} %fusion.3.rows_ref, f32[128,16]{1,0:T(8,128)} %fusion.1.keys_ref, bf16[2,512,128]{2,1,0:T(8,128)(2,1)} %project_kva.1.kva, ...), custom_call_target="tpu_custom_call" | custom-call | flops 1879048192 | bytes 6291456 | tf_op jit(solution)/shard_map/attend_own/pallas_call | solution.py:378
  101.4 3.0 %attend_second.1 = bf16[8,128,128]{2,1,0:T(8,128)(2,1)} custom-call(s32[1]{0:T(128)} %bitcast.section_ref.refs_0_, s32[2,16]{1,0:T(2,128)} %pad_add_fusion.place_ref, f32[16,1024]{1,0:T(8,128)} %get-tuple-element.49.keep_hbm, bf16[1024,128]{1,0:T(8,128)(2,1)} %get-tuple-element.50.q_hbm, f32[1024,128]{1,0:T(8,128)} %get-tuple-element.51.num_hbm, ...), custom_call_target="tpu_custom_call" | custom-call | flops 268435456 | bytes 2097152 | tf_op jit(solution)/shard_map/attend_second/pallas_call | solution.py:401
  104.4 14.1 %all_to_all.15.attn_ref = bf16[8,128,128]{2,1,0:T(8,128)(2,1)S(1)} all-to-all(bf16[8,128,128]{2,1,0:T(8,128)(2,1)} %attend_second.1), channel_id=1, replica_groups=mesh['section'=2,'seq'=8,'tp'=2] {'seq'}, dimensions={0} | all-to-all | bytes 524288 | tf_op jit(solution)/shard_map/all_to_all | solution.py:543
  119.1 1.6 %collective-permute-start.19 = (bf16[128,1536]{1,0:T(8,128)(2,1)S(1)}, bf16[128,1536]{1,0:T(8,128)(2,1)S(1)}, u32[]{:S(2)}, u32[]{:S(2)}) collective-permute-start(bf16[128,1536]{1,0:T(8,128)(2,1)S(1)} %out_sent.1), channel_id=1, source_target_pairs={{0,1},{1,0},{2,3},{3,2},{4,5},{5,4},{6,7},{7,6},{8,9},{9,8},{10,11... | collective-permute-start | bytes 1179656 | tf_op jit(solution)/shard_map/ppermute | solution.py:480
  122.1 7.6 %collective-permute-done.19 = bf16[128,1536]{1,0:T(8,128)(2,1)S(1)} collective-permute-done((bf16[128,1536]{1,0:T(8,128)(2,1)S(1)}, bf16[128,1536]{1,0:T(8,128)(2,1)S(1)}, u32[]{:S(2)}, u32[]{:S(2)}) %collective-permute-start.19) | collective-permute-done | bytes 393248 | tf_op jit(solution)/shard_map/ppermute | solution.py:480
  (106 shorter events, 25.0 us)
Async XLA Ops:
  3.0 18.0 %collective-permute-start.2 = (bf16[64,3072]{1,0:T(8,128)(2,1)}, bf16[64,3072]{1,0:T(8,128)(2,1)}, u32[]{:S(2)}, u32[]{:S(2)}) collective-permute-start(bf16[64,3072]{1,0:T(8,128)(2,1)} %get-tuple-element.30), channel_id=1, source_target_pairs={{0,4},{2,6},{4,0},{6,2},{8,12},{10,14},{12,8},{14,10},{1,5},{3,7},... | collective-permute-start | bytes 1179656 | tf_op jit(solution)/shard_map/ppermute | solution.py:474
  6.1 18.2 %collective-permute-start = (bf16[64,3072]{1,0:T(8,128)(2,1)}, bf16[64,3072]{1,0:T(8,128)(2,1)}, u32[]{:S(2)}, u32[]{:S(2)}) collective-permute-start(bf16[64,3072]{1,0:T(8,128)(2,1)} %get-tuple-element.30), channel_id=1, source_target_pairs={{4,8},{6,10},{8,4},{10,6},{5,9},{7,11},{9,5},{11,7},{20,24},{22,26... | collective-permute-start | bytes 1179656 | tf_op jit(solution)/shard_map/ppermute | solution.py:474
  9.6 27.7 %all-to-all-start = ((bf16[8,384,128]{2,1,0:T(8,128)(2,1)}), bf16[8,384,128]{2,1,0:T(8,128)(2,1)S(1)}, u32[]{:S(2)}, u32[]{:S(2)}) async-start(bf16[8,384,128]{2,1,0:T(8,128)(2,1)} %kv_weights.1), calls=%async_computation | async-start | bytes 1572864 | tf_op jit(solution)/shard_map/all_to_all | solution.py:469
  14.5 54.6 %collective-permute-start.10 = (bf16[128,3072]{1,0:T(8,128)(2,1)}, bf16[128,3072]{1,0:T(8,128)(2,1)}, u32[]{:S(2)}, u32[]{:S(2)}) collective-permute-start(bf16[128,3072]{1,0:T(8,128)(2,1)} %get-tuple-element.43.refs_6_.refs_0_), channel_id=1, source_target_pairs={{0,2},{2,0},{4,6},{6,4},{8,10},{10,8},{12,14},{14,12},{1,3},{3,1},... | collective-permute-start | bytes 2359304 | tf_op jit(solution)/shard_map/ppermute | solution.py:477
  21.4 34.6 %collective-permute-start.3 = (bf16[64,3072]{1,0:T(8,128)(2,1)}, bf16[64,3072]{1,0:T(8,128)(2,1)}, u32[]{:S(2)}, u32[]{:S(2)}) collective-permute-start(bf16[64,3072]{1,0:T(8,128)(2,1)} %collective-permute-done.2.refs_8_.refs_2_), channel_id=1, source_target_pairs={{0,1},{1,0},{2,3},{3,2},{4,5},{5,4},{6,7},{7,6},{8,9},{9,8},{10,11... | collective-permute-start | bytes 1179656 | tf_op jit(solution)/shard_map/ppermute | solution.py:480
  22.9 21.9 %collective-permute-start.4 = (bf16[64,3072]{1,0:T(8,128)(2,1)}, bf16[64,3072]{1,0:T(8,128)(2,1)}, u32[]{:S(2)}, u32[]{:S(2)}) collective-permute-start(bf16[64,3072]{1,0:T(8,128)(2,1)} %collective-permute-done.2.refs_8_.refs_2_), channel_id=1, source_target_pairs={{4,8},{6,10},{8,4},{10,6},{5,9},{7,11},{9,5},{11,7},{20,24},{22,26... | collective-permute-start | bytes 1179656 | tf_op jit(solution)/shard_map/ppermute | solution.py:474
  24.3 30.6 %collective-permute-start.1 = (bf16[64,3072]{1,0:T(8,128)(2,1)}, bf16[64,3072]{1,0:T(8,128)(2,1)}, u32[]{:S(2)}, u32[]{:S(2)}) collective-permute-start(bf16[64,3072]{1,0:T(8,128)(2,1)} %collective-permute-done), channel_id=1, source_target_pairs={{4,0},{6,2},{8,12},{10,14},{5,1},{7,3},{9,13},{11,15},{20,16},{22,... | collective-permute-start | bytes 1179656 | tf_op jit(solution)/shard_map/ppermute | solution.py:474
  38.4 9.4 %collective-permute-start.7 = (bf16[4,384,128]{2,1,0:T(8,128)(2,1)S(1)}, bf16[4,384,128]{2,1,0:T(8,128)(2,1)S(1)}, u32[]{:S(2)}, u32[]{:S(2)}) collective-permute-start(bf16[4,384,128]{2,1,0:T(8,128)(2,1)S(1)} %get-tuple-element.58), channel_id=1, source_target_pairs={{0,16},{16,0},{1,17},{17,1},{2,18},{18,2},{3,19},{19,3},{4,20},{20... | collective-permute-start | bytes 1179656 | tf_op jit(solution)/shard_map/ppermute | solution.py:500
  44.8 24.2 %collective-permute-start.11 = (bf16[64,3072]{1,0:T(8,128)(2,1)}, bf16[64,3072]{1,0:T(8,128)(2,1)}, u32[]{:S(2)}, u32[]{:S(2)}) collective-permute-start(bf16[64,3072]{1,0:T(8,128)(2,1)} %collective-permute-done.2.refs_8_.refs_2_), channel_id=1, source_target_pairs={{0,2},{2,0},{4,6},{6,4},{8,10},{10,8},{12,14},{14,12},{1,3},{3,1},... | collective-permute-start | bytes 1179656 | tf_op jit(solution)/shard_map/ppermute | solution.py:477
  47.8 11.0 %collective-permute-start.5 = (bf16[64,3072]{1,0:T(8,128)(2,1)}, bf16[64,3072]{1,0:T(8,128)(2,1)}, u32[]{:S(2)}, u32[]{:S(2)}) collective-permute-start(bf16[64,3072]{1,0:T(8,128)(2,1)} %collective-permute-done.4), channel_id=1, source_target_pairs={{4,0},{6,2},{8,12},{10,14},{5,1},{7,3},{9,13},{11,15},{20,16},{22,... | collective-permute-start | bytes 1179656 | tf_op jit(solution)/shard_map/ppermute | solution.py:474
  49.1 41.3 %all-to-all-start.1 = ((bf16[8,528,128]{2,1,0:T(8,128)(2,1)}), bf16[8,528,128]{2,1,0:T(8,128)(2,1)}, u32[]{:S(2)}, u32[]{:S(2)}) async-start(bf16[8,528,128]{2,1,0:T(8,128)(2,1)} %direct_rows.1), calls=%async_computation.1 | async-start | bytes 2162688 | tf_op jit(solution)/shard_map/all_to_all | solution.py:502
  56.0 26.6 %copy-start.2 = (bf16[64,3072]{1,0:T(8,128)(2,1)}, bf16[64,3072]{1,0:T(8,128)(2,1)S(1)}, u32[]{:S(2)}) copy-start(bf16[64,3072]{1,0:T(8,128)(2,1)S(1)} %broadcast_select_fusion.1.refs_6_) | copy-start | bytes 1179652
  56.0 11.6 %collective-permute-start.6 = (bf16[64,3072]{1,0:T(8,128)(2,1)S(1)}, bf16[64,3072]{1,0:T(8,128)(2,1)S(1)}, u32[]{:S(2)}, u32[]{:S(2)}) collective-permute-start(bf16[64,3072]{1,0:T(8,128)(2,1)S(1)} %broadcast_select_fusion.1.refs_6_), channel_id=1, source_target_pairs={{0,1},{1,0},{2,3},{3,2},{4,5},{5,4},{6,7},{7,6},{8,9},{9,8},{10,11... | collective-permute-start | bytes 1179656 | tf_op jit(solution)/shard_map/ppermute | solution.py:480
  57.6 12.0 %collective-permute-start.12 = (bf16[64,3072]{1,0:T(8,128)(2,1)}, bf16[64,3072]{1,0:T(8,128)(2,1)S(1)}, u32[]{:S(2)}, u32[]{:S(2)}) collective-permute-start(bf16[64,3072]{1,0:T(8,128)(2,1)} %collective-permute-done.3.refs_9_.refs_3_), channel_id=1, source_target_pairs={{0,2},{2,0},{4,6},{6,4},{8,10},{10,8},{12,14},{14,12},{1,3},{3,1},... | collective-permute-start | bytes 1179656 | tf_op jit(solution)/shard_map/ppermute | solution.py:477
  58.8 10.8 %collective-permute-start.9 = (bf16[4,384,128]{2,1,0:T(8,128)(2,1)}, bf16[4,384,128]{2,1,0:T(8,128)(2,1)S(1)}, u32[]{:S(2)}, u32[]{:S(2)}) collective-permute-start(bf16[4,384,128]{2,1,0:T(8,128)(2,1)} %get-tuple-element.57), channel_id=1, source_target_pairs={{0,16},{16,0},{1,17},{17,1},{2,18},{18,2},{3,19},{19,3},{4,20},{20... | collective-permute-start | bytes 1179656 | tf_op jit(solution)/shard_map/ppermute | solution.py:500
  67.6 10.8 %collective-permute-start.8 = (bf16[64,3072]{1,0:T(8,128)(2,1)S(1)}, bf16[64,3072]{1,0:T(8,128)(2,1)S(1)}, u32[]{:S(2)}, u32[]{:S(2)}) collective-permute-start(bf16[64,3072]{1,0:T(8,128)(2,1)S(1)} %broadcast_select_fusion.refs_10_), channel_id=1, source_target_pairs={{0,1},{1,0},{2,3},{3,2},{4,5},{5,4},{6,7},{7,6},{8,9},{9,8},{10,11... | collective-permute-start | bytes 1179656 | tf_op jit(solution)/shard_map/ppermute | solution.py:480
  69.1 13.4 %collective-permute-start.13 = (bf16[64,3072]{1,0:T(8,128)(2,1)S(1)}, bf16[64,3072]{1,0:T(8,128)(2,1)S(1)}, u32[]{:S(2)}, u32[]{:S(2)}) collective-permute-start(bf16[64,3072]{1,0:T(8,128)(2,1)S(1)} %broadcast_select_fusion.1.refs_6_), channel_id=1, source_target_pairs={{0,2},{2,0},{4,6},{6,4},{8,10},{10,8},{12,14},{14,12},{1,3},{3,1},... | collective-permute-start | bytes 1179656 | tf_op jit(solution)/shard_map/ppermute | solution.py:477
  69.1 13.4 %collective-permute-start.15 = (bf16[64,3072]{1,0:T(8,128)(2,1)S(1)}, bf16[64,3072]{1,0:T(8,128)(2,1)S(1)}, u32[]{:S(2)}, u32[]{:S(2)}) collective-permute-start(bf16[64,3072]{1,0:T(8,128)(2,1)S(1)} %broadcast_select_fusion.refs_10_), channel_id=1, source_target_pairs={{0,2},{2,0},{4,6},{6,4},{8,10},{10,8},{12,14},{14,12},{1,3},{3,1},... | collective-permute-start | bytes 1179656 | tf_op jit(solution)/shard_map/ppermute | solution.py:477
  69.6 12.9 %collective-permute-start.14 = (bf16[64,3072]{1,0:T(8,128)(2,1)S(1)}, bf16[64,3072]{1,0:T(8,128)(2,1)S(1)}, u32[]{:S(2)}, u32[]{:S(2)}) collective-permute-start(bf16[64,3072]{1,0:T(8,128)(2,1)S(1)} %collective-permute-done.6.refs_7_), channel_id=1, source_target_pairs={{0,2},{2,0},{4,6},{6,4},{8,10},{10,8},{12,14},{14,12},{1,3},{3,1},... | collective-permute-start | bytes 1179656 | tf_op jit(solution)/shard_map/ppermute | solution.py:477
  78.4 4.2 %collective-permute-start.16 = (bf16[64,3072]{1,0:T(8,128)(2,1)S(1)}, bf16[64,3072]{1,0:T(8,128)(2,1)S(1)}, u32[]{:S(2)}, u32[]{:S(2)}) collective-permute-start(bf16[64,3072]{1,0:T(8,128)(2,1)S(1)} %collective-permute-done.8.refs_11_), channel_id=1, source_target_pairs={{0,2},{2,0},{4,6},{6,4},{8,10},{10,8},{12,14},{14,12},{1,3},{3,1},... | collective-permute-start | bytes 1179656 | tf_op jit(solution)/shard_map/ppermute | solution.py:477
  78.4 12.0 %collective-permute-start.17 = (bf16[2,512,128]{2,1,0:T(8,128)(2,1)}, bf16[2,512,128]{2,1,0:T(8,128)(2,1)}, u32[]{:S(2)}, u32[]{:S(2)}) collective-permute-start(bf16[2,512,128]{2,1,0:T(8,128)(2,1)} %project_kva.1.kva), channel_id=1, source_target_pairs={{0,16},{1,17},{2,18},{3,19},{4,20},{5,21},{6,22},{7,23},{8,24},{9,... | collective-permute-start | bytes 786440 | tf_op jit(solution)/shard_map/ppermute | solution.py:531
  88.9 11.8 %collective-permute-start.18 = (bf16[2,512,128]{2,1,0:T(8,128)(2,1)}, bf16[2,512,128]{2,1,0:T(8,128)(2,1)S(1)}, u32[]{:S(2)}, u32[]{:S(2)}) collective-permute-start(bf16[2,512,128]{2,1,0:T(8,128)(2,1)} %project_kvb.1.kvb), channel_id=1, source_target_pairs={{0,16},{1,17},{2,18},{3,19},{4,20},{5,21},{6,22},{7,23},{8,24},{9,... | collective-permute-start | bytes 786440 | tf_op jit(solution)/shard_map/ppermute | solution.py:537
  90.4 28.1 %copy-start = (bf16[1024,1536]{1,0:T(8,128)(2,1)S(1)}, bf16[1024,1536]{1,0:T(8,128)(2,1)}, u32[]{:S(2)}) copy-start(bf16[1024,1536]{1,0:T(8,128)(2,1)} %get-tuple-element.54.w_ref) | copy-start | bytes 9437188
  119.1 10.5 %collective-permute-start.19 = (bf16[128,1536]{1,0:T(8,128)(2,1)S(1)}, bf16[128,1536]{1,0:T(8,128)(2,1)S(1)}, u32[]{:S(2)}, u32[]{:S(2)}) collective-permute-start(bf16[128,1536]{1,0:T(8,128)(2,1)S(1)} %out_sent.1), channel_id=1, source_target_pairs={{0,1},{1,0},{2,3},{3,2},{4,5},{5,4},{6,7},{7,6},{8,9},{9,8},{10,11... | collective-permute-start | bytes 1179656 | tf_op jit(solution)/shard_map/ppermute | solution.py:480
  (17 other events, 151.0 us)
